TPU v7x, 128 devices: a whole 4x4x4 slice. The times are simulated.
128 devices in a mesh: dp: 4 (over x), seq: 4 (over y_hi, core), tensor: 8 (over z, y_lo).
Axes of the slice: x: 4, y: 4 (y_hi: 2, y_lo: 2; y = y_hi * 2 + y_lo), z: 4, core: 2. Of those that a mesh axis runs over, the one named last changes fastest.
Arguments:
- encoder_out: bfloat16 [4, 1024, 4096], P('dp', 'seq', 'tensor'), may hold values from -6 to 6
- w_key: bfloat16 [2, 4096, 4096], P(None, None, 'tensor'), may hold values from -0.09375 to 0.09375
- w_value: bfloat16 [2, 4096, 4096], P(None, None, 'tensor'), may hold values from -0.09375 to 0.09375
- queries: bfloat16 [2, 4, 512, 4096], P(None, 'dp', 'seq', 'tensor'), may hold values from -140 to 140
- grad_context: bfloat16 [2, 4, 512, 4096], P(None, 'dp', 'seq', 'tensor'), may hold values from -6 to 6
Outputs:
- grad_queries: bfloat16 [2, 4, 512, 4096], P(None, 'dp', 'seq', 'tensor')
- grad_encoder: bfloat16 [4, 1024, 4096], P('dp', 'seq', 'tensor')
- grad_w_key: bfloat16 [2, 4096, 4096], P(None, ('dp', 'seq'), 'tensor')
- grad_w_value: bfloat16 [2, 4096, 4096], P(None, ('dp', 'seq'), 'tensor')
All inputs are finite; a program needn't handle non-finite values.
Results may differ from a plain program's by a relative error of at most 0.035.
The roundings to bfloat16 on the way count: a program that leaves them out, or rounds other values in their place, can miss the bound.
Values may be sent and summed in bfloat16 or wider, within the bound.
No kernel may reach another device: no remote copies, remote signals or barrier semaphores. Data moves between devices by JAX's collectives and lax.ppermute only.
A program may use at most 128 MiB of HBM per device.

v0:
```python
import jax
import jax.numpy as jnp
from jax import lax
from jax.sharding import PartitionSpec as P

DH = 256


def on_device(encoder_out, w_key, w_value, queries, grad_context):
    layers = w_key.shape[0]
    full_enc = lax.all_gather(encoder_out, "tensor", axis=2, tiled=True)
    batch, rows, width = full_enc.shape
    flat_enc = full_enc.reshape(batch * rows, width)
    scale = DH ** (-0.5)

    def project(layer):
        keys = (
            jnp.dot(flat_enc, w_key[layer], preferred_element_type=jnp.float32)
            .astype(jnp.bfloat16)
            .reshape(batch, rows, -1)
        )
        values = (
            jnp.dot(flat_enc, w_value[layer], preferred_element_type=jnp.float32)
            .astype(jnp.bfloat16)
            .reshape(batch, rows, -1)
        )
        return (keys, values)

    def attend_keys(layer):
        keys_local, values_local = project(layer)
        keys, values = (
            lax.all_gather(keys_local, "seq", axis=1, tiled=True),
            lax.all_gather(values_local, "seq", axis=1, tiled=True),
        )
        query_rows = queries[layer]
        grad_rows = grad_context[layer]
        qcount = query_rows.shape[1]
        local_heads = query_rows.shape[2] // DH
        all_rows = keys.shape[1]
        query4 = query_rows.reshape(batch, qcount, local_heads, DH)
        grad4 = grad_rows.reshape(batch, qcount, local_heads, DH)
        keys4 = keys.reshape(batch, all_rows, local_heads, DH)
        values4 = values.reshape(batch, all_rows, local_heads, DH)
        scores = (
            jnp.einsum("bqhe,bkhe->bhqk", query4, keys4, preferred_element_type=jnp.float32) * scale
        )
        probs = jax.nn.softmax(scores, axis=-1)
        dprobs = jnp.einsum("bqhe,bkhe->bhqk", grad4, values4, preferred_element_type=jnp.float32)
        delta = jnp.sum(probs * dprobs, axis=-1, keepdims=True)
        dscores = (probs * (dprobs - delta) * scale).astype(jnp.bfloat16)
        probs_low = probs.astype(jnp.bfloat16)
        grad_q = jnp.einsum("bhqk,bkhe->bqhe", dscores, keys4, preferred_element_type=jnp.float32)
        grad_q = grad_q.astype(jnp.bfloat16).reshape(batch, qcount, -1)
        grad_k = jnp.einsum(
            "bhqk,bqhe->bkhe", dscores, query4, preferred_element_type=jnp.float32
        ).reshape(batch, all_rows, -1)
        grad_v = jnp.einsum(
            "bhqk,bqhe->bkhe", probs_low, grad4, preferred_element_type=jnp.float32
        ).reshape(batch, all_rows, -1)
        sum_k, sum_v = (
            lax.psum_scatter(
                grad_k.astype(jnp.bfloat16), "seq", scatter_dimension=1, tiled=True
            ).astype(jnp.float32),
            lax.psum_scatter(
                grad_v.astype(jnp.bfloat16), "seq", scatter_dimension=1, tiled=True
            ).astype(jnp.float32),
        )
        return (grad_q, sum_k.astype(jnp.bfloat16), sum_v.astype(jnp.bfloat16))

    grad_q_list = []
    grad_wk_list = []
    grad_wv_list = []
    enc_shares = jnp.zeros((batch, rows, width // lax.axis_size("tensor")), jnp.float32)
    for layer in range(layers):
        grad_q, low_k, low_v = attend_keys(layer)
        enc_term = jnp.einsum(
            "bsh,dh->bsd", low_k, w_key[layer], preferred_element_type=jnp.float32
        )
        enc_term = enc_term + jnp.einsum(
            "bsh,dh->bsd", low_v, w_value[layer], preferred_element_type=jnp.float32
        )
        joined = jnp.concatenate([low_k, low_v], axis=2).reshape(batch * rows, -1)
        grads = lax.psum_scatter(
            jnp.einsum("rd,rh->dh", flat_enc, joined, preferred_element_type=jnp.float32).astype(
                jnp.bfloat16
            ),
            ("dp", "seq"),
            scatter_dimension=0,
            tiled=True,
        ).astype(jnp.float32)
        half = low_k.shape[2]
        enc_term, grad_wk, grad_wv = (
            enc_term,
            grads[:, :half].astype(jnp.bfloat16),
            grads[:, half:].astype(jnp.bfloat16),
        )
        grad_q_list.append(grad_q)
        grad_wk_list.append(grad_wk)
        grad_wv_list.append(grad_wv)
        enc_shares = enc_shares + lax.psum_scatter(
            enc_term, "tensor", scatter_dimension=2, tiled=True
        )
    return (
        jnp.stack(grad_q_list),
        enc_shares.astype(jnp.bfloat16),
        jnp.stack(grad_wk_list),
        jnp.stack(grad_wv_list),
    )


def solution(mesh):
    placed = (
        P("dp", "seq", "tensor"),
        P(None, None, "tensor"),
        P(None, None, "tensor"),
        P(None, "dp", "seq", "tensor"),
        P(None, "dp", "seq", "tensor"),
    )
    return jax.shard_map(
        on_device,
        mesh=mesh,
        in_specs=placed,
        out_specs=(
            P(None, "dp", "seq", "tensor"),
            P("dp", "seq", "tensor"),
            P(None, ("dp", "seq"), "tensor"),
            P(None, ("dp", "seq"), "tensor"),
        ),
        check_vma=False,
    )
```

profile of v0, /device:TPU:0, one launch (start us, length us, event | category | flops | bytes accessed | tf_op | source)
XLA Modules:
  0.0 613.7 jit_solution(2924226980580428709)
XLA Ops:
  7.9 56.5 %all-gather.10.cloned.1.call-done = bf16[1,256,4096]{2,1,0:T(8,128)(2,1)} async-done(((bf16[1,256,512]{2,1,0:T(8,128)(2,1)}), bf16[1,256,4096]{2,1,0:T(8,128)(2,1)}) %all-gather.10.cloned.1.call-update) | async-done | bytes 2097168 | tf_op jit(solution)/shard_map/all_gather | solution.py:11
  64.5 4.9 fusion.58
  69.5 4.1 fusion.63
  73.7 4.1 fusion.48
  77.9 4.4 fusion.53
  84.0 5.5 all-gather.16.cloned.1.call-done
  89.5 1.5 copy.68
  91.5 1.0 copy-done.2
  92.5 1.3 fusion.106
  93.8 18.1 %all-gather.18.cloned.1.call-done = bf16[1024,512]{1,0:T(8,128)(2,1)} async-done(((bf16[256,512]{1,0:T(8,128)(2,1)}), bf16[1024,512]{1,0:T(8,128)(2,1)}) %all-gather.18.cloned.1.call-update) | async-done | bytes 1048592 | tf_op jit(solution)/shard_map/all_gather | solution.py:33
  111.9 2.6 convolution_bitcast_fusion
  114.5 3.8 convolution_convert_fusion.1
  118.4 1.0 copy.63
  119.5 1.0 copy.64
  120.5 13.7 %all-gather.12.cloned.1.call-done = bf16[1024,512]{1,0:T(8,128)(2,1)} async-done(((bf16[256,512]{1,0:T(8,128)(2,1)}), bf16[1024,512]{1,0:T(8,128)(2,1)}) %all-gather.12.cloned.1.call-update) | async-done | bytes 1048592 | tf_op jit(solution)/shard_map/all_gather | solution.py:32
  134.2 2.3 copy.67
  136.5 1.8 fusion.45
  138.3 1.0 copy-done.3
  139.3 1.4 fusion.107
  140.6 15.9 %all-gather.14.cloned.1.call-done = bf16[1024,512]{1,0:T(8,128)(2,1)} async-done(((bf16[256,512]{1,0:T(8,128)(2,1)}), bf16[1024,512]{1,0:T(8,128)(2,1)}) %all-gather.14.cloned.1.call-update) | async-done | bytes 1048592 | tf_op jit(solution)/shard_map/all_gather | solution.py:33
  156.5 2.7 convolution_bitcast_fusion.1
  159.2 3.8 convolution_convert_fusion.3
  163.1 3.2 convolution_convert_fusion
  166.3 3.2 convolution_convert_fusion.2
  169.8 20.5 %reduce-scatter.12.cloned.1.call-done = bf16[1,256,512]{1,2,0:T(8,128)(2,1)} async-done(((bf16[1,1024,512]{1,2,0:T(8,128)(2,1)}), bf16[1,256,512]{1,2,0:T(8,128)(2,1)}) %reduce-scatter.12.cloned.1.call-update) | async-done | bytes 262160 | tf_op jit(solution)/shard_map/reduce_scatter | solution.py:61
  190.3 5.5 fusion.9
  195.8 28.5 %reduce-scatter.8.cloned.1.call-done = bf16[1,256,512]{1,2,0:T(8,128)(2,1)} async-done(((bf16[1,1024,512]{1,2,0:T(8,128)(2,1)}), bf16[1,256,512]{1,2,0:T(8,128)(2,1)}) %reduce-scatter.8.cloned.1.call-update) | async-done | bytes 262160 | tf_op jit(solution)/shard_map/reduce_scatter | solution.py:61
  224.3 5.5 fusion.16
  229.9 28.4 %reduce-scatter.14.cloned.1.call-done = bf16[1,256,512]{1,2,0:T(8,128)(2,1)} async-done(((bf16[1,1024,512]{1,2,0:T(8,128)(2,1)}), bf16[1,256,512]{1,2,0:T(8,128)(2,1)}) %reduce-scatter.14.cloned.1.call-update) | async-done | bytes 262160 | tf_op jit(solution)/shard_map/reduce_scatter | solution.py:64
  258.2 6.8 %convolution_add_fusion = f32[256,4096]{1,0:T(8,128)} fusion(f32[256,4096]{1,0:T(8,128)} %fusion.9, bf16[2,4096,512]{2,1,0:T(8,128)(2,1)} %param.7, bf16[1,256,512]{1,2,0:T(8,128)(2,1)} %reduce-scatter.14.cloned.1.call-done), kind=kOutput, calls=%fused_computation.6 | convolution fusion | flops 1074790400 | bytes 12845056 | tf_op jit(solution)/shard_map/bsh,dh->bsd/dot_general | solution.py:79
  265.0 27.3 %reduce-scatter.10.cloned.1.call-done = bf16[1,256,512]{1,2,0:T(8,128)(2,1)} async-done(((bf16[1,1024,512]{1,2,0:T(8,128)(2,1)}), bf16[1,256,512]{1,2,0:T(8,128)(2,1)}) %reduce-scatter.10.cloned.1.call-update) | async-done | bytes 262160 | tf_op jit(solution)/shard_map/reduce_scatter | solution.py:64
  292.3 8.0 %fusion.5 = f32[1,256,4096]{2,1,0:T(8,128)} fusion(f32[256,4096]{1,0:T(8,128)} %convolution_add_fusion, f32[256,4096]{1,0:T(8,128)} %fusion.16, bf16[2,4096,512]{2,1,0:T(8,128)(2,1)} %param.7, bf16[1,256,512]{1,2,0:T(8,128)(2,1)} %reduce-scatter.10.cloned.1.call-done), kind=kOutput, calls=%fused_computation.9 | convolution fusion | flops 1075838976 | bytes 17039360 | tf_op jit(solution)/shard_map/bsh,dh->bsd/dot_general | solution.py:79
  300.4 0.9 copy-done.4
  301.2 6.5 %convert_bitcast_fusion.1 = bf16[4096,1024]{0,1:T(8,128)(2,1)} fusion(bf16[1,256,4096]{2,1,0:T(8,128)(2,1)S(1)} %copy-done, bf16[1,256,512]{1,2,0:T(8,128)(2,1)S(1)} %copy-done.4, bf16[1,256,512]{1,2,0:T(8,128)(2,1)} %reduce-scatter.8.cloned.1.call-done), kind=kOutput, calls=%fused_computation.5 | convolution fusion | flops 2152726528 | bytes 11010048 | tf_op jit(solution)/shard_map/rd,rh->dh/dot_general | solution.py:84
  308.0 0.7 copy-done.5
  308.7 6.5 %convert_bitcast_fusion = bf16[4096,1024]{0,1:T(8,128)(2,1)} fusion(bf16[1,256,4096]{2,1,0:T(8,128)(2,1)S(1)} %copy-done, bf16[1,256,512]{1,2,0:T(8,128)(2,1)} %reduce-scatter.14.cloned.1.call-done, bf16[1,256,512]{1,2,0:T(8,128)(2,1)S(1)} %copy-done.5), kind=kOutput, calls=%fused_computation.4 | convolution fusion | flops 2152726528 | bytes 11010048 | tf_op jit(solution)/shard_map/rd,rh->dh/dot_general | solution.py:84
  315.3 1.2 copy-done.1
  316.5 2.9 convolution_convert_fusion.5
  319.5 2.9 convolution_convert_fusion.4
  322.5 0.7 pad_maximum_fusion.2
  323.3 68.0 %reduce-scatter.20.cloned.1.call-done = f32[1,256,512]{2,1,0:T(8,128)} async-done(((f32[1,256,4096]{2,1,0:T(8,128)}), f32[1,256,512]{2,1,0:T(8,128)}) %reduce-scatter.20.cloned.1.call-update) | async-done | bytes 524304 | tf_op jit(solution)/shard_map/reduce_scatter | solution.py:100
  391.3 1.8 convert_element_type.201
  393.1 104.9 %reduce-scatter.16.cloned.1.call-done = bf16[256,1024]{0,1:T(8,128)(2,1)} async-done(((bf16[4096,1024]{0,1:T(8,128)(2,1)}), bf16[256,1024]{0,1:T(8,128)(2,1)}) %reduce-scatter.16.cloned.1.call-update) | async-done | bytes 524304 | tf_op jit(solution)/shard_map/reduce_scatter | solution.py:83
  498.0 1.1 slice_bitcast_fusion.1
  499.1 104.5 %reduce-scatter.18.cloned.1.call-done = bf16[256,1024]{0,1:T(8,128)(2,1)} async-done(((bf16[4096,1024]{0,1:T(8,128)(2,1)}), bf16[256,1024]{0,1:T(8,128)(2,1)}) %reduce-scatter.18.cloned.1.call-update) | async-done | bytes 524304 | tf_op jit(solution)/shard_map/reduce_scatter | solution.py:83
  603.6 1.1 slice_bitcast_fusion
  604.8 1.0 copy.51
  605.8 1.0 copy.52
  (43 shorter events, 4.2 us)
Async XLA Ops:
  7.2 57.3 %all-gather.10.cloned.1.call-start = ((), (), s32[]{:S(2)}) async-start(), calls=%async_computation.7 | async-start | bytes 2359296 | tf_op jit(solution)/shard_map/all_gather | solution.py:11
  7.9 81.6 %all-gather.16.cloned.1.call-start = ((), (), s32[]{:S(2)}) async-start(), calls=%async_computation.16 | async-start | bytes 1310720 | tf_op jit(solution)/shard_map/all_gather | solution.py:32
  64.5 5.0 copy-start
  69.4 42.5 %all-gather.18.cloned.1.call-start = ((), (), s32[]{:S(2)}) async-start(), calls=%async_computation.17 | async-start | bytes 1310720 | tf_op jit(solution)/shard_map/all_gather | solution.py:33
  73.6 60.6 %all-gather.12.cloned.1.call-start = ((), (), s32[]{:S(2)}) async-start(), calls=%async_computation.14 | async-start | bytes 1310720 | tf_op jit(solution)/shard_map/all_gather | solution.py:32
  77.9 4.5 copy-start.6
  77.9 5.3 copy-start.7
  77.9 78.6 %all-gather.14.cloned.1.call-start = ((), (), s32[]{:S(2)}) async-start(), calls=%async_computation.15 | async-start | bytes 1310720 | tf_op jit(solution)/shard_map/all_gather | solution.py:33
  82.3 107.9 %reduce-scatter.12.cloned.1.call-start = ((), (), s32[]{:S(2)}) async-start(), calls=%async_computation.10 | async-start | bytes 1310720 | tf_op jit(solution)/shard_map/reduce_scatter | solution.py:61
  91.5 1.0 copy-start.2
  118.4 106.0 %reduce-scatter.8.cloned.1.call-start = ((), (), s32[]{:S(2)}) async-start(), calls=%async_computation.8 | async-start | bytes 1310720 | tf_op jit(solution)/shard_map/reduce_scatter | solution.py:61
  138.3 1.0 copy-start.3
  163.0 95.2 %reduce-scatter.14.cloned.1.call-start = ((), (), s32[]{:S(2)}) async-start(), calls=%async_computation.11 | async-start | bytes 1310720 | tf_op jit(solution)/shard_map/reduce_scatter | solution.py:64
  166.3 126.0 %reduce-scatter.10.cloned.1.call-start = ((), (), s32[]{:S(2)}) async-start(), calls=%async_computation.9 | async-start | bytes 1310720 | tf_op jit(solution)/shard_map/reduce_scatter | solution.py:64
  169.6 221.7 %reduce-scatter.20.cloned.1.call-start = ((), (), s32[]{:S(2)}) async-start(), calls=%async_computation.18 | async-start | bytes 4718592 | tf_op jit(solution)/shard_map/reduce_scatter | solution.py:100
  300.3 0.9 copy-start.4
  300.3 197.7 %reduce-scatter.16.cloned.1.call-start = ((), (), s32[]{:S(2)}) async-start(), calls=%async_computation.12 | async-start | bytes 8912896 | tf_op jit(solution)/shard_map/reduce_scatter | solution.py:83
  307.7 1.0 copy-start.5
  307.8 295.9 %reduce-scatter.18.cloned.1.call-start = ((), (), s32[]{:S(2)}) async-start(), calls=%async_computation.13 | async-start | bytes 8912896 | tf_op jit(solution)/shard_map/reduce_scatter | solution.py:83
  315.3 1.2 copy-start.1
Sparse Core Ops, SparseCore 0:
  9.6 54.7 all-gather.9
  69.5 19.8 all-gather.15
  91.7 20.1 all-gather.17
  114.0 20.1 all-gather.11
  136.3 20.1 all-gather.13
  159.0 31.2 reduce-scatter.11
  193.1 31.1 reduce-scatter.7
  227.0 31.2 reduce-scatter.13
  261.0 31.1 reduce-scatter.9
  300.4 90.8 reduce-scatter.19
  395.6 102.3 reduce-scatter.15
  502.2 101.3 reduce-scatter.17
where the time goes:
time: 614 us
  waiting for transfers between devices  493 us (80%)
  matrix products  83.8 us (14%)
  local copies, waits for them, and re-layouts  16.5 us (3%)
  between operations  14.3 us (2%)
    reduce_scatter x2, waiting for transfers between devices, on_device(): lax.psum_scatter(jnp.einsum('rd,rh->dh', flat_enc, joined, preferred_elem...  209 us
    reduce_scatter x1, waiting for transfers between devices, on_device(): lax.psum_scatter(enc_term, 'tensor', scatter_dimension=2, tiled=True)  68 us
    all_gather x1, waiting for transfers between devices, on_device(): full_enc = lax.all_gather(encoder_out, 'tensor', axis=2, tiled=True)  56.5 us
    reduce_scatter x2, waiting for transfers between devices, attend_keys(): lax.psum_scatter(grad_v.astype(jnp.bfloat16), 'seq', scatter_dimension=1,...  55.6 us
    reduce_scatter x2, waiting for transfers between devices, attend_keys(): lax.psum_scatter(grad_k.astype(jnp.bfloat16), 'seq', scatter_dimension=1,...  49 us
    all_gather x2, waiting for transfers between devices, attend_keys(): lax.all_gather(values_local, 'seq', axis=1, tiled=True)  34 us
    all_gather x2, waiting for transfers between devices, attend_keys(): lax.all_gather(keys_local, 'seq', axis=1, tiled=True)  19.2 us
    dot_general x2, matrix products, on_device(): jnp.einsum('bsh,dh->bsd', low_v, w_value[layer], preferred_element_type=j...  14.8 us
  transfers between devices with their start and end apart: 12, of which 12 were waited for; matrix products, arithmetic and copies ran while one was open for 14% of the time, Pallas kernels for 0%

commit v1 on v0

v1 whole, which is shorter than its diff:
```python
import functools

import jax
import jax.numpy as jnp
from jax import lax
from jax.experimental import pallas as pl
from jax.experimental.pallas import tpu as pltpu
from jax.sharding import PartitionSpec as P

DH = 256
BF = jnp.bfloat16
F32 = jnp.float32
NT = (((1,), (1,)), ((), ()))
TN = (((0,), (0,)), ((), ()))
MB = 1024 * 1024


def params(mb):
    return pltpu.CompilerParams(vmem_limit_bytes=mb * MB)


def cost(flops, nbytes):
    return pl.CostEstimate(flops=flops, bytes_accessed=nbytes, transcendentals=0)


def swap_core(x):
    return lax.ppermute(x, "seq", [(s, s ^ 1) for s in range(4)])


def swap_yhi(x):
    return lax.ppermute(x, "seq", [(s, s ^ 2) for s in range(4)])


def swap_ylo(x):
    return lax.ppermute(x, "tensor", [(t, t ^ 1) for t in range(8)])


def swap_x(x, m):
    return lax.ppermute(x, "dp", [(d, d ^ m) for d in range(4)])


def swap_z(x, m):
    return lax.ppermute(x, "tensor", [(t, t ^ (2 * m)) for t in range(8)])


def shift_z(x, k):
    return lax.ppermute(x, "tensor", [(t, (t + 2 * k) % 8) for t in range(8)])


def shift_y(x, k):
    pairs = []
    for s in range(4):
        for t in range(8):
            y = ((s // 2) * 2 + t % 2 + k) % 4
            pairs.append((s * 8 + t, ((y // 2) * 2 + s % 2) * 8 + (t // 2) * 2 + y % 2))
    return lax.ppermute(x, ("seq", "tensor"), pairs)


def place(idx, k, j, first):
    y = idx[5]
    z = idx[3]
    if first:
        yy, zz = lax.rem(y + 4 - j, 4), lax.rem(z + 4 - k, 4)
    else:
        yy, zz = lax.rem(y + 4 - k, 4), lax.rem(z + 4 - j, 4)
    hh = lax.div(yy, 2)
    tt = zz * 2 + lax.rem(yy, 2)
    return hh, tt


def project_body(idx, *refs):
    pieces = refs[:8]
    wk, wv, send, keep, enc, acc = refs[8:]
    i = pl.program_id(0)
    c = idx[1]

    @pl.when(i == 0)
    def _():
        for half in range(2):
            for k in range(4):
                for j in range(4):
                    hh, tt = place(idx, k, j, half == 0)
                    rows = pl.ds(pl.multiple_of(hh * 256, 256), 256)
                    chunk = lax.div(tt, 2)
                    cols = pl.ds(
                        pl.multiple_of(lax.rem(tt, 2) * 512 + half * 256, 256), 256
                    )
                    enc[chunk, rows, cols] = pieces[half * 4 + k][j]
        acc[...] = jnp.zeros_like(acc)

    e = enc[i]
    acc[:, :512] += jnp.dot(e, wk[0], preferred_element_type=F32)
    acc[:, 512:] += jnp.dot(e, wv[0], preferred_element_type=F32)

    @pl.when(i == 3)
    def _():
        mine = pl.multiple_of(c * 256, 256)
        other = pl.multiple_of((1 - c) * 256, 256)
        keep[:, :256] = acc[:, pl.ds(mine, 256)].astype(BF)
        keep[:, 256:] = acc[:, pl.ds(mine + 512, 256)].astype(BF)
        send[:, :256] = acc[:, pl.ds(other, 256)].astype(BF)
        send[:, 256:] = acc[:, pl.ds(other + 512, 256)].astype(BF)


def project(idx, pieces, w_key, w_value):
    whole = pl.BlockSpec((4, 256, 256), lambda i, idx: (0, 0, 0))
    wspec = pl.BlockSpec((1, 1024, 512), lambda i, idx: (idx[0], i, 0))
    out = pl.BlockSpec((512, 512), lambda i, idx: (0, 0))
    return pl.pallas_call(
        project_body,
        grid_spec=pltpu.PrefetchScalarGridSpec(
            num_scalar_prefetch=1,
            grid=(4,),
            in_specs=[whole] * 8 + [wspec, wspec],
            out_specs=[out, out],
            scratch_shapes=[pltpu.VMEM((4, 512, 1024), BF), pltpu.VMEM((512, 1024), F32)],
        ),
        out_shape=[jax.ShapeDtypeStruct((512, 512), BF)] * 2,
        compiler_params=params(32),
        cost_estimate=cost(2 * 512 * 4096 * 1024, 14 * MB),
        name="project",
    )(idx, *pieces, w_key, w_value)


def sort_body(idx, *refs):
    pieces = refs[:8]
    keep, send = refs[8:]
    c = idx[1]
    for half in range(2):
        for k in range(4):
            for j in range(4):
                hh, tt = place(idx, k, j, half == 0)
                rows = pl.ds(pl.multiple_of(hh * 256, 256), 256)
                cols = pl.ds(pl.multiple_of(tt * 256, 256), 256)
                piece = pieces[half * 4 + k]

                @pl.when(c == half)
                def _():
                    keep[rows, cols] = piece[j]

                @pl.when(c != half)
                def _():
                    send[rows, cols] = piece[j]


def sort_pieces(idx, pieces):
    whole = pl.BlockSpec((4, 256, 256), lambda i, idx: (0, 0, 0))
    out = pl.BlockSpec((512, 2048), lambda i, idx: (0, 0))
    return pl.pallas_call(
        sort_body,
        grid_spec=pltpu.PrefetchScalarGridSpec(
            num_scalar_prefetch=1, grid=(1,), in_specs=[whole] * 8, out_specs=[out, out]
        ),
        out_shape=[jax.ShapeDtypeStruct((512, 2048), BF)] * 2,
        compiler_params=params(24),
        cost_estimate=cost(0, 8 * MB),
        name="sort_pieces",
    )(idx, *pieces)


def attend_body(kv_own, kv_oth, qg_own, qg_oth, gk, gv, gq, gk_acc, gv_acc):
    scale = DH ** (-0.5)
    gk_acc[...] = jnp.zeros_like(gk_acc)
    gv_acc[...] = jnp.zeros_like(gv_acc)
    for block in range(4):
        src = (qg_own, qg_oth)[block // 2]
        q = src[block % 2, 0]
        g = src[block % 2, 1]
        s = [
            lax.dot_general(kv[:, :256], q, NT, preferred_element_type=F32) * scale
            for kv in (kv_own, kv_oth)
        ]
        top = jnp.maximum(
            jnp.max(s[0], axis=0, keepdims=True), jnp.max(s[1], axis=0, keepdims=True)
        )
        p = [jnp.exp(part - top) for part in s]
        total = jnp.sum(p[0], axis=0, keepdims=True) + jnp.sum(p[1], axis=0, keepdims=True)
        p = [part / total for part in p]
        dp = [
            lax.dot_general(kv[:, 256:], g, NT, preferred_element_type=F32)
            for kv in (kv_own, kv_oth)
        ]
        delta = jnp.sum(p[0] * dp[0], axis=0, keepdims=True) + jnp.sum(
            p[1] * dp[1], axis=0, keepdims=True
        )
        ds = [(a * (b - delta) * scale).astype(BF) for a, b in zip(p, dp)]
        low = [a.astype(BF) for a in p]
        total_q = jnp.zeros((128, 256), F32)
        for part, kv in enumerate((kv_own, kv_oth)):
            rows = slice(part * 512, part * 512 + 512)
            gv_acc[rows] += jnp.dot(low[part], g, preferred_element_type=F32).astype(BF).astype(F32)
            gk_acc[rows] += jnp.dot(ds[part], q, preferred_element_type=F32).astype(BF).astype(F32)
            total_q += lax.dot_general(ds[part], kv[:, :256], TN, preferred_element_type=F32)
        gq[block] = total_q.astype(BF)
    gk[...] = gk_acc[...].astype(BF)
    gv[...] = gv_acc[...].astype(BF)


def attend(kv_own, kv_oth, qg_own, qg_oth):
    return pl.pallas_call(
        attend_body,
        out_shape=[
            jax.ShapeDtypeStruct((1024, 256), BF),
            jax.ShapeDtypeStruct((1024, 256), BF),
            jax.ShapeDtypeStruct((4, 128, 256), BF),
        ],
        scratch_shapes=[pltpu.VMEM((1024, 256), F32)] * 2,
        compiler_params=params(24),
        cost_estimate=cost(10 * 512 * 1024 * 256, 4 * MB),
        name="attend",
    )(kv_own, kv_oth, qg_own, qg_oth)


def weights_body(idx, ta, tb, ea, oa, eb, ob, kc, ko, vc, vo, out_a, out_b):
    c = idx[1]
    mine = pl.multiple_of(c * 256, 256)
    other = pl.multiple_of((1 - c) * 256, 256)
    for e, o, out in ((ea, oa, out_a), (eb, ob, out_b)):
        e1 = e[...]
        o1 = o[...]
        for base, gc, go in ((0, kc, ko), (512, vc, vo)):
            left = lax.dot_general(e1, gc[:512], TN, preferred_element_type=F32)
            left += lax.dot_general(o1, gc[512:], TN, preferred_element_type=F32)
            right = lax.dot_general(e1, go[512:], TN, preferred_element_type=F32)
            right += lax.dot_general(o1, go[:512], TN, preferred_element_type=F32)
            out[0, :, pl.ds(mine + base, 256)] = left.astype(out.dtype)
            out[0, :, pl.ds(other + base, 256)] = right.astype(out.dtype)


def weight_grads(idx, ta, tb, e_keep, e_oth, kc, ko, vc, vo, dtype):
    at_a = pl.BlockSpec((512, 256), lambda i, idx, ta, tb: (0, ta[i]))
    at_b = pl.BlockSpec((512, 256), lambda i, idx, ta, tb: (0, tb[i]))
    whole = pl.BlockSpec((1024, 256), lambda i, idx, ta, tb: (0, 0))
    out = pl.BlockSpec((1, 256, 1024), lambda i, idx, ta, tb: (i, 0, 0))
    return pl.pallas_call(
        weights_body,
        grid_spec=pltpu.PrefetchScalarGridSpec(
            num_scalar_prefetch=3,
            grid=(2,),
            in_specs=[at_a, at_a, at_b, at_b] + [whole] * 4,
            out_specs=[out, out],
        ),
        out_shape=[jax.ShapeDtypeStruct((2, 256, 1024), dtype)] * 2,
        compiler_params=params(24),
        cost_estimate=cost(2 * 1024 * 1024 * 1024, 6 * MB),
        name="weight_grads",
    )(idx, ta, tb, e_keep, e_oth, e_keep, e_oth, kc, ko, vc, vo)


def encoder_body(idx, ta, tb, *refs):
    g_own = refs[0:4]
    g_recv = refs[4]
    weights = (refs[5:9], refs[9:13])
    outs = refs[13:15]
    c = idx[1]
    mine = pl.ds(pl.multiple_of(c * 256, 256), 256)
    other = pl.ds(pl.multiple_of((1 - c) * 256, 256), 256)
    for (wk0, wv0, wk1, wv1), out in zip(weights, outs):
        total = lax.dot_general(g_own[0][...], wk0[0, :, mine], NT, preferred_element_type=F32)
        total += lax.dot_general(g_own[1][...], wk0[0, :, other], NT, preferred_element_type=F32)
        total += lax.dot_general(g_own[2][...], wv0[0, :, mine], NT, preferred_element_type=F32)
        total += lax.dot_general(g_own[3][...], wv0[0, :, other], NT, preferred_element_type=F32)
        total += lax.dot_general(g_recv[0], wk1[0, :, mine], NT, preferred_element_type=F32)
        total += lax.dot_general(g_recv[1], wk1[0, :, other], NT, preferred_element_type=F32)
        total += lax.dot_general(g_recv[2], wv1[0, :, mine], NT, preferred_element_type=F32)
        total += lax.dot_general(g_recv[3], wv1[0, :, other], NT, preferred_element_type=F32)
        out[0] = total.astype(out.dtype)


def encoder_grads(idx, ta, tb, kc, ko, vc, vo, g_recv, w_key, w_value, dtype):
    first = pl.BlockSpec((256, 256), lambda i, idx, ta, tb: (idx[0], 0))
    second = pl.BlockSpec((256, 256), lambda i, idx, ta, tb: (idx[0] + 2, 0))
    recv = pl.BlockSpec((4, 256, 256), lambda i, idx, ta, tb: (0, 0, 0))
    own_a = pl.BlockSpec((1, 512, 512), lambda i, idx, ta, tb: (idx[0], ta[i], 0))
    oth_a = pl.BlockSpec((1, 512, 512), lambda i, idx, ta, tb: (1 - idx[0], ta[i], 0))
    own_b = pl.BlockSpec((1, 512, 512), lambda i, idx, ta, tb: (idx[0], tb[i], 0))
    oth_b = pl.BlockSpec((1, 512, 512), lambda i, idx, ta, tb: (1 - idx[0], tb[i], 0))
    out = pl.BlockSpec((1, 256, 512), lambda i, idx, ta, tb: (i, 0, 0))
    return pl.pallas_call(
        encoder_body,
        grid_spec=pltpu.PrefetchScalarGridSpec(
            num_scalar_prefetch=3,
            grid=(2,),
            in_specs=[first, second, first, second, recv]
            + [own_a, own_a, oth_a, oth_a, own_b, own_b, oth_b, oth_b],
            out_specs=[out, out],
        ),
        out_shape=[jax.ShapeDtypeStruct((2, 256, 512), dtype)] * 2,
        compiler_params=params(32),
        cost_estimate=cost(2 * 256 * 2048 * 2048, 10 * MB),
        name="encoder_grads",
    )(
        idx, ta, tb, kc, ko, vc, vo, g_recv,
        w_key, w_value, w_key, w_value, w_key, w_value, w_key, w_value,
    )


def pick(x, index):
    return lax.dynamic_index_in_dim(x, index, 0, keepdims=False)


def on_device(encoder_out, w_key, w_value, queries, grad_context):
    d = lax.axis_index("dp")
    seq = lax.axis_index("seq")
    tensor = lax.axis_index("tensor")
    h, c = seq // 2, seq % 2
    z, yl = tensor // 2, tensor % 2
    idx = jnp.stack([h, c, d, z, yl, h * 2 + yl]).astype(jnp.int32)

    enc = encoder_out[0]
    ya = jnp.stack([enc[:, :256]] + [shift_y(enc[:, :256], k) for k in (1, 2, 3)])
    zb = jnp.stack([enc[:, 256:]] + [shift_z(enc[:, 256:], k) for k in (1, 2, 3)])
    pieces = [ya] + [shift_z(ya, k) for k in (1, 2, 3)]
    pieces += [zb] + [shift_y(zb, k) for k in (1, 2, 3)]

    qg = jnp.stack([queries[:, 0], grad_context[:, 0]], axis=1)
    two = jnp.stack([pick(qg, h), swap_yhi(pick(qg, 1 - h))])
    heads = jnp.stack([two[..., :256], two[..., 256:]])
    qg_own = pick(heads, c)
    qg_oth = swap_core(pick(heads, 1 - c))

    kv_send, kv_own = project(idx, pieces, w_key, w_value)
    kv_oth = swap_core(kv_send)
    gk, gv, gq = attend(kv_own, kv_oth, qg_own, qg_oth)

    e_keep, e_send = sort_pieces(idx, pieces)
    e_oth = swap_core(e_send)
    gk_o = swap_core(gk)
    gv_o = swap_core(gv)

    def rows_of(x, start):
        return lax.dynamic_slice_in_dim(x, start, 256, 0)

    away = (1 - h) * 256
    g_recv = swap_yhi(
        jnp.stack(
            [rows_of(gk, away), rows_of(gk_o, away + 512), rows_of(gv, away), rows_of(gv_o, away + 512)]
        )
    )

    def xor_lists(me):
        send = (jnp.stack([2 * (me ^ 1), 2 * (me ^ 2)]), jnp.stack([2 * (me ^ 3) + 1, 2 * (me ^ 2) + 1]))
        keep = (jnp.stack([2 * me, 2 * (me ^ 3)]), jnp.stack([2 * me + 1, 2 * (me ^ 1) + 1]))
        return [x.astype(jnp.int32) for x in send + keep]

    sa, sb, ka, kb = xor_lists(d)
    args = (e_keep, e_oth, gk, gk_o, gv, gv_o)
    send_a, send_b = weight_grads(idx, sa, sb, *args, BF)
    got_a, got_b = swap_x(send_a, 1), swap_x(send_b, 3)
    keep_a, keep_b = weight_grads(idx, ka, kb, *args, F32)
    part_a = keep_a + got_a.astype(F32)
    part_b = keep_b + got_b.astype(F32)
    last_a = swap_x(part_a[1].astype(BF), 3)
    last_b = swap_x(part_b[1].astype(BF), 1)
    done_a = (part_a[0] + last_a.astype(F32)).astype(BF)
    done_b = (part_b[0] + last_b.astype(F32)).astype(BF)
    mine = jnp.where(h == 0, done_a, done_b)
    theirs = swap_yhi(jnp.where(h == 0, done_b, done_a))
    grad_w = jnp.where(h == 0, jnp.stack([mine, theirs]), jnp.stack([theirs, mine]))

    sa, sb, ka, kb = xor_lists(z)
    args = (gk, gk_o, gv, gv_o, g_recv, w_key, w_value)
    send_a, send_b = encoder_grads(idx, sa, sb, *args, BF)
    got_a, got_b = swap_z(send_a, 1), swap_z(send_b, 3)
    keep_a, keep_b = encoder_grads(idx, ka, kb, *args, F32)
    part_a = keep_a + got_a.astype(F32)
    part_b = keep_b + got_b.astype(F32)
    last_a = swap_z(part_a[1].astype(BF), 3)
    last_b = swap_z(part_b[1].astype(BF), 1)
    done_a = part_a[0] + last_a.astype(F32)
    done_b = part_b[0] + last_b.astype(F32)
    mine = jnp.where(yl == 0, done_a, done_b)
    theirs = swap_ylo(jnp.where(yl == 0, done_b, done_a).astype(BF))
    grad_enc = (mine + theirs.astype(F32)).astype(BF)[None]

    gq = gq.reshape(2, 2, 128, 256)
    back = swap_core(gq[1])
    both = jnp.where(
        c == 0, jnp.concatenate([gq[0], back], axis=-1), jnp.concatenate([back, gq[0]], axis=-1)
    )
    theirs = swap_yhi(both[1])
    grad_q = jnp.where(h == 0, jnp.stack([both[0], theirs]), jnp.stack([theirs, both[0]]))[:, None]

    return grad_q, grad_enc, grad_w[..., :512], grad_w[..., 512:]


def solution(mesh):
    placed = (
        P("dp", "seq", "tensor"),
        P(None, None, "tensor"),
        P(None, None, "tensor"),
        P(None, "dp", "seq", "tensor"),
        P(None, "dp", "seq", "tensor"),
    )
    return jax.shard_map(
        on_device,
        mesh=mesh,
        in_specs=placed,
        out_specs=(
            P(None, "dp", "seq", "tensor"),
            P("dp", "seq", "tensor"),
            P(None, ("dp", "seq"), "tensor"),
            P(None, ("dp", "seq"), "tensor"),
        ),
        check_vma=False,
    )
```

time: 614 us -> 190 us (0.31)
  waiting for transfers between devices: 493 us -> 82.9 us
  matrix products: 83.8 us -> 0 us
  starting transfers between devices: 0.9 us -> 44 us
  Pallas kernels: 0 us -> 35.3 us
  between operations: 14.3 us -> 0.95 us
    reduce_scatter x7 -> x0, waiting for transfers between devices: 382 us -> none  [the longest x2 209 us: on_device(): lax.psum_scatter(jnp.einsum('rd,rh->dh', flat_enc, joined, preferred_elem...]
    all_gather x5 -> x0, waiting for transfers between devices: 110 us -> none  [the longest x1 56.5 us: on_device(): full_enc = lax.all_gather(encoder_out, 'tensor', axis=2, tiled=True)]
    dot_general x20 -> x0, matrix products: 83.8 us -> none  [the longest x2 14.8 us: on_device(): jnp.einsum('bsh,dh->bsd', low_v, w_value[layer], preferred_element_type=j...]
    ppermute x0 -> x31, waiting for transfers between devices: none -> 82.9 us  [the longest x4 24.9 us: swap_x(): return lax.ppermute(x, 'dp', [(d, d ^ m) for d in range(4)])]
    ppermute x0 -> x31, starting transfers between devices: none -> 44 us  [the longest x6 11.4 us: shift_z(): return lax.ppermute(x, 'tensor', [(t, (t + 2 * k) % 8) for t in range(8)])]
    pallas_call x0 -> x7, Pallas kernels: none -> 35.3 us  [the longest x2 9.6 us: weight_grads(): pl.pallas_call(weights_body, grid_spec=pltpu.PrefetchScalarGridSpec(num_s...]
    unnamed x22 -> x31, local copies, waits for them, and re-layouts: 9.08 us -> 14.4 us
  transfers between devices with their start and end apart: 12 -> 31, of which waited for: 12 -> 14; matrix products, arithmetic and copies ran while one was open for 14% -> 5% of each run, Pallas kernels for 0% -> 19%
where the time goes in v1:
time: 190 us
  waiting for transfers between devices  82.9 us (44%)
  starting transfers between devices  44 us (23%)
  Pallas kernels  35.3 us (19%)
  local copies, waits for them, and re-layouts  20.4 us (11%)
  other arithmetic  6.18 us (3%)
    ppermute x4, waiting for transfers between devices, swap_x(): return lax.ppermute(x, 'dp', [(d, d ^ m) for d in range(4)])  24.9 us
    ppermute x4, waiting for transfers between devices, swap_yhi(): return lax.ppermute(x, 'seq', [(s, s ^ 2) for s in range(4)])  22 us
    ppermute x6, waiting for transfers between devices, shift_z(): return lax.ppermute(x, 'tensor', [(t, (t + 2 * k) % 8) for t in range(8)])  18.6 us
    ppermute x6, waiting for transfers between devices, shift_y(): return lax.ppermute(x, ('seq', 'tensor'), pairs)  15.9 us
    unnamed x31, local copies, waits for them, and re-layouts  14.4 us
    ppermute x6, starting transfers between devices, shift_z(): return lax.ppermute(x, 'tensor', [(t, (t + 2 * k) % 8) for t in range(8)])  11.4 us
    ppermute x4, starting transfers between devices, swap_yhi(): return lax.ppermute(x, 'seq', [(s, s ^ 2) for s in range(4)])  10.7 us
    pallas_call x2, Pallas kernels, weight_grads(): pl.pallas_call(weights_body, grid_spec=pltpu.PrefetchScalarGridSpec(num_s...  9.6 us
  transfers between devices with their start and end apart: 31, of which 14 were waited for; matrix products, arithmetic and copies ran while one was open for 5% of the time, Pallas kernels for 19%

profile of v1, /device:TPU:0, one launch (start us, length us, event | category | flops | bytes accessed | tf_op | source)
XLA Modules:
  0.0 189.7 jit_solution(18147205885433078185)
XLA Ops:
  0.6 1.0 slice_bitcast_fusion.6
  1.7 2.1 %collective-permute-start.6 = (bf16[256,256]{1,0:T(8,128)(2,1)S(1)}, bf16[256,256]{1,0:T(8,128)(2,1)S(1)}, u32[]{:S(2)}, u32[]{:S(2)}) collective-permute-start(bf16[256,256]{1,0:T(8,128)(2,1)S(1)} %get-tuple-element.50), channel_id=1, source_target_pairs={{0,2},{1,3},{2,4},{3,5},{4,6},{5,7},{6,0},{7,1},{8,10},{9,11},{10,... | collective-permute-start | bytes 393224 | tf_op jit(solution)/shard_map/ppermute | solution.py:47
  3.8 3.6 %collective-permute-start.7 = (bf16[256,256]{1,0:T(8,128)(2,1)S(1)}, bf16[256,256]{1,0:T(8,128)(2,1)S(1)}, u32[]{:S(2)}, u32[]{:S(2)}) collective-permute-start(bf16[256,256]{1,0:T(8,128)(2,1)S(1)} %get-tuple-element.50), channel_id=1, source_target_pairs={{0,4},{1,5},{2,6},{3,7},{4,0},{5,1},{6,2},{7,3},{8,12},{9,13},{10,... | collective-permute-start | bytes 393224 | tf_op jit(solution)/shard_map/ppermute | solution.py:47
  7.3 1.0 collective-permute-start.8
  8.4 1.0 collective-permute-done.6
  9.4 4.0 %collective-permute-done.7 = bf16[256,256]{1,0:T(8,128)(2,1)S(1)} collective-permute-done((bf16[256,256]{1,0:T(8,128)(2,1)S(1)}, bf16[256,256]{1,0:T(8,128)(2,1)S(1)}, u32[]{:S(2)}, u32[]{:S(2)}) %collective-permute-start.7) | collective-permute-done | bytes 131104 | tf_op jit(solution)/shard_map/ppermute | solution.py:47
  13.4 3.3 %collective-permute-start.10 = (bf16[4,256,256]{2,1,0:T(8,128)(2,1)S(1)}, bf16[4,256,256]{2,1,0:T(8,128)(2,1)S(1)}, u32[]{:S(2)}, u32[]{:S(2)}) collective-permute-start(bf16[4,256,256]{2,1,0:T(8,128)(2,1)S(1)} %pad_maximum_fusion.1.refs_4_), channel_id=1, source_target_pairs={{0,16},{1,17},{2,18},{3,19},{4,20},{5,21},{6,22},{7,23},{8,24},{9,... | collective-permute-start | bytes 1572872 | tf_op jit(solution)/shard_map/ppermute | solution.py:56
  16.7 1.1 collective-permute-start.2
  17.8 1.0 collective-permute-start
  19.5 2.6 %collective-permute-start.11 = (bf16[4,256,256]{2,1,0:T(8,128)(2,1)S(1)}, bf16[4,256,256]{2,1,0:T(8,128)(2,1)S(1)}, u32[]{:S(2)}, u32[]{:S(2)}) collective-permute-start(bf16[4,256,256]{2,1,0:T(8,128)(2,1)S(1)} %pad_maximum_fusion.1.refs_4_), channel_id=1, source_target_pairs={{0,17},{1,0},{2,19},{3,2},{4,21},{5,4},{6,23},{7,6},{8,25},{9,8},{... | collective-permute-start | bytes 1572872 | tf_op jit(solution)/shard_map/ppermute | solution.py:56
  22.1 11.0 %collective-permute-done.2 = bf16[256,256]{1,0:T(8,128)(2,1)S(1)} collective-permute-done((bf16[256,256]{1,0:T(8,128)(2,1)S(1)}, bf16[256,256]{1,0:T(8,128)(2,1)S(1)}, u32[]{:S(2)}, u32[]{:S(2)}) %collective-permute-start.2) | collective-permute-done | bytes 131104 | tf_op jit(solution)/shard_map/ppermute | solution.py:56
  33.8 2.0 %collective-permute-start.3 = (bf16[4,256,256]{2,1,0:T(8,128)(2,1)S(1)}, bf16[4,256,256]{2,1,0:T(8,128)(2,1)S(1)}, u32[]{:S(2)}, u32[]{:S(2)}) collective-permute-start(bf16[4,256,256]{2,1,0:T(8,128)(2,1)S(1)} %pad_maximum_fusion.refs_0_), channel_id=1, source_target_pairs={{0,2},{1,3},{2,4},{3,5},{4,6},{5,7},{6,0},{7,1},{8,10},{9,11},{10,... | collective-permute-start | bytes 1572872 | tf_op jit(solution)/shard_map/ppermute | solution.py:47
  35.8 2.2 %collective-permute-start.4 = (bf16[4,256,256]{2,1,0:T(8,128)(2,1)S(1)}, bf16[4,256,256]{2,1,0:T(8,128)(2,1)}, u32[]{:S(2)}, u32[]{:S(2)}) collective-permute-start(bf16[4,256,256]{2,1,0:T(8,128)(2,1)S(1)} %pad_maximum_fusion.refs_0_), channel_id=1, source_target_pairs={{0,4},{1,5},{2,6},{3,7},{4,0},{5,1},{6,2},{7,3},{8,12},{9,13},{10,... | collective-permute-start | bytes 1572872 | tf_op jit(solution)/shard_map/ppermute | solution.py:47
  38.6 1.0 constant_dynamic-update-slice_fusion
  40.4 4.7 %collective-permute-done.11.refs_7_ = bf16[4,256,256]{2,1,0:T(8,128)(2,1)S(1)} collective-permute-done((bf16[4,256,256]{2,1,0:T(8,128)(2,1)S(1)}, bf16[4,256,256]{2,1,0:T(8,128)(2,1)S(1)}, u32[]{:S(2)}, u32[]{:S(2)}) %collective-permute-start.11) | collective-permute-done | bytes 524320 | tf_op jit(solution)/shard_map/ppermute | solution.py:56
  45.1 1.8 collective-permute-start.13
  47.1 1.9 %collective-permute-done.3.refs_1_ = bf16[4,256,256]{2,1,0:T(8,128)(2,1)S(1)} collective-permute-done((bf16[4,256,256]{2,1,0:T(8,128)(2,1)S(1)}, bf16[4,256,256]{2,1,0:T(8,128)(2,1)S(1)}, u32[]{:S(2)}, u32[]{:S(2)}) %collective-permute-start.3) | collective-permute-done | bytes 524320 | tf_op jit(solution)/shard_map/ppermute | solution.py:47
  49.1 11.6 %collective-permute-done.4.refs_2_ = bf16[4,256,256]{2,1,0:T(8,128)(2,1)} collective-permute-done((bf16[4,256,256]{2,1,0:T(8,128)(2,1)S(1)}, bf16[4,256,256]{2,1,0:T(8,128)(2,1)}, u32[]{:S(2)}, u32[]{:S(2)}) %collective-permute-start.4) | collective-permute-done | bytes 524320 | tf_op jit(solution)/shard_map/ppermute | solution.py:47
  60.7 3.4 %copy-done = bf16[2,4096,512]{2,1,0:T(8,128)(2,1)S(1)} copy-done((bf16[2,4096,512]{2,1,0:T(8,128)(2,1)S(1)}, bf16[2,4096,512]{2,1,0:T(8,128)(2,1)}, u32[]{:S(2)}) %copy-start) | copy-done | bytes 8388632
  64.1 3.4 %copy-done.2 = bf16[2,4096,512]{2,1,0:T(8,128)(2,1)S(1)} copy-done((bf16[2,4096,512]{2,1,0:T(8,128)(2,1)S(1)}, bf16[2,4096,512]{2,1,0:T(8,128)(2,1)}, u32[]{:S(2)}) %copy-start.2) | copy-done | bytes 8388632
  67.5 8.6 %project.1 = (bf16[512,512]{1,0:T(8,128)(2,1)}, bf16[512,512]{1,0:T(8,128)(2,1)S(1)}) custom-call(s32[6]{0:T(128)S(1)} %stack.189.idx, bf16[4,256,256]{2,1,0:T(8,128)(2,1)S(1)} %pad_maximum_fusion.refs_0_, bf16[4,256,256]{2,1,0:T(8,128)(2,1)S(1)} %collective-permute-done.3.refs_1_, bf16[4,256,256]{2,1,0:T(8,128)(2,1)} %collective-permute-done.4.refs_2_, ...), custom_call_target="tpu_custom_call" | custom-call | flops 4294967296 | bytes 14680064 | tf_op jit(solution)/shard_map/project/pallas_call | solution.py:109
  76.9 1.1 fusion.17
  78.9 3.9 %sort_pieces.1 = (bf16[512,2048]{1,0:T(8,128)(2,1)S(1)}, bf16[512,2048]{1,0:T(8,128)(2,1)}) custom-call(s32[6]{0:T(128)S(1)} %stack.189.idx, bf16[4,256,256]{2,1,0:T(8,128)(2,1)S(1)} %pad_maximum_fusion.refs_0_, bf16[4,256,256]{2,1,0:T(8,128)(2,1)S(1)} %copy-done.11, bf16[4,256,256]{2,1,0:T(8,128)(2,1)} %collective-permute-done.4.refs_2_, ...), custom_call_target="tpu_custom_call" | custom-call | bytes 8388608 | tf_op jit(solution)/shard_map/sort_pieces/pallas_call | solution.py:149
  82.9 4.6 %attend.1 = (bf16[1024,256]{1,0:T(8,128)(2,1)S(1)}, bf16[1024,256]{1,0:T(8,128)(2,1)S(1)}, bf16[4,128,256]{2,1,0:T(8,128)(2,1)S(1)}) custom-call(bf16[512,512]{1,0:T(8,128)(2,1)S(1)} %copy-done.13, bf16[512,512]{1,0:T(8,128)(2,1)} %collective-permute-done.12.kv_oth, bf16[2,2,128,256]{3,2,1,0:T(8,128)(2,1)S(1)} %get-tuple-element.39.qg_own, ...), custom_call_target="tpu_custom_call" | custom-call | flops 1342177280 | bytes 4194304 | tf_op jit(solution)/shard_map/attend/pallas_call | solution.py:200
  88.1 1.5 collective-permute-done.18.refs_3_.vo
  89.6 0.9 dynamic-slice_bitcast_fusion.1
  90.5 0.9 dynamic-slice_bitcast_fusion.3
  92.3 2.9 %collective-permute-start.19 = (bf16[4,256,256]{2,1,0:T(8,128)(2,1)}, bf16[4,256,256]{2,1,0:T(8,128)(2,1)}, u32[]{:S(2)}, u32[]{:S(2)}) collective-permute-start(bf16[4,256,256]{2,1,0:T(8,128)(2,1)} %pad_maximum_fusion.2), channel_id=1, source_target_pairs={{0,16},{8,24},{16,0},{24,8},{1,17},{9,25},{17,1},{25,9},{2,18},{10... | collective-permute-start | bytes 1572872 | tf_op jit(solution)/shard_map/ppermute | solution.py:31
  95.5 12.8 %collective-permute-done.19.refs_4_ = bf16[4,256,256]{2,1,0:T(8,128)(2,1)} collective-permute-done((bf16[4,256,256]{2,1,0:T(8,128)(2,1)}, bf16[4,256,256]{2,1,0:T(8,128)(2,1)}, u32[]{:S(2)}, u32[]{:S(2)}) %collective-permute-start.19) | collective-permute-done | bytes 524320 | tf_op jit(solution)/shard_map/ppermute | solution.py:31
  108.3 3.4 %copy-done.1 = bf16[2,4096,512]{2,1,0:T(8,128)(2,1)S(1)} copy-done((bf16[2,4096,512]{2,1,0:T(8,128)(2,1)S(1)}, bf16[2,4096,512]{2,1,0:T(8,128)(2,1)}, u32[]{:S(2)}) %copy-start.1) | copy-done | bytes 8388632
  111.7 3.4 %copy-done.3 = bf16[2,4096,512]{2,1,0:T(8,128)(2,1)S(1)} copy-done((bf16[2,4096,512]{2,1,0:T(8,128)(2,1)S(1)}, bf16[2,4096,512]{2,1,0:T(8,128)(2,1)}, u32[]{:S(2)}) %copy-start.3) | copy-done | bytes 8388632
  115.1 4.4 %encoder_grads.3 = (bf16[2,256,512]{2,1,0:T(8,128)(2,1)S(1)}, bf16[2,256,512]{2,1,0:T(8,128)(2,1)S(1)}) custom-call(s32[6]{0:T(128)S(1)} %stack.189.idx, s32[2]{0:T(128)S(1)} %get-tuple-element.54.ta, s32[2]{0:T(128)S(1)} %get-tuple-element.55.tb, bf16[1024,256]{1,0:T(8,128)(2,1)S(1)} %get-tuple-element.22.refs_0_.kc, ...), custom_call_target="tpu_custom_call" | custom-call | flops 2147483648 | bytes 10485760 | tf_op jit(solution)/shard_map/encoder_grads/pallas_call | solution.py:279
  119.5 2.5 %collective-permute-start.22 = (bf16[2,256,512]{2,1,0:T(8,128)(2,1)S(1)}, bf16[2,256,512]{2,1,0:T(8,128)(2,1)S(1)}, u32[]{:S(2)}, u32[]{:S(2)}) collective-permute-start(bf16[2,256,512]{2,1,0:T(8,128)(2,1)S(1)} %get-tuple-element.27), channel_id=1, source_target_pairs={{0,6},{1,7},{2,4},{3,5},{4,2},{5,3},{6,0},{7,1},{8,14},{9,15},{10,... | collective-permute-start | bytes 1572872 | tf_op jit(solution)/shard_map/ppermute | solution.py:43
  122.2 4.4 %encoder_grads.2 = (f32[2,256,512]{2,1,0:T(8,128)S(1)}, f32[2,256,512]{2,1,0:T(8,128)S(1)}) custom-call(s32[6]{0:T(128)S(1)} %stack.189.idx, s32[2]{0:T(128)S(1)} %get-tuple-element.52.ta, s32[2]{0:T(128)S(1)} %get-tuple-element.53.tb, bf16[1024,256]{1,0:T(8,128)(2,1)S(1)} %get-tuple-element.22.refs_0_.kc, ...), custom_call_target="tpu_custom_call" | custom-call | flops 2147483648 | bytes 10485760 | tf_op jit(solution)/shard_map/encoder_grads/pallas_call | solution.py:279
  126.5 4.8 %weight_grads.3 = (bf16[2,256,1024]{2,1,0:T(8,128)(2,1)S(1)}, bf16[2,256,1024]{2,1,0:T(8,128)(2,1)S(1)}) custom-call(s32[6]{0:T(128)S(1)} %stack.189.idx, s32[2]{0:T(128)S(1)} %get-tuple-element.58.ta, s32[2]{0:T(128)S(1)} %get-tuple-element.59.tb, bf16[512,2048]{1,0:T(8,128)(2,1)S(1)} %get-tuple-element.28.ea.eb, ...), custom_call_target="tpu_custom_call" | custom-call | flops 2147483648 | bytes 6291456 | tf_op jit(solution)/shard_map/weight_grads/pallas_call | solution.py:235
  131.4 2.8 %collective-permute-start.28 = (bf16[2,256,1024]{2,1,0:T(8,128)(2,1)S(1)}, bf16[2,256,1024]{2,1,0:T(8,128)(2,1)S(1)}, u32[]{:S(2)}, u32[]{:S(2)}) collective-permute-start(bf16[2,256,1024]{2,1,0:T(8,128)(2,1)S(1)} %get-tuple-element.33), channel_id=1, source_target_pairs={{0,96},{32,64},{64,32},{96,0},{1,97},{33,65},{65,33},{97,1},{2,98}... | collective-permute-start | bytes 3145736 | tf_op jit(solution)/shard_map/ppermute | solution.py:39
  134.6 2.1 %collective-permute-start.23 = (bf16[256,512]{1,0:T(8,128)(2,1)S(1)}, bf16[256,512]{1,0:T(8,128)(2,1)S(1)}, u32[]{:S(2)}, u32[]{:S(2)}) collective-permute-start(bf16[256,512]{1,0:T(8,128)(2,1)S(1)} %fusion.12), channel_id=1, source_target_pairs={{0,2},{1,3},{2,0},{3,1},{4,6},{5,7},{6,4},{7,5},{8,10},{9,11},{10,... | collective-permute-start | bytes 786440 | tf_op jit(solution)/shard_map/ppermute | solution.py:43
  137.0 0.9 collective-permute-start.21
  137.9 4.8 %weight_grads.2 = (f32[2,256,1024]{2,1,0:T(8,128)S(1)}, f32[2,256,1024]{2,1,0:T(8,128)S(1)}) custom-call(s32[6]{0:T(128)S(1)} %stack.189.idx, s32[2]{0:T(128)S(1)} %get-tuple-element.56.ta, s32[2]{0:T(128)S(1)} %get-tuple-element.57.tb, bf16[512,2048]{1,0:T(8,128)(2,1)S(1)} %get-tuple-element.28.ea.eb, bf16[512,2048]{1,0:T(8,128)(2,1)} %collective-permute-done.25.oa.ob, ...), custom_call_target="tpu_custom_call" | custom-call | flops 2147483648 | bytes 6291456 | tf_op jit(solution)/shard_map/weight_grads/pallas_call | solution.py:235
  142.7 15.5 %collective-permute-done.28 = bf16[2,256,1024]{2,1,0:T(8,128)(2,1)S(1)} collective-permute-done((bf16[2,256,1024]{2,1,0:T(8,128)(2,1)S(1)}, bf16[2,256,1024]{2,1,0:T(8,128)(2,1)S(1)}, u32[]{:S(2)}, u32[]{:S(2)}) %collective-permute-start.28) | collective-permute-done | bytes 1048608 | tf_op jit(solution)/shard_map/ppermute | solution.py:39
  159.8 2.1 %collective-permute-start.27 = (bf16[256,1024]{1,0:T(8,128)(2,1)S(1)}, bf16[256,1024]{1,0:T(8,128)(2,1)S(1)}, u32[]{:S(2)}, u32[]{:S(2)}) collective-permute-start(bf16[256,1024]{1,0:T(8,128)(2,1)S(1)} %fusion.4), channel_id=1, source_target_pairs={{0,96},{32,64},{64,32},{96,0},{1,97},{33,65},{65,33},{97,1},{2,98}... | collective-permute-start | bytes 1572872 | tf_op jit(solution)/shard_map/ppermute | solution.py:39
  162.1 3.0 %collective-permute-start.16 = (bf16[128,512]{1,0:T(8,128)(2,1)S(1)}, bf16[128,512]{1,0:T(8,128)(2,1)S(1)}, u32[]{:S(2)}, u32[]{:S(2)}) collective-permute-start(bf16[128,512]{1,0:T(8,128)(2,1)S(1)} %get-tuple-element.45), channel_id=1, source_target_pairs={{0,16},{8,24},{16,0},{24,8},{1,17},{9,25},{17,1},{25,9},{2,18},{10... | collective-permute-start | bytes 393224 | tf_op jit(solution)/shard_map/ppermute | solution.py:31
  165.3 6.8 %collective-permute-done.29 = bf16[256,1024]{1,0:T(8,128)(2,1)S(1)} collective-permute-done((bf16[256,1024]{1,0:T(8,128)(2,1)S(1)}, bf16[256,1024]{1,0:T(8,128)(2,1)S(1)}, u32[]{:S(2)}, u32[]{:S(2)}) %collective-permute-start.29) | collective-permute-done | bytes 524320 | tf_op jit(solution)/shard_map/ppermute | solution.py:39
  172.1 2.2 %collective-permute-done.27 = bf16[256,1024]{1,0:T(8,128)(2,1)S(1)} collective-permute-done((bf16[256,1024]{1,0:T(8,128)(2,1)S(1)}, bf16[256,1024]{1,0:T(8,128)(2,1)S(1)}, u32[]{:S(2)}, u32[]{:S(2)}) %collective-permute-start.27) | collective-permute-done | bytes 524320 | tf_op jit(solution)/shard_map/ppermute | solution.py:39
  174.7 3.0 %collective-permute-start.30 = (bf16[256,1024]{1,0:T(8,128)(2,1)S(1)}, bf16[256,1024]{1,0:T(8,128)(2,1)S(1)}, u32[]{:S(2)}, u32[]{:S(2)}) collective-permute-start(bf16[256,1024]{1,0:T(8,128)(2,1)S(1)} %get-tuple-element.35), channel_id=1, source_target_pairs={{0,16},{8,24},{16,0},{24,8},{1,17},{9,25},{17,1},{25,9},{2,18},{10... | collective-permute-start | bytes 1572872 | tf_op jit(solution)/shard_map/ppermute | solution.py:31
  178.4 0.9 fusion.8
  179.3 9.2 %collective-permute-done.30 = bf16[256,1024]{1,0:T(8,128)(2,1)S(1)} collective-permute-done((bf16[256,1024]{1,0:T(8,128)(2,1)S(1)}, bf16[256,1024]{1,0:T(8,128)(2,1)S(1)}, u32[]{:S(2)}, u32[]{:S(2)}) %collective-permute-start.30) | collective-permute-done | bytes 524320 | tf_op jit(solution)/shard_map/ppermute | solution.py:31
  188.7 1.0 fusion.18
  (85 shorter events, 10.9 us)
Async XLA Ops:
  0.6 38.0 %copy-start.14 = (bf16[2,1,128,512]{3,2,1,0:T(8,128)(2,1)S(1)}, bf16[2,1,128,512]{3,2,1,0:T(8,128)(2,1)}, u32[]{:S(2)}) copy-start(bf16[2,1,128,512]{3,2,1,0:T(8,128)(2,1)} %param.8) | copy-start | bytes 786436
  1.7 7.7 %collective-permute-start.6 = (bf16[256,256]{1,0:T(8,128)(2,1)S(1)}, bf16[256,256]{1,0:T(8,128)(2,1)S(1)}, u32[]{:S(2)}, u32[]{:S(2)}) collective-permute-start(bf16[256,256]{1,0:T(8,128)(2,1)S(1)} %get-tuple-element.50), channel_id=1, source_target_pairs={{0,2},{1,3},{2,4},{3,5},{4,6},{5,7},{6,0},{7,1},{8,10},{9,11},{10,... | collective-permute-start | bytes 393224 | tf_op jit(solution)/shard_map/ppermute | solution.py:47
  3.8 9.6 %collective-permute-start.7 = (bf16[256,256]{1,0:T(8,128)(2,1)S(1)}, bf16[256,256]{1,0:T(8,128)(2,1)S(1)}, u32[]{:S(2)}, u32[]{:S(2)}) collective-permute-start(bf16[256,256]{1,0:T(8,128)(2,1)S(1)} %get-tuple-element.50), channel_id=1, source_target_pairs={{0,4},{1,5},{2,6},{3,7},{4,0},{5,1},{6,2},{7,3},{8,12},{9,13},{10,... | collective-permute-start | bytes 393224 | tf_op jit(solution)/shard_map/ppermute | solution.py:47
  7.3 6.0 %collective-permute-start.8 = (bf16[256,256]{1,0:T(8,128)(2,1)S(1)}, bf16[256,256]{1,0:T(8,128)(2,1)S(1)}, u32[]{:S(2)}, u32[]{:S(2)}) collective-permute-start(bf16[256,256]{1,0:T(8,128)(2,1)S(1)} %get-tuple-element.50), channel_id=1, source_target_pairs={{0,6},{1,7},{2,0},{3,1},{4,2},{5,3},{6,4},{7,5},{8,14},{9,15},{10,... | collective-permute-start | bytes 393224 | tf_op jit(solution)/shard_map/ppermute | solution.py:47
  13.4 24.5 %collective-permute-start.10 = (bf16[4,256,256]{2,1,0:T(8,128)(2,1)S(1)}, bf16[4,256,256]{2,1,0:T(8,128)(2,1)S(1)}, u32[]{:S(2)}, u32[]{:S(2)}) collective-permute-start(bf16[4,256,256]{2,1,0:T(8,128)(2,1)S(1)} %pad_maximum_fusion.1.refs_4_), channel_id=1, source_target_pairs={{0,16},{1,17},{2,18},{3,19},{4,20},{5,21},{6,22},{7,23},{8,24},{9,... | collective-permute-start | bytes 1572872 | tf_op jit(solution)/shard_map/ppermute | solution.py:56
  16.7 16.4 %collective-permute-start.2 = (bf16[256,256]{1,0:T(8,128)(2,1)S(1)}, bf16[256,256]{1,0:T(8,128)(2,1)S(1)}, u32[]{:S(2)}, u32[]{:S(2)}) collective-permute-start(bf16[256,256]{1,0:T(8,128)(2,1)S(1)} %get-tuple-element.51), channel_id=1, source_target_pairs={{0,17},{1,0},{2,19},{3,2},{4,21},{5,4},{6,23},{7,6},{8,25},{9,8},{... | collective-permute-start | bytes 393224 | tf_op jit(solution)/shard_map/ppermute | solution.py:56
  17.8 15.9 %collective-permute-start = (bf16[256,256]{1,0:T(8,128)(2,1)S(1)}, bf16[256,256]{1,0:T(8,128)(2,1)S(1)}, u32[]{:S(2)}, u32[]{:S(2)}) collective-permute-start(bf16[256,256]{1,0:T(8,128)(2,1)S(1)} %get-tuple-element.51), channel_id=1, source_target_pairs={{0,1},{1,16},{2,3},{3,18},{4,5},{5,20},{6,7},{7,22},{8,9},{9,24},{... | collective-permute-start | bytes 393224 | tf_op jit(solution)/shard_map/ppermute | solution.py:56
  18.7 15.0 %collective-permute-start.1 = (bf16[256,256]{1,0:T(8,128)(2,1)S(1)}, bf16[256,256]{1,0:T(8,128)(2,1)S(1)}, u32[]{:S(2)}, u32[]{:S(2)}) collective-permute-start(bf16[256,256]{1,0:T(8,128)(2,1)S(1)} %get-tuple-element.51), channel_id=1, source_target_pairs={{0,16},{1,17},{2,18},{3,19},{4,20},{5,21},{6,22},{7,23},{8,24},{9,... | collective-permute-start | bytes 393224 | tf_op jit(solution)/shard_map/ppermute | solution.py:56
  19.5 25.6 %collective-permute-start.11 = (bf16[4,256,256]{2,1,0:T(8,128)(2,1)S(1)}, bf16[4,256,256]{2,1,0:T(8,128)(2,1)S(1)}, u32[]{:S(2)}, u32[]{:S(2)}) collective-permute-start(bf16[4,256,256]{2,1,0:T(8,128)(2,1)S(1)} %pad_maximum_fusion.1.refs_4_), channel_id=1, source_target_pairs={{0,17},{1,0},{2,19},{3,2},{4,21},{5,4},{6,23},{7,6},{8,25},{9,8},{... | collective-permute-start | bytes 1572872 | tf_op jit(solution)/shard_map/ppermute | solution.py:56
  33.1 14.1 %collective-permute-start.9 = (bf16[4,256,256]{2,1,0:T(8,128)(2,1)S(1)}, bf16[4,256,256]{2,1,0:T(8,128)(2,1)S(1)}, u32[]{:S(2)}, u32[]{:S(2)}) collective-permute-start(bf16[4,256,256]{2,1,0:T(8,128)(2,1)S(1)} %pad_maximum_fusion.1.refs_4_), channel_id=1, source_target_pairs={{0,1},{1,16},{2,3},{3,18},{4,5},{5,20},{6,7},{7,22},{8,9},{9,24},{... | collective-permute-start | bytes 1572872 | tf_op jit(solution)/shard_map/ppermute | solution.py:56
  33.8 15.3 %collective-permute-start.3 = (bf16[4,256,256]{2,1,0:T(8,128)(2,1)S(1)}, bf16[4,256,256]{2,1,0:T(8,128)(2,1)S(1)}, u32[]{:S(2)}, u32[]{:S(2)}) collective-permute-start(bf16[4,256,256]{2,1,0:T(8,128)(2,1)S(1)} %pad_maximum_fusion.refs_0_), channel_id=1, source_target_pairs={{0,2},{1,3},{2,4},{3,5},{4,6},{5,7},{6,0},{7,1},{8,10},{9,11},{10,... | collective-permute-start | bytes 1572872 | tf_op jit(solution)/shard_map/ppermute | solution.py:47
  35.8 24.9 %collective-permute-start.4 = (bf16[4,256,256]{2,1,0:T(8,128)(2,1)S(1)}, bf16[4,256,256]{2,1,0:T(8,128)(2,1)}, u32[]{:S(2)}, u32[]{:S(2)}) collective-permute-start(bf16[4,256,256]{2,1,0:T(8,128)(2,1)S(1)} %pad_maximum_fusion.refs_0_), channel_id=1, source_target_pairs={{0,4},{1,5},{2,6},{3,7},{4,0},{5,1},{6,2},{7,3},{8,12},{9,13},{10,... | collective-permute-start | bytes 1572872 | tf_op jit(solution)/shard_map/ppermute | solution.py:47
  37.9 38.1 %copy-start.4 = (bf16[4,256,256]{2,1,0:T(8,128)(2,1)}, bf16[4,256,256]{2,1,0:T(8,128)(2,1)S(1)}, u32[]{:S(2)}) copy-start(bf16[4,256,256]{2,1,0:T(8,128)(2,1)S(1)} %collective-permute-done.10.refs_6_) | copy-start | bytes 1572868
  37.9 22.8 %collective-permute-start.5 = (bf16[4,256,256]{2,1,0:T(8,128)(2,1)S(1)}, bf16[4,256,256]{2,1,0:T(8,128)(2,1)}, u32[]{:S(2)}, u32[]{:S(2)}) collective-permute-start(bf16[4,256,256]{2,1,0:T(8,128)(2,1)S(1)} %pad_maximum_fusion.refs_0_), channel_id=1, source_target_pairs={{0,6},{1,7},{2,0},{3,1},{4,2},{5,3},{6,4},{7,5},{8,14},{9,15},{10,... | collective-permute-start | bytes 1572872 | tf_op jit(solution)/shard_map/ppermute | solution.py:47
  45.1 31.0 %copy-start.6 = (bf16[4,256,256]{2,1,0:T(8,128)(2,1)}, bf16[4,256,256]{2,1,0:T(8,128)(2,1)S(1)}, u32[]{:S(2)}) copy-start(bf16[4,256,256]{2,1,0:T(8,128)(2,1)S(1)} %collective-permute-done.11.refs_7_) | copy-start | bytes 1572868
  45.1 31.8 %collective-permute-start.13 = (bf16[2,128,512]{2,1,0:T(8,128)(2,1)}, bf16[2,128,512]{2,1,0:T(8,128)(2,1)}, u32[]{:S(2)}, u32[]{:S(2)}) collective-permute-start(bf16[2,128,512]{2,1,0:T(8,128)(2,1)} %get-tuple-element.42), channel_id=1, source_target_pairs={{0,16},{8,24},{16,0},{24,8},{1,17},{9,25},{17,1},{25,9},{2,18},{10... | collective-permute-start | bytes 786440 | tf_op jit(solution)/shard_map/ppermute | solution.py:31
  47.1 28.9 %copy-start.8 = (bf16[4,256,256]{2,1,0:T(8,128)(2,1)}, bf16[4,256,256]{2,1,0:T(8,128)(2,1)S(1)}, u32[]{:S(2)}) copy-start(bf16[4,256,256]{2,1,0:T(8,128)(2,1)S(1)} %collective-permute-done.9.refs_5_) | copy-start | bytes 1572868
  49.1 27.0 %copy-start.10 = (bf16[4,256,256]{2,1,0:T(8,128)(2,1)}, bf16[4,256,256]{2,1,0:T(8,128)(2,1)S(1)}, u32[]{:S(2)}) copy-start(bf16[4,256,256]{2,1,0:T(8,128)(2,1)S(1)} %collective-permute-done.3.refs_1_) | copy-start | bytes 1572868
  60.7 3.4 %copy-start = (bf16[2,4096,512]{2,1,0:T(8,128)(2,1)S(1)}, bf16[2,4096,512]{2,1,0:T(8,128)(2,1)}, u32[]{:S(2)}) copy-start(bf16[2,4096,512]{2,1,0:T(8,128)(2,1)} %refs_11_.3) | copy-start | bytes 25165828
  64.1 3.4 %copy-start.2 = (bf16[2,4096,512]{2,1,0:T(8,128)(2,1)S(1)}, bf16[2,4096,512]{2,1,0:T(8,128)(2,1)}, u32[]{:S(2)}) copy-start(bf16[2,4096,512]{2,1,0:T(8,128)(2,1)} %refs_12_.3) | copy-start | bytes 25165828
  76.1 0.8 copy-start.12
  76.9 6.0 %collective-permute-start.12 = (bf16[512,512]{1,0:T(8,128)(2,1)}, bf16[512,512]{1,0:T(8,128)(2,1)}, u32[]{:S(2)}, u32[]{:S(2)}) collective-permute-start(bf16[512,512]{1,0:T(8,128)(2,1)} %get-tuple-element.20), channel_id=1, source_target_pairs={{0,8},{8,0},{16,24},{24,16},{1,9},{9,1},{17,25},{25,17},{2,10},{10... | collective-permute-start | bytes 1572872 | tf_op jit(solution)/shard_map/ppermute | solution.py:27
  76.9 2.0 %copy-start.5 = (bf16[4,256,256]{2,1,0:T(8,128)(2,1)S(1)}, bf16[4,256,256]{2,1,0:T(8,128)(2,1)}, u32[]{:S(2)}) copy-start(bf16[4,256,256]{2,1,0:T(8,128)(2,1)} %copy-done.4) | copy-start | bytes 1572868
  76.9 2.0 %copy-start.7 = (bf16[4,256,256]{2,1,0:T(8,128)(2,1)S(1)}, bf16[4,256,256]{2,1,0:T(8,128)(2,1)}, u32[]{:S(2)}) copy-start(bf16[4,256,256]{2,1,0:T(8,128)(2,1)} %copy-done.6) | copy-start | bytes 1572868
  76.9 2.0 %copy-start.9 = (bf16[4,256,256]{2,1,0:T(8,128)(2,1)S(1)}, bf16[4,256,256]{2,1,0:T(8,128)(2,1)}, u32[]{:S(2)}) copy-start(bf16[4,256,256]{2,1,0:T(8,128)(2,1)} %copy-done.8) | copy-start | bytes 1572868
  76.9 2.0 %copy-start.11 = (bf16[4,256,256]{2,1,0:T(8,128)(2,1)S(1)}, bf16[4,256,256]{2,1,0:T(8,128)(2,1)}, u32[]{:S(2)}) copy-start(bf16[4,256,256]{2,1,0:T(8,128)(2,1)} %copy-done.10) | copy-start | bytes 1572868
  78.3 4.6 %copy-start.13 = (bf16[512,512]{1,0:T(8,128)(2,1)S(1)}, bf16[512,512]{1,0:T(8,128)(2,1)}, u32[]{:S(2)}) copy-start(bf16[512,512]{1,0:T(8,128)(2,1)} %copy-done.12) | copy-start | bytes 1572868
  78.3 4.6 %collective-permute-start.14 = (bf16[2,2,128,256]{3,2,1,0:T(8,128)(2,1)S(1)}, bf16[2,2,128,256]{3,2,1,0:T(8,128)(2,1)S(1)}, u32[]{:S(2)}, u32[]{:S(2)}) collective-permute-start(bf16[2,2,128,256]{3,2,1,0:T(8,128)(2,1)S(1)} %get-tuple-element.38), channel_id=1, source_target_pairs={{0,8},{8,0},{16,24},{24,16},{1,9},{9,1},{17,25},{25,17},{2,10},{10... | collective-permute-start | bytes 786440 | tf_op jit(solution)/shard_map/ppermute | solution.py:27
  82.8 43.8 %collective-permute-start.25 = (bf16[512,2048]{1,0:T(8,128)(2,1)}, bf16[512,2048]{1,0:T(8,128)(2,1)}, u32[]{:S(2)}, u32[]{:S(2)}) collective-permute-start(bf16[512,2048]{1,0:T(8,128)(2,1)} %get-tuple-element.29), channel_id=1, source_target_pairs={{0,8},{8,0},{16,24},{24,16},{1,9},{9,1},{17,25},{25,17},{2,10},{10... | collective-permute-start | bytes 6291464 | tf_op jit(solution)/shard_map/ppermute | solution.py:27
  87.5 2.1 %collective-permute-start.18 = (bf16[1024,256]{1,0:T(8,128)(2,1)S(1)}, bf16[1024,256]{1,0:T(8,128)(2,1)}, u32[]{:S(2)}, u32[]{:S(2)}) collective-permute-start(bf16[1024,256]{1,0:T(8,128)(2,1)S(1)} %get-tuple-element.23.refs_2_.vc), channel_id=1, source_target_pairs={{0,8},{8,0},{16,24},{24,16},{1,9},{9,1},{17,25},{25,17},{2,10},{10... | collective-permute-start | bytes 1572872 | tf_op jit(solution)/shard_map/ppermute | solution.py:27
  87.9 2.6 %collective-permute-start.17 = (bf16[1024,256]{1,0:T(8,128)(2,1)S(1)}, bf16[1024,256]{1,0:T(8,128)(2,1)}, u32[]{:S(2)}, u32[]{:S(2)}) collective-permute-start(bf16[1024,256]{1,0:T(8,128)(2,1)S(1)} %get-tuple-element.22.refs_0_.kc), channel_id=1, source_target_pairs={{0,8},{8,0},{16,24},{24,16},{1,9},{9,1},{17,25},{25,17},{2,10},{10... | collective-permute-start | bytes 1572872 | tf_op jit(solution)/shard_map/ppermute | solution.py:27
  92.3 16.0 %collective-permute-start.19 = (bf16[4,256,256]{2,1,0:T(8,128)(2,1)}, bf16[4,256,256]{2,1,0:T(8,128)(2,1)}, u32[]{:S(2)}, u32[]{:S(2)}) collective-permute-start(bf16[4,256,256]{2,1,0:T(8,128)(2,1)} %pad_maximum_fusion.2), channel_id=1, source_target_pairs={{0,16},{8,24},{16,0},{24,8},{1,17},{9,25},{17,1},{25,9},{2,18},{10... | collective-permute-start | bytes 1572872 | tf_op jit(solution)/shard_map/ppermute | solution.py:31
  108.3 3.4 %copy-start.1 = (bf16[2,4096,512]{2,1,0:T(8,128)(2,1)S(1)}, bf16[2,4096,512]{2,1,0:T(8,128)(2,1)}, u32[]{:S(2)}) copy-start(bf16[2,4096,512]{2,1,0:T(8,128)(2,1)} %refs_11_.3) | copy-start | bytes 25165828
  111.7 3.4 %copy-start.3 = (bf16[2,4096,512]{2,1,0:T(8,128)(2,1)S(1)}, bf16[2,4096,512]{2,1,0:T(8,128)(2,1)}, u32[]{:S(2)}) copy-start(bf16[2,4096,512]{2,1,0:T(8,128)(2,1)} %refs_12_.3) | copy-start | bytes 25165828
  119.5 15.0 %collective-permute-start.22 = (bf16[2,256,512]{2,1,0:T(8,128)(2,1)S(1)}, bf16[2,256,512]{2,1,0:T(8,128)(2,1)S(1)}, u32[]{:S(2)}, u32[]{:S(2)}) collective-permute-start(bf16[2,256,512]{2,1,0:T(8,128)(2,1)S(1)} %get-tuple-element.27), channel_id=1, source_target_pairs={{0,6},{1,7},{2,4},{3,5},{4,2},{5,3},{6,0},{7,1},{8,14},{9,15},{10,... | collective-permute-start | bytes 1572872 | tf_op jit(solution)/shard_map/ppermute | solution.py:43
  122.0 39.9 %collective-permute-start.15 = (bf16[2,128,256]{2,1,0:T(8,128)(2,1)S(1)}, bf16[2,128,256]{2,1,0:T(8,128)(2,1)S(1)}, u32[]{:S(2)}, u32[]{:S(2)}) collective-permute-start(bf16[2,128,256]{2,1,0:T(8,128)(2,1)S(1)} %get-tuple-element.47), channel_id=1, source_target_pairs={{0,8},{8,0},{16,24},{24,16},{1,9},{9,1},{17,25},{25,17},{2,10},{10... | collective-permute-start | bytes 393224 | tf_op jit(solution)/shard_map/ppermute | solution.py:27
  122.1 14.7 %collective-permute-start.20 = (bf16[2,256,512]{2,1,0:T(8,128)(2,1)S(1)}, bf16[2,256,512]{2,1,0:T(8,128)(2,1)S(1)}, u32[]{:S(2)}, u32[]{:S(2)}) collective-permute-start(bf16[2,256,512]{2,1,0:T(8,128)(2,1)S(1)} %get-tuple-element.25), channel_id=1, source_target_pairs={{0,2},{1,3},{2,0},{3,1},{4,6},{5,7},{6,4},{7,5},{8,10},{9,11},{10,... | collective-permute-start | bytes 1572872 | tf_op jit(solution)/shard_map/ppermute | solution.py:43
  131.4 26.8 %collective-permute-start.28 = (bf16[2,256,1024]{2,1,0:T(8,128)(2,1)S(1)}, bf16[2,256,1024]{2,1,0:T(8,128)(2,1)S(1)}, u32[]{:S(2)}, u32[]{:S(2)}) collective-permute-start(bf16[2,256,1024]{2,1,0:T(8,128)(2,1)S(1)} %get-tuple-element.33), channel_id=1, source_target_pairs={{0,96},{32,64},{64,32},{96,0},{1,97},{33,65},{65,33},{97,1},{2,98}... | collective-permute-start | bytes 3145736 | tf_op jit(solution)/shard_map/ppermute | solution.py:39
  134.2 25.2 %collective-permute-start.26 = (bf16[2,256,1024]{2,1,0:T(8,128)(2,1)S(1)}, bf16[2,256,1024]{2,1,0:T(8,128)(2,1)S(1)}, u32[]{:S(2)}, u32[]{:S(2)}) collective-permute-start(bf16[2,256,1024]{2,1,0:T(8,128)(2,1)S(1)} %get-tuple-element.31), channel_id=1, source_target_pairs={{0,32},{32,0},{64,96},{96,64},{1,33},{33,1},{65,97},{97,65},{2,34}... | collective-permute-start | bytes 3145736 | tf_op jit(solution)/shard_map/ppermute | solution.py:39
  134.6 30.4 %collective-permute-start.23 = (bf16[256,512]{1,0:T(8,128)(2,1)S(1)}, bf16[256,512]{1,0:T(8,128)(2,1)S(1)}, u32[]{:S(2)}, u32[]{:S(2)}) collective-permute-start(bf16[256,512]{1,0:T(8,128)(2,1)S(1)} %fusion.12), channel_id=1, source_target_pairs={{0,2},{1,3},{2,0},{3,1},{4,6},{5,7},{6,4},{7,5},{8,10},{9,11},{10,... | collective-permute-start | bytes 786440 | tf_op jit(solution)/shard_map/ppermute | solution.py:43
  137.0 28.1 %collective-permute-start.21 = (bf16[256,512]{1,0:T(8,128)(2,1)S(1)}, bf16[256,512]{1,0:T(8,128)(2,1)S(1)}, u32[]{:S(2)}, u32[]{:S(2)}) collective-permute-start(bf16[256,512]{1,0:T(8,128)(2,1)S(1)} %fusion.11), channel_id=1, source_target_pairs={{0,6},{1,7},{2,4},{3,5},{4,2},{5,3},{6,0},{7,1},{8,14},{9,15},{10,... | collective-permute-start | bytes 786440 | tf_op jit(solution)/shard_map/ppermute | solution.py:43
  158.6 13.5 %collective-permute-start.29 = (bf16[256,1024]{1,0:T(8,128)(2,1)S(1)}, bf16[256,1024]{1,0:T(8,128)(2,1)S(1)}, u32[]{:S(2)}, u32[]{:S(2)}) collective-permute-start(bf16[256,1024]{1,0:T(8,128)(2,1)S(1)} %fusion.5), channel_id=1, source_target_pairs={{0,32},{32,0},{64,96},{96,64},{1,33},{33,1},{65,97},{97,65},{2,34}... | collective-permute-start | bytes 1572872 | tf_op jit(solution)/shard_map/ppermute | solution.py:39
  159.8 14.4 %collective-permute-start.27 = (bf16[256,1024]{1,0:T(8,128)(2,1)S(1)}, bf16[256,1024]{1,0:T(8,128)(2,1)S(1)}, u32[]{:S(2)}, u32[]{:S(2)}) collective-permute-start(bf16[256,1024]{1,0:T(8,128)(2,1)S(1)} %fusion.4), channel_id=1, source_target_pairs={{0,96},{32,64},{64,32},{96,0},{1,97},{33,65},{65,33},{97,1},{2,98}... | collective-permute-start | bytes 1572872 | tf_op jit(solution)/shard_map/ppermute | solution.py:39
  162.1 15.6 %collective-permute-start.16 = (bf16[128,512]{1,0:T(8,128)(2,1)S(1)}, bf16[128,512]{1,0:T(8,128)(2,1)S(1)}, u32[]{:S(2)}, u32[]{:S(2)}) collective-permute-start(bf16[128,512]{1,0:T(8,128)(2,1)S(1)} %get-tuple-element.45), channel_id=1, source_target_pairs={{0,16},{8,24},{16,0},{24,8},{1,17},{9,25},{17,1},{25,9},{2,18},{10... | collective-permute-start | bytes 393224 | tf_op jit(solution)/shard_map/ppermute | solution.py:31
  165.2 13.2 %collective-permute-start.24 = (bf16[256,512]{1,0:T(8,128)(2,1)S(1)}, bf16[256,512]{1,0:T(8,128)(2,1)S(1)}, u32[]{:S(2)}, u32[]{:S(2)}) collective-permute-start(bf16[256,512]{1,0:T(8,128)(2,1)S(1)} %select_convert_fusion), channel_id=1, source_target_pairs={{0,1},{1,0},{2,3},{3,2},{4,5},{5,4},{6,7},{7,6},{8,9},{9,8},{10,11... | collective-permute-start | bytes 786440 | tf_op jit(solution)/shard_map/ppermute | solution.py:35
  174.7 13.8 %collective-permute-start.30 = (bf16[256,1024]{1,0:T(8,128)(2,1)S(1)}, bf16[256,1024]{1,0:T(8,128)(2,1)S(1)}, u32[]{:S(2)}, u32[]{:S(2)}) collective-permute-start(bf16[256,1024]{1,0:T(8,128)(2,1)S(1)} %get-tuple-element.35), channel_id=1, source_target_pairs={{0,16},{8,24},{16,0},{24,8},{1,17},{9,25},{17,1},{25,9},{2,18},{10... | collective-permute-start | bytes 1572872 | tf_op jit(solution)/shard_map/ppermute | solution.py:31

commit v2 on v0

v2 whole, which is shorter than its diff:
```python
import jax
import jax.numpy as jnp
from jax import lax
from jax.experimental import pallas as pl
from jax.experimental.pallas import tpu as pltpu
from jax.sharding import PartitionSpec as P

DH = 256
BF = jnp.bfloat16
F32 = jnp.float32
NT = (((1,), (1,)), ((), ()))
TN = (((0,), (0,)), ((), ()))
MB = 1024 * 1024
VMEM = pl.BlockSpec(memory_space=pltpu.VMEM)
ANY = pl.BlockSpec(memory_space=pl.ANY)
H, C, Z, YL, D, T = range(6)


def arr(shape, dtype=BF):
    return jax.ShapeDtypeStruct(shape, dtype)


def call(body, name, inputs, outputs, scratch=(), hbm=(), mb=12, alias=None, flops=1):
    def wrapped(*refs):
        n = len(inputs)
        seq, t = lax.axis_index("seq"), lax.axis_index("tensor")
        place = [seq >> 1, seq & 1, t >> 1, t & 1, lax.axis_index("dp"), t]
        body(place, *refs[1:n], *refs[n + 1 :])

    args = [inputs[0]]
    specs = [ANY]
    for i, x in enumerate(inputs[1:]):
        pinned = i in hbm
        args.append(pltpu.with_memory_space_constraint(x, pltpu.HBM) if pinned else x)
        specs.append(ANY if pinned else VMEM)
    return pl.pallas_call(
        wrapped,
        in_specs=specs,
        out_specs=[ANY] + [VMEM] * len(outputs),
        out_shape=[arr(inputs[0].shape, inputs[0].dtype)] + list(outputs),
        scratch_shapes=list(scratch),
        input_output_aliases={0: 0, **(alias or {})},
        compiler_params=pltpu.CompilerParams(vmem_limit_bytes=mb * MB),
        cost_estimate=pl.CostEstimate(flops=flops, bytes_accessed=1, transcendentals=0),
        name=name,
    )(*args)


def swap_seq(x, m):
    return lax.ppermute(x, "seq", [(s, s ^ m) for s in range(4)])


def swap_ylo(x):
    return lax.ppermute(x, "tensor", [(t, t ^ 1) for t in range(8)])


def swap_x(x, m):
    return lax.ppermute(x, "dp", [(d, d ^ m) for d in range(4)])


def swap_z(x, m):
    return lax.ppermute(x, "tensor", [(t, t ^ (2 * m)) for t in range(8)])


def swap_y(x, m):
    pairs = []
    for s in range(4):
        for t in range(8):
            y = ((s // 2) * 2 + t % 2) ^ m
            pairs.append((s * 8 + t, ((y // 2) * 2 + s % 2) * 8 + (t // 2) * 2 + y % 2))
    return lax.ppermute(x, ("seq", "tensor"), pairs)


def cols(which):
    return pl.ds(pl.multiple_of(which * 256, 256), 256)


def join_body(idx, y0, y1, y2, y3, z0, z1, z2, z3, q, gc, ya, zb, qg_own, qg_send, sems):
    h = idx[H]
    copies = []
    for i, (layer, out) in enumerate(((h, qg_own), (1 - h, qg_send))):
        for n, x in enumerate((q, gc)):
            copies.append(pltpu.make_async_copy(x.at[layer, 0], out.at[n], sems.at[i, n]))
    for copy in copies:
        copy.start()
    ya[0, :256] = y0[...]
    ya[0, 256:] = y2[...]
    ya[1, :256] = y1[...]
    ya[1, 256:] = y3[...]
    zb[0] = z0[...]
    zb[1] = z1[...]
    zb[2] = z2[...]
    zb[3] = z3[...]
    for copy in copies:
        copy.wait()


def weight_rows(w, idx, m, b, which):
    base = (idx[Z] ^ m) * 1024 + (idx[YL] ^ b) * 512 + which * 256
    return w[idx[H], pl.ds(pl.multiple_of(base, 256), 256)]


def product(idx, w, terms):
    left = jnp.concatenate([block for block, _, _, _ in terms], axis=1)
    right = jnp.concatenate([weight_rows(w, idx, m, b, which) for _, m, b, which in terms], axis=0)
    return jnp.dot(left, right, preferred_element_type=F32)


def project_first_body(idx, wk, wv, ya, zb, az1, az3, by1, by3, acc, es):
    c = idx[C]
    terms = [(ya[0], 0, 0, c), (ya[1], 0, 1, c)]
    terms += [(az1[0], 1, 0, c), (az1[1], 1, 1, c), (az3[0], 3, 0, c), (az3[1], 3, 1, c)]
    terms += [(jnp.concatenate([by1[m], by3[m]], axis=0), m, 1, 1 - c) for m in range(4)]
    for n, w in enumerate((wk, wv)):
        at = slice(n * 512, n * 512 + 512)
        acc[:, at] = product(idx, w, terms)
        acc[:256, at] += product(idx, w, [(zb[m], m, 0, 1 - c) for m in range(4)])
    for n, b in enumerate((zb, by1, by3)):
        es[n] = b[...]


def project_last_body(idx, wk, wv, acc, az20, az21, by20, by21, send, keep, es, total):
    c = idx[C]
    by2 = [by20[0], by20[1], by21[0], by21[1]]
    for n, w in enumerate((wk, wv)):
        at = slice(n * 512, n * 512 + 512)
        total[:, at] = acc[:, at] + product(idx, w, [(az20[0], 2, 0, c), (az21[0], 2, 1, c)])
        total[256:, at] += product(idx, w, [(by2[m], m, 0, 1 - c) for m in range(4)])
    for out, which in ((keep, c), (send, 1 - c)):
        out[:, :256] = total[:, cols(which)].astype(BF)
        out[:, 256:] = total[:, cols(2 + which)].astype(BF)
    es[:2] = by20[...]
    es[2:] = by21[...]


def turn_keep_body(idx, ya, az1, az20, az21, az3, qg1, qg3, es_in, late_in, out, es, late):
    for r, block in enumerate(
        (ya[0], ya[1], az1[0], az1[1], az20[0], az21[0], az3[0], az3[1])
    ):
        out[r] = block.T


def turn_other_body(idx, es, late, out):
    for m in range(4):
        out[2 * m, :, :256] = es[0, m].T
        out[2 * m, :, 256:] = late[m].T
        out[2 * m + 1, :, :256] = es[1, m].T
        out[2 * m + 1, :, 256:] = es[2, m].T


def attend_body(idx, kv_own, kv_oth, qg0, qg1, qg2, qg3, g, g_far, gq_own, gq_core, gq_yhi, acc):
    mine = cols(idx[C])
    scale = DH ** (-0.5)
    acc[...] = jnp.zeros_like(acc)
    blocks = ((qg0, gq_own), (qg1, gq_core.at[0]), (qg2, gq_yhi), (qg3, gq_core.at[1]))
    for qg, gq in blocks:
        q = qg[0, :, mine]
        gc = qg[1, :, mine]
        s = [
            lax.dot_general(kv[:, :256], q, NT, preferred_element_type=F32) * scale
            for kv in (kv_own, kv_oth)
        ]
        top = jnp.maximum(
            jnp.max(s[0], axis=0, keepdims=True), jnp.max(s[1], axis=0, keepdims=True)
        )
        p = [jnp.exp(part - top) for part in s]
        total = jnp.sum(p[0], axis=0, keepdims=True) + jnp.sum(p[1], axis=0, keepdims=True)
        p = [part / total for part in p]
        dp = [
            lax.dot_general(kv[:, 256:], gc, NT, preferred_element_type=F32)
            for kv in (kv_own, kv_oth)
        ]
        delta = jnp.sum(p[0] * dp[0], axis=0, keepdims=True) + jnp.sum(
            p[1] * dp[1], axis=0, keepdims=True
        )
        ds = [(a * (b - delta) * scale).astype(BF) for a, b in zip(p, dp)]
        low = [a.astype(BF) for a in p]
        total_q = jnp.zeros((128, 256), F32)
        for part, kv in enumerate((kv_own, kv_oth)):
            rows = slice(part * 512, part * 512 + 512)
            acc[0, rows] += jnp.dot(ds[part], q, preferred_element_type=F32).astype(BF).astype(F32)
            acc[1, rows] += jnp.dot(low[part], gc, preferred_element_type=F32).astype(BF).astype(F32)
            total_q += lax.dot_general(ds[part], kv[:, :256], TN, preferred_element_type=F32)
        gq[...] = total_q.astype(BF)
    for n in range(2):
        g[n] = acc[n].astype(BF)
        g_far[0, n] = acc[n, 256:512].astype(BF)
        g_far[1, n] = acc[n, 768:].astype(BF)


def weight_job(idx, keep_t, oth_t, g, gp, n, dp_to, parity, out):
    r = (2 * dp_to + parity) ^ idx[T]
    own, oth = keep_t[r], oth_t[r]
    c = idx[C]
    left = jnp.dot(own, g[n, :512], preferred_element_type=F32)
    left += jnp.dot(oth, g[n, 512:], preferred_element_type=F32)
    right = jnp.dot(own, gp[n, 512:], preferred_element_type=F32)
    right += jnp.dot(oth, gp[n, :512], preferred_element_type=F32)
    out[:, cols(c)] = left.astype(out.dtype)
    out[:, cols(1 - c)] = right.astype(out.dtype)


SENT = ((1, 2), (3, 2))
KEPT = ((0, 3), (0, 1))


def weights_first_body(idx, keep_t, oth_t, g, gp, sk, sv):
    for n, out in enumerate((sk, sv)):
        for slot in range(2):
            weight_job(idx, keep_t, oth_t, g, gp, n, idx[D] ^ SENT[n][slot], 1 - idx[H], out.at[slot])


def weights_rest_body(idx, keep_t, oth_t, g, gp, sk, sv, k1k, k1v, k2k, k2v):
    for n, out in enumerate((sk, sv)):
        for slot in range(2):
            weight_job(idx, keep_t, oth_t, g, gp, n, idx[D] ^ SENT[n][slot], idx[H], out.at[slot])
    for parity, outs in ((1 - idx[H], (k1k, k1v)), (idx[H], (k2k, k2v))):
        for n, out in enumerate(outs):
            for slot in range(2):
                weight_job(idx, keep_t, oth_t, g, gp, n, idx[D] ^ KEPT[n][slot], parity, out.at[slot])


def add(keep, got, x, f):
    x[...] = (keep[1] + got[1].astype(F32)).astype(BF)
    f[...] = keep[0] + got[0].astype(F32)


def add_body(idx, ka, kb, ga, gb, xa, xb, fa, fb):
    add(ka, ga, xa, fa)
    add(kb, gb, xb, fb)


def pair_body(idx, fk, fv, gk, gv, sk_in, sv_in, gq0, gq1, gq2, pair, sk, sv, grad_q):
    pair[0] = (fk[...] + gk[...].astype(F32)).astype(BF)
    pair[1] = (fv[...] + gv[...].astype(F32)).astype(BF)
    h, c = idx[H], idx[C]
    grad_q[h, 0, :, cols(c)] = gq0[...]
    grad_q[h, 0, :, cols(1 - c)] = gq1[0]
    grad_q[1 - h, 0] = gq2[...]


def finish_weights_body(idx, fk, fv, gk, gv, theirs, wk, wv):
    h = idx[H]
    wk[h] = (fk[...] + gk[...].astype(F32)).astype(BF)
    wv[h] = (fv[...] + gv[...].astype(F32)).astype(BF)
    wk[1 - h] = theirs[0]
    wv[1 - h] = theirs[1]


def encoder_rows(idx, steps, parity, slot):
    start = ((idx[Z] ^ steps[parity][slot]) * 2 + parity) * 512
    return pl.ds(pl.multiple_of(start, 512), 512)


def turn_grads(idx, rhs, at, first, second):
    for n in range(2):
        rhs[cols(at + 2 * n + idx[C])] = first(n).T
        rhs[cols(at + 2 * n + 1 - idx[C])] = second(n).T


def encoder_own_body(idx, wk, wv, g, gp, out, rhs):
    turn_grads(idx, rhs, 0, lambda n: g[n, :256], lambda n: gp[n, 512:768])
    for slot in range(2):
        for parity in range(2):
            rows = encoder_rows(idx, SENT, parity, slot)
            left = jnp.concatenate([wk[idx[H], rows], wv[idx[H], rows]], axis=1)
            out[parity, slot] = jnp.dot(left, rhs[...], preferred_element_type=F32)


def relay_body(idx, x, out):
    pass


def encoder_sent_body(idx, wk, wv, own, far, far_core, gq_yhi, gq_got, out_a, out_b, gq_send, rhs):
    gq_send[:, cols(idx[C])] = gq_yhi[...]
    gq_send[:, cols(1 - idx[C])] = gq_got[1]
    turn_grads(idx, rhs, 0, lambda n: far[0, n], lambda n: far_core[0, n])
    for slot in range(2):
        for parity, out in enumerate((out_a, out_b)):
            rows = encoder_rows(idx, SENT, parity, slot)
            left = jnp.concatenate([wk[1 - idx[H], rows], wv[1 - idx[H], rows]], axis=1)
            total = own[parity, slot] + jnp.dot(left, rhs[...], preferred_element_type=F32)
            out[slot] = total.astype(BF)


def encoder_kept_body(idx, wk, wv, g, gp, far, far_core, out_a, out_b, rhs):
    turn_grads(idx, rhs, 0, lambda n: g[n, :256], lambda n: gp[n, 512:768])
    turn_grads(idx, rhs, 4, lambda n: far[0, n], lambda n: far_core[0, n])
    h = idx[H]
    for slot in range(2):
        for parity, out in enumerate((out_a, out_b)):
            rows = encoder_rows(idx, KEPT, parity, slot)
            left = jnp.concatenate([wk[h, rows], wv[h, rows], wk[1 - h, rows], wv[1 - h, rows]], axis=1)
            out[slot] = jnp.dot(left, rhs[...], preferred_element_type=F32)


def encoder_pair_body(idx, fa, fb, ga, gb, mine, theirs):
    yl = idx[YL]

    @pl.when(yl == 0)
    def _():
        mine[...] = fa[...] + ga[...].astype(F32)
        theirs[...] = (fb[...] + gb[...].astype(F32)).astype(BF)

    @pl.when(yl == 1)
    def _():
        mine[...] = fb[...] + gb[...].astype(F32)
        theirs[...] = (fa[...] + ga[...].astype(F32)).astype(BF)


def finish_encoder_body(idx, mine, theirs, out):
    out[0] = (mine[...] + theirs[...].astype(F32)).T.astype(BF)


def on_device(encoder_out, w_key, w_value, queries, grad_context):
    idx = jnp.zeros((8, 128), jnp.int32)
    c = lax.axis_index("seq") & 1
    dma = pltpu.SemaphoreType.DMA
    qg_block = arr((2, 128, 512))

    halves = jnp.stack([encoder_out[0, :, :256], encoder_out[0, :, 256:]])
    mine = lax.dynamic_index_in_dim(halves, c, 0, keepdims=False)
    other = lax.dynamic_index_in_dim(halves, 1 - c, 0, keepdims=False)
    parts = [mine] + [swap_y(mine, m) for m in (1, 2, 3)] + [other] + [swap_z(other, m) for m in (1, 2, 3)]
    idx, ya, zb, qg0, qg_send = call(
        join_body, "join", [idx, *parts, queries, grad_context],
        [arr((2, 512, 256)), arr((4, 256, 256)), qg_block, qg_block], [dma((2, 2))], hbm=(8, 9), flops=30_000_000_000,
    )
    az1, az3 = swap_z(ya, 1), swap_z(ya, 3)
    by1, by3 = swap_y(zb, 1), swap_y(zb, 3)
    az20, az21 = swap_z(az1[:1], 3), swap_z(az3[1:], 1)
    by20, by21 = swap_y(by1[:2], 3), swap_y(by3[2:], 1)

    ws = [w_key, w_value]
    qg2 = swap_seq(qg_send, 2)
    qg1, qg3 = swap_seq(qg0, 1), swap_seq(qg2, 1)
    idx, acc, es = call(
        project_first_body, "project_first", [idx, *ws, ya, zb, az1, az3, by1, by3],
        [arr((512, 1024), F32), arr((3, 4, 256, 256))],
    )
    idx, kv_send, kv_own, late = call(
        project_last_body, "project_last", [idx, *ws, acc, az20, az21, by20, by21],
        [arr((512, 512)), arr((512, 512)), arr((4, 256, 256))], [pltpu.VMEM((512, 1024), F32)],
    )
    kv_oth = swap_seq(kv_send, 1)
    idx, keep_t, es, late = call(
        turn_keep_body, "turn_keep", [idx, ya, az1, az20, az21, az3, qg1, qg3, es, late],
        [arr((8, 256, 512)), arr((3, 4, 256, 256)), arr((4, 256, 256))], alias={8: 2, 9: 3},
    )
    es_oth, late_oth = swap_seq(es, 1), swap_seq(late, 1)

    idx, g, g_far, gq_own, gq_core, gq_yhi = call(
        attend_body, "attend", [idx, kv_own, kv_oth, qg0, qg1, qg2, qg3],
        [arr((2, 1024, 256)), arr((2, 2, 256, 256)), arr((128, 256)), arr((2, 128, 256)), arr((128, 256))],
        [pltpu.VMEM((2, 1024, 256), F32)],
    )
    gp = swap_seq(g, 1)
    far = swap_seq(g_far, 2)
    gq_got = swap_seq(gq_core, 1)
    idx, oth_t = call(turn_other_body, "turn_other", [idx, es_oth, late_oth], [arr((8, 256, 512))])

    one, two = (256, 512), (2, 256, 512)
    mats = [keep_t, oth_t, g, gp]
    idx, s1k, s1v = call(weights_first_body, "weights_first", [idx, *mats], [arr(two)] * 2)
    got1k, got1v = swap_x(s1k, 1), swap_x(s1v, 3)
    idx, s2k, s2v, k1k, k1v, k2k, k2v = call(
        weights_rest_body, "weights_rest", [idx, *mats], [arr(two)] * 2 + [arr(two, F32)] * 4
    )

    one_t, two_t = (512, 256), (2, 512, 256)
    rhs = [pltpu.VMEM((2048, 256), BF)]
    rhs_half = [pltpu.VMEM((1024, 256), BF)]
    idx, own = call(
        encoder_own_body, "encoder_own", [idx, *ws, g, gp], [arr((2, *two_t), F32)], rhs_half
    )
    idx, far = call(relay_body, "relay", [idx, far], [arr((2, 2, 256, 256))], alias={1: 1})
    far_core = swap_seq(far[1:], 1)
    idx, ea, eb, gq_send = call(
        encoder_sent_body, "encoder_sent", [idx, *ws, own, far, far_core, gq_yhi, gq_got],
        [arr(two_t)] * 2 + [arr((128, 512))], rhs_half,
    )
    gq_theirs = swap_seq(gq_send, 2)
    got_a, got_b = swap_z(ea, 1), swap_z(eb, 3)
    idx, x1k, x1v, f1k, f1v = call(
        add_body, "add_first", [idx, k1k, k1v, got1k, got1v], [arr(one)] * 2 + [arr(one, F32)] * 2
    )
    last1k, last1v = swap_x(x1k, 3), swap_x(x1v, 1)
    idx, ka, kb = call(
        encoder_kept_body, "encoder_kept", [idx, *ws, g, gp, far, far_core], [arr(two_t, F32)] * 2, rhs
    )
    idx, pair, s2k, s2v, grad_q = call(
        pair_body, "weights_pair",
        [idx, f1k, f1v, last1k, last1v, s2k, s2v, gq_own, gq_got, gq_theirs],
        [arr(two)] * 3 + [arr((2, 1, 128, 512))], alias={5: 2, 6: 3},
    )
    w_theirs = swap_seq(pair, 2)
    got2k, got2v = swap_x(s2k, 1), swap_x(s2v, 3)
    idx, xa, xb, fa, fb = call(
        add_body, "encoder_add", [idx, ka, kb, got_a, got_b], [arr(one_t)] * 2 + [arr(one_t, F32)] * 2
    )
    last_a, last_b = swap_z(xa, 3), swap_z(xb, 1)
    idx, x2k, x2v, f2k, f2v = call(
        add_body, "weights_add", [idx, k2k, k2v, got2k, got2v], [arr(one)] * 2 + [arr(one, F32)] * 2
    )
    last2k, last2v = swap_x(x2k, 3), swap_x(x2v, 1)
    idx, e_mine, e_theirs = call(
        encoder_pair_body, "encoder_pair", [idx, fa, fb, last_a, last_b], [arr(one_t, F32), arr(one_t)]
    )
    e_got = swap_ylo(e_theirs)
    idx, grad_enc = call(finish_encoder_body, "finish_encoder", [idx, e_mine, e_got], [arr((1, 256, 512))])
    idx, grad_wk, grad_wv = call(
        finish_weights_body, "finish_weights", [idx, f2k, f2v, last2k, last2v, w_theirs], [arr(two)] * 2
    )
    return grad_q, grad_enc, grad_wk, grad_wv


def solution(mesh):
    placed = (
        P("dp", "seq", "tensor"),
        P(None, None, "tensor"),
        P(None, None, "tensor"),
        P(None, "dp", "seq", "tensor"),
        P(None, "dp", "seq", "tensor"),
    )
    return jax.shard_map(
        on_device,
        mesh=mesh,
        in_specs=placed,
        out_specs=(
            P(None, "dp", "seq", "tensor"),
            P("dp", "seq", "tensor"),
            P(None, ("dp", "seq"), "tensor"),
            P(None, ("dp", "seq"), "tensor"),
        ),
        check_vma=False,
    )
```

time: 614 us -> 116 us (0.19)
  waiting for transfers between devices: 493 us -> 45.3 us
  matrix products: 83.8 us -> 0 us
  starting transfers between devices: 0.9 us -> 44 us
  Pallas kernels: 0 us -> 24.8 us
  local copies, waits for them, and re-layouts: 16.5 us -> 1.1 us
  between operations: 14.3 us -> 0.9 us
    reduce_scatter x7 -> x0, waiting for transfers between devices: 382 us -> none  [the longest x2 209 us: on_device(): lax.psum_scatter(jnp.einsum('rd,rh->dh', flat_enc, joined, preferred_elem...]
    all_gather x5 -> x0, waiting for transfers between devices: 110 us -> none  [the longest x1 56.5 us: on_device(): full_enc = lax.all_gather(encoder_out, 'tensor', axis=2, tiled=True)]
    dot_general x20 -> x0, matrix products: 83.8 us -> none  [the longest x2 14.8 us: on_device(): jnp.einsum('bsh,dh->bsd', low_v, w_value[layer], preferred_element_type=j...]
    ppermute x0 -> x39, waiting for transfers between devices: none -> 45.3 us  [the longest x7 15.4 us: swap_y(): return lax.ppermute(x, ('seq', 'tensor'), pairs)]
    ppermute x0 -> x39, starting transfers between devices: none -> 44 us  [the longest x11 18 us: swap_z(): return lax.ppermute(x, 'tensor', [(t, t ^ 2 * m) for t in range(8)])]
    pallas_call x0 -> x19, Pallas kernels: none -> 24.8 us  [call(): pl.pallas_call(wrapped, in_specs=specs, out_specs=[ANY] + [VMEM] * len(ou...]
    unnamed x22 -> x8, local copies, waits for them, and re-layouts: 9.08 us -> 0.02 us
  transfers between devices with their start and end apart: 12 -> 39, of which waited for: 12 -> 19; matrix products, arithmetic and copies ran while one was open for 14% -> 0% of each run, Pallas kernels for 0% -> 19%
where the time goes in v2:
time: 116 us
  waiting for transfers between devices  45.3 us (39%)
  starting transfers between devices  44 us (38%)
  Pallas kernels  24.8 us (21%)
    pallas_call x19, Pallas kernels, call(): pl.pallas_call(wrapped, in_specs=specs, out_specs=[ANY] + [VMEM] * len(ou...  24.8 us
    ppermute x11, starting transfers between devices, swap_z(): return lax.ppermute(x, 'tensor', [(t, t ^ 2 * m) for t in range(8)])  18 us
    ppermute x7, waiting for transfers between devices, swap_y(): return lax.ppermute(x, ('seq', 'tensor'), pairs)  15.4 us
    ppermute x12, waiting for transfers between devices, swap_seq(): return lax.ppermute(x, 'seq', [(s, s ^ m) for s in range(4)])  10.9 us
    ppermute x8, starting transfers between devices, swap_x(): return lax.ppermute(x, 'dp', [(d, d ^ m) for d in range(4)])  10.2 us
    ppermute x7, starting transfers between devices, swap_y(): return lax.ppermute(x, ('seq', 'tensor'), pairs)  9.61 us
    ppermute x8, waiting for transfers between devices, swap_x(): return lax.ppermute(x, 'dp', [(d, d ^ m) for d in range(4)])  9 us
    ppermute x1, waiting for transfers between devices, swap_ylo(): return lax.ppermute(x, 'tensor', [(t, t ^ 1) for t in range(8)])  7.3 us
  transfers between devices with their start and end apart: 39, of which 19 were waited for; matrix products, arithmetic and copies ran while one was open for 0% of the time, Pallas kernels for 19%

profile of v2, /device:TPU:0, one launch (start us, length us, event | category | flops | bytes accessed | tf_op | source)
XLA Modules:
  0.0 116.2 jit_solution(17433828059601496857)
XLA Ops:
  0.6 1.0 fusion.4
  1.8 4.2 %collective-permute-start.5 = (bf16[256,256]{1,0:T(8,128)(2,1)S(1)}, bf16[256,256]{1,0:T(8,128)(2,1)S(1)}, u32[]{:S(2)}, u32[]{:S(2)}) collective-permute-start(bf16[256,256]{1,0:T(8,128)(2,1)S(1)} %get-tuple-element.148.refs_5_), channel_id=1, source_target_pairs={{0,6},{1,7},{2,4},{3,5},{4,2},{5,3},{6,0},{7,1},{8,14},{9,15},{10,... | collective-permute-start | bytes 393224 | tf_op jit(solution)/shard_map/ppermute | solution.py:62
  6.0 0.9 collective-permute-start.3
  6.9 3.0 %collective-permute-start.2 = (bf16[256,256]{1,0:T(8,128)(2,1)S(1)}, bf16[256,256]{1,0:T(8,128)(2,1)S(1)}, u32[]{:S(2)}, u32[]{:S(2)}) collective-permute-start(bf16[256,256]{1,0:T(8,128)(2,1)S(1)} %get-tuple-element.149.refs_1_), channel_id=1, source_target_pairs={{0,17},{1,16},{2,19},{3,18},{4,21},{5,20},{6,23},{7,22},{8,25},{9,... | collective-permute-start | bytes 393224 | tf_op jit(solution)/shard_map/ppermute | solution.py:71
  10.5 1.0 collective-permute-done.5.refs_8_
  11.5 1.6 %collective-permute-start = (bf16[256,256]{1,0:T(8,128)(2,1)S(1)}, bf16[256,256]{1,0:T(8,128)(2,1)S(1)}, u32[]{:S(2)}, u32[]{:S(2)}) collective-permute-start(bf16[256,256]{1,0:T(8,128)(2,1)S(1)} %get-tuple-element.149.refs_1_), channel_id=1, source_target_pairs={{0,1},{1,0},{2,3},{3,2},{4,5},{5,4},{6,7},{7,6},{8,9},{9,8},{10,11... | collective-permute-start | bytes 393224 | tf_op jit(solution)/shard_map/ppermute | solution.py:71
  13.1 0.7 collective-permute-done.4.refs_7_
  13.8 1.1 collective-permute-done.2.refs_4_
  14.9 1.8 %collective-permute-done.1.refs_3_ = bf16[256,256]{1,0:T(8,128)(2,1)S(1)} collective-permute-done((bf16[256,256]{1,0:T(8,128)(2,1)S(1)}, bf16[256,256]{1,0:T(8,128)(2,1)S(1)}, u32[]{:S(2)}, u32[]{:S(2)}) %collective-permute-start.1) | collective-permute-done | bytes 131104 | tf_op jit(solution)/shard_map/ppermute | solution.py:71
  16.8 1.3 %join.1 = (s32[8,128]{1,0:T(8,128)S(1)}, bf16[2,512,256]{2,1,0:T(8,128)(2,1)S(1)}, bf16[4,256,256]{2,1,0:T(8,128)(2,1)S(1)}, bf16[2,128,512]{2,1,0:T(8,128)(2,1)S(1)}, bf16[2,128,512]{2,1,0:T(8,128)(2,1)S(1)}) custom-call(s32[8,128]{1,0:T(8,128)S(1)} %broadcast_in_dim.3.refs_0_, ...), custom_call_target="tpu_custom_call", output_to_operand_aliasing={{0}: (0, {})} | custom-call | flops 30000001024 | bytes 1 | tf_op jit(solution)/shard_map/join/pallas_call | solution.py:36
  18.1 3.1 %collective-permute-start.9 = (bf16[4,256,256]{2,1,0:T(8,128)(2,1)S(1)}, bf16[4,256,256]{2,1,0:T(8,128)(2,1)S(1)}, u32[]{:S(2)}, u32[]{:S(2)}) collective-permute-start(bf16[4,256,256]{2,1,0:T(8,128)(2,1)S(1)} %get-tuple-element.78.refs_4_), channel_id=1, source_target_pairs={{0,17},{1,16},{2,19},{3,18},{4,21},{5,20},{6,23},{7,22},{8,25},{9,... | collective-permute-start | bytes 1572872 | tf_op jit(solution)/shard_map/ppermute | solution.py:71
  21.3 3.5 %collective-permute-start.7 = (bf16[2,512,256]{2,1,0:T(8,128)(2,1)S(1)}, bf16[2,512,256]{2,1,0:T(8,128)(2,1)S(1)}, u32[]{:S(2)}, u32[]{:S(2)}) collective-permute-start(bf16[2,512,256]{2,1,0:T(8,128)(2,1)S(1)} %get-tuple-element.77.refs_3_.refs_1_), channel_id=1, source_target_pairs={{0,6},{1,7},{2,4},{3,5},{4,2},{5,3},{6,0},{7,1},{8,14},{9,15},{10,... | collective-permute-start | bytes 1572872 | tf_op jit(solution)/shard_map/ppermute | solution.py:62
  24.8 1.5 %collective-permute-start.15 = (bf16[2,128,512]{2,1,0:T(8,128)(2,1)S(1)}, bf16[2,128,512]{2,1,0:T(8,128)(2,1)S(1)}, u32[]{:S(2)}, u32[]{:S(2)}) collective-permute-start(bf16[2,128,512]{2,1,0:T(8,128)(2,1)S(1)} %get-tuple-element.83), channel_id=1, source_target_pairs={{0,16},{8,24},{16,0},{24,8},{1,17},{9,25},{17,1},{25,9},{2,18},{10... | collective-permute-start | bytes 786440 | tf_op jit(solution)/shard_map/ppermute | solution.py:50
  26.3 6.8 %collective-permute-done.9.refs_8_ = bf16[4,256,256]{2,1,0:T(8,128)(2,1)S(1)} collective-permute-done((bf16[4,256,256]{2,1,0:T(8,128)(2,1)S(1)}, bf16[4,256,256]{2,1,0:T(8,128)(2,1)S(1)}, u32[]{:S(2)}, u32[]{:S(2)}) %collective-permute-start.9) | collective-permute-done | bytes 524320 | tf_op jit(solution)/shard_map/ppermute | solution.py:71
  33.8 2.2 %collective-permute-done.8.refs_7_ = bf16[4,256,256]{2,1,0:T(8,128)(2,1)S(1)} collective-permute-done((bf16[4,256,256]{2,1,0:T(8,128)(2,1)S(1)}, bf16[4,256,256]{2,1,0:T(8,128)(2,1)S(1)}, u32[]{:S(2)}, u32[]{:S(2)}) %collective-permute-start.8) | collective-permute-done | bytes 524320 | tf_op jit(solution)/shard_map/ppermute | solution.py:71
  36.6 1.5 %collective-permute-start.11 = (bf16[1,512,256]{2,1,0:T(8,128)(2,1)S(1)}, bf16[1,512,256]{2,1,0:T(8,128)(2,1)S(1)}, u32[]{:S(2)}, u32[]{:S(2)}) collective-permute-start(bf16[1,512,256]{2,1,0:T(8,128)(2,1)S(1)} %slice.29), channel_id=1, source_target_pairs={{0,2},{1,3},{2,0},{3,1},{4,6},{5,7},{6,4},{7,5},{8,10},{9,11},{10,... | collective-permute-start | bytes 786440 | tf_op jit(solution)/shard_map/ppermute | solution.py:62
  38.1 2.3 %collective-permute-start.10 = (bf16[1,512,256]{2,1,0:T(8,128)(2,1)S(1)}, bf16[1,512,256]{2,1,0:T(8,128)(2,1)S(1)}, u32[]{:S(2)}, u32[]{:S(2)}) collective-permute-start(bf16[1,512,256]{2,1,0:T(8,128)(2,1)S(1)} %slice.28), channel_id=1, source_target_pairs={{0,6},{1,7},{2,4},{3,5},{4,2},{5,3},{6,0},{7,1},{8,14},{9,15},{10,... | collective-permute-start | bytes 786440 | tf_op jit(solution)/shard_map/ppermute | solution.py:62
  40.4 1.0 collective-permute-done.15.refs_5_
  41.4 3.5 %collective-permute-done.13.refs_7_ = bf16[2,256,256]{2,1,0:T(8,128)(2,1)S(1)} collective-permute-done((bf16[2,256,256]{2,1,0:T(8,128)(2,1)S(1)}, bf16[2,256,256]{2,1,0:T(8,128)(2,1)S(1)}, u32[]{:S(2)}, u32[]{:S(2)}) %collective-permute-start.13) | collective-permute-done | bytes 262176 | tf_op jit(solution)/shard_map/ppermute | solution.py:71
  44.9 3.4 %project_first.1 = (s32[8,128]{1,0:T(8,128)S(1)}, f32[512,1024]{1,0:T(8,128)S(1)}, bf16[3,4,256,256]{3,2,1,0:T(8,128)(2,1)S(1)}) custom-call(s32[8,128]{1,0:T(8,128)S(1)} %get-tuple-element.76.refs_0_, bf16[2,4096,512]{2,1,0:T(8,128)(2,1)S(1)} %bitcast.5, bf16[2,4096,512]{2,1,0:T(8,128)(2,1)S(1)} %bitcast.7, ...), custom_call_target="tpu_custom_call", output_to_operand_aliasing={{0}: (0, {})} | custom-call | flops 1 | bytes 1 | tf_op jit(solution)/shard_map/project_first/pallas_call | solution.py:36
  48.4 1.7 %project_last.1 = (s32[8,128]{1,0:T(8,128)S(1)}, bf16[512,512]{1,0:T(8,128)(2,1)S(1)}, bf16[512,512]{1,0:T(8,128)(2,1)S(1)}, bf16[4,256,256]{2,1,0:T(8,128)(2,1)S(1)}) custom-call(s32[8,128]{1,0:T(8,128)S(1)} %get-tuple-element.79.refs_0_, bf16[2,4096,512]{2,1,0:T(8,128)(2,1)S(1)} %bitcast.5, ...), custom_call_target="tpu_custom_call", output_to_operand_aliasing={{0}: (0, {})} | custom-call | flops 1 | bytes 1 | tf_op jit(solution)/shard_map/project_last/pallas_call | solution.py:36
  52.1 3.9 %attend.1 = (s32[8,128]{1,0:T(8,128)S(1)}, bf16[2,1024,256]{2,1,0:T(8,128)(2,1)S(1)}, bf16[2,2,256,256]{3,2,1,0:T(8,128)(2,1)S(1)}, bf16[128,256]{1,0:T(8,128)(2...) custom-call(s32[8,128]{1,0:T(8,128)S(1)} %get-tuple-element.86.refs_0_, ...), custom_call_target="tpu_custom_call", output_to_operand_aliasing={{0}: (0, {})} | custom-call | flops 1 | bytes 1 | tf_op jit(solution)/shard_map/attend/pallas_call | solution.py:36
  57.4 2.2 %collective-permute-done.19.refs_2_ = bf16[4,256,256]{2,1,0:T(8,128)(2,1)S(1)} collective-permute-done((bf16[4,256,256]{2,1,0:T(8,128)(2,1)S(1)}, bf16[4,256,256]{2,1,0:T(8,128)(2,1)S(1)}, u32[]{:S(2)}, u32[]{:S(2)}) %collective-permute-start.19) | collective-permute-done | bytes 524320 | tf_op jit(solution)/shard_map/ppermute | solution.py:50
  60.2 1.3 %weights_first.1 = (s32[8,128]{1,0:T(8,128)S(1)}, bf16[2,256,512]{2,1,0:T(8,128)(2,1)S(1)}, bf16[2,256,512]{2,1,0:T(8,128)(2,1)S(1)}) custom-call(s32[8,128]{1,0:T(8,128)S(1)} %get-tuple-element.92.refs_0_, bf16[8,256,512]{2,1,0:T(8,128)(2,1)S(1)} %get-tuple-element.93.refs_1_, ...), custom_call_target="tpu_custom_call", output_to_operand_aliasing={{0}: (0, {})} | custom-call | flops 1 | bytes 1 | tf_op jit(solution)/shard_map/weights_first/pallas_call | solution.py:36
  61.4 1.6 %collective-permute-start.24 = (bf16[2,256,512]{2,1,0:T(8,128)(2,1)S(1)}, bf16[2,256,512]{2,1,0:T(8,128)(2,1)S(1)}, u32[]{:S(2)}, u32[]{:S(2)}) collective-permute-start(bf16[2,256,512]{2,1,0:T(8,128)(2,1)S(1)} %get-tuple-element.108), channel_id=1, source_target_pairs={{0,32},{32,0},{64,96},{96,64},{1,33},{33,1},{65,97},{97,65},{2,34}... | collective-permute-start | bytes 1572872 | tf_op jit(solution)/shard_map/ppermute | solution.py:58
  63.0 2.1 %collective-permute-start.25 = (bf16[2,256,512]{2,1,0:T(8,128)(2,1)S(1)}, bf16[2,256,512]{2,1,0:T(8,128)(2,1)S(1)}, u32[]{:S(2)}, u32[]{:S(2)}) collective-permute-start(bf16[2,256,512]{2,1,0:T(8,128)(2,1)S(1)} %get-tuple-element.109), channel_id=1, source_target_pairs={{0,96},{32,64},{64,32},{96,0},{1,97},{33,65},{65,33},{97,1},{2,98}... | collective-permute-start | bytes 1572872 | tf_op jit(solution)/shard_map/ppermute | solution.py:58
  65.1 3.4 %weights_rest.1 = (s32[8,128]{1,0:T(8,128)S(1)}, bf16[2,256,512]{2,1,0:T(8,128)(2,1)S(1)}, bf16[2,256,512]{2,1,0:T(8,128)(2,1)S(1)}, f32[2,256,512]{2,1,0:T(8,12...) custom-call(s32[8,128]{1,0:T(8,128)S(1)} %get-tuple-element.96.refs_, ...), custom_call_target="tpu_custom_call", output_to_operand_aliasing={{0}: (0, {})} | custom-call | flops 1 | bytes 1 | tf_op jit(solution)/shard_map/weights_rest/pallas_call | solution.py:36
  68.5 1.4 %encoder_own.1 = (s32[8,128]{1,0:T(8,128)S(1)}, f32[2,2,512,256]{3,2,1,0:T(8,128)S(1)}) custom-call(s32[8,128]{1,0:T(8,128)S(1)} %get-tuple-element.97.refs_0_, bf16[2,4096,512]{2,1,0:T(8,128)(2,1)S(1)} %bitcast.5, bf16[2,4096,512]{2,1,0:T(8,128)(2,1)S(1)} %bitcast.7, ...), custom_call_target="tpu_custom_call", output_to_operand_aliasing={{0}: (0, {})} | custom-call | flops 1 | bytes 1 | tf_op jit(solution)/shard_map/encoder_own/pallas_call | solution.py:36
  69.9 2.4 %collective-permute-done.21.refs_1_ = bf16[2,2,256,256]{3,2,1,0:T(8,128)(2,1)S(1)} collective-permute-done((bf16[2,2,256,256]{3,2,1,0:T(8,128)(2,1)S(1)}, bf16[2,2,256,256]{3,2,1,0:T(8,128)(2,1)S(1)}, u32[]{:S(2)}, u32[]{:S(2)}) %collective-permute-start.21) | collective-permute-done | bytes 524320 | tf_op jit(solution)/shard_map/ppermute | solution.py:50
  73.0 1.2 %collective-permute-done.23.refs_7_.refs_8_ = bf16[2,128,256]{2,1,0:T(8,128)(2,1)S(1)} collective-permute-done((bf16[2,128,256]{2,1,0:T(8,128)(2,1)S(1)}, bf16[2,128,256]{2,1,0:T(8,128)(2,1)S(1)}, u32[]{:S(2)}, u32[]{:S(2)}) %collective-permute-start.23) | collective-permute-done | bytes 131104 | tf_op jit(solution)/shard_map/ppermute | solution.py:50
  74.2 1.4 %encoder_sent.1 = (s32[8,128]{1,0:T(8,128)S(1)}, bf16[2,512,256]{2,1,0:T(8,128)(2,1)S(1)}, bf16[2,512,256]{2,1,0:T(8,128)(2,1)S(1)}, bf16[128,512]{1,0:T(8,128)(2,1)S(1)}) custom-call(s32[8,128]{1,0:T(8,128)S(1)} %get-tuple-element.100.refs_0_, bf16[2,4096,512]{2,1,0:T(8,128)(2,1)S(1)} %bitcast.5, ...), custom_call_target="tpu_custom_call", output_to_operand_aliasing={{0}: (0, {})} | custom-call | flops 1 | bytes 1 | tf_op jit(solution)/shard_map/encoder_sent/pallas_call | solution.py:36
  75.7 2.4 %collective-permute-done.25.refs_4_ = bf16[2,256,512]{2,1,0:T(8,128)(2,1)S(1)} collective-permute-done((bf16[2,256,512]{2,1,0:T(8,128)(2,1)S(1)}, bf16[2,256,512]{2,1,0:T(8,128)(2,1)S(1)}, u32[]{:S(2)}, u32[]{:S(2)}) %collective-permute-start.25) | collective-permute-done | bytes 524320 | tf_op jit(solution)/shard_map/ppermute | solution.py:58
  78.3 2.2 %collective-permute-start.26 = (bf16[256,512]{1,0:T(8,128)(2,1)S(1)}, bf16[256,512]{1,0:T(8,128)(2,1)S(1)}, u32[]{:S(2)}, u32[]{:S(2)}) collective-permute-start(bf16[256,512]{1,0:T(8,128)(2,1)S(1)} %get-tuple-element.114), channel_id=1, source_target_pairs={{0,96},{32,64},{64,32},{96,0},{1,97},{33,65},{65,33},{97,1},{2,98}... | collective-permute-start | bytes 786440 | tf_op jit(solution)/shard_map/ppermute | solution.py:58
  80.5 0.7 collective-permute-start.29
  81.2 2.2 %collective-permute-start.30 = (bf16[2,512,256]{2,1,0:T(8,128)(2,1)S(1)}, bf16[2,512,256]{2,1,0:T(8,128)(2,1)S(1)}, u32[]{:S(2)}, u32[]{:S(2)}) collective-permute-start(bf16[2,512,256]{2,1,0:T(8,128)(2,1)S(1)} %get-tuple-element.125), channel_id=1, source_target_pairs={{0,6},{1,7},{2,4},{3,5},{4,2},{5,3},{6,0},{7,1},{8,14},{9,15},{10,... | collective-permute-start | bytes 1572872 | tf_op jit(solution)/shard_map/ppermute | solution.py:62
  84.1 2.4 %encoder_kept.1 = (s32[8,128]{1,0:T(8,128)S(1)}, f32[2,512,256]{2,1,0:T(8,128)S(1)}, f32[2,512,256]{2,1,0:T(8,128)S(1)}) custom-call(s32[8,128]{1,0:T(8,128)S(1)} %get-tuple-element.110.refs_0_, bf16[2,4096,512]{2,1,0:T(8,128)(2,1)S(1)} %bitcast.5, bf16[2,4096,512]{2,1,0:T(8,128)(2,1)S(1)} %bitcast.7, ...), custom_call_target="tpu_custom_call", output_to_operand_aliasing={{0}: (0, {})} | custom-call | flops 1 | bytes 1 | tf_op jit(solution)/shard_map/encoder_kept/pallas_call | solution.py:36
  86.5 3.4 %collective-permute-done.28.refs_9_ = bf16[128,512]{1,0:T(8,128)(2,1)S(1)} collective-permute-done((bf16[128,512]{1,0:T(8,128)(2,1)S(1)}, bf16[128,512]{1,0:T(8,128)(2,1)S(1)}, u32[]{:S(2)}, u32[]{:S(2)}) %collective-permute-start.28) | collective-permute-done | bytes 131104 | tf_op jit(solution)/shard_map/ppermute | solution.py:50
  89.9 0.8 weights_pair.1
  90.7 2.0 %collective-permute-start.31 = (bf16[2,256,512]{2,1,0:T(8,128)(2,1)S(1)}, bf16[2,256,512]{2,1,0:T(8,128)(2,1)S(1)}, u32[]{:S(2)}, u32[]{:S(2)}) collective-permute-start(bf16[2,256,512]{2,1,0:T(8,128)(2,1)S(1)} %get-tuple-element.129), channel_id=1, source_target_pairs={{0,32},{32,0},{64,96},{96,64},{1,33},{33,1},{65,97},{97,65},{2,34}... | collective-permute-start | bytes 1572872 | tf_op jit(solution)/shard_map/ppermute | solution.py:58
  92.8 1.1 collective-permute-start.32
  93.9 1.0 collective-permute-done.30.refs_4_
  95.1 2.6 %collective-permute-start.33 = (bf16[512,256]{1,0:T(8,128)(2,1)S(1)}, bf16[512,256]{1,0:T(8,128)(2,1)S(1)}, u32[]{:S(2)}, u32[]{:S(2)}) collective-permute-start(bf16[512,256]{1,0:T(8,128)(2,1)S(1)} %get-tuple-element.134), channel_id=1, source_target_pairs={{0,6},{1,7},{2,4},{3,5},{4,2},{5,3},{6,0},{7,1},{8,14},{9,15},{10,... | collective-permute-start | bytes 786440 | tf_op jit(solution)/shard_map/ppermute | solution.py:62
  98.3 3.8 %collective-permute-done.31.refs_3_ = bf16[2,256,512]{2,1,0:T(8,128)(2,1)S(1)} collective-permute-done((bf16[2,256,512]{2,1,0:T(8,128)(2,1)S(1)}, bf16[2,256,512]{2,1,0:T(8,128)(2,1)S(1)}, u32[]{:S(2)}, u32[]{:S(2)}) %collective-permute-start.31) | collective-permute-done | bytes 524320 | tf_op jit(solution)/shard_map/ppermute | solution.py:58
  102.1 2.7 %collective-permute-done.32.refs_4_ = bf16[2,256,512]{2,1,0:T(8,128)(2,1)S(1)} collective-permute-done((bf16[2,256,512]{2,1,0:T(8,128)(2,1)S(1)}, bf16[2,256,512]{2,1,0:T(8,128)(2,1)S(1)}, u32[]{:S(2)}, u32[]{:S(2)}) %collective-permute-start.32) | collective-permute-done | bytes 524320 | tf_op jit(solution)/shard_map/ppermute | solution.py:58
  105.8 1.2 collective-permute-start.36
  106.9 7.3 %collective-permute-done.35.refs_2_ = bf16[512,256]{1,0:T(8,128)(2,1)S(1)} collective-permute-done((bf16[512,256]{1,0:T(8,128)(2,1)S(1)}, bf16[512,256]{1,0:T(8,128)(2,1)S(1)}, u32[]{:S(2)}, u32[]{:S(2)}) %collective-permute-start.35) | collective-permute-done | bytes 262176 | tf_op jit(solution)/shard_map/ppermute | solution.py:54
  114.2 0.9 finish_encoder.1
  115.1 1.1 finish_weights.1
  (67 shorter events, 9.5 us)
Async XLA Ops:
  1.8 9.8 %collective-permute-start.5 = (bf16[256,256]{1,0:T(8,128)(2,1)S(1)}, bf16[256,256]{1,0:T(8,128)(2,1)S(1)}, u32[]{:S(2)}, u32[]{:S(2)}) collective-permute-start(bf16[256,256]{1,0:T(8,128)(2,1)S(1)} %get-tuple-element.148.refs_5_), channel_id=1, source_target_pairs={{0,6},{1,7},{2,4},{3,5},{4,2},{5,3},{6,0},{7,1},{8,14},{9,15},{10,... | collective-permute-start | bytes 393224 | tf_op jit(solution)/shard_map/ppermute | solution.py:62
  6.0 7.9 %collective-permute-start.4 = (bf16[256,256]{1,0:T(8,128)(2,1)S(1)}, bf16[256,256]{1,0:T(8,128)(2,1)S(1)}, u32[]{:S(2)}, u32[]{:S(2)}) collective-permute-start(bf16[256,256]{1,0:T(8,128)(2,1)S(1)} %get-tuple-element.148.refs_5_), channel_id=1, source_target_pairs={{0,4},{1,5},{2,6},{3,7},{4,0},{5,1},{6,2},{7,3},{8,12},{9,13},{10,... | collective-permute-start | bytes 393224 | tf_op jit(solution)/shard_map/ppermute | solution.py:62
  6.0 7.9 %collective-permute-start.3 = (bf16[256,256]{1,0:T(8,128)(2,1)S(1)}, bf16[256,256]{1,0:T(8,128)(2,1)S(1)}, u32[]{:S(2)}, u32[]{:S(2)}) collective-permute-start(bf16[256,256]{1,0:T(8,128)(2,1)S(1)} %get-tuple-element.148.refs_5_), channel_id=1, source_target_pairs={{0,2},{1,3},{2,0},{3,1},{4,6},{5,7},{6,4},{7,5},{8,10},{9,11},{10,... | collective-permute-start | bytes 393224 | tf_op jit(solution)/shard_map/ppermute | solution.py:62
  6.9 8.0 %collective-permute-start.2 = (bf16[256,256]{1,0:T(8,128)(2,1)S(1)}, bf16[256,256]{1,0:T(8,128)(2,1)S(1)}, u32[]{:S(2)}, u32[]{:S(2)}) collective-permute-start(bf16[256,256]{1,0:T(8,128)(2,1)S(1)} %get-tuple-element.149.refs_1_), channel_id=1, source_target_pairs={{0,17},{1,16},{2,19},{3,18},{4,21},{5,20},{6,23},{7,22},{8,25},{9,... | collective-permute-start | bytes 393224 | tf_op jit(solution)/shard_map/ppermute | solution.py:71
  9.9 6.8 %collective-permute-start.1 = (bf16[256,256]{1,0:T(8,128)(2,1)S(1)}, bf16[256,256]{1,0:T(8,128)(2,1)S(1)}, u32[]{:S(2)}, u32[]{:S(2)}) collective-permute-start(bf16[256,256]{1,0:T(8,128)(2,1)S(1)} %get-tuple-element.149.refs_1_), channel_id=1, source_target_pairs={{0,16},{1,17},{2,18},{3,19},{4,20},{5,21},{6,22},{7,23},{8,24},{9,... | collective-permute-start | bytes 393224 | tf_op jit(solution)/shard_map/ppermute | solution.py:71
  11.5 5.2 %collective-permute-start = (bf16[256,256]{1,0:T(8,128)(2,1)S(1)}, bf16[256,256]{1,0:T(8,128)(2,1)S(1)}, u32[]{:S(2)}, u32[]{:S(2)}) collective-permute-start(bf16[256,256]{1,0:T(8,128)(2,1)S(1)} %get-tuple-element.149.refs_1_), channel_id=1, source_target_pairs={{0,1},{1,0},{2,3},{3,2},{4,5},{5,4},{6,7},{7,6},{8,9},{9,8},{10,11... | collective-permute-start | bytes 393224 | tf_op jit(solution)/shard_map/ppermute | solution.py:71
  16.7 28.1 %slice-start = ((s8[8388608]{0:T(1024)(128)(4,1)}), s8[4194304]{0:T(1024)(128)(4,1)S(1)}, s32[]{:S(2)}) async-start(s8[8388608]{0:T(1024)(128)(4,1)} %bitcast.4), calls=%async_computation | async-start | bytes 8388608
  16.7 28.1 %slice-start.2 = ((s8[8388608]{0:T(1024)(128)(4,1)}), s8[4194304]{0:T(1024)(128)(4,1)S(1)}, s32[]{:S(2)}) async-start(s8[8388608]{0:T(1024)(128)(4,1)} %bitcast.6), calls=%async_computation.2 | async-start | bytes 8388608
  16.8 28.1 %slice-start.1 = ((s8[8388608]{0:T(1024)(128)(4,1)}), s8[4194304]{0:T(1024)(128)(4,1)S(1)}, s32[]{:S(2)}) async-start(s8[8388608]{0:T(1024)(128)(4,1)} %bitcast.4), calls=%async_computation.1 | async-start | bytes 8388608
  16.8 28.1 %slice-start.3 = ((s8[8388608]{0:T(1024)(128)(4,1)}), s8[4194304]{0:T(1024)(128)(4,1)S(1)}, s32[]{:S(2)}) async-start(s8[8388608]{0:T(1024)(128)(4,1)} %bitcast.6), calls=%async_computation.3 | async-start | bytes 8388608
  18.1 15.1 %collective-permute-start.9 = (bf16[4,256,256]{2,1,0:T(8,128)(2,1)S(1)}, bf16[4,256,256]{2,1,0:T(8,128)(2,1)S(1)}, u32[]{:S(2)}, u32[]{:S(2)}) collective-permute-start(bf16[4,256,256]{2,1,0:T(8,128)(2,1)S(1)} %get-tuple-element.78.refs_4_), channel_id=1, source_target_pairs={{0,17},{1,16},{2,19},{3,18},{4,21},{5,20},{6,23},{7,22},{8,25},{9,... | collective-permute-start | bytes 1572872 | tf_op jit(solution)/shard_map/ppermute | solution.py:71
  21.2 14.9 %collective-permute-start.8 = (bf16[4,256,256]{2,1,0:T(8,128)(2,1)S(1)}, bf16[4,256,256]{2,1,0:T(8,128)(2,1)S(1)}, u32[]{:S(2)}, u32[]{:S(2)}) collective-permute-start(bf16[4,256,256]{2,1,0:T(8,128)(2,1)S(1)} %get-tuple-element.78.refs_4_), channel_id=1, source_target_pairs={{0,1},{1,0},{2,3},{3,2},{4,5},{5,4},{6,7},{7,6},{8,9},{9,8},{10,11... | collective-permute-start | bytes 1572872 | tf_op jit(solution)/shard_map/ppermute | solution.py:71
  21.3 15.3 %collective-permute-start.7 = (bf16[2,512,256]{2,1,0:T(8,128)(2,1)S(1)}, bf16[2,512,256]{2,1,0:T(8,128)(2,1)S(1)}, u32[]{:S(2)}, u32[]{:S(2)}) collective-permute-start(bf16[2,512,256]{2,1,0:T(8,128)(2,1)S(1)} %get-tuple-element.77.refs_3_.refs_1_), channel_id=1, source_target_pairs={{0,6},{1,7},{2,4},{3,5},{4,2},{5,3},{6,0},{7,1},{8,14},{9,15},{10,... | collective-permute-start | bytes 1572872 | tf_op jit(solution)/shard_map/ppermute | solution.py:62
  24.8 13.3 %collective-permute-start.6 = (bf16[2,512,256]{2,1,0:T(8,128)(2,1)S(1)}, bf16[2,512,256]{2,1,0:T(8,128)(2,1)S(1)}, u32[]{:S(2)}, u32[]{:S(2)}) collective-permute-start(bf16[2,512,256]{2,1,0:T(8,128)(2,1)S(1)} %get-tuple-element.77.refs_3_.refs_1_), channel_id=1, source_target_pairs={{0,2},{1,3},{2,0},{3,1},{4,6},{5,7},{6,4},{7,5},{8,10},{9,11},{10,... | collective-permute-start | bytes 1572872 | tf_op jit(solution)/shard_map/ppermute | solution.py:62
  24.8 16.6 %collective-permute-start.15 = (bf16[2,128,512]{2,1,0:T(8,128)(2,1)S(1)}, bf16[2,128,512]{2,1,0:T(8,128)(2,1)S(1)}, u32[]{:S(2)}, u32[]{:S(2)}) collective-permute-start(bf16[2,128,512]{2,1,0:T(8,128)(2,1)S(1)} %get-tuple-element.83), channel_id=1, source_target_pairs={{0,16},{8,24},{16,0},{24,8},{1,17},{9,25},{17,1},{25,9},{2,18},{10... | collective-permute-start | bytes 786440 | tf_op jit(solution)/shard_map/ppermute | solution.py:50
  33.2 11.7 %collective-permute-start.13 = (bf16[2,256,256]{2,1,0:T(8,128)(2,1)S(1)}, bf16[2,256,256]{2,1,0:T(8,128)(2,1)S(1)}, u32[]{:S(2)}, u32[]{:S(2)}) collective-permute-start(bf16[2,256,256]{2,1,0:T(8,128)(2,1)S(1)} %slice.31), channel_id=1, source_target_pairs={{0,1},{1,0},{2,3},{3,2},{4,5},{5,4},{6,7},{7,6},{8,9},{9,8},{10,11... | collective-permute-start | bytes 786440 | tf_op jit(solution)/shard_map/ppermute | solution.py:71
  36.0 12.3 %collective-permute-start.12 = (bf16[2,256,256]{2,1,0:T(8,128)(2,1)S(1)}, bf16[2,256,256]{2,1,0:T(8,128)(2,1)S(1)}, u32[]{:S(2)}, u32[]{:S(2)}) collective-permute-start(bf16[2,256,256]{2,1,0:T(8,128)(2,1)S(1)} %slice.30), channel_id=1, source_target_pairs={{0,17},{1,16},{2,19},{3,18},{4,21},{5,20},{6,23},{7,22},{8,25},{9,... | collective-permute-start | bytes 786440 | tf_op jit(solution)/shard_map/ppermute | solution.py:71
  36.6 11.8 %collective-permute-start.11 = (bf16[1,512,256]{2,1,0:T(8,128)(2,1)S(1)}, bf16[1,512,256]{2,1,0:T(8,128)(2,1)S(1)}, u32[]{:S(2)}, u32[]{:S(2)}) collective-permute-start(bf16[1,512,256]{2,1,0:T(8,128)(2,1)S(1)} %slice.29), channel_id=1, source_target_pairs={{0,2},{1,3},{2,0},{3,1},{4,6},{5,7},{6,4},{7,5},{8,10},{9,11},{10,... | collective-permute-start | bytes 786440 | tf_op jit(solution)/shard_map/ppermute | solution.py:62
  38.1 10.3 %collective-permute-start.10 = (bf16[1,512,256]{2,1,0:T(8,128)(2,1)S(1)}, bf16[1,512,256]{2,1,0:T(8,128)(2,1)S(1)}, u32[]{:S(2)}, u32[]{:S(2)}) collective-permute-start(bf16[1,512,256]{2,1,0:T(8,128)(2,1)S(1)} %slice.28), channel_id=1, source_target_pairs={{0,6},{1,7},{2,4},{3,5},{4,2},{5,3},{6,0},{7,1},{8,14},{9,15},{10,... | collective-permute-start | bytes 786440 | tf_op jit(solution)/shard_map/ppermute | solution.py:62
  41.4 9.2 %collective-permute-start.14 = (bf16[2,128,512]{2,1,0:T(8,128)(2,1)S(1)}, bf16[2,128,512]{2,1,0:T(8,128)(2,1)S(1)}, u32[]{:S(2)}, u32[]{:S(2)}) collective-permute-start(bf16[2,128,512]{2,1,0:T(8,128)(2,1)S(1)} %get-tuple-element.82.refs_3_), channel_id=1, source_target_pairs={{0,8},{8,0},{16,24},{24,16},{1,9},{9,1},{17,25},{25,17},{2,10},{10... | collective-permute-start | bytes 786440 | tf_op jit(solution)/shard_map/ppermute | solution.py:50
  44.9 5.7 %collective-permute-start.16 = (bf16[2,128,512]{2,1,0:T(8,128)(2,1)S(1)}, bf16[2,128,512]{2,1,0:T(8,128)(2,1)S(1)}, u32[]{:S(2)}, u32[]{:S(2)}) collective-permute-start(bf16[2,128,512]{2,1,0:T(8,128)(2,1)S(1)} %collective-permute-done.15.refs_5_), channel_id=1, source_target_pairs={{0,8},{8,0},{16,24},{24,16},{1,9},{9,1},{17,25},{25,17},{2,10},{10... | collective-permute-start | bytes 786440 | tf_op jit(solution)/shard_map/ppermute | solution.py:50
  50.0 2.1 %collective-permute-start.17 = (bf16[512,512]{1,0:T(8,128)(2,1)S(1)}, bf16[512,512]{1,0:T(8,128)(2,1)S(1)}, u32[]{:S(2)}, u32[]{:S(2)}) collective-permute-start(bf16[512,512]{1,0:T(8,128)(2,1)S(1)} %get-tuple-element.88), channel_id=1, source_target_pairs={{0,8},{8,0},{16,24},{24,16},{1,9},{9,1},{17,25},{25,17},{2,10},{10... | collective-permute-start | bytes 1572872 | tf_op jit(solution)/shard_map/ppermute | solution.py:50
  51.2 8.4 %collective-permute-start.18 = (bf16[3,4,256,256]{3,2,1,0:T(8,128)(2,1)S(1)}, bf16[3,4,256,256]{3,2,1,0:T(8,128)(2,1)S(1)}, u32[]{:S(2)}, u32[]{:S(2)}) collective-permute-start(bf16[3,4,256,256]{3,2,1,0:T(8,128)(2,1)S(1)} %get-tuple-element.90), channel_id=1, source_target_pairs={{0,8},{8,0},{16,24},{24,16},{1,9},{9,1},{17,25},{25,17},{2,10},{10... | collective-permute-start | bytes 4718600 | tf_op jit(solution)/shard_map/ppermute | solution.py:50
  56.1 4.1 %collective-permute-start.20 = (bf16[2,1024,256]{2,1,0:T(8,128)(2,1)S(1)}, bf16[2,1024,256]{2,1,0:T(8,128)(2,1)S(1)}, u32[]{:S(2)}, u32[]{:S(2)}) collective-permute-start(bf16[2,1024,256]{2,1,0:T(8,128)(2,1)S(1)} %get-tuple-element.95.refs_3_), channel_id=1, source_target_pairs={{0,8},{8,0},{16,24},{24,16},{1,9},{9,1},{17,25},{25,17},{2,10},{10... | collective-permute-start | bytes 3145736 | tf_op jit(solution)/shard_map/ppermute | solution.py:50
  56.5 3.1 %collective-permute-start.19 = (bf16[4,256,256]{2,1,0:T(8,128)(2,1)S(1)}, bf16[4,256,256]{2,1,0:T(8,128)(2,1)S(1)}, u32[]{:S(2)}, u32[]{:S(2)}) collective-permute-start(bf16[4,256,256]{2,1,0:T(8,128)(2,1)S(1)} %get-tuple-element.91), channel_id=1, source_target_pairs={{0,8},{8,0},{16,24},{24,16},{1,9},{9,1},{17,25},{25,17},{2,10},{10... | collective-permute-start | bytes 1572872 | tf_op jit(solution)/shard_map/ppermute | solution.py:50
  56.7 15.7 %collective-permute-start.21 = (bf16[2,2,256,256]{3,2,1,0:T(8,128)(2,1)S(1)}, bf16[2,2,256,256]{3,2,1,0:T(8,128)(2,1)S(1)}, u32[]{:S(2)}, u32[]{:S(2)}) collective-permute-start(bf16[2,2,256,256]{3,2,1,0:T(8,128)(2,1)S(1)} %get-tuple-element.99), channel_id=1, source_target_pairs={{0,16},{8,24},{16,0},{24,8},{1,17},{9,25},{17,1},{25,9},{2,18},{10... | collective-permute-start | bytes 1572872 | tf_op jit(solution)/shard_map/ppermute | solution.py:50
  61.4 14.3 %collective-permute-start.24 = (bf16[2,256,512]{2,1,0:T(8,128)(2,1)S(1)}, bf16[2,256,512]{2,1,0:T(8,128)(2,1)S(1)}, u32[]{:S(2)}, u32[]{:S(2)}) collective-permute-start(bf16[2,256,512]{2,1,0:T(8,128)(2,1)S(1)} %get-tuple-element.108), channel_id=1, source_target_pairs={{0,32},{32,0},{64,96},{96,64},{1,33},{33,1},{65,97},{97,65},{2,34}... | collective-permute-start | bytes 1572872 | tf_op jit(solution)/shard_map/ppermute | solution.py:58
  63.0 15.1 %collective-permute-start.25 = (bf16[2,256,512]{2,1,0:T(8,128)(2,1)S(1)}, bf16[2,256,512]{2,1,0:T(8,128)(2,1)S(1)}, u32[]{:S(2)}, u32[]{:S(2)}) collective-permute-start(bf16[2,256,512]{2,1,0:T(8,128)(2,1)S(1)} %get-tuple-element.109), channel_id=1, source_target_pairs={{0,96},{32,64},{64,32},{96,0},{1,97},{33,65},{65,33},{97,1},{2,98}... | collective-permute-start | bytes 1572872 | tf_op jit(solution)/shard_map/ppermute | solution.py:58
  72.4 1.8 %collective-permute-start.22 = (bf16[1,2,256,256]{3,2,1,0:T(8,128)(2,1)S(1)}, bf16[1,2,256,256]{3,2,1,0:T(8,128)(2,1)S(1)}, u32[]{:S(2)}, u32[]{:S(2)}) collective-permute-start(bf16[1,2,256,256]{3,2,1,0:T(8,128)(2,1)S(1)} %slice.27), channel_id=1, source_target_pairs={{0,8},{8,0},{16,24},{24,16},{1,9},{9,1},{17,25},{25,17},{2,10},{10... | collective-permute-start | bytes 786440 | tf_op jit(solution)/shard_map/ppermute | solution.py:50
  72.5 1.7 %collective-permute-start.23 = (bf16[2,128,256]{2,1,0:T(8,128)(2,1)S(1)}, bf16[2,128,256]{2,1,0:T(8,128)(2,1)S(1)}, u32[]{:S(2)}, u32[]{:S(2)}) collective-permute-start(bf16[2,128,256]{2,1,0:T(8,128)(2,1)S(1)} %get-tuple-element.104), channel_id=1, source_target_pairs={{0,8},{8,0},{16,24},{24,16},{1,9},{9,1},{17,25},{25,17},{2,10},{10... | collective-permute-start | bytes 393224 | tf_op jit(solution)/shard_map/ppermute | solution.py:50
  78.3 11.7 %collective-permute-start.26 = (bf16[256,512]{1,0:T(8,128)(2,1)S(1)}, bf16[256,512]{1,0:T(8,128)(2,1)S(1)}, u32[]{:S(2)}, u32[]{:S(2)}) collective-permute-start(bf16[256,512]{1,0:T(8,128)(2,1)S(1)} %get-tuple-element.114), channel_id=1, source_target_pairs={{0,96},{32,64},{64,32},{96,0},{1,97},{33,65},{65,33},{97,1},{2,98}... | collective-permute-start | bytes 786440 | tf_op jit(solution)/shard_map/ppermute | solution.py:58
  80.5 9.5 %collective-permute-start.27 = (bf16[256,512]{1,0:T(8,128)(2,1)S(1)}, bf16[256,512]{1,0:T(8,128)(2,1)S(1)}, u32[]{:S(2)}, u32[]{:S(2)}) collective-permute-start(bf16[256,512]{1,0:T(8,128)(2,1)S(1)} %get-tuple-element.115), channel_id=1, source_target_pairs={{0,32},{32,0},{64,96},{96,64},{1,33},{33,1},{65,97},{97,65},{2,34}... | collective-permute-start | bytes 786440 | tf_op jit(solution)/shard_map/ppermute | solution.py:58
  80.5 13.4 %collective-permute-start.29 = (bf16[2,512,256]{2,1,0:T(8,128)(2,1)S(1)}, bf16[2,512,256]{2,1,0:T(8,128)(2,1)S(1)}, u32[]{:S(2)}, u32[]{:S(2)}) collective-permute-start(bf16[2,512,256]{2,1,0:T(8,128)(2,1)S(1)} %get-tuple-element.124), channel_id=1, source_target_pairs={{0,2},{1,3},{2,0},{3,1},{4,6},{5,7},{6,4},{7,5},{8,10},{9,11},{10,... | collective-permute-start | bytes 1572872 | tf_op jit(solution)/shard_map/ppermute | solution.py:62
  81.2 13.7 %collective-permute-start.30 = (bf16[2,512,256]{2,1,0:T(8,128)(2,1)S(1)}, bf16[2,512,256]{2,1,0:T(8,128)(2,1)S(1)}, u32[]{:S(2)}, u32[]{:S(2)}) collective-permute-start(bf16[2,512,256]{2,1,0:T(8,128)(2,1)S(1)} %get-tuple-element.125), channel_id=1, source_target_pairs={{0,6},{1,7},{2,4},{3,5},{4,2},{5,3},{6,0},{7,1},{8,14},{9,15},{10,... | collective-permute-start | bytes 1572872 | tf_op jit(solution)/shard_map/ppermute | solution.py:62
  83.5 6.5 %collective-permute-start.28 = (bf16[128,512]{1,0:T(8,128)(2,1)S(1)}, bf16[128,512]{1,0:T(8,128)(2,1)S(1)}, u32[]{:S(2)}, u32[]{:S(2)}) collective-permute-start(bf16[128,512]{1,0:T(8,128)(2,1)S(1)} %get-tuple-element.119), channel_id=1, source_target_pairs={{0,16},{8,24},{16,0},{24,8},{1,17},{9,25},{17,1},{25,9},{2,18},{10... | collective-permute-start | bytes 393224 | tf_op jit(solution)/shard_map/ppermute | solution.py:50
  90.7 11.3 %collective-permute-start.31 = (bf16[2,256,512]{2,1,0:T(8,128)(2,1)S(1)}, bf16[2,256,512]{2,1,0:T(8,128)(2,1)S(1)}, u32[]{:S(2)}, u32[]{:S(2)}) collective-permute-start(bf16[2,256,512]{2,1,0:T(8,128)(2,1)S(1)} %get-tuple-element.129), channel_id=1, source_target_pairs={{0,32},{32,0},{64,96},{96,64},{1,33},{33,1},{65,97},{97,65},{2,34}... | collective-permute-start | bytes 1572872 | tf_op jit(solution)/shard_map/ppermute | solution.py:58
  92.8 12.0 %collective-permute-start.32 = (bf16[2,256,512]{2,1,0:T(8,128)(2,1)S(1)}, bf16[2,256,512]{2,1,0:T(8,128)(2,1)S(1)}, u32[]{:S(2)}, u32[]{:S(2)}) collective-permute-start(bf16[2,256,512]{2,1,0:T(8,128)(2,1)S(1)} %get-tuple-element.130), channel_id=1, source_target_pairs={{0,96},{32,64},{64,32},{96,0},{1,97},{33,65},{65,33},{97,1},{2,98}... | collective-permute-start | bytes 1572872 | tf_op jit(solution)/shard_map/ppermute | solution.py:58
  95.1 9.9 %collective-permute-start.33 = (bf16[512,256]{1,0:T(8,128)(2,1)S(1)}, bf16[512,256]{1,0:T(8,128)(2,1)S(1)}, u32[]{:S(2)}, u32[]{:S(2)}) collective-permute-start(bf16[512,256]{1,0:T(8,128)(2,1)S(1)} %get-tuple-element.134), channel_id=1, source_target_pairs={{0,6},{1,7},{2,4},{3,5},{4,2},{5,3},{6,0},{7,1},{8,14},{9,15},{10,... | collective-permute-start | bytes 786440 | tf_op jit(solution)/shard_map/ppermute | solution.py:62
  97.7 7.3 %collective-permute-start.34 = (bf16[512,256]{1,0:T(8,128)(2,1)S(1)}, bf16[512,256]{1,0:T(8,128)(2,1)S(1)}, u32[]{:S(2)}, u32[]{:S(2)}) collective-permute-start(bf16[512,256]{1,0:T(8,128)(2,1)S(1)} %get-tuple-element.135), channel_id=1, source_target_pairs={{0,2},{1,3},{2,0},{3,1},{4,6},{5,7},{6,4},{7,5},{8,10},{9,11},{10,... | collective-permute-start | bytes 786440 | tf_op jit(solution)/shard_map/ppermute | solution.py:62
  97.7 17.4 %collective-permute-start.38 = (bf16[2,256,512]{2,1,0:T(8,128)(2,1)S(1)}, bf16[2,256,512]{2,1,0:T(8,128)(2,1)S(1)}, u32[]{:S(2)}, u32[]{:S(2)}) collective-permute-start(bf16[2,256,512]{2,1,0:T(8,128)(2,1)S(1)} %get-tuple-element.145), channel_id=1, source_target_pairs={{0,16},{8,24},{16,0},{24,8},{1,17},{9,25},{17,1},{25,9},{2,18},{10... | collective-permute-start | bytes 1572872 | tf_op jit(solution)/shard_map/ppermute | solution.py:50
  105.1 9.1 %collective-permute-start.35 = (bf16[512,256]{1,0:T(8,128)(2,1)S(1)}, bf16[512,256]{1,0:T(8,128)(2,1)S(1)}, u32[]{:S(2)}, u32[]{:S(2)}) collective-permute-start(bf16[512,256]{1,0:T(8,128)(2,1)S(1)} %get-tuple-element.138), channel_id=1, source_target_pairs={{0,1},{1,0},{2,3},{3,2},{4,5},{5,4},{6,7},{7,6},{8,9},{9,8},{10,11... | collective-permute-start | bytes 786440 | tf_op jit(solution)/shard_map/ppermute | solution.py:54
  105.8 9.3 %collective-permute-start.36 = (bf16[256,512]{1,0:T(8,128)(2,1)S(1)}, bf16[256,512]{1,0:T(8,128)(2,1)S(1)}, u32[]{:S(2)}, u32[]{:S(2)}) collective-permute-start(bf16[256,512]{1,0:T(8,128)(2,1)S(1)} %get-tuple-element.143), channel_id=1, source_target_pairs={{0,96},{32,64},{64,32},{96,0},{1,97},{33,65},{65,33},{97,1},{2,98}... | collective-permute-start | bytes 786440 | tf_op jit(solution)/shard_map/ppermute | solution.py:58
  106.9 8.2 %collective-permute-start.37 = (bf16[256,512]{1,0:T(8,128)(2,1)S(1)}, bf16[256,512]{1,0:T(8,128)(2,1)S(1)}, u32[]{:S(2)}, u32[]{:S(2)}) collective-permute-start(bf16[256,512]{1,0:T(8,128)(2,1)S(1)} %get-tuple-element.144), channel_id=1, source_target_pairs={{0,32},{32,0},{64,96},{96,64},{1,33},{33,1},{65,97},{97,65},{2,34}... | collective-permute-start | bytes 786440 | tf_op jit(solution)/shard_map/ppermute | solution.py:58

commit v3 on v2

--- a/solution.py
+++ b/solution.py
@@ -75,7 +75,7 @@
     return pl.ds(pl.multiple_of(which * 256, 256), 256)
 
 
-def join_body(idx, y0, y1, y2, y3, z0, z1, z2, z3, q, gc, ya, zb, qg_own, qg_send, sems):
+def join_y_body(idx, y0, y1, y2, y3, q, gc, ya, qg_own, qg_send, sems):
     h = idx[H]
     copies = []
     for i, (layer, out) in enumerate(((h, qg_own), (1 - h, qg_send))):
@@ -87,12 +87,13 @@
     ya[0, 256:] = y2[...]
     ya[1, :256] = y1[...]
     ya[1, 256:] = y3[...]
-    zb[0] = z0[...]
-    zb[1] = z1[...]
-    zb[2] = z2[...]
-    zb[3] = z3[...]
     for copy in copies:
         copy.wait()
+
+
+def join_z_body(idx, z0, z1, z2, z3, zb):
+    for m, z in enumerate((z0, z1, z2, z3)):
+        zb[m] = z[...]
 
 
 def weight_rows(w, idx, m, b, which):
@@ -106,20 +107,27 @@
     return jnp.dot(left, right, preferred_element_type=F32)
 
 
-def project_first_body(idx, wk, wv, ya, zb, az1, az3, by1, by3, acc, es):
+def project_first_body(idx, wk, wv, ya, zb, by1, by3, acc, es):
     c = idx[C]
     terms = [(ya[0], 0, 0, c), (ya[1], 0, 1, c)]
-    terms += [(az1[0], 1, 0, c), (az1[1], 1, 1, c), (az3[0], 3, 0, c), (az3[1], 3, 1, c)]
     terms += [(jnp.concatenate([by1[m], by3[m]], axis=0), m, 1, 1 - c) for m in range(4)]
     for n, w in enumerate((wk, wv)):
         at = slice(n * 512, n * 512 + 512)
         acc[:, at] = product(idx, w, terms)
         acc[:256, at] += product(idx, w, [(zb[m], m, 0, 1 - c) for m in range(4)])
-    for n, b in enumerate((zb, by1, by3)):
-        es[n] = b[...]
-
-
-def project_last_body(idx, wk, wv, acc, az20, az21, by20, by21, send, keep, es, total):
+    for m, b in ((0, zb), (1, by1), (3, by3)):
+        es[4 * m : 4 * m + 4] = b[...]
+
+
+def project_next_body(idx, wk, wv, acc_in, az1, az3, acc):
+    c = idx[C]
+    terms = [(az1[0], 1, 0, c), (az1[1], 1, 1, c), (az3[0], 3, 0, c), (az3[1], 3, 1, c)]
+    for n, w in enumerate((wk, wv)):
+        at = slice(n * 512, n * 512 + 512)
+        acc[:, at] = acc_in[:, at] + product(idx, w, terms)
+
+
+def project_last_body(idx, wk, wv, acc, by20, by21, az20, az21, qg_own, qg_far, es_in, send, keep, es, total):
     c = idx[C]
     by2 = [by20[0], by20[1], by21[0], by21[1]]
     for n, w in enumerate((wk, wv)):
@@ -127,37 +135,42 @@
         total[:, at] = acc[:, at] + product(idx, w, [(az20[0], 2, 0, c), (az21[0], 2, 1, c)])
         total[256:, at] += product(idx, w, [(by2[m], m, 0, 1 - c) for m in range(4)])
     for out, which in ((keep, c), (send, 1 - c)):
-        out[:, :256] = total[:, cols(which)].astype(BF)
-        out[:, 256:] = total[:, cols(2 + which)].astype(BF)
-    es[:2] = by20[...]
-    es[2:] = by21[...]
-
-
-def turn_keep_body(idx, ya, az1, az20, az21, az3, qg1, qg3, es_in, late_in, out, es, late):
+        out[:512, :256] = total[:, cols(which)].astype(BF)
+        out[:512, 256:] = total[:, cols(2 + which)].astype(BF)
+    for i, qg in enumerate((qg_own, qg_far)):
+        for n in range(2):
+            send[512 + 128 * i : 640 + 128 * i, 256 * n : 256 * n + 256] = qg[n, :, cols(1 - c)]
+    es[8:10] = by20[...]
+    es[10:12] = by21[...]
+
+
+def turn_keep_body(idx, ya, az1, az20, az21, az3, out):
     for r, block in enumerate(
         (ya[0], ya[1], az1[0], az1[1], az20[0], az21[0], az3[0], az3[1])
     ):
         out[r] = block.T
 
 
-def turn_other_body(idx, es, late, out):
+def turn_other_body(idx, es, out):
     for m in range(4):
-        out[2 * m, :, :256] = es[0, m].T
-        out[2 * m, :, 256:] = late[m].T
-        out[2 * m + 1, :, :256] = es[1, m].T
-        out[2 * m + 1, :, 256:] = es[2, m].T
-
-
-def attend_body(idx, kv_own, kv_oth, qg0, qg1, qg2, qg3, g, g_far, gq_own, gq_core, gq_yhi, acc):
+        for b in range(2):
+            out[2 * m + b, :, :256] = es[4 * b + m].T
+            out[2 * m + b, :, 256:] = es[4 * (2 + b) + m].T
+
+
+def attend_body(idx, kv_own, kv_oth, qg_own, qg_far, g, g_far, gq_own, gq_far, acc):
     mine = cols(idx[C])
     scale = DH ** (-0.5)
     acc[...] = jnp.zeros_like(acc)
-    blocks = ((qg0, gq_own), (qg1, gq_core.at[0]), (qg2, gq_yhi), (qg3, gq_core.at[1]))
-    for qg, gq in blocks:
-        q = qg[0, :, mine]
-        gc = qg[1, :, mine]
+    blocks = [
+        (qg_own[0, :, mine], qg_own[1, :, mine], gq_own),
+        (kv_oth[512:640, :256], kv_oth[512:640, 256:], g.at[2048:2176]),
+        (qg_far[0, :, mine], qg_far[1, :, mine], gq_far),
+        (kv_oth[640:, :256], kv_oth[640:, 256:], g.at[2176:]),
+    ]
+    for q, gc, gq in blocks:
         s = [
-            lax.dot_general(kv[:, :256], q, NT, preferred_element_type=F32) * scale
+            lax.dot_general(kv[:512, :256], q, NT, preferred_element_type=F32) * scale
             for kv in (kv_own, kv_oth)
         ]
         top = jnp.maximum(
@@ -165,9 +178,10 @@
         )
         p = [jnp.exp(part - top) for part in s]
         total = jnp.sum(p[0], axis=0, keepdims=True) + jnp.sum(p[1], axis=0, keepdims=True)
-        p = [part / total for part in p]
+        inverse = 1.0 / total
+        p = [part * inverse for part in p]
         dp = [
-            lax.dot_general(kv[:, 256:], gc, NT, preferred_element_type=F32)
+            lax.dot_general(kv[:512, 256:], gc, NT, preferred_element_type=F32)
             for kv in (kv_own, kv_oth)
         ]
         delta = jnp.sum(p[0] * dp[0], axis=0, keepdims=True) + jnp.sum(
@@ -180,22 +194,23 @@
             rows = slice(part * 512, part * 512 + 512)
             acc[0, rows] += jnp.dot(ds[part], q, preferred_element_type=F32).astype(BF).astype(F32)
             acc[1, rows] += jnp.dot(low[part], gc, preferred_element_type=F32).astype(BF).astype(F32)
-            total_q += lax.dot_general(ds[part], kv[:, :256], TN, preferred_element_type=F32)
+            total_q += lax.dot_general(ds[part], kv[:512, :256], TN, preferred_element_type=F32)
         gq[...] = total_q.astype(BF)
     for n in range(2):
-        g[n] = acc[n].astype(BF)
-        g_far[0, n] = acc[n, 256:512].astype(BF)
-        g_far[1, n] = acc[n, 768:].astype(BF)
+        g[n * 1024 : n * 1024 + 1024] = acc[n].astype(BF)
+        g_far[0, n * 256 : n * 256 + 256] = acc[n, 256:512].astype(BF)
+        g_far[1, n * 256 : n * 256 + 256] = acc[n, 768:].astype(BF)
 
 
 def weight_job(idx, keep_t, oth_t, g, gp, n, dp_to, parity, out):
     r = (2 * dp_to + parity) ^ idx[T]
     own, oth = keep_t[r], oth_t[r]
     c = idx[C]
-    left = jnp.dot(own, g[n, :512], preferred_element_type=F32)
-    left += jnp.dot(oth, g[n, 512:], preferred_element_type=F32)
-    right = jnp.dot(own, gp[n, 512:], preferred_element_type=F32)
-    right += jnp.dot(oth, gp[n, :512], preferred_element_type=F32)
+    one, two = slice(n * 1024, n * 1024 + 512), slice(n * 1024 + 512, n * 1024 + 1024)
+    left = jnp.dot(own, g[one], preferred_element_type=F32)
+    left += jnp.dot(oth, g[two], preferred_element_type=F32)
+    right = jnp.dot(own, gp[two], preferred_element_type=F32)
+    right += jnp.dot(oth, gp[one], preferred_element_type=F32)
     out[:, cols(c)] = left.astype(out.dtype)
     out[:, cols(1 - c)] = right.astype(out.dtype)
 
@@ -230,21 +245,27 @@
     add(kb, gb, xb, fb)
 
 
-def pair_body(idx, fk, fv, gk, gv, sk_in, sv_in, gq0, gq1, gq2, pair, sk, sv, grad_q):
-    pair[0] = (fk[...] + gk[...].astype(F32)).astype(BF)
-    pair[1] = (fv[...] + gv[...].astype(F32)).astype(BF)
+def add_body(idx, ka, kb, ga, gb, xa, xb, fa, fb):
+    add(ka, ga, xa, fa)
+    add(kb, gb, xb, fb)
+
+
+def pair_body(idx, fk, fv, gk, gv, gq_far, gp, sk_in, sv_in, pair, sk, sv):
+    pair[:256] = (fk[...] + gk[...].astype(F32)).astype(BF)
+    pair[256:512] = (fv[...] + gv[...].astype(F32)).astype(BF)
+    pair[512:, cols(idx[C])] = gq_far[...]
+    pair[512:, cols(1 - idx[C])] = gp[2176:]
+
+
+def finish_weights_body(idx, fk, fv, gk, gv, theirs, gq_own, gp, wk, wv, grad_q):
     h, c = idx[H], idx[C]
-    grad_q[h, 0, :, cols(c)] = gq0[...]
-    grad_q[h, 0, :, cols(1 - c)] = gq1[0]
-    grad_q[1 - h, 0] = gq2[...]
-
-
-def finish_weights_body(idx, fk, fv, gk, gv, theirs, wk, wv):
-    h = idx[H]
     wk[h] = (fk[...] + gk[...].astype(F32)).astype(BF)
     wv[h] = (fv[...] + gv[...].astype(F32)).astype(BF)
-    wk[1 - h] = theirs[0]
-    wv[1 - h] = theirs[1]
+    wk[1 - h] = theirs[:256]
+    wv[1 - h] = theirs[256:512]
+    grad_q[h, 0, :, cols(c)] = gq_own[...]
+    grad_q[h, 0, :, cols(1 - c)] = gp[2048:2176]
+    grad_q[1 - h, 0] = theirs[512:]
 
 
 def encoder_rows(idx, steps, parity, slot):
@@ -259,7 +280,7 @@
 
 
 def encoder_own_body(idx, wk, wv, g, gp, out, rhs):
-    turn_grads(idx, rhs, 0, lambda n: g[n, :256], lambda n: gp[n, 512:768])
+    turn_grads(idx, rhs, 0, lambda n: g[n * 1024 : n * 1024 + 256], lambda n: gp[n * 1024 + 512 : n * 1024 + 768])
     for slot in range(2):
         for parity in range(2):
             rows = encoder_rows(idx, SENT, parity, slot)
@@ -267,14 +288,12 @@
             out[parity, slot] = jnp.dot(left, rhs[...], preferred_element_type=F32)
 
 
-def relay_body(idx, x, out):
+def relay_body(idx, *refs):
     pass
 
 
-def encoder_sent_body(idx, wk, wv, own, far, far_core, gq_yhi, gq_got, out_a, out_b, gq_send, rhs):
-    gq_send[:, cols(idx[C])] = gq_yhi[...]
-    gq_send[:, cols(1 - idx[C])] = gq_got[1]
-    turn_grads(idx, rhs, 0, lambda n: far[0, n], lambda n: far_core[0, n])
+def encoder_sent_body(idx, wk, wv, own, far, far_core, out_a, out_b, rhs):
+    turn_grads(idx, rhs, 0, lambda n: far[0, n * 256 : n * 256 + 256], lambda n: far_core[0, n * 256 : n * 256 + 256])
     for slot in range(2):
         for parity, out in enumerate((out_a, out_b)):
             rows = encoder_rows(idx, SENT, parity, slot)
@@ -284,8 +303,8 @@
 
 
 def encoder_kept_body(idx, wk, wv, g, gp, far, far_core, out_a, out_b, rhs):
-    turn_grads(idx, rhs, 0, lambda n: g[n, :256], lambda n: gp[n, 512:768])
-    turn_grads(idx, rhs, 4, lambda n: far[0, n], lambda n: far_core[0, n])
+    turn_grads(idx, rhs, 0, lambda n: g[n * 1024 : n * 1024 + 256], lambda n: gp[n * 1024 + 512 : n * 1024 + 768])
+    turn_grads(idx, rhs, 4, lambda n: far[0, n * 256 : n * 256 + 256], lambda n: far_core[0, n * 256 : n * 256 + 256])
     h = idx[H]
     for slot in range(2):
         for parity, out in enumerate((out_a, out_b)):
@@ -294,7 +313,7 @@
             out[slot] = jnp.dot(left, rhs[...], preferred_element_type=F32)
 
 
-def encoder_pair_body(idx, fa, fb, ga, gb, mine, theirs):
+def encoder_pair_body(idx, fa, fb, ga, gb, arrived, mine, theirs):
     yl = idx[YL]
 
     @pl.when(yl == 0)
@@ -321,43 +340,47 @@
     halves = jnp.stack([encoder_out[0, :, :256], encoder_out[0, :, 256:]])
     mine = lax.dynamic_index_in_dim(halves, c, 0, keepdims=False)
     other = lax.dynamic_index_in_dim(halves, 1 - c, 0, keepdims=False)
-    parts = [mine] + [swap_y(mine, m) for m in (1, 2, 3)] + [other] + [swap_z(other, m) for m in (1, 2, 3)]
-    idx, ya, zb, qg0, qg_send = call(
-        join_body, "join", [idx, *parts, queries, grad_context],
-        [arr((2, 512, 256)), arr((4, 256, 256)), qg_block, qg_block], [dma((2, 2))], hbm=(8, 9), flops=30_000_000_000,
-    )
+    from_y = [mine] + [swap_y(mine, m) for m in (1, 2, 3)]
+    from_z = [other] + [swap_z(other, m) for m in (1, 2, 3)]
+    idx, ya, qg0, qg_send = call(
+        join_y_body, "join_y", [idx, *from_y, queries, grad_context],
+        [arr((2, 512, 256)), qg_block, qg_block], [dma((2, 2))], hbm=(4, 5),
+    )
+    idx, zb = call(join_z_body, "join_z", [idx, *from_z], [arr((4, 256, 256))], flops=30_000_000_000)
+    by1, by3 = swap_y(zb, 1), swap_y(zb, 3)
     az1, az3 = swap_z(ya, 1), swap_z(ya, 3)
-    by1, by3 = swap_y(zb, 1), swap_y(zb, 3)
+    by20, by21 = swap_y(by1[:2], 3), swap_y(by3[2:], 1)
     az20, az21 = swap_z(az1[:1], 3), swap_z(az3[1:], 1)
-    by20, by21 = swap_y(by1[:2], 3), swap_y(by3[2:], 1)
 
     ws = [w_key, w_value]
     qg2 = swap_seq(qg_send, 2)
-    qg1, qg3 = swap_seq(qg0, 1), swap_seq(qg2, 1)
     idx, acc, es = call(
-        project_first_body, "project_first", [idx, *ws, ya, zb, az1, az3, by1, by3],
-        [arr((512, 1024), F32), arr((3, 4, 256, 256))],
-    )
-    idx, kv_send, kv_own, late = call(
-        project_last_body, "project_last", [idx, *ws, acc, az20, az21, by20, by21],
-        [arr((512, 512)), arr((512, 512)), arr((4, 256, 256))], [pltpu.VMEM((512, 1024), F32)],
+        project_first_body, "project_first", [idx, *ws, ya, zb, by1, by3],
+        [arr((512, 1024), F32), arr((16, 256, 256))],
+    )
+    idx, acc = call(
+        project_next_body, "project_next", [idx, *ws, acc, az1, az3], [arr((512, 1024), F32)]
+    )
+    idx, kv_send, kv_own, es = call(
+        project_last_body, "project_last", [idx, *ws, acc, by20, by21, az20, az21, qg0, qg2, es],
+        [arr((768, 512)), arr((512, 512)), arr((16, 256, 256))], [pltpu.VMEM((512, 1024), F32)],
+        alias={10: 3},
     )
     kv_oth = swap_seq(kv_send, 1)
-    idx, keep_t, es, late = call(
-        turn_keep_body, "turn_keep", [idx, ya, az1, az20, az21, az3, qg1, qg3, es, late],
-        [arr((8, 256, 512)), arr((3, 4, 256, 256)), arr((4, 256, 256))], alias={8: 2, 9: 3},
-    )
-    es_oth, late_oth = swap_seq(es, 1), swap_seq(late, 1)
-
-    idx, g, g_far, gq_own, gq_core, gq_yhi = call(
-        attend_body, "attend", [idx, kv_own, kv_oth, qg0, qg1, qg2, qg3],
-        [arr((2, 1024, 256)), arr((2, 2, 256, 256)), arr((128, 256)), arr((2, 128, 256)), arr((128, 256))],
+    idx, keep_t = call(
+        turn_keep_body, "turn_keep", [idx, ya, az1, az20, az21, az3], [arr((8, 256, 512))]
+    )
+    idx, es = call(relay_body, "relay_rows", [idx, es, kv_oth], [arr((16, 256, 256))], alias={1: 1})
+    es_oth = swap_seq(es, 1)
+
+    idx, g, g_far, gq_own, gq_far = call(
+        attend_body, "attend", [idx, kv_own, kv_oth, qg0, qg2],
+        [arr((2304, 256)), arr((2, 512, 256)), arr((128, 256)), arr((128, 256))],
         [pltpu.VMEM((2, 1024, 256), F32)],
     )
     gp = swap_seq(g, 1)
     far = swap_seq(g_far, 2)
-    gq_got = swap_seq(gq_core, 1)
-    idx, oth_t = call(turn_other_body, "turn_other", [idx, es_oth, late_oth], [arr((8, 256, 512))])
+    idx, oth_t = call(turn_other_body, "turn_other", [idx, es_oth], [arr((8, 256, 512))])
 
     one, two = (256, 512), (2, 256, 512)
     mats = [keep_t, oth_t, g, gp]
@@ -373,25 +396,23 @@
     idx, own = call(
         encoder_own_body, "encoder_own", [idx, *ws, g, gp], [arr((2, *two_t), F32)], rhs_half
     )
-    idx, far = call(relay_body, "relay", [idx, far], [arr((2, 2, 256, 256))], alias={1: 1})
+    idx, far = call(relay_body, "relay", [idx, far], [arr((2, 512, 256))], alias={1: 1})
     far_core = swap_seq(far[1:], 1)
-    idx, ea, eb, gq_send = call(
-        encoder_sent_body, "encoder_sent", [idx, *ws, own, far, far_core, gq_yhi, gq_got],
-        [arr(two_t)] * 2 + [arr((128, 512))], rhs_half,
-    )
-    gq_theirs = swap_seq(gq_send, 2)
+    idx, ea, eb = call(
+        encoder_sent_body, "encoder_sent", [idx, *ws, own, far, far_core], [arr(two_t)] * 2, rhs_half
+    )
     got_a, got_b = swap_z(ea, 1), swap_z(eb, 3)
     idx, x1k, x1v, f1k, f1v = call(
         add_body, "add_first", [idx, k1k, k1v, got1k, got1v], [arr(one)] * 2 + [arr(one, F32)] * 2
     )
     last1k, last1v = swap_x(x1k, 3), swap_x(x1v, 1)
     idx, ka, kb = call(
-        encoder_kept_body, "encoder_kept", [idx, *ws, g, gp, far, far_core], [arr(two_t, F32)] * 2, rhs
-    )
-    idx, pair, s2k, s2v, grad_q = call(
-        pair_body, "weights_pair",
-        [idx, f1k, f1v, last1k, last1v, s2k, s2v, gq_own, gq_got, gq_theirs],
-        [arr(two)] * 3 + [arr((2, 1, 128, 512))], alias={5: 2, 6: 3},
+        encoder_kept_body, "encoder_kept",
+        [idx, *ws, g, gp, far, far_core], [arr(two_t, F32)] * 2, rhs,
+    )
+    idx, pair, s2k, s2v = call(
+        pair_body, "weights_pair", [idx, f1k, f1v, last1k, last1v, gq_far, gp, s2k, s2v],
+        [arr((640, 512)), arr(two), arr(two)], alias={7: 2, 8: 3},
     )
     w_theirs = swap_seq(pair, 2)
     got2k, got2v = swap_x(s2k, 1), swap_x(s2v, 3)
@@ -404,13 +425,15 @@
     )
     last2k, last2v = swap_x(x2k, 3), swap_x(x2v, 1)
     idx, e_mine, e_theirs = call(
-        encoder_pair_body, "encoder_pair", [idx, fa, fb, last_a, last_b], [arr(one_t, F32), arr(one_t)]
+        encoder_pair_body, "encoder_pair", [idx, fa, fb, last_a, last_b, w_theirs], [arr(one_t, F32), arr(one_t)]
     )
     e_got = swap_ylo(e_theirs)
+    idx, grad_wk, grad_wv, grad_q = call(
+        finish_weights_body, "finish_weights",
+        [idx, f2k, f2v, last2k, last2v, w_theirs, gq_own, gp],
+        [arr(two)] * 2 + [arr((2, 1, 128, 512))],
+    )
     idx, grad_enc = call(finish_encoder_body, "finish_encoder", [idx, e_mine, e_got], [arr((1, 256, 512))])
-    idx, grad_wk, grad_wv = call(
-        finish_weights_body, "finish_weights", [idx, f2k, f2v, last2k, last2v, w_theirs], [arr(two)] * 2
-    )
     return grad_q, grad_enc, grad_wk, grad_wv
 
 

time: 116 us -> 109 us (0.940); the launches traced: 116 us -> 108 us
  waiting for transfers between devices: 45.3 us -> 37.8 us
    ppermute x1, waiting for transfers between devices: 7.3 us -> 0.01 us  [swap_ylo(): return lax.ppermute(x, 'tensor', [(t, t ^ 1) for t in range(8)])]
    ppermute x11, waiting for transfers between devices: 2.72 us -> 7.43 us  [swap_z(): return lax.ppermute(x, 'tensor', [(t, t ^ 2 * m) for t in range(8)])]
    ppermute x7, waiting for transfers between devices: 15.4 us -> 11.2 us  [swap_y(): return lax.ppermute(x, ('seq', 'tensor'), pairs)]
    ppermute x12 -> x7, waiting for transfers between devices: 10.9 us -> 6.75 us  [swap_seq(): return lax.ppermute(x, 'seq', [(s, s ^ m) for s in range(4)])]
    ppermute x8, waiting for transfers between devices: 9 us -> 12.5 us  [swap_x(): return lax.ppermute(x, 'dp', [(d, d ^ m) for d in range(4)])]
    ppermute x1, starting transfers between devices: 0.65 us -> 2.19 us  [swap_ylo(): return lax.ppermute(x, 'tensor', [(t, t ^ 1) for t in range(8)])]
    ppermute x7, starting transfers between devices: 9.61 us -> 8.27 us  [swap_y(): return lax.ppermute(x, ('seq', 'tensor'), pairs)]
    pallas_call x19 -> x22, Pallas kernels: 24.8 us -> 24.2 us  [call(): pl.pallas_call(wrapped, in_specs=specs, out_specs=[ANY] + [VMEM] * len(ou...]
  transfers between devices with their start and end apart: 39 -> 34, of which waited for: 19 -> 21; matrix products, arithmetic and copies ran while one was open for 0% -> 0% of each run, Pallas kernels for 19% -> 20%
where the time goes in v3:
time: 109 us; the launch traced here: 108 us
  starting transfers between devices  43.7 us (40%)
  waiting for transfers between devices  37.8 us (35%)
  Pallas kernels  24.2 us (22%)
  local copies, waits for them, and re-layouts  1.09 us (1%)
    pallas_call x22, Pallas kernels, call(): pl.pallas_call(wrapped, in_specs=specs, out_specs=[ANY] + [VMEM] * len(ou...  24.2 us
    ppermute x11, starting transfers between devices, swap_z(): return lax.ppermute(x, 'tensor', [(t, t ^ 2 * m) for t in range(8)])  18.7 us
    ppermute x8, waiting for transfers between devices, swap_x(): return lax.ppermute(x, 'dp', [(d, d ^ m) for d in range(4)])  12.5 us
    ppermute x7, waiting for transfers between devices, swap_y(): return lax.ppermute(x, ('seq', 'tensor'), pairs)  11.2 us
    ppermute x8, starting transfers between devices, swap_x(): return lax.ppermute(x, 'dp', [(d, d ^ m) for d in range(4)])  9.15 us
    ppermute x7, starting transfers between devices, swap_y(): return lax.ppermute(x, ('seq', 'tensor'), pairs)  8.27 us
    ppermute x11, waiting for transfers between devices, swap_z(): return lax.ppermute(x, 'tensor', [(t, t ^ 2 * m) for t in range(8)])  7.43 us
    ppermute x7, waiting for transfers between devices, swap_seq(): return lax.ppermute(x, 'seq', [(s, s ^ m) for s in range(4)])  6.75 us
  transfers between devices with their start and end apart: 34, of which 21 were waited for; matrix products, arithmetic and copies ran while one was open for 0% of the time, Pallas kernels for 20%

profile of v3, /device:TPU:0, one launch (start us, length us, event | category | flops | bytes accessed | tf_op | source)
XLA Modules:
  0.0 107.9 jit_solution(5551731235206504309)
XLA Ops:
  0.6 1.0 fusion.4
  1.8 3.2 %collective-permute-start.2 = (bf16[256,256]{1,0:T(8,128)(2,1)S(1)}, bf16[256,256]{1,0:T(8,128)(2,1)S(1)}, u32[]{:S(2)}, u32[]{:S(2)}) collective-permute-start(bf16[256,256]{1,0:T(8,128)(2,1)S(1)} %get-tuple-element.151.refs_1_), channel_id=1, source_target_pairs={{0,17},{1,16},{2,19},{3,18},{4,21},{5,20},{6,23},{7,22},{8,25},{9,... | collective-permute-start | bytes 393224 | tf_op jit(solution)/shard_map/ppermute | solution.py:71
  5.9 4.1 %collective-permute-start.5 = (bf16[256,256]{1,0:T(8,128)(2,1)S(1)}, bf16[256,256]{1,0:T(8,128)(2,1)S(1)}, u32[]{:S(2)}, u32[]{:S(2)}) collective-permute-start(bf16[256,256]{1,0:T(8,128)(2,1)S(1)} %get-tuple-element.150.refs_1_), channel_id=1, source_target_pairs={{0,6},{1,7},{2,4},{3,5},{4,2},{5,3},{6,0},{7,1},{8,14},{9,15},{10,... | collective-permute-start | bytes 393224 | tf_op jit(solution)/shard_map/ppermute | solution.py:62
  10.5 1.9 %collective-permute-start.3 = (bf16[256,256]{1,0:T(8,128)(2,1)S(1)}, bf16[256,256]{1,0:T(8,128)(2,1)S(1)}, u32[]{:S(2)}, u32[]{:S(2)}) collective-permute-start(bf16[256,256]{1,0:T(8,128)(2,1)S(1)} %get-tuple-element.150.refs_1_), channel_id=1, source_target_pairs={{0,2},{1,3},{2,0},{3,1},{4,6},{5,7},{6,4},{7,5},{8,10},{9,11},{10,... | collective-permute-start | bytes 393224 | tf_op jit(solution)/shard_map/ppermute | solution.py:62
  12.8 1.1 %join_y.1 = (s32[8,128]{1,0:T(8,128)S(1)}, bf16[2,512,256]{2,1,0:T(8,128)(2,1)S(1)}, bf16[2,128,512]{2,1,0:T(8,128)(2,1)S(1)}, bf16[2,128,512]{2,1,0:T(8,128)(2,1)S(1)}) custom-call(s32[8,128]{1,0:T(8,128)S(1)} %broadcast_in_dim.3.refs_0_, bf16[256,256]{1,0:T(8,128)(2,1)S(1)} %get-tuple-element.151.refs_1_, ...), custom_call_target="tpu_custom_call", output_to_operand_aliasing={{0}: (0, {})} | custom-call | flops 1 | bytes 1 | tf_op jit(solution)/shard_map/join_y/pallas_call | solution.py:36
  13.9 1.0 collective-permute-done.5.refs_4_
  15.0 2.1 %collective-permute-done.4.refs_3_ = bf16[256,256]{1,0:T(8,128)(2,1)S(1)} collective-permute-done((bf16[256,256]{1,0:T(8,128)(2,1)S(1)}, bf16[256,256]{1,0:T(8,128)(2,1)S(1)}, u32[]{:S(2)}, u32[]{:S(2)}) %collective-permute-start.4) | collective-permute-done | bytes 131104 | tf_op jit(solution)/shard_map/ppermute | solution.py:62
  17.1 2.7 %collective-permute-start.7 = (bf16[4,256,256]{2,1,0:T(8,128)(2,1)S(1)}, bf16[4,256,256]{2,1,0:T(8,128)(2,1)S(1)}, u32[]{:S(2)}, u32[]{:S(2)}) collective-permute-start(bf16[4,256,256]{2,1,0:T(8,128)(2,1)S(1)} %get-tuple-element.80.refs_4_), channel_id=1, source_target_pairs={{0,17},{1,16},{2,19},{3,18},{4,21},{5,20},{6,23},{7,22},{8,25},{9,... | collective-permute-start | bytes 1572872 | tf_op jit(solution)/shard_map/ppermute | solution.py:71
  20.4 3.0 %collective-permute-start.9 = (bf16[2,512,256]{2,1,0:T(8,128)(2,1)S(1)}, bf16[2,512,256]{2,1,0:T(8,128)(2,1)S(1)}, u32[]{:S(2)}, u32[]{:S(2)}) collective-permute-start(bf16[2,512,256]{2,1,0:T(8,128)(2,1)S(1)} %get-tuple-element.79.refs_3_.refs_1_), channel_id=1, source_target_pairs={{0,6},{1,7},{2,4},{3,5},{4,2},{5,3},{6,0},{7,1},{8,14},{9,15},{10,... | collective-permute-start | bytes 1572872 | tf_op jit(solution)/shard_map/ppermute | solution.py:62
  23.4 1.6 %collective-permute-start.14 = (bf16[2,128,512]{2,1,0:T(8,128)(2,1)S(1)}, bf16[2,128,512]{2,1,0:T(8,128)(2,1)S(1)}, u32[]{:S(2)}, u32[]{:S(2)}) collective-permute-start(bf16[2,128,512]{2,1,0:T(8,128)(2,1)S(1)} %get-tuple-element.86), channel_id=1, source_target_pairs={{0,16},{8,24},{16,0},{24,8},{1,17},{9,25},{17,1},{25,9},{2,18},{10... | collective-permute-start | bytes 786440 | tf_op jit(solution)/shard_map/ppermute | solution.py:50
  24.9 7.2 %collective-permute-done.7.refs_6_ = bf16[4,256,256]{2,1,0:T(8,128)(2,1)S(1)} collective-permute-done((bf16[4,256,256]{2,1,0:T(8,128)(2,1)S(1)}, bf16[4,256,256]{2,1,0:T(8,128)(2,1)S(1)}, u32[]{:S(2)}, u32[]{:S(2)}) %collective-permute-start.7) | collective-permute-done | bytes 524320 | tf_op jit(solution)/shard_map/ppermute | solution.py:71
  32.3 2.4 %collective-permute-done.6.refs_5_ = bf16[4,256,256]{2,1,0:T(8,128)(2,1)S(1)} collective-permute-done((bf16[4,256,256]{2,1,0:T(8,128)(2,1)S(1)}, bf16[4,256,256]{2,1,0:T(8,128)(2,1)S(1)}, u32[]{:S(2)}, u32[]{:S(2)}) %collective-permute-start.6) | collective-permute-done | bytes 524320 | tf_op jit(solution)/shard_map/ppermute | solution.py:71
  34.7 0.7 collective-permute-start.10
  35.4 1.4 %collective-permute-start.13 = (bf16[1,512,256]{2,1,0:T(8,128)(2,1)S(1)}, bf16[1,512,256]{2,1,0:T(8,128)(2,1)S(1)}, u32[]{:S(2)}, u32[]{:S(2)}) collective-permute-start(bf16[1,512,256]{2,1,0:T(8,128)(2,1)S(1)} %slice.31), channel_id=1, source_target_pairs={{0,2},{1,3},{2,0},{3,1},{4,6},{5,7},{6,4},{7,5},{8,10},{9,11},{10,... | collective-permute-start | bytes 786440 | tf_op jit(solution)/shard_map/ppermute | solution.py:62
  36.8 2.6 %collective-permute-start.12 = (bf16[1,512,256]{2,1,0:T(8,128)(2,1)S(1)}, bf16[1,512,256]{2,1,0:T(8,128)(2,1)S(1)}, u32[]{:S(2)}, u32[]{:S(2)}) collective-permute-start(bf16[1,512,256]{2,1,0:T(8,128)(2,1)S(1)} %slice.30), channel_id=1, source_target_pairs={{0,6},{1,7},{2,4},{3,5},{4,2},{5,3},{6,0},{7,1},{8,14},{9,15},{10,... | collective-permute-start | bytes 786440 | tf_op jit(solution)/shard_map/ppermute | solution.py:62
  39.5 2.3 %project_first.1 = (s32[8,128]{1,0:T(8,128)S(1)}, f32[512,1024]{1,0:T(8,128)S(1)}, bf16[16,256,256]{2,1,0:T(8,128)(2,1)S(1)}) custom-call(s32[8,128]{1,0:T(8,128)S(1)} %get-tuple-element.78.refs_0_, bf16[2,4096,512]{2,1,0:T(8,128)(2,1)S(1)} %bitcast.5, bf16[2,4096,512]{2,1,0:T(8,128)(2,1)S(1)} %bitcast.7, ...), custom_call_target="tpu_custom_call", output_to_operand_aliasing={{0}: (0, {})} | custom-call | flops 1 | bytes 1 | tf_op jit(solution)/shard_map/project_first/pallas_call | solution.py:36
  41.8 1.3 %project_next.1 = (s32[8,128]{1,0:T(8,128)S(1)}, f32[512,1024]{1,0:T(8,128)S(1)}) custom-call(s32[8,128]{1,0:T(8,128)S(1)} %get-tuple-element.81.refs_0_, bf16[2,4096,512]{2,1,0:T(8,128)(2,1)S(1)} %bitcast.5, bf16[2,4096,512]{2,1,0:T(8,128)(2,1)S(1)} %bitcast.7, f32[512,1024]{1,0:T(8,128)S(1)} %get-tuple-element.82.refs_3_, ...), custom_call_target="tpu_custom_call", output_to_operand_aliasing={{0}: (0, {})} | custom-call | flops 1 | bytes 1 | tf_op jit(solution)/shard_map/project_next/pallas_call | solution.py:36
  43.1 0.7 collective-permute-done.11.refs_5_
  43.8 0.7 collective-permute-done.12.refs_6_.refs_3_
  44.5 1.6 %project_last.1 = (s32[8,128]{1,0:T(8,128)S(1)}, bf16[768,512]{1,0:T(8,128)(2,1)S(1)}, bf16[512,512]{1,0:T(8,128)(2,1)S(1)}, bf16[16,256,256]{2,1,0:T(8,128)(2,1)S(1)}) custom-call(s32[8,128]{1,0:T(8,128)S(1)} %get-tuple-element.83.refs_0_, bf16[2,4096,512]{2,1,0:T(8,128)(2,1)S(1)} %bitcast.5, ...), custom_call_target="tpu_custom_call", output_to_operand_aliasing={{0}: (0, {}), {3}: (10, {})} | custom-call | flops 1 | bytes 1 | tf_op jit(solution)/shard_map/project_last/pallas_call | solution.py:36
  46.8 1.7 %collective-permute-done.15.refs_2_ = bf16[768,512]{1,0:T(8,128)(2,1)S(1)} collective-permute-done((bf16[768,512]{1,0:T(8,128)(2,1)S(1)}, bf16[768,512]{1,0:T(8,128)(2,1)S(1)}, u32[]{:S(2)}, u32[]{:S(2)}) %collective-permute-start.15) | collective-permute-done | bytes 786464 | tf_op jit(solution)/shard_map/ppermute | solution.py:50
  48.7 3.9 %attend.1 = (s32[8,128]{1,0:T(8,128)S(1)}, bf16[2304,256]{1,0:T(8,128)(2,1)S(1)}, bf16[2,512,256]{2,1,0:T(8,128)(2,1)S(1)}, bf16[128,256]{1,0:T(8,128)(2,1)S(1)}, bf16[128,256]{1,0:T(8,128)(2,1)S(1)}) custom-call(s32[8,128]{1,0:T(8,128)S(1)} %get-tuple-element.92.refs_0_, ...), custom_call_target="tpu_custom_call", output_to_operand_aliasing={{0}: (0, {})} | custom-call | flops 1 | bytes 1 | tf_op jit(solution)/shard_map/attend/pallas_call | solution.py:36
  53.1 1.6 %collective-permute-start.18 = (bf16[2,512,256]{2,1,0:T(8,128)(2,1)S(1)}, bf16[2,512,256]{2,1,0:T(8,128)(2,1)S(1)}, u32[]{:S(2)}, u32[]{:S(2)}) collective-permute-start(bf16[2,512,256]{2,1,0:T(8,128)(2,1)S(1)} %get-tuple-element.103), channel_id=1, source_target_pairs={{0,16},{8,24},{16,0},{24,8},{1,17},{9,25},{17,1},{25,9},{2,18},{10... | collective-permute-start | bytes 1572872 | tf_op jit(solution)/shard_map/ppermute | solution.py:50
  55.5 1.2 %weights_first.1 = (s32[8,128]{1,0:T(8,128)S(1)}, bf16[2,256,512]{2,1,0:T(8,128)(2,1)S(1)}, bf16[2,256,512]{2,1,0:T(8,128)(2,1)S(1)}) custom-call(s32[8,128]{1,0:T(8,128)S(1)} %get-tuple-element.96.refs_0_, bf16[8,256,512]{2,1,0:T(8,128)(2,1)S(1)} %get-tuple-element.97.refs_1_, ...), custom_call_target="tpu_custom_call", output_to_operand_aliasing={{0}: (0, {})} | custom-call | flops 1 | bytes 1 | tf_op jit(solution)/shard_map/weights_first/pallas_call | solution.py:36
  56.8 1.6 %collective-permute-start.20 = (bf16[2,256,512]{2,1,0:T(8,128)(2,1)S(1)}, bf16[2,256,512]{2,1,0:T(8,128)(2,1)S(1)}, u32[]{:S(2)}, u32[]{:S(2)}) collective-permute-start(bf16[2,256,512]{2,1,0:T(8,128)(2,1)S(1)} %get-tuple-element.110), channel_id=1, source_target_pairs={{0,32},{32,0},{64,96},{96,64},{1,33},{33,1},{65,97},{97,65},{2,34}... | collective-permute-start | bytes 1572872 | tf_op jit(solution)/shard_map/ppermute | solution.py:58
  58.4 2.1 %collective-permute-start.21 = (bf16[2,256,512]{2,1,0:T(8,128)(2,1)S(1)}, bf16[2,256,512]{2,1,0:T(8,128)(2,1)S(1)}, u32[]{:S(2)}, u32[]{:S(2)}) collective-permute-start(bf16[2,256,512]{2,1,0:T(8,128)(2,1)S(1)} %get-tuple-element.111), channel_id=1, source_target_pairs={{0,96},{32,64},{64,32},{96,0},{1,97},{33,65},{65,33},{97,1},{2,98}... | collective-permute-start | bytes 1572872 | tf_op jit(solution)/shard_map/ppermute | solution.py:58
  60.5 3.4 %weights_rest.1 = (s32[8,128]{1,0:T(8,128)S(1)}, bf16[2,256,512]{2,1,0:T(8,128)(2,1)S(1)}, bf16[2,256,512]{2,1,0:T(8,128)(2,1)S(1)}, f32[2,256,512]{2,1,0:T(8,12...) custom-call(s32[8,128]{1,0:T(8,128)S(1)} %get-tuple-element.100.refs, ...), custom_call_target="tpu_custom_call", output_to_operand_aliasing={{0}: (0, {})} | custom-call | flops 1 | bytes 1 | tf_op jit(solution)/shard_map/weights_rest/pallas_call | solution.py:36
  63.9 1.4 %encoder_own.1 = (s32[8,128]{1,0:T(8,128)S(1)}, f32[2,2,512,256]{3,2,1,0:T(8,128)S(1)}) custom-call(s32[8,128]{1,0:T(8,128)S(1)} %get-tuple-element.101.refs_0_, bf16[2,4096,512]{2,1,0:T(8,128)(2,1)S(1)} %bitcast.5, bf16[2,4096,512]{2,1,0:T(8,128)(2,1)S(1)} %bitcast.7, ...), custom_call_target="tpu_custom_call", output_to_operand_aliasing={{0}: (0, {})} | custom-call | flops 1 | bytes 1 | tf_op jit(solution)/shard_map/encoder_own/pallas_call | solution.py:36
  65.3 3.2 %collective-permute-done.18.refs_1_ = bf16[2,512,256]{2,1,0:T(8,128)(2,1)S(1)} collective-permute-done((bf16[2,512,256]{2,1,0:T(8,128)(2,1)S(1)}, bf16[2,512,256]{2,1,0:T(8,128)(2,1)S(1)}, u32[]{:S(2)}, u32[]{:S(2)}) %collective-permute-start.18) | collective-permute-done | bytes 524320 | tf_op jit(solution)/shard_map/ppermute | solution.py:50
  68.6 1.5 %collective-permute-done.19.refs_5_.refs_6_ = bf16[1,512,256]{2,1,0:T(8,128)(2,1)S(1)} collective-permute-done((bf16[1,512,256]{2,1,0:T(8,128)(2,1)S(1)}, bf16[1,512,256]{2,1,0:T(8,128)(2,1)S(1)}, u32[]{:S(2)}, u32[]{:S(2)}) %collective-permute-start.19) | collective-permute-done | bytes 262176 | tf_op jit(solution)/shard_map/ppermute | solution.py:50
  70.2 1.4 %encoder_sent.1 = (s32[8,128]{1,0:T(8,128)S(1)}, bf16[2,512,256]{2,1,0:T(8,128)(2,1)S(1)}, bf16[2,512,256]{2,1,0:T(8,128)(2,1)S(1)}) custom-call(s32[8,128]{1,0:T(8,128)S(1)} %get-tuple-element.104.refs_0_, bf16[2,4096,512]{2,1,0:T(8,128)(2,1)S(1)} %bitcast.5, bf16[2,4096,512]{2,1,0:T(8,128)(2,1)S(1)} %bitcast.7, ...), custom_call_target="tpu_custom_call", output_to_operand_aliasing={{0}: (0, {})} | custom-call | flops 1 | bytes 1 | tf_op jit(solution)/shard_map/encoder_sent/pallas_call | solution.py:36
  71.5 2.0 %collective-permute-done.21.refs_4_ = bf16[2,256,512]{2,1,0:T(8,128)(2,1)S(1)} collective-permute-done((bf16[2,256,512]{2,1,0:T(8,128)(2,1)S(1)}, bf16[2,256,512]{2,1,0:T(8,128)(2,1)S(1)}, u32[]{:S(2)}, u32[]{:S(2)}) %collective-permute-start.21) | collective-permute-done | bytes 524320 | tf_op jit(solution)/shard_map/ppermute | solution.py:58
  73.7 2.2 %collective-permute-start.22 = (bf16[256,512]{1,0:T(8,128)(2,1)S(1)}, bf16[256,512]{1,0:T(8,128)(2,1)S(1)}, u32[]{:S(2)}, u32[]{:S(2)}) collective-permute-start(bf16[256,512]{1,0:T(8,128)(2,1)S(1)} %get-tuple-element.116), channel_id=1, source_target_pairs={{0,96},{32,64},{64,32},{96,0},{1,97},{33,65},{65,33},{97,1},{2,98}... | collective-permute-start | bytes 786440 | tf_op jit(solution)/shard_map/ppermute | solution.py:58
  76.2 2.6 %collective-permute-start.25 = (bf16[2,512,256]{2,1,0:T(8,128)(2,1)S(1)}, bf16[2,512,256]{2,1,0:T(8,128)(2,1)S(1)}, u32[]{:S(2)}, u32[]{:S(2)}) collective-permute-start(bf16[2,512,256]{2,1,0:T(8,128)(2,1)S(1)} %get-tuple-element.125), channel_id=1, source_target_pairs={{0,6},{1,7},{2,4},{3,5},{4,2},{5,3},{6,0},{7,1},{8,14},{9,15},{10,... | collective-permute-start | bytes 1572872 | tf_op jit(solution)/shard_map/ppermute | solution.py:62
  78.8 2.4 %encoder_kept.1 = (s32[8,128]{1,0:T(8,128)S(1)}, f32[2,512,256]{2,1,0:T(8,128)S(1)}, f32[2,512,256]{2,1,0:T(8,128)S(1)}) custom-call(s32[8,128]{1,0:T(8,128)S(1)} %get-tuple-element.112.refs_0_, bf16[2,4096,512]{2,1,0:T(8,128)(2,1)S(1)} %bitcast.5, bf16[2,4096,512]{2,1,0:T(8,128)(2,1)S(1)} %bitcast.7, ...), custom_call_target="tpu_custom_call", output_to_operand_aliasing={{0}: (0, {})} | custom-call | flops 1 | bytes 1 | tf_op jit(solution)/shard_map/encoder_kept/pallas_call | solution.py:36
  81.2 1.2 %collective-permute-done.22.refs_3_ = bf16[256,512]{1,0:T(8,128)(2,1)S(1)} collective-permute-done((bf16[256,512]{1,0:T(8,128)(2,1)S(1)}, bf16[256,512]{1,0:T(8,128)(2,1)S(1)}, u32[]{:S(2)}, u32[]{:S(2)}) %collective-permute-start.22) | collective-permute-done | bytes 262176 | tf_op jit(solution)/shard_map/ppermute | solution.py:58
  83.1 1.6 %collective-permute-start.30 = (bf16[640,512]{1,0:T(8,128)(2,1)S(1)}, bf16[640,512]{1,0:T(8,128)(2,1)S(1)}, u32[]{:S(2)}, u32[]{:S(2)}) collective-permute-start(bf16[640,512]{1,0:T(8,128)(2,1)S(1)} %get-tuple-element.136), channel_id=1, source_target_pairs={{0,16},{8,24},{16,0},{24,8},{1,17},{9,25},{17,1},{25,9},{2,18},{10... | collective-permute-start | bytes 1966088 | tf_op jit(solution)/shard_map/ppermute | solution.py:50
  85.0 1.1 %collective-permute-start.27 = (bf16[2,256,512]{2,1,0:T(8,128)(2,1)S(1)}, bf16[2,256,512]{2,1,0:T(8,128)(2,1)S(1)}, u32[]{:S(2)}, u32[]{:S(2)}) collective-permute-start(bf16[2,256,512]{2,1,0:T(8,128)(2,1)S(1)} %get-tuple-element.130), channel_id=1, source_target_pairs={{0,96},{32,64},{64,32},{96,0},{1,97},{33,65},{65,33},{97,1},{2,98}... | collective-permute-start | bytes 1572872 | tf_op jit(solution)/shard_map/ppermute | solution.py:58
  86.2 2.5 %collective-permute-done.24.refs_3_ = bf16[2,512,256]{2,1,0:T(8,128)(2,1)S(1)} collective-permute-done((bf16[2,512,256]{2,1,0:T(8,128)(2,1)S(1)}, bf16[2,512,256]{2,1,0:T(8,128)(2,1)S(1)}, u32[]{:S(2)}, u32[]{:S(2)}) %collective-permute-start.24) | collective-permute-done | bytes 524320 | tf_op jit(solution)/shard_map/ppermute | solution.py:62
  88.6 1.2 %collective-permute-done.25.refs_4_ = bf16[2,512,256]{2,1,0:T(8,128)(2,1)S(1)} collective-permute-done((bf16[2,512,256]{2,1,0:T(8,128)(2,1)S(1)}, bf16[2,512,256]{2,1,0:T(8,128)(2,1)S(1)}, u32[]{:S(2)}, u32[]{:S(2)}) %collective-permute-start.25) | collective-permute-done | bytes 524320 | tf_op jit(solution)/shard_map/ppermute | solution.py:62
  90.1 2.7 %collective-permute-start.28 = (bf16[512,256]{1,0:T(8,128)(2,1)S(1)}, bf16[512,256]{1,0:T(8,128)(2,1)S(1)}, u32[]{:S(2)}, u32[]{:S(2)}) collective-permute-start(bf16[512,256]{1,0:T(8,128)(2,1)S(1)} %get-tuple-element.134), channel_id=1, source_target_pairs={{0,6},{1,7},{2,4},{3,5},{4,2},{5,3},{6,0},{7,1},{8,14},{9,15},{10,... | collective-permute-start | bytes 786440 | tf_op jit(solution)/shard_map/ppermute | solution.py:62
  92.8 3.4 %collective-permute-done.26.refs_3_ = bf16[2,256,512]{2,1,0:T(8,128)(2,1)S(1)} collective-permute-done((bf16[2,256,512]{2,1,0:T(8,128)(2,1)S(1)}, bf16[2,256,512]{2,1,0:T(8,128)(2,1)S(1)}, u32[]{:S(2)}, u32[]{:S(2)}) %collective-permute-start.26) | collective-permute-done | bytes 524320 | tf_op jit(solution)/shard_map/ppermute | solution.py:58
  96.2 1.5 %collective-permute-done.27.refs_4_ = bf16[2,256,512]{2,1,0:T(8,128)(2,1)S(1)} collective-permute-done((bf16[2,256,512]{2,1,0:T(8,128)(2,1)S(1)}, bf16[2,256,512]{2,1,0:T(8,128)(2,1)S(1)}, u32[]{:S(2)}, u32[]{:S(2)}) %collective-permute-start.27) | collective-permute-done | bytes 524320 | tf_op jit(solution)/shard_map/ppermute | solution.py:58
  97.9 1.6 %collective-permute-start.31 = (bf16[256,512]{1,0:T(8,128)(2,1)S(1)}, bf16[256,512]{1,0:T(8,128)(2,1)S(1)}, u32[]{:S(2)}, u32[]{:S(2)}) collective-permute-start(bf16[256,512]{1,0:T(8,128)(2,1)S(1)} %get-tuple-element.140), channel_id=1, source_target_pairs={{0,96},{32,64},{64,32},{96,0},{1,97},{33,65},{65,33},{97,1},{2,98}... | collective-permute-start | bytes 786440 | tf_op jit(solution)/shard_map/ppermute | solution.py:58
  99.8 2.2 %collective-permute-start.33 = (bf16[512,256]{1,0:T(8,128)(2,1)S(1)}, bf16[512,256]{1,0:T(8,128)(2,1)S(1)}, u32[]{:S(2)}, u32[]{:S(2)}) collective-permute-start(bf16[512,256]{1,0:T(8,128)(2,1)S(1)} %get-tuple-element.146), channel_id=1, source_target_pairs={{0,1},{1,0},{2,3},{3,2},{4,5},{5,4},{6,7},{7,6},{8,9},{9,8},{10,11... | collective-permute-start | bytes 786440 | tf_op jit(solution)/shard_map/ppermute | solution.py:54
  102.0 3.5 %collective-permute-done.31.refs_3_ = bf16[256,512]{1,0:T(8,128)(2,1)S(1)} collective-permute-done((bf16[256,512]{1,0:T(8,128)(2,1)S(1)}, bf16[256,512]{1,0:T(8,128)(2,1)S(1)}, u32[]{:S(2)}, u32[]{:S(2)}) %collective-permute-start.31) | collective-permute-done | bytes 262176 | tf_op jit(solution)/shard_map/ppermute | solution.py:58
  105.8 1.2 %finish_weights.1 = (s32[8,128]{1,0:T(8,128)S(1)}, bf16[2,256,512]{2,1,0:T(8,128)(2,1)}, bf16[2,256,512]{2,1,0:T(8,128)(2,1)}, bf16[2,1,128,512]{3,2,1,0:T(8,128)(2,1)}) custom-call(s32[8,128]{1,0:T(8,128)S(1)} %get-tuple-element.137.refs_0_, f32[256,512]{1,0:T(8,128)S(1)} %get-tuple-element.138.refs_1_, ...), custom_call_target="tpu_custom_call", output_to_operand_aliasing={{0}: (0, {})} | custom-call | flops 1 | bytes 1 | tf_op jit(solution)/shard_map/finish_weights/pallas_call | solution.py:36
  107.0 0.8 finish_encoder.1
  (60 shorter events, 7.6 us)
Async XLA Ops:
  1.8 8.8 %collective-permute-start.2 = (bf16[256,256]{1,0:T(8,128)(2,1)S(1)}, bf16[256,256]{1,0:T(8,128)(2,1)S(1)}, u32[]{:S(2)}, u32[]{:S(2)}) collective-permute-start(bf16[256,256]{1,0:T(8,128)(2,1)S(1)} %get-tuple-element.151.refs_1_), channel_id=1, source_target_pairs={{0,17},{1,16},{2,19},{3,18},{4,21},{5,20},{6,23},{7,22},{8,25},{9,... | collective-permute-start | bytes 393224 | tf_op jit(solution)/shard_map/ppermute | solution.py:71
  4.9 7.9 %collective-permute-start.1 = (bf16[256,256]{1,0:T(8,128)(2,1)S(1)}, bf16[256,256]{1,0:T(8,128)(2,1)S(1)}, u32[]{:S(2)}, u32[]{:S(2)}) collective-permute-start(bf16[256,256]{1,0:T(8,128)(2,1)S(1)} %get-tuple-element.151.refs_1_), channel_id=1, source_target_pairs={{0,16},{1,17},{2,18},{3,19},{4,20},{5,21},{6,22},{7,23},{8,24},{9,... | collective-permute-start | bytes 393224 | tf_op jit(solution)/shard_map/ppermute | solution.py:71
  5.6 7.2 %collective-permute-start = (bf16[256,256]{1,0:T(8,128)(2,1)S(1)}, bf16[256,256]{1,0:T(8,128)(2,1)S(1)}, u32[]{:S(2)}, u32[]{:S(2)}) collective-permute-start(bf16[256,256]{1,0:T(8,128)(2,1)S(1)} %get-tuple-element.151.refs_1_), channel_id=1, source_target_pairs={{0,1},{1,0},{2,3},{3,2},{4,5},{5,4},{6,7},{7,6},{8,9},{9,8},{10,11... | collective-permute-start | bytes 393224 | tf_op jit(solution)/shard_map/ppermute | solution.py:71
  5.9 9.0 %collective-permute-start.5 = (bf16[256,256]{1,0:T(8,128)(2,1)S(1)}, bf16[256,256]{1,0:T(8,128)(2,1)S(1)}, u32[]{:S(2)}, u32[]{:S(2)}) collective-permute-start(bf16[256,256]{1,0:T(8,128)(2,1)S(1)} %get-tuple-element.150.refs_1_), channel_id=1, source_target_pairs={{0,6},{1,7},{2,4},{3,5},{4,2},{5,3},{6,0},{7,1},{8,14},{9,15},{10,... | collective-permute-start | bytes 393224 | tf_op jit(solution)/shard_map/ppermute | solution.py:62
  10.0 7.0 %collective-permute-start.4 = (bf16[256,256]{1,0:T(8,128)(2,1)S(1)}, bf16[256,256]{1,0:T(8,128)(2,1)S(1)}, u32[]{:S(2)}, u32[]{:S(2)}) collective-permute-start(bf16[256,256]{1,0:T(8,128)(2,1)S(1)} %get-tuple-element.150.refs_1_), channel_id=1, source_target_pairs={{0,4},{1,5},{2,6},{3,7},{4,0},{5,1},{6,2},{7,3},{8,12},{9,13},{10,... | collective-permute-start | bytes 393224 | tf_op jit(solution)/shard_map/ppermute | solution.py:62
  10.5 6.5 %collective-permute-start.3 = (bf16[256,256]{1,0:T(8,128)(2,1)S(1)}, bf16[256,256]{1,0:T(8,128)(2,1)S(1)}, u32[]{:S(2)}, u32[]{:S(2)}) collective-permute-start(bf16[256,256]{1,0:T(8,128)(2,1)S(1)} %get-tuple-element.150.refs_1_), channel_id=1, source_target_pairs={{0,2},{1,3},{2,0},{3,1},{4,6},{5,7},{6,4},{7,5},{8,10},{9,11},{10,... | collective-permute-start | bytes 393224 | tf_op jit(solution)/shard_map/ppermute | solution.py:62
  17.0 22.4 %slice-start = ((s8[8388608]{0:T(1024)(128)(4,1)}), s8[4194304]{0:T(1024)(128)(4,1)S(1)}, s32[]{:S(2)}) async-start(s8[8388608]{0:T(1024)(128)(4,1)} %bitcast.4), calls=%async_computation | async-start | bytes 8388608
  17.0 22.4 %slice-start.2 = ((s8[8388608]{0:T(1024)(128)(4,1)}), s8[4194304]{0:T(1024)(128)(4,1)S(1)}, s32[]{:S(2)}) async-start(s8[8388608]{0:T(1024)(128)(4,1)} %bitcast.6), calls=%async_computation.2 | async-start | bytes 8388608
  17.0 22.4 %slice-start.1 = ((s8[8388608]{0:T(1024)(128)(4,1)}), s8[4194304]{0:T(1024)(128)(4,1)S(1)}, s32[]{:S(2)}) async-start(s8[8388608]{0:T(1024)(128)(4,1)} %bitcast.4), calls=%async_computation.1 | async-start | bytes 8388608
  17.0 22.4 %slice-start.3 = ((s8[8388608]{0:T(1024)(128)(4,1)}), s8[4194304]{0:T(1024)(128)(4,1)S(1)}, s32[]{:S(2)}) async-start(s8[8388608]{0:T(1024)(128)(4,1)} %bitcast.6), calls=%async_computation.3 | async-start | bytes 8388608
  17.1 15.1 %collective-permute-start.7 = (bf16[4,256,256]{2,1,0:T(8,128)(2,1)S(1)}, bf16[4,256,256]{2,1,0:T(8,128)(2,1)S(1)}, u32[]{:S(2)}, u32[]{:S(2)}) collective-permute-start(bf16[4,256,256]{2,1,0:T(8,128)(2,1)S(1)} %get-tuple-element.80.refs_4_), channel_id=1, source_target_pairs={{0,17},{1,16},{2,19},{3,18},{4,21},{5,20},{6,23},{7,22},{8,25},{9,... | collective-permute-start | bytes 1572872 | tf_op jit(solution)/shard_map/ppermute | solution.py:71
  19.8 14.9 %collective-permute-start.6 = (bf16[4,256,256]{2,1,0:T(8,128)(2,1)S(1)}, bf16[4,256,256]{2,1,0:T(8,128)(2,1)S(1)}, u32[]{:S(2)}, u32[]{:S(2)}) collective-permute-start(bf16[4,256,256]{2,1,0:T(8,128)(2,1)S(1)} %get-tuple-element.80.refs_4_), channel_id=1, source_target_pairs={{0,1},{1,0},{2,3},{3,2},{4,5},{5,4},{6,7},{7,6},{8,9},{9,8},{10,11... | collective-permute-start | bytes 1572872 | tf_op jit(solution)/shard_map/ppermute | solution.py:71
  20.4 15.0 %collective-permute-start.9 = (bf16[2,512,256]{2,1,0:T(8,128)(2,1)S(1)}, bf16[2,512,256]{2,1,0:T(8,128)(2,1)S(1)}, u32[]{:S(2)}, u32[]{:S(2)}) collective-permute-start(bf16[2,512,256]{2,1,0:T(8,128)(2,1)S(1)} %get-tuple-element.79.refs_3_.refs_1_), channel_id=1, source_target_pairs={{0,6},{1,7},{2,4},{3,5},{4,2},{5,3},{6,0},{7,1},{8,14},{9,15},{10,... | collective-permute-start | bytes 1572872 | tf_op jit(solution)/shard_map/ppermute | solution.py:62
  23.4 13.4 %collective-permute-start.8 = (bf16[2,512,256]{2,1,0:T(8,128)(2,1)S(1)}, bf16[2,512,256]{2,1,0:T(8,128)(2,1)S(1)}, u32[]{:S(2)}, u32[]{:S(2)}) collective-permute-start(bf16[2,512,256]{2,1,0:T(8,128)(2,1)S(1)} %get-tuple-element.79.refs_3_.refs_1_), channel_id=1, source_target_pairs={{0,2},{1,3},{2,0},{3,1},{4,6},{5,7},{6,4},{7,5},{8,10},{9,11},{10,... | collective-permute-start | bytes 1572872 | tf_op jit(solution)/shard_map/ppermute | solution.py:62
  23.4 19.7 %collective-permute-start.14 = (bf16[2,128,512]{2,1,0:T(8,128)(2,1)S(1)}, bf16[2,128,512]{2,1,0:T(8,128)(2,1)S(1)}, u32[]{:S(2)}, u32[]{:S(2)}) collective-permute-start(bf16[2,128,512]{2,1,0:T(8,128)(2,1)S(1)} %get-tuple-element.86), channel_id=1, source_target_pairs={{0,16},{8,24},{16,0},{24,8},{1,17},{9,25},{17,1},{25,9},{2,18},{10... | collective-permute-start | bytes 786440 | tf_op jit(solution)/shard_map/ppermute | solution.py:50
  32.2 11.7 %collective-permute-start.11 = (bf16[2,256,256]{2,1,0:T(8,128)(2,1)S(1)}, bf16[2,256,256]{2,1,0:T(8,128)(2,1)S(1)}, u32[]{:S(2)}, u32[]{:S(2)}) collective-permute-start(bf16[2,256,256]{2,1,0:T(8,128)(2,1)S(1)} %slice.29), channel_id=1, source_target_pairs={{0,1},{1,0},{2,3},{3,2},{4,5},{5,4},{6,7},{7,6},{8,9},{9,8},{10,11... | collective-permute-start | bytes 786440 | tf_op jit(solution)/shard_map/ppermute | solution.py:71
  34.7 9.2 %collective-permute-start.10 = (bf16[2,256,256]{2,1,0:T(8,128)(2,1)S(1)}, bf16[2,256,256]{2,1,0:T(8,128)(2,1)S(1)}, u32[]{:S(2)}, u32[]{:S(2)}) collective-permute-start(bf16[2,256,256]{2,1,0:T(8,128)(2,1)S(1)} %slice.28), channel_id=1, source_target_pairs={{0,17},{1,16},{2,19},{3,18},{4,21},{5,20},{6,23},{7,22},{8,25},{9,... | collective-permute-start | bytes 786440 | tf_op jit(solution)/shard_map/ppermute | solution.py:71
  35.4 8.4 %collective-permute-start.13 = (bf16[1,512,256]{2,1,0:T(8,128)(2,1)S(1)}, bf16[1,512,256]{2,1,0:T(8,128)(2,1)S(1)}, u32[]{:S(2)}, u32[]{:S(2)}) collective-permute-start(bf16[1,512,256]{2,1,0:T(8,128)(2,1)S(1)} %slice.31), channel_id=1, source_target_pairs={{0,2},{1,3},{2,0},{3,1},{4,6},{5,7},{6,4},{7,5},{8,10},{9,11},{10,... | collective-permute-start | bytes 786440 | tf_op jit(solution)/shard_map/ppermute | solution.py:62
  36.8 7.7 %collective-permute-start.12 = (bf16[1,512,256]{2,1,0:T(8,128)(2,1)S(1)}, bf16[1,512,256]{2,1,0:T(8,128)(2,1)S(1)}, u32[]{:S(2)}, u32[]{:S(2)}) collective-permute-start(bf16[1,512,256]{2,1,0:T(8,128)(2,1)S(1)} %slice.30), channel_id=1, source_target_pairs={{0,6},{1,7},{2,4},{3,5},{4,2},{5,3},{6,0},{7,1},{8,14},{9,15},{10,... | collective-permute-start | bytes 786440 | tf_op jit(solution)/shard_map/ppermute | solution.py:62
  46.1 2.4 %collective-permute-start.15 = (bf16[768,512]{1,0:T(8,128)(2,1)S(1)}, bf16[768,512]{1,0:T(8,128)(2,1)S(1)}, u32[]{:S(2)}, u32[]{:S(2)}) collective-permute-start(bf16[768,512]{1,0:T(8,128)(2,1)S(1)} %get-tuple-element.91), channel_id=1, source_target_pairs={{0,8},{8,0},{16,24},{24,16},{1,9},{9,1},{17,25},{25,17},{2,10},{10... | collective-permute-start | bytes 2359304 | tf_op jit(solution)/shard_map/ppermute | solution.py:50
  48.5 6.1 %collective-permute-start.16 = (bf16[16,256,256]{2,1,0:T(8,128)(2,1)S(1)}, bf16[16,256,256]{2,1,0:T(8,128)(2,1)S(1)}, u32[]{:S(2)}, u32[]{:S(2)}) collective-permute-start(bf16[16,256,256]{2,1,0:T(8,128)(2,1)S(1)} %get-tuple-element.95), channel_id=1, source_target_pairs={{0,8},{8,0},{16,24},{24,16},{1,9},{9,1},{17,25},{25,17},{2,10},{10... | collective-permute-start | bytes 6291464 | tf_op jit(solution)/shard_map/ppermute | solution.py:50
  52.6 2.9 %collective-permute-start.17 = (bf16[2304,256]{1,0:T(8,128)(2,1)S(1)}, bf16[2304,256]{1,0:T(8,128)(2,1)S(1)}, u32[]{:S(2)}, u32[]{:S(2)}) collective-permute-start(bf16[2304,256]{1,0:T(8,128)(2,1)S(1)} %get-tuple-element.99.refs_3_), channel_id=1, source_target_pairs={{0,8},{8,0},{16,24},{24,16},{1,9},{9,1},{17,25},{25,17},{2,10},{10... | collective-permute-start | bytes 3538952 | tf_op jit(solution)/shard_map/ppermute | solution.py:50
  53.1 15.5 %collective-permute-start.18 = (bf16[2,512,256]{2,1,0:T(8,128)(2,1)S(1)}, bf16[2,512,256]{2,1,0:T(8,128)(2,1)S(1)}, u32[]{:S(2)}, u32[]{:S(2)}) collective-permute-start(bf16[2,512,256]{2,1,0:T(8,128)(2,1)S(1)} %get-tuple-element.103), channel_id=1, source_target_pairs={{0,16},{8,24},{16,0},{24,8},{1,17},{9,25},{17,1},{25,9},{2,18},{10... | collective-permute-start | bytes 1572872 | tf_op jit(solution)/shard_map/ppermute | solution.py:50
  56.8 14.7 %collective-permute-start.20 = (bf16[2,256,512]{2,1,0:T(8,128)(2,1)S(1)}, bf16[2,256,512]{2,1,0:T(8,128)(2,1)S(1)}, u32[]{:S(2)}, u32[]{:S(2)}) collective-permute-start(bf16[2,256,512]{2,1,0:T(8,128)(2,1)S(1)} %get-tuple-element.110), channel_id=1, source_target_pairs={{0,32},{32,0},{64,96},{96,64},{1,33},{33,1},{65,97},{97,65},{2,34}... | collective-permute-start | bytes 1572872 | tf_op jit(solution)/shard_map/ppermute | solution.py:58
  58.4 15.1 %collective-permute-start.21 = (bf16[2,256,512]{2,1,0:T(8,128)(2,1)S(1)}, bf16[2,256,512]{2,1,0:T(8,128)(2,1)S(1)}, u32[]{:S(2)}, u32[]{:S(2)}) collective-permute-start(bf16[2,256,512]{2,1,0:T(8,128)(2,1)S(1)} %get-tuple-element.111), channel_id=1, source_target_pairs={{0,96},{32,64},{64,32},{96,0},{1,97},{33,65},{65,33},{97,1},{2,98}... | collective-permute-start | bytes 1572872 | tf_op jit(solution)/shard_map/ppermute | solution.py:58
  68.5 1.6 %collective-permute-start.19 = (bf16[1,512,256]{2,1,0:T(8,128)(2,1)S(1)}, bf16[1,512,256]{2,1,0:T(8,128)(2,1)S(1)}, u32[]{:S(2)}, u32[]{:S(2)}) collective-permute-start(bf16[1,512,256]{2,1,0:T(8,128)(2,1)S(1)} %slice.27), channel_id=1, source_target_pairs={{0,8},{8,0},{16,24},{24,16},{1,9},{9,1},{17,25},{25,17},{2,10},{10... | collective-permute-start | bytes 786440 | tf_op jit(solution)/shard_map/ppermute | solution.py:50
  73.7 8.7 %collective-permute-start.22 = (bf16[256,512]{1,0:T(8,128)(2,1)S(1)}, bf16[256,512]{1,0:T(8,128)(2,1)S(1)}, u32[]{:S(2)}, u32[]{:S(2)}) collective-permute-start(bf16[256,512]{1,0:T(8,128)(2,1)S(1)} %get-tuple-element.116), channel_id=1, source_target_pairs={{0,96},{32,64},{64,32},{96,0},{1,97},{33,65},{65,33},{97,1},{2,98}... | collective-permute-start | bytes 786440 | tf_op jit(solution)/shard_map/ppermute | solution.py:58
  75.8 7.2 %collective-permute-start.23 = (bf16[256,512]{1,0:T(8,128)(2,1)S(1)}, bf16[256,512]{1,0:T(8,128)(2,1)S(1)}, u32[]{:S(2)}, u32[]{:S(2)}) collective-permute-start(bf16[256,512]{1,0:T(8,128)(2,1)S(1)} %get-tuple-element.117), channel_id=1, source_target_pairs={{0,32},{32,0},{64,96},{96,64},{1,33},{33,1},{65,97},{97,65},{2,34}... | collective-permute-start | bytes 786440 | tf_op jit(solution)/shard_map/ppermute | solution.py:58
  75.8 12.8 %collective-permute-start.24 = (bf16[2,512,256]{2,1,0:T(8,128)(2,1)S(1)}, bf16[2,512,256]{2,1,0:T(8,128)(2,1)S(1)}, u32[]{:S(2)}, u32[]{:S(2)}) collective-permute-start(bf16[2,512,256]{2,1,0:T(8,128)(2,1)S(1)} %get-tuple-element.124), channel_id=1, source_target_pairs={{0,2},{1,3},{2,0},{3,1},{4,6},{5,7},{6,4},{7,5},{8,10},{9,11},{10,... | collective-permute-start | bytes 1572872 | tf_op jit(solution)/shard_map/ppermute | solution.py:62
  76.2 13.7 %collective-permute-start.25 = (bf16[2,512,256]{2,1,0:T(8,128)(2,1)S(1)}, bf16[2,512,256]{2,1,0:T(8,128)(2,1)S(1)}, u32[]{:S(2)}, u32[]{:S(2)}) collective-permute-start(bf16[2,512,256]{2,1,0:T(8,128)(2,1)S(1)} %get-tuple-element.125), channel_id=1, source_target_pairs={{0,6},{1,7},{2,4},{3,5},{4,2},{5,3},{6,0},{7,1},{8,14},{9,15},{10,... | collective-permute-start | bytes 1572872 | tf_op jit(solution)/shard_map/ppermute | solution.py:62
  83.1 16.6 %collective-permute-start.30 = (bf16[640,512]{1,0:T(8,128)(2,1)S(1)}, bf16[640,512]{1,0:T(8,128)(2,1)S(1)}, u32[]{:S(2)}, u32[]{:S(2)}) collective-permute-start(bf16[640,512]{1,0:T(8,128)(2,1)S(1)} %get-tuple-element.136), channel_id=1, source_target_pairs={{0,16},{8,24},{16,0},{24,8},{1,17},{9,25},{17,1},{25,9},{2,18},{10... | collective-permute-start | bytes 1966088 | tf_op jit(solution)/shard_map/ppermute | solution.py:50
  84.7 11.5 %collective-permute-start.26 = (bf16[2,256,512]{2,1,0:T(8,128)(2,1)S(1)}, bf16[2,256,512]{2,1,0:T(8,128)(2,1)S(1)}, u32[]{:S(2)}, u32[]{:S(2)}) collective-permute-start(bf16[2,256,512]{2,1,0:T(8,128)(2,1)S(1)} %get-tuple-element.129), channel_id=1, source_target_pairs={{0,32},{32,0},{64,96},{96,64},{1,33},{33,1},{65,97},{97,65},{2,34}... | collective-permute-start | bytes 1572872 | tf_op jit(solution)/shard_map/ppermute | solution.py:58
  85.0 12.6 %collective-permute-start.27 = (bf16[2,256,512]{2,1,0:T(8,128)(2,1)S(1)}, bf16[2,256,512]{2,1,0:T(8,128)(2,1)S(1)}, u32[]{:S(2)}, u32[]{:S(2)}) collective-permute-start(bf16[2,256,512]{2,1,0:T(8,128)(2,1)S(1)} %get-tuple-element.130), channel_id=1, source_target_pairs={{0,96},{32,64},{64,32},{96,0},{1,97},{33,65},{65,33},{97,1},{2,98}... | collective-permute-start | bytes 1572872 | tf_op jit(solution)/shard_map/ppermute | solution.py:58
  90.1 9.6 %collective-permute-start.28 = (bf16[512,256]{1,0:T(8,128)(2,1)S(1)}, bf16[512,256]{1,0:T(8,128)(2,1)S(1)}, u32[]{:S(2)}, u32[]{:S(2)}) collective-permute-start(bf16[512,256]{1,0:T(8,128)(2,1)S(1)} %get-tuple-element.134), channel_id=1, source_target_pairs={{0,6},{1,7},{2,4},{3,5},{4,2},{5,3},{6,0},{7,1},{8,14},{9,15},{10,... | collective-permute-start | bytes 786440 | tf_op jit(solution)/shard_map/ppermute | solution.py:62
  92.8 6.9 %collective-permute-start.29 = (bf16[512,256]{1,0:T(8,128)(2,1)S(1)}, bf16[512,256]{1,0:T(8,128)(2,1)S(1)}, u32[]{:S(2)}, u32[]{:S(2)}) collective-permute-start(bf16[512,256]{1,0:T(8,128)(2,1)S(1)} %get-tuple-element.135), channel_id=1, source_target_pairs={{0,2},{1,3},{2,0},{3,1},{4,6},{5,7},{6,4},{7,5},{8,10},{9,11},{10,... | collective-permute-start | bytes 786440 | tf_op jit(solution)/shard_map/ppermute | solution.py:62
  97.9 7.7 %collective-permute-start.31 = (bf16[256,512]{1,0:T(8,128)(2,1)S(1)}, bf16[256,512]{1,0:T(8,128)(2,1)S(1)}, u32[]{:S(2)}, u32[]{:S(2)}) collective-permute-start(bf16[256,512]{1,0:T(8,128)(2,1)S(1)} %get-tuple-element.140), channel_id=1, source_target_pairs={{0,96},{32,64},{64,32},{96,0},{1,97},{33,65},{65,33},{97,1},{2,98}... | collective-permute-start | bytes 786440 | tf_op jit(solution)/shard_map/ppermute | solution.py:58
  99.5 6.4 %collective-permute-start.32 = (bf16[256,512]{1,0:T(8,128)(2,1)S(1)}, bf16[256,512]{1,0:T(8,128)(2,1)S(1)}, u32[]{:S(2)}, u32[]{:S(2)}) collective-permute-start(bf16[256,512]{1,0:T(8,128)(2,1)S(1)} %get-tuple-element.141), channel_id=1, source_target_pairs={{0,32},{32,0},{64,96},{96,64},{1,33},{33,1},{65,97},{97,65},{2,34}... | collective-permute-start | bytes 786440 | tf_op jit(solution)/shard_map/ppermute | solution.py:58
  99.8 7.2 %collective-permute-start.33 = (bf16[512,256]{1,0:T(8,128)(2,1)S(1)}, bf16[512,256]{1,0:T(8,128)(2,1)S(1)}, u32[]{:S(2)}, u32[]{:S(2)}) collective-permute-start(bf16[512,256]{1,0:T(8,128)(2,1)S(1)} %get-tuple-element.146), channel_id=1, source_target_pairs={{0,1},{1,0},{2,3},{3,2},{4,5},{5,4},{6,7},{7,6},{8,9},{9,8},{10,11... | collective-permute-start | bytes 786440 | tf_op jit(solution)/shard_map/ppermute | solution.py:54

commit v4 on v3

--- a/solution.py
+++ b/solution.py
@@ -93,7 +93,8 @@
 
 def join_z_body(idx, z0, z1, z2, z3, zb):
     for m, z in enumerate((z0, z1, z2, z3)):
-        zb[m] = z[...]
+        zb[256 * m : 256 * m + 256] = z[...]
+    zb[1024:] = jnp.zeros((32, 256), BF)
 
 
 def weight_rows(w, idx, m, b, which):
@@ -107,16 +108,20 @@
     return jnp.dot(left, right, preferred_element_type=F32)
 
 
+def block(x, m):
+    return x[256 * m : 256 * m + 256]
+
+
 def project_first_body(idx, wk, wv, ya, zb, by1, by3, acc, es):
     c = idx[C]
     terms = [(ya[0], 0, 0, c), (ya[1], 0, 1, c)]
-    terms += [(jnp.concatenate([by1[m], by3[m]], axis=0), m, 1, 1 - c) for m in range(4)]
+    terms += [(jnp.concatenate([block(by1, m), block(by3, m)], axis=0), m, 1, 1 - c) for m in range(4)]
     for n, w in enumerate((wk, wv)):
         at = slice(n * 512, n * 512 + 512)
         acc[:, at] = product(idx, w, terms)
-        acc[:256, at] += product(idx, w, [(zb[m], m, 0, 1 - c) for m in range(4)])
+        acc[:256, at] += product(idx, w, [(block(zb, m), m, 0, 1 - c) for m in range(4)])
     for m, b in ((0, zb), (1, by1), (3, by3)):
-        es[4 * m : 4 * m + 4] = b[...]
+        es[1024 * m : 1024 * m + 1024] = b[:1024]
 
 
 def project_next_body(idx, wk, wv, acc_in, az1, az3, acc):
@@ -129,7 +134,7 @@
 
 def project_last_body(idx, wk, wv, acc, by20, by21, az20, az21, qg_own, qg_far, es_in, send, keep, es, total):
     c = idx[C]
-    by2 = [by20[0], by20[1], by21[0], by21[1]]
+    by2 = [by20[:256], by20[256:512], by21[:256], by21[256:512]]
     for n, w in enumerate((wk, wv)):
         at = slice(n * 512, n * 512 + 512)
         total[:, at] = acc[:, at] + product(idx, w, [(az20[0], 2, 0, c), (az21[0], 2, 1, c)])
@@ -140,8 +145,8 @@
     for i, qg in enumerate((qg_own, qg_far)):
         for n in range(2):
             send[512 + 128 * i : 640 + 128 * i, 256 * n : 256 * n + 256] = qg[n, :, cols(1 - c)]
-    es[8:10] = by20[...]
-    es[10:12] = by21[...]
+    es[2048:2560] = by20[:512]
+    es[2560:3072] = by21[:512]
 
 
 def turn_keep_body(idx, ya, az1, az20, az21, az3, out):
@@ -154,8 +159,8 @@
 def turn_other_body(idx, es, out):
     for m in range(4):
         for b in range(2):
-            out[2 * m + b, :, :256] = es[4 * b + m].T
-            out[2 * m + b, :, 256:] = es[4 * (2 + b) + m].T
+            out[2 * m + b, :, :256] = block(es, 4 * b + m).T
+            out[2 * m + b, :, 256:] = block(es, 8 + 4 * b + m).T
 
 
 def attend_body(idx, kv_own, kv_oth, qg_own, qg_far, g, g_far, gq_own, gq_far, acc):
@@ -342,35 +347,35 @@
     other = lax.dynamic_index_in_dim(halves, 1 - c, 0, keepdims=False)
     from_y = [mine] + [swap_y(mine, m) for m in (1, 2, 3)]
     from_z = [other] + [swap_z(other, m) for m in (1, 2, 3)]
+    idx, zb = call(join_z_body, "join_z", [idx, *from_z], [arr((1056, 256))])
     idx, ya, qg0, qg_send = call(
         join_y_body, "join_y", [idx, *from_y, queries, grad_context],
-        [arr((2, 512, 256)), qg_block, qg_block], [dma((2, 2))], hbm=(4, 5),
-    )
-    idx, zb = call(join_z_body, "join_z", [idx, *from_z], [arr((4, 256, 256))], flops=30_000_000_000)
+        [arr((2, 512, 256)), qg_block, qg_block], [dma((2, 2))], hbm=(4, 5), flops=30_000_000_000,
+    )
     by1, by3 = swap_y(zb, 1), swap_y(zb, 3)
     az1, az3 = swap_z(ya, 1), swap_z(ya, 3)
-    by20, by21 = swap_y(by1[:2], 3), swap_y(by3[2:], 1)
+    by20, by21 = swap_y(by1[:528], 3), swap_y(by3[512:1040], 1)
     az20, az21 = swap_z(az1[:1], 3), swap_z(az3[1:], 1)
 
     ws = [w_key, w_value]
     qg2 = swap_seq(qg_send, 2)
     idx, acc, es = call(
         project_first_body, "project_first", [idx, *ws, ya, zb, by1, by3],
-        [arr((512, 1024), F32), arr((16, 256, 256))],
+        [arr((512, 1024), F32), arr((4096, 256))],
     )
     idx, acc = call(
         project_next_body, "project_next", [idx, *ws, acc, az1, az3], [arr((512, 1024), F32)]
     )
     idx, kv_send, kv_own, es = call(
         project_last_body, "project_last", [idx, *ws, acc, by20, by21, az20, az21, qg0, qg2, es],
-        [arr((768, 512)), arr((512, 512)), arr((16, 256, 256))], [pltpu.VMEM((512, 1024), F32)],
+        [arr((768, 512)), arr((512, 512)), arr((4096, 256))], [pltpu.VMEM((512, 1024), F32)],
         alias={10: 3},
     )
     kv_oth = swap_seq(kv_send, 1)
     idx, keep_t = call(
         turn_keep_body, "turn_keep", [idx, ya, az1, az20, az21, az3], [arr((8, 256, 512))]
     )
-    idx, es = call(relay_body, "relay_rows", [idx, es, kv_oth], [arr((16, 256, 256))], alias={1: 1})
+    idx, es = call(relay_body, "relay_rows", [idx, es, kv_oth], [arr((4096, 256))], alias={1: 1})
     es_oth = swap_seq(es, 1)
 
     idx, g, g_far, gq_own, gq_far = call(

time: 109 us -> 107 us (0.982); the launches traced: 108 us -> 107 us
  waiting for transfers between devices: 37.8 us -> 35.2 us
  starting transfers between devices: 43.7 us -> 45.4 us
    ppermute x7, waiting for transfers between devices: 11.2 us -> 7.54 us  [swap_y(): return lax.ppermute(x, ('seq', 'tensor'), pairs)]
    ppermute x7, starting transfers between devices: 8.27 us -> 11.5 us  [swap_y(): return lax.ppermute(x, ('seq', 'tensor'), pairs)]
    ppermute x11, starting transfers between devices: 18.7 us -> 16.5 us  [swap_z(): return lax.ppermute(x, 'tensor', [(t, t ^ 2 * m) for t in range(8)])]
    ppermute x7, waiting for transfers between devices: 6.75 us -> 8.38 us  [swap_seq(): return lax.ppermute(x, 'seq', [(s, s ^ m) for s in range(4)])]
    ppermute x7, starting transfers between devices: 5.48 us -> 6.92 us  [swap_seq(): return lax.ppermute(x, 'seq', [(s, s ^ m) for s in range(4)])]
    ppermute x11, waiting for transfers between devices: 7.43 us -> 6.14 us  [swap_z(): return lax.ppermute(x, 'tensor', [(t, t ^ 2 * m) for t in range(8)])]
  transfers between devices with their start and end apart: 34 -> 34, of which waited for: 21 -> 19; matrix products, arithmetic and copies ran while one was open for 0% -> 0% of each run, Pallas kernels for 20% -> 20%
where the time goes in v4:
time: 107 us
  starting transfers between devices  45.4 us (42%)
  waiting for transfers between devices  35.2 us (33%)
  Pallas kernels  24.3 us (23%)
  local copies, waits for them, and re-layouts  1.1 us (1%)
    pallas_call x22, Pallas kernels, call(): pl.pallas_call(wrapped, in_specs=specs, out_specs=[ANY] + [VMEM] * len(ou...  24.3 us
    ppermute x11, starting transfers between devices, swap_z(): return lax.ppermute(x, 'tensor', [(t, t ^ 2 * m) for t in range(8)])  16.5 us
    ppermute x8, waiting for transfers between devices, swap_x(): return lax.ppermute(x, 'dp', [(d, d ^ m) for d in range(4)])  13.2 us
    ppermute x7, starting transfers between devices, swap_y(): return lax.ppermute(x, ('seq', 'tensor'), pairs)  11.5 us
    ppermute x8, starting transfers between devices, swap_x(): return lax.ppermute(x, 'dp', [(d, d ^ m) for d in range(4)])  9.1 us
    ppermute x7, waiting for transfers between devices, swap_seq(): return lax.ppermute(x, 'seq', [(s, s ^ m) for s in range(4)])  8.38 us
    ppermute x7, waiting for transfers between devices, swap_y(): return lax.ppermute(x, ('seq', 'tensor'), pairs)  7.54 us
    ppermute x7, starting transfers between devices, swap_seq(): return lax.ppermute(x, 'seq', [(s, s ^ m) for s in range(4)])  6.92 us
  transfers between devices with their start and end apart: 34, of which 19 were waited for; matrix products, arithmetic and copies ran while one was open for 0% of the time, Pallas kernels for 20%

profile of v4, /device:TPU:0, one launch (start us, length us, event | category | flops | bytes accessed | tf_op | source)
XLA Modules:
  0.0 107.0 jit_solution(380895053726879387)
XLA Ops:
  0.6 1.0 fusion.4
  1.8 4.2 %collective-permute-start.2 = (bf16[256,256]{1,0:T(8,128)(2,1)S(1)}, bf16[256,256]{1,0:T(8,128)(2,1)S(1)}, u32[]{:S(2)}, u32[]{:S(2)}) collective-permute-start(bf16[256,256]{1,0:T(8,128)(2,1)S(1)} %get-tuple-element.151.refs_1_), channel_id=1, source_target_pairs={{0,6},{1,7},{2,4},{3,5},{4,2},{5,3},{6,0},{7,1},{8,14},{9,15},{10,... | collective-permute-start | bytes 393224 | tf_op jit(solution)/shard_map/ppermute | solution.py:62
  6.0 0.9 collective-permute-start
  6.9 3.0 %collective-permute-start.5 = (bf16[256,256]{1,0:T(8,128)(2,1)S(1)}, bf16[256,256]{1,0:T(8,128)(2,1)S(1)}, u32[]{:S(2)}, u32[]{:S(2)}) collective-permute-start(bf16[256,256]{1,0:T(8,128)(2,1)S(1)} %get-tuple-element.150.refs_1_), channel_id=1, source_target_pairs={{0,17},{1,16},{2,19},{3,18},{4,21},{5,20},{6,23},{7,22},{8,25},{9,... | collective-permute-start | bytes 393224 | tf_op jit(solution)/shard_map/ppermute | solution.py:71
  10.5 1.0 collective-permute-done.2.refs_4_
  11.5 1.6 %collective-permute-start.3 = (bf16[256,256]{1,0:T(8,128)(2,1)S(1)}, bf16[256,256]{1,0:T(8,128)(2,1)S(1)}, u32[]{:S(2)}, u32[]{:S(2)}) collective-permute-start(bf16[256,256]{1,0:T(8,128)(2,1)S(1)} %get-tuple-element.150.refs_1_), channel_id=1, source_target_pairs={{0,1},{1,0},{2,3},{3,2},{4,5},{5,4},{6,7},{7,6},{8,9},{9,8},{10,11... | collective-permute-start | bytes 393224 | tf_op jit(solution)/shard_map/ppermute | solution.py:71
  13.1 0.7 collective-permute-done.1.refs_3_
  13.9 3.1 %collective-permute-start.7 = (bf16[1056,256]{1,0:T(8,128)(2,1)S(1)}, bf16[1056,256]{1,0:T(8,128)(2,1)S(1)}, u32[]{:S(2)}, u32[]{:S(2)}) collective-permute-start(bf16[1056,256]{1,0:T(8,128)(2,1)S(1)} %get-tuple-element.80.refs_4_), channel_id=1, source_target_pairs={{0,17},{1,16},{2,19},{3,18},{4,21},{5,20},{6,23},{7,22},{8,25},{9,... | collective-permute-start | bytes 1622024 | tf_op jit(solution)/shard_map/ppermute | solution.py:71
  17.2 1.3 %join_y.1 = (s32[8,128]{1,0:T(8,128)S(1)}, bf16[2,512,256]{2,1,0:T(8,128)(2,1)S(1)}, bf16[2,128,512]{2,1,0:T(8,128)(2,1)S(1)}, bf16[2,128,512]{2,1,0:T(8,128)(2,1)S(1)}) custom-call(s32[8,128]{1,0:T(8,128)S(1)} %get-tuple-element.77.refs_0_, bf16[256,256]{1,0:T(8,128)(2,1)S(1)} %get-tuple-element.150.refs_1_, ...), custom_call_target="tpu_custom_call", output_to_operand_aliasing={{0}: (0, {})} | custom-call | flops 30000001024 | bytes 1 | tf_op jit(solution)/shard_map/join_y/pallas_call | solution.py:36
  18.5 3.2 %collective-permute-start.9 = (bf16[2,512,256]{2,1,0:T(8,128)(2,1)S(1)}, bf16[2,512,256]{2,1,0:T(8,128)(2,1)S(1)}, u32[]{:S(2)}, u32[]{:S(2)}) collective-permute-start(bf16[2,512,256]{2,1,0:T(8,128)(2,1)S(1)} %get-tuple-element.79.refs_3_.refs_1_), channel_id=1, source_target_pairs={{0,6},{1,7},{2,4},{3,5},{4,2},{5,3},{6,0},{7,1},{8,14},{9,15},{10,... | collective-permute-start | bytes 1572872 | tf_op jit(solution)/shard_map/ppermute | solution.py:62
  22.0 6.0 %collective-permute-done.7.refs_6_ = bf16[1056,256]{1,0:T(8,128)(2,1)S(1)} collective-permute-done((bf16[1056,256]{1,0:T(8,128)(2,1)S(1)}, bf16[1056,256]{1,0:T(8,128)(2,1)S(1)}, u32[]{:S(2)}, u32[]{:S(2)}) %collective-permute-start.7) | collective-permute-done | bytes 540704 | tf_op jit(solution)/shard_map/ppermute | solution.py:71
  28.3 1.1 %collective-permute-done.6.refs_5_ = bf16[1056,256]{1,0:T(8,128)(2,1)S(1)} collective-permute-done((bf16[1056,256]{1,0:T(8,128)(2,1)S(1)}, bf16[1056,256]{1,0:T(8,128)(2,1)S(1)}, u32[]{:S(2)}, u32[]{:S(2)}) %collective-permute-start.6) | collective-permute-done | bytes 540704 | tf_op jit(solution)/shard_map/ppermute | solution.py:71
  29.4 2.9 %collective-permute-start.10 = (bf16[528,256]{1,0:T(8,128)(2,1)S(1)}, bf16[528,256]{1,0:T(8,128)(2,1)S(1)}, u32[]{:S(2)}, u32[]{:S(2)}) collective-permute-start(bf16[528,256]{1,0:T(8,128)(2,1)S(1)} %slice.28), channel_id=1, source_target_pairs={{0,17},{1,16},{2,19},{3,18},{4,21},{5,20},{6,23},{7,22},{8,25},{9,... | collective-permute-start | bytes 811016 | tf_op jit(solution)/shard_map/ppermute | solution.py:71
  32.3 0.9 collective-permute-start.14
  33.2 0.8 collective-permute-start.13
  34.6 1.6 %collective-permute-start.12 = (bf16[1,512,256]{2,1,0:T(8,128)(2,1)S(1)}, bf16[1,512,256]{2,1,0:T(8,128)(2,1)S(1)}, u32[]{:S(2)}, u32[]{:S(2)}) collective-permute-start(bf16[1,512,256]{2,1,0:T(8,128)(2,1)S(1)} %slice.30), channel_id=1, source_target_pairs={{0,6},{1,7},{2,4},{3,5},{4,2},{5,3},{6,0},{7,1},{8,14},{9,15},{10,... | collective-permute-start | bytes 786440 | tf_op jit(solution)/shard_map/ppermute | solution.py:62
  36.2 2.3 %project_first.1 = (s32[8,128]{1,0:T(8,128)S(1)}, f32[512,1024]{1,0:T(8,128)S(1)}, bf16[4096,256]{1,0:T(8,128)(2,1)S(1)}) custom-call(s32[8,128]{1,0:T(8,128)S(1)} %get-tuple-element.78.refs_0_, bf16[2,4096,512]{2,1,0:T(8,128)(2,1)S(1)} %bitcast.5, bf16[2,4096,512]{2,1,0:T(8,128)(2,1)S(1)} %bitcast.7, ...), custom_call_target="tpu_custom_call", output_to_operand_aliasing={{0}: (0, {})} | custom-call | flops 1 | bytes 1 | tf_op jit(solution)/shard_map/project_first/pallas_call | solution.py:36
  38.6 1.3 %project_next.1 = (s32[8,128]{1,0:T(8,128)S(1)}, f32[512,1024]{1,0:T(8,128)S(1)}) custom-call(s32[8,128]{1,0:T(8,128)S(1)} %get-tuple-element.81.refs_0_, bf16[2,4096,512]{2,1,0:T(8,128)(2,1)S(1)} %bitcast.5, bf16[2,4096,512]{2,1,0:T(8,128)(2,1)S(1)} %bitcast.7, f32[512,1024]{1,0:T(8,128)S(1)} %get-tuple-element.82.refs_3_, ...), custom_call_target="tpu_custom_call", output_to_operand_aliasing={{0}: (0, {})} | custom-call | flops 1 | bytes 1 | tf_op jit(solution)/shard_map/project_next/pallas_call | solution.py:36
  39.8 2.5 %collective-permute-done.14.refs_9_.refs_4_ = bf16[2,128,512]{2,1,0:T(8,128)(2,1)S(1)} collective-permute-done((bf16[2,128,512]{2,1,0:T(8,128)(2,1)S(1)}, bf16[2,128,512]{2,1,0:T(8,128)(2,1)S(1)}, u32[]{:S(2)}, u32[]{:S(2)}) %collective-permute-start.14) | collective-permute-done | bytes 262176 | tf_op jit(solution)/shard_map/ppermute | solution.py:50
  42.7 1.7 %project_last.1 = (s32[8,128]{1,0:T(8,128)S(1)}, bf16[768,512]{1,0:T(8,128)(2,1)S(1)}, bf16[512,512]{1,0:T(8,128)(2,1)S(1)}, bf16[4096,256]{1,0:T(8,128)(2,1)S(1)}) custom-call(s32[8,128]{1,0:T(8,128)S(1)} %get-tuple-element.83.refs_0_, bf16[2,4096,512]{2,1,0:T(8,128)(2,1)S(1)} %bitcast.5, ...), custom_call_target="tpu_custom_call", output_to_operand_aliasing={{0}: (0, {}), {3}: (10, {})} | custom-call | flops 1 | bytes 1 | tf_op jit(solution)/shard_map/project_last/pallas_call | solution.py:36
  45.0 1.7 %collective-permute-done.15.refs_2_ = bf16[768,512]{1,0:T(8,128)(2,1)S(1)} collective-permute-done((bf16[768,512]{1,0:T(8,128)(2,1)S(1)}, bf16[768,512]{1,0:T(8,128)(2,1)S(1)}, u32[]{:S(2)}, u32[]{:S(2)}) %collective-permute-start.15) | collective-permute-done | bytes 786464 | tf_op jit(solution)/shard_map/ppermute | solution.py:50
  46.9 3.9 %attend.1 = (s32[8,128]{1,0:T(8,128)S(1)}, bf16[2304,256]{1,0:T(8,128)(2,1)S(1)}, bf16[2,512,256]{2,1,0:T(8,128)(2,1)S(1)}, bf16[128,256]{1,0:T(8,128)(2,1)S(1)}, bf16[128,256]{1,0:T(8,128)(2,1)S(1)}) custom-call(s32[8,128]{1,0:T(8,128)S(1)} %get-tuple-element.92.refs_0_, ...), custom_call_target="tpu_custom_call", output_to_operand_aliasing={{0}: (0, {})} | custom-call | flops 1 | bytes 1 | tf_op jit(solution)/shard_map/attend/pallas_call | solution.py:36
  51.3 2.5 %collective-permute-start.18 = (bf16[2,512,256]{2,1,0:T(8,128)(2,1)S(1)}, bf16[2,512,256]{2,1,0:T(8,128)(2,1)S(1)}, u32[]{:S(2)}, u32[]{:S(2)}) collective-permute-start(bf16[2,512,256]{2,1,0:T(8,128)(2,1)S(1)} %get-tuple-element.103), channel_id=1, source_target_pairs={{0,16},{8,24},{16,0},{24,8},{1,17},{9,25},{17,1},{25,9},{2,18},{10... | collective-permute-start | bytes 1572872 | tf_op jit(solution)/shard_map/ppermute | solution.py:50
  54.3 1.3 %weights_first.1 = (s32[8,128]{1,0:T(8,128)S(1)}, bf16[2,256,512]{2,1,0:T(8,128)(2,1)S(1)}, bf16[2,256,512]{2,1,0:T(8,128)(2,1)S(1)}) custom-call(s32[8,128]{1,0:T(8,128)S(1)} %get-tuple-element.96.refs_0_, bf16[8,256,512]{2,1,0:T(8,128)(2,1)S(1)} %get-tuple-element.97.refs_1_, ...), custom_call_target="tpu_custom_call", output_to_operand_aliasing={{0}: (0, {})} | custom-call | flops 1 | bytes 1 | tf_op jit(solution)/shard_map/weights_first/pallas_call | solution.py:36
  55.6 1.6 %collective-permute-start.20 = (bf16[2,256,512]{2,1,0:T(8,128)(2,1)S(1)}, bf16[2,256,512]{2,1,0:T(8,128)(2,1)S(1)}, u32[]{:S(2)}, u32[]{:S(2)}) collective-permute-start(bf16[2,256,512]{2,1,0:T(8,128)(2,1)S(1)} %get-tuple-element.110), channel_id=1, source_target_pairs={{0,32},{32,0},{64,96},{96,64},{1,33},{33,1},{65,97},{97,65},{2,34}... | collective-permute-start | bytes 1572872 | tf_op jit(solution)/shard_map/ppermute | solution.py:58
  57.1 2.1 %collective-permute-start.21 = (bf16[2,256,512]{2,1,0:T(8,128)(2,1)S(1)}, bf16[2,256,512]{2,1,0:T(8,128)(2,1)S(1)}, u32[]{:S(2)}, u32[]{:S(2)}) collective-permute-start(bf16[2,256,512]{2,1,0:T(8,128)(2,1)S(1)} %get-tuple-element.111), channel_id=1, source_target_pairs={{0,96},{32,64},{64,32},{96,0},{1,97},{33,65},{65,33},{97,1},{2,98}... | collective-permute-start | bytes 1572872 | tf_op jit(solution)/shard_map/ppermute | solution.py:58
  59.2 3.4 %weights_rest.1 = (s32[8,128]{1,0:T(8,128)S(1)}, bf16[2,256,512]{2,1,0:T(8,128)(2,1)S(1)}, bf16[2,256,512]{2,1,0:T(8,128)(2,1)S(1)}, f32[2,256,512]{2,1,0:T(8,12...) custom-call(s32[8,128]{1,0:T(8,128)S(1)} %get-tuple-element.100.refs, ...), custom_call_target="tpu_custom_call", output_to_operand_aliasing={{0}: (0, {})} | custom-call | flops 1 | bytes 1 | tf_op jit(solution)/shard_map/weights_rest/pallas_call | solution.py:36
  62.7 1.4 %encoder_own.1 = (s32[8,128]{1,0:T(8,128)S(1)}, f32[2,2,512,256]{3,2,1,0:T(8,128)S(1)}) custom-call(s32[8,128]{1,0:T(8,128)S(1)} %get-tuple-element.101.refs_0_, bf16[2,4096,512]{2,1,0:T(8,128)(2,1)S(1)} %bitcast.5, bf16[2,4096,512]{2,1,0:T(8,128)(2,1)S(1)} %bitcast.7, ...), custom_call_target="tpu_custom_call", output_to_operand_aliasing={{0}: (0, {})} | custom-call | flops 1 | bytes 1 | tf_op jit(solution)/shard_map/encoder_own/pallas_call | solution.py:36
  64.0 2.7 %collective-permute-done.18.refs_1_ = bf16[2,512,256]{2,1,0:T(8,128)(2,1)S(1)} collective-permute-done((bf16[2,512,256]{2,1,0:T(8,128)(2,1)S(1)}, bf16[2,512,256]{2,1,0:T(8,128)(2,1)S(1)}, u32[]{:S(2)}, u32[]{:S(2)}) %collective-permute-start.18) | collective-permute-done | bytes 524320 | tf_op jit(solution)/shard_map/ppermute | solution.py:50
  66.8 1.5 %collective-permute-done.19.refs_5_.refs_6_ = bf16[1,512,256]{2,1,0:T(8,128)(2,1)S(1)} collective-permute-done((bf16[1,512,256]{2,1,0:T(8,128)(2,1)S(1)}, bf16[1,512,256]{2,1,0:T(8,128)(2,1)S(1)}, u32[]{:S(2)}, u32[]{:S(2)}) %collective-permute-start.19) | collective-permute-done | bytes 262176 | tf_op jit(solution)/shard_map/ppermute | solution.py:50
  68.4 1.4 %encoder_sent.1 = (s32[8,128]{1,0:T(8,128)S(1)}, bf16[2,512,256]{2,1,0:T(8,128)(2,1)S(1)}, bf16[2,512,256]{2,1,0:T(8,128)(2,1)S(1)}) custom-call(s32[8,128]{1,0:T(8,128)S(1)} %get-tuple-element.104.refs_0_, bf16[2,4096,512]{2,1,0:T(8,128)(2,1)S(1)} %bitcast.5, bf16[2,4096,512]{2,1,0:T(8,128)(2,1)S(1)} %bitcast.7, ...), custom_call_target="tpu_custom_call", output_to_operand_aliasing={{0}: (0, {})} | custom-call | flops 1 | bytes 1 | tf_op jit(solution)/shard_map/encoder_sent/pallas_call | solution.py:36
  69.8 2.0 %collective-permute-done.21.refs_4_ = bf16[2,256,512]{2,1,0:T(8,128)(2,1)S(1)} collective-permute-done((bf16[2,256,512]{2,1,0:T(8,128)(2,1)S(1)}, bf16[2,256,512]{2,1,0:T(8,128)(2,1)S(1)}, u32[]{:S(2)}, u32[]{:S(2)}) %collective-permute-start.21) | collective-permute-done | bytes 524320 | tf_op jit(solution)/shard_map/ppermute | solution.py:58
  71.9 2.2 %collective-permute-start.22 = (bf16[256,512]{1,0:T(8,128)(2,1)S(1)}, bf16[256,512]{1,0:T(8,128)(2,1)S(1)}, u32[]{:S(2)}, u32[]{:S(2)}) collective-permute-start(bf16[256,512]{1,0:T(8,128)(2,1)S(1)} %get-tuple-element.116), channel_id=1, source_target_pairs={{0,96},{32,64},{64,32},{96,0},{1,97},{33,65},{65,33},{97,1},{2,98}... | collective-permute-start | bytes 786440 | tf_op jit(solution)/shard_map/ppermute | solution.py:58
  74.1 1.3 %collective-permute-start.24 = (bf16[2,512,256]{2,1,0:T(8,128)(2,1)S(1)}, bf16[2,512,256]{2,1,0:T(8,128)(2,1)S(1)}, u32[]{:S(2)}, u32[]{:S(2)}) collective-permute-start(bf16[2,512,256]{2,1,0:T(8,128)(2,1)S(1)} %get-tuple-element.124), channel_id=1, source_target_pairs={{0,2},{1,3},{2,0},{3,1},{4,6},{5,7},{6,4},{7,5},{8,10},{9,11},{10,... | collective-permute-start | bytes 1572872 | tf_op jit(solution)/shard_map/ppermute | solution.py:62
  75.5 1.9 %collective-permute-start.25 = (bf16[2,512,256]{2,1,0:T(8,128)(2,1)S(1)}, bf16[2,512,256]{2,1,0:T(8,128)(2,1)S(1)}, u32[]{:S(2)}, u32[]{:S(2)}) collective-permute-start(bf16[2,512,256]{2,1,0:T(8,128)(2,1)S(1)} %get-tuple-element.125), channel_id=1, source_target_pairs={{0,6},{1,7},{2,4},{3,5},{4,2},{5,3},{6,0},{7,1},{8,14},{9,15},{10,... | collective-permute-start | bytes 1572872 | tf_op jit(solution)/shard_map/ppermute | solution.py:62
  77.3 2.4 %encoder_kept.1 = (s32[8,128]{1,0:T(8,128)S(1)}, f32[2,512,256]{2,1,0:T(8,128)S(1)}, f32[2,512,256]{2,1,0:T(8,128)S(1)}) custom-call(s32[8,128]{1,0:T(8,128)S(1)} %get-tuple-element.112.refs_0_, bf16[2,4096,512]{2,1,0:T(8,128)(2,1)S(1)} %bitcast.5, bf16[2,4096,512]{2,1,0:T(8,128)(2,1)S(1)} %bitcast.7, ...), custom_call_target="tpu_custom_call", output_to_operand_aliasing={{0}: (0, {})} | custom-call | flops 1 | bytes 1 | tf_op jit(solution)/shard_map/encoder_kept/pallas_call | solution.py:36
  81.0 2.9 %collective-permute-start.30 = (bf16[640,512]{1,0:T(8,128)(2,1)S(1)}, bf16[640,512]{1,0:T(8,128)(2,1)S(1)}, u32[]{:S(2)}, u32[]{:S(2)}) collective-permute-start(bf16[640,512]{1,0:T(8,128)(2,1)S(1)} %get-tuple-element.136), channel_id=1, source_target_pairs={{0,16},{8,24},{16,0},{24,8},{1,17},{9,25},{17,1},{25,9},{2,18},{10... | collective-permute-start | bytes 1966088 | tf_op jit(solution)/shard_map/ppermute | solution.py:50
  84.1 1.2 %collective-permute-start.27 = (bf16[2,256,512]{2,1,0:T(8,128)(2,1)S(1)}, bf16[2,256,512]{2,1,0:T(8,128)(2,1)S(1)}, u32[]{:S(2)}, u32[]{:S(2)}) collective-permute-start(bf16[2,256,512]{2,1,0:T(8,128)(2,1)S(1)} %get-tuple-element.130), channel_id=1, source_target_pairs={{0,96},{32,64},{64,32},{96,0},{1,97},{33,65},{65,33},{97,1},{2,98}... | collective-permute-start | bytes 1572872 | tf_op jit(solution)/shard_map/ppermute | solution.py:58
  85.3 1.2 %collective-permute-done.24.refs_3_ = bf16[2,512,256]{2,1,0:T(8,128)(2,1)S(1)} collective-permute-done((bf16[2,512,256]{2,1,0:T(8,128)(2,1)S(1)}, bf16[2,512,256]{2,1,0:T(8,128)(2,1)S(1)}, u32[]{:S(2)}, u32[]{:S(2)}) %collective-permute-start.24) | collective-permute-done | bytes 524320 | tf_op jit(solution)/shard_map/ppermute | solution.py:62
  86.5 2.7 %collective-permute-done.25.refs_4_ = bf16[2,512,256]{2,1,0:T(8,128)(2,1)S(1)} collective-permute-done((bf16[2,512,256]{2,1,0:T(8,128)(2,1)S(1)}, bf16[2,512,256]{2,1,0:T(8,128)(2,1)S(1)}, u32[]{:S(2)}, u32[]{:S(2)}) %collective-permute-start.25) | collective-permute-done | bytes 524320 | tf_op jit(solution)/shard_map/ppermute | solution.py:62
  89.3 2.2 %collective-permute-start.28 = (bf16[512,256]{1,0:T(8,128)(2,1)S(1)}, bf16[512,256]{1,0:T(8,128)(2,1)S(1)}, u32[]{:S(2)}, u32[]{:S(2)}) collective-permute-start(bf16[512,256]{1,0:T(8,128)(2,1)S(1)} %get-tuple-element.134), channel_id=1, source_target_pairs={{0,6},{1,7},{2,4},{3,5},{4,2},{5,3},{6,0},{7,1},{8,14},{9,15},{10,... | collective-permute-start | bytes 786440 | tf_op jit(solution)/shard_map/ppermute | solution.py:62
  91.5 3.9 %collective-permute-done.26.refs_3_ = bf16[2,256,512]{2,1,0:T(8,128)(2,1)S(1)} collective-permute-done((bf16[2,256,512]{2,1,0:T(8,128)(2,1)S(1)}, bf16[2,256,512]{2,1,0:T(8,128)(2,1)S(1)}, u32[]{:S(2)}, u32[]{:S(2)}) %collective-permute-start.26) | collective-permute-done | bytes 524320 | tf_op jit(solution)/shard_map/ppermute | solution.py:58
  95.4 1.5 %collective-permute-done.27.refs_4_ = bf16[2,256,512]{2,1,0:T(8,128)(2,1)S(1)} collective-permute-done((bf16[2,256,512]{2,1,0:T(8,128)(2,1)S(1)}, bf16[2,256,512]{2,1,0:T(8,128)(2,1)S(1)}, u32[]{:S(2)}, u32[]{:S(2)}) %collective-permute-start.27) | collective-permute-done | bytes 524320 | tf_op jit(solution)/shard_map/ppermute | solution.py:58
  97.1 1.6 %collective-permute-start.31 = (bf16[256,512]{1,0:T(8,128)(2,1)S(1)}, bf16[256,512]{1,0:T(8,128)(2,1)S(1)}, u32[]{:S(2)}, u32[]{:S(2)}) collective-permute-start(bf16[256,512]{1,0:T(8,128)(2,1)S(1)} %get-tuple-element.140), channel_id=1, source_target_pairs={{0,96},{32,64},{64,32},{96,0},{1,97},{33,65},{65,33},{97,1},{2,98}... | collective-permute-start | bytes 786440 | tf_op jit(solution)/shard_map/ppermute | solution.py:58
  98.9 1.4 %collective-permute-start.33 = (bf16[512,256]{1,0:T(8,128)(2,1)S(1)}, bf16[512,256]{1,0:T(8,128)(2,1)S(1)}, u32[]{:S(2)}, u32[]{:S(2)}) collective-permute-start(bf16[512,256]{1,0:T(8,128)(2,1)S(1)} %get-tuple-element.146), channel_id=1, source_target_pairs={{0,1},{1,0},{2,3},{3,2},{4,5},{5,4},{6,7},{7,6},{8,9},{9,8},{10,11... | collective-permute-start | bytes 786440 | tf_op jit(solution)/shard_map/ppermute | solution.py:54
  100.3 4.4 %collective-permute-done.31.refs_3_ = bf16[256,512]{1,0:T(8,128)(2,1)S(1)} collective-permute-done((bf16[256,512]{1,0:T(8,128)(2,1)S(1)}, bf16[256,512]{1,0:T(8,128)(2,1)S(1)}, u32[]{:S(2)}, u32[]{:S(2)}) %collective-permute-start.31) | collective-permute-done | bytes 262176 | tf_op jit(solution)/shard_map/ppermute | solution.py:58
  105.0 1.2 %finish_weights.1 = (s32[8,128]{1,0:T(8,128)S(1)}, bf16[2,256,512]{2,1,0:T(8,128)(2,1)}, bf16[2,256,512]{2,1,0:T(8,128)(2,1)}, bf16[2,1,128,512]{3,2,1,0:T(8,128)(2,1)}) custom-call(s32[8,128]{1,0:T(8,128)S(1)} %get-tuple-element.137.refs_0_, f32[256,512]{1,0:T(8,128)S(1)} %get-tuple-element.138.refs_1_, ...), custom_call_target="tpu_custom_call", output_to_operand_aliasing={{0}: (0, {})} | custom-call | flops 1 | bytes 1 | tf_op jit(solution)/shard_map/finish_weights/pallas_call | solution.py:36
  106.2 0.8 finish_encoder.1
  (60 shorter events, 7.1 us)
Async XLA Ops:
  1.8 9.8 %collective-permute-start.2 = (bf16[256,256]{1,0:T(8,128)(2,1)S(1)}, bf16[256,256]{1,0:T(8,128)(2,1)S(1)}, u32[]{:S(2)}, u32[]{:S(2)}) collective-permute-start(bf16[256,256]{1,0:T(8,128)(2,1)S(1)} %get-tuple-element.151.refs_1_), channel_id=1, source_target_pairs={{0,6},{1,7},{2,4},{3,5},{4,2},{5,3},{6,0},{7,1},{8,14},{9,15},{10,... | collective-permute-start | bytes 393224 | tf_op jit(solution)/shard_map/ppermute | solution.py:62
  6.0 7.9 %collective-permute-start.1 = (bf16[256,256]{1,0:T(8,128)(2,1)S(1)}, bf16[256,256]{1,0:T(8,128)(2,1)S(1)}, u32[]{:S(2)}, u32[]{:S(2)}) collective-permute-start(bf16[256,256]{1,0:T(8,128)(2,1)S(1)} %get-tuple-element.151.refs_1_), channel_id=1, source_target_pairs={{0,4},{1,5},{2,6},{3,7},{4,0},{5,1},{6,2},{7,3},{8,12},{9,13},{10,... | collective-permute-start | bytes 393224 | tf_op jit(solution)/shard_map/ppermute | solution.py:62
  6.0 7.9 %collective-permute-start = (bf16[256,256]{1,0:T(8,128)(2,1)S(1)}, bf16[256,256]{1,0:T(8,128)(2,1)S(1)}, u32[]{:S(2)}, u32[]{:S(2)}) collective-permute-start(bf16[256,256]{1,0:T(8,128)(2,1)S(1)} %get-tuple-element.151.refs_1_), channel_id=1, source_target_pairs={{0,2},{1,3},{2,0},{3,1},{4,6},{5,7},{6,4},{7,5},{8,10},{9,11},{10,... | collective-permute-start | bytes 393224 | tf_op jit(solution)/shard_map/ppermute | solution.py:62
  6.9 10.2 %collective-permute-start.5 = (bf16[256,256]{1,0:T(8,128)(2,1)S(1)}, bf16[256,256]{1,0:T(8,128)(2,1)S(1)}, u32[]{:S(2)}, u32[]{:S(2)}) collective-permute-start(bf16[256,256]{1,0:T(8,128)(2,1)S(1)} %get-tuple-element.150.refs_1_), channel_id=1, source_target_pairs={{0,17},{1,16},{2,19},{3,18},{4,21},{5,20},{6,23},{7,22},{8,25},{9,... | collective-permute-start | bytes 393224 | tf_op jit(solution)/shard_map/ppermute | solution.py:71
  9.9 7.2 %collective-permute-start.4 = (bf16[256,256]{1,0:T(8,128)(2,1)S(1)}, bf16[256,256]{1,0:T(8,128)(2,1)S(1)}, u32[]{:S(2)}, u32[]{:S(2)}) collective-permute-start(bf16[256,256]{1,0:T(8,128)(2,1)S(1)} %get-tuple-element.150.refs_1_), channel_id=1, source_target_pairs={{0,16},{1,17},{2,18},{3,19},{4,20},{5,21},{6,22},{7,23},{8,24},{9,... | collective-permute-start | bytes 393224 | tf_op jit(solution)/shard_map/ppermute | solution.py:71
  11.5 5.6 %collective-permute-start.3 = (bf16[256,256]{1,0:T(8,128)(2,1)S(1)}, bf16[256,256]{1,0:T(8,128)(2,1)S(1)}, u32[]{:S(2)}, u32[]{:S(2)}) collective-permute-start(bf16[256,256]{1,0:T(8,128)(2,1)S(1)} %get-tuple-element.150.refs_1_), channel_id=1, source_target_pairs={{0,1},{1,0},{2,3},{3,2},{4,5},{5,4},{6,7},{7,6},{8,9},{9,8},{10,11... | collective-permute-start | bytes 393224 | tf_op jit(solution)/shard_map/ppermute | solution.py:71
  13.9 14.2 %collective-permute-start.7 = (bf16[1056,256]{1,0:T(8,128)(2,1)S(1)}, bf16[1056,256]{1,0:T(8,128)(2,1)S(1)}, u32[]{:S(2)}, u32[]{:S(2)}) collective-permute-start(bf16[1056,256]{1,0:T(8,128)(2,1)S(1)} %get-tuple-element.80.refs_4_), channel_id=1, source_target_pairs={{0,17},{1,16},{2,19},{3,18},{4,21},{5,20},{6,23},{7,22},{8,25},{9,... | collective-permute-start | bytes 1622024 | tf_op jit(solution)/shard_map/ppermute | solution.py:71
  17.0 12.4 %collective-permute-start.6 = (bf16[1056,256]{1,0:T(8,128)(2,1)S(1)}, bf16[1056,256]{1,0:T(8,128)(2,1)S(1)}, u32[]{:S(2)}, u32[]{:S(2)}) collective-permute-start(bf16[1056,256]{1,0:T(8,128)(2,1)S(1)} %get-tuple-element.80.refs_4_), channel_id=1, source_target_pairs={{0,1},{1,0},{2,3},{3,2},{4,5},{5,4},{6,7},{7,6},{8,9},{9,8},{10,11... | collective-permute-start | bytes 1622024 | tf_op jit(solution)/shard_map/ppermute | solution.py:71
  17.1 19.1 %slice-start = ((s8[8388608]{0:T(1024)(128)(4,1)}), s8[4194304]{0:T(1024)(128)(4,1)S(1)}, s32[]{:S(2)}) async-start(s8[8388608]{0:T(1024)(128)(4,1)} %bitcast.4), calls=%async_computation | async-start | bytes 8388608
  17.1 19.1 %slice-start.2 = ((s8[8388608]{0:T(1024)(128)(4,1)}), s8[4194304]{0:T(1024)(128)(4,1)S(1)}, s32[]{:S(2)}) async-start(s8[8388608]{0:T(1024)(128)(4,1)} %bitcast.6), calls=%async_computation.2 | async-start | bytes 8388608
  17.1 19.1 %slice-start.1 = ((s8[8388608]{0:T(1024)(128)(4,1)}), s8[4194304]{0:T(1024)(128)(4,1)S(1)}, s32[]{:S(2)}) async-start(s8[8388608]{0:T(1024)(128)(4,1)} %bitcast.4), calls=%async_computation.1 | async-start | bytes 8388608
  17.1 19.0 %slice-start.3 = ((s8[8388608]{0:T(1024)(128)(4,1)}), s8[4194304]{0:T(1024)(128)(4,1)S(1)}, s32[]{:S(2)}) async-start(s8[8388608]{0:T(1024)(128)(4,1)} %bitcast.6), calls=%async_computation.3 | async-start | bytes 8388608
  18.5 14.7 %collective-permute-start.9 = (bf16[2,512,256]{2,1,0:T(8,128)(2,1)S(1)}, bf16[2,512,256]{2,1,0:T(8,128)(2,1)S(1)}, u32[]{:S(2)}, u32[]{:S(2)}) collective-permute-start(bf16[2,512,256]{2,1,0:T(8,128)(2,1)S(1)} %get-tuple-element.79.refs_3_.refs_1_), channel_id=1, source_target_pairs={{0,6},{1,7},{2,4},{3,5},{4,2},{5,3},{6,0},{7,1},{8,14},{9,15},{10,... | collective-permute-start | bytes 1572872 | tf_op jit(solution)/shard_map/ppermute | solution.py:62
  21.6 13.0 %collective-permute-start.8 = (bf16[2,512,256]{2,1,0:T(8,128)(2,1)S(1)}, bf16[2,512,256]{2,1,0:T(8,128)(2,1)S(1)}, u32[]{:S(2)}, u32[]{:S(2)}) collective-permute-start(bf16[2,512,256]{2,1,0:T(8,128)(2,1)S(1)} %get-tuple-element.79.refs_3_.refs_1_), channel_id=1, source_target_pairs={{0,2},{1,3},{2,0},{3,1},{4,6},{5,7},{6,4},{7,5},{8,10},{9,11},{10,... | collective-permute-start | bytes 1572872 | tf_op jit(solution)/shard_map/ppermute | solution.py:62
  28.1 14.2 %collective-permute-start.11 = (bf16[528,256]{1,0:T(8,128)(2,1)S(1)}, bf16[528,256]{1,0:T(8,128)(2,1)S(1)}, u32[]{:S(2)}, u32[]{:S(2)}) collective-permute-start(bf16[528,256]{1,0:T(8,128)(2,1)S(1)} %slice.29), channel_id=1, source_target_pairs={{0,1},{1,0},{2,3},{3,2},{4,5},{5,4},{6,7},{7,6},{8,9},{9,8},{10,11... | collective-permute-start | bytes 811016 | tf_op jit(solution)/shard_map/ppermute | solution.py:71
  29.4 13.3 %collective-permute-start.10 = (bf16[528,256]{1,0:T(8,128)(2,1)S(1)}, bf16[528,256]{1,0:T(8,128)(2,1)S(1)}, u32[]{:S(2)}, u32[]{:S(2)}) collective-permute-start(bf16[528,256]{1,0:T(8,128)(2,1)S(1)} %slice.28), channel_id=1, source_target_pairs={{0,17},{1,16},{2,19},{3,18},{4,21},{5,20},{6,23},{7,22},{8,25},{9,... | collective-permute-start | bytes 811016 | tf_op jit(solution)/shard_map/ppermute | solution.py:71
  32.3 10.0 %collective-permute-start.14 = (bf16[2,128,512]{2,1,0:T(8,128)(2,1)S(1)}, bf16[2,128,512]{2,1,0:T(8,128)(2,1)S(1)}, u32[]{:S(2)}, u32[]{:S(2)}) collective-permute-start(bf16[2,128,512]{2,1,0:T(8,128)(2,1)S(1)} %get-tuple-element.86), channel_id=1, source_target_pairs={{0,16},{8,24},{16,0},{24,8},{1,17},{9,25},{17,1},{25,9},{2,18},{10... | collective-permute-start | bytes 786440 | tf_op jit(solution)/shard_map/ppermute | solution.py:50
  33.2 9.1 %collective-permute-start.13 = (bf16[1,512,256]{2,1,0:T(8,128)(2,1)S(1)}, bf16[1,512,256]{2,1,0:T(8,128)(2,1)S(1)}, u32[]{:S(2)}, u32[]{:S(2)}) collective-permute-start(bf16[1,512,256]{2,1,0:T(8,128)(2,1)S(1)} %slice.31), channel_id=1, source_target_pairs={{0,2},{1,3},{2,0},{3,1},{4,6},{5,7},{6,4},{7,5},{8,10},{9,11},{10,... | collective-permute-start | bytes 786440 | tf_op jit(solution)/shard_map/ppermute | solution.py:62
  34.6 7.7 %collective-permute-start.12 = (bf16[1,512,256]{2,1,0:T(8,128)(2,1)S(1)}, bf16[1,512,256]{2,1,0:T(8,128)(2,1)S(1)}, u32[]{:S(2)}, u32[]{:S(2)}) collective-permute-start(bf16[1,512,256]{2,1,0:T(8,128)(2,1)S(1)} %slice.30), channel_id=1, source_target_pairs={{0,6},{1,7},{2,4},{3,5},{4,2},{5,3},{6,0},{7,1},{8,14},{9,15},{10,... | collective-permute-start | bytes 786440 | tf_op jit(solution)/shard_map/ppermute | solution.py:62
  44.4 2.4 %collective-permute-start.15 = (bf16[768,512]{1,0:T(8,128)(2,1)S(1)}, bf16[768,512]{1,0:T(8,128)(2,1)S(1)}, u32[]{:S(2)}, u32[]{:S(2)}) collective-permute-start(bf16[768,512]{1,0:T(8,128)(2,1)S(1)} %get-tuple-element.91), channel_id=1, source_target_pairs={{0,8},{8,0},{16,24},{24,16},{1,9},{9,1},{17,25},{25,17},{2,10},{10... | collective-permute-start | bytes 2359304 | tf_op jit(solution)/shard_map/ppermute | solution.py:50
  46.7 7.0 %collective-permute-start.16 = (bf16[4096,256]{1,0:T(8,128)(2,1)S(1)}, bf16[4096,256]{1,0:T(8,128)(2,1)S(1)}, u32[]{:S(2)}, u32[]{:S(2)}) collective-permute-start(bf16[4096,256]{1,0:T(8,128)(2,1)S(1)} %get-tuple-element.95), channel_id=1, source_target_pairs={{0,8},{8,0},{16,24},{24,16},{1,9},{9,1},{17,25},{25,17},{2,10},{10... | collective-permute-start | bytes 6291464 | tf_op jit(solution)/shard_map/ppermute | solution.py:50
  50.8 3.5 %collective-permute-start.17 = (bf16[2304,256]{1,0:T(8,128)(2,1)S(1)}, bf16[2304,256]{1,0:T(8,128)(2,1)S(1)}, u32[]{:S(2)}, u32[]{:S(2)}) collective-permute-start(bf16[2304,256]{1,0:T(8,128)(2,1)S(1)} %get-tuple-element.99.refs_3_), channel_id=1, source_target_pairs={{0,8},{8,0},{16,24},{24,16},{1,9},{9,1},{17,25},{25,17},{2,10},{10... | collective-permute-start | bytes 3538952 | tf_op jit(solution)/shard_map/ppermute | solution.py:50
  51.3 15.5 %collective-permute-start.18 = (bf16[2,512,256]{2,1,0:T(8,128)(2,1)S(1)}, bf16[2,512,256]{2,1,0:T(8,128)(2,1)S(1)}, u32[]{:S(2)}, u32[]{:S(2)}) collective-permute-start(bf16[2,512,256]{2,1,0:T(8,128)(2,1)S(1)} %get-tuple-element.103), channel_id=1, source_target_pairs={{0,16},{8,24},{16,0},{24,8},{1,17},{9,25},{17,1},{25,9},{2,18},{10... | collective-permute-start | bytes 1572872 | tf_op jit(solution)/shard_map/ppermute | solution.py:50
  55.6 14.2 %collective-permute-start.20 = (bf16[2,256,512]{2,1,0:T(8,128)(2,1)S(1)}, bf16[2,256,512]{2,1,0:T(8,128)(2,1)S(1)}, u32[]{:S(2)}, u32[]{:S(2)}) collective-permute-start(bf16[2,256,512]{2,1,0:T(8,128)(2,1)S(1)} %get-tuple-element.110), channel_id=1, source_target_pairs={{0,32},{32,0},{64,96},{96,64},{1,33},{33,1},{65,97},{97,65},{2,34}... | collective-permute-start | bytes 1572872 | tf_op jit(solution)/shard_map/ppermute | solution.py:58
  57.1 14.6 %collective-permute-start.21 = (bf16[2,256,512]{2,1,0:T(8,128)(2,1)S(1)}, bf16[2,256,512]{2,1,0:T(8,128)(2,1)S(1)}, u32[]{:S(2)}, u32[]{:S(2)}) collective-permute-start(bf16[2,256,512]{2,1,0:T(8,128)(2,1)S(1)} %get-tuple-element.111), channel_id=1, source_target_pairs={{0,96},{32,64},{64,32},{96,0},{1,97},{33,65},{65,33},{97,1},{2,98}... | collective-permute-start | bytes 1572872 | tf_op jit(solution)/shard_map/ppermute | solution.py:58
  66.8 1.6 %collective-permute-start.19 = (bf16[1,512,256]{2,1,0:T(8,128)(2,1)S(1)}, bf16[1,512,256]{2,1,0:T(8,128)(2,1)S(1)}, u32[]{:S(2)}, u32[]{:S(2)}) collective-permute-start(bf16[1,512,256]{2,1,0:T(8,128)(2,1)S(1)} %slice.27), channel_id=1, source_target_pairs={{0,8},{8,0},{16,24},{24,16},{1,9},{9,1},{17,25},{25,17},{2,10},{10... | collective-permute-start | bytes 786440 | tf_op jit(solution)/shard_map/ppermute | solution.py:50
  71.9 8.2 %collective-permute-start.22 = (bf16[256,512]{1,0:T(8,128)(2,1)S(1)}, bf16[256,512]{1,0:T(8,128)(2,1)S(1)}, u32[]{:S(2)}, u32[]{:S(2)}) collective-permute-start(bf16[256,512]{1,0:T(8,128)(2,1)S(1)} %get-tuple-element.116), channel_id=1, source_target_pairs={{0,96},{32,64},{64,32},{96,0},{1,97},{33,65},{65,33},{97,1},{2,98}... | collective-permute-start | bytes 786440 | tf_op jit(solution)/shard_map/ppermute | solution.py:58
  74.1 6.7 %collective-permute-start.23 = (bf16[256,512]{1,0:T(8,128)(2,1)S(1)}, bf16[256,512]{1,0:T(8,128)(2,1)S(1)}, u32[]{:S(2)}, u32[]{:S(2)}) collective-permute-start(bf16[256,512]{1,0:T(8,128)(2,1)S(1)} %get-tuple-element.117), channel_id=1, source_target_pairs={{0,32},{32,0},{64,96},{96,64},{1,33},{33,1},{65,97},{97,65},{2,34}... | collective-permute-start | bytes 786440 | tf_op jit(solution)/shard_map/ppermute | solution.py:58
  74.1 12.4 %collective-permute-start.24 = (bf16[2,512,256]{2,1,0:T(8,128)(2,1)S(1)}, bf16[2,512,256]{2,1,0:T(8,128)(2,1)S(1)}, u32[]{:S(2)}, u32[]{:S(2)}) collective-permute-start(bf16[2,512,256]{2,1,0:T(8,128)(2,1)S(1)} %get-tuple-element.124), channel_id=1, source_target_pairs={{0,2},{1,3},{2,0},{3,1},{4,6},{5,7},{6,4},{7,5},{8,10},{9,11},{10,... | collective-permute-start | bytes 1572872 | tf_op jit(solution)/shard_map/ppermute | solution.py:62
  75.5 13.7 %collective-permute-start.25 = (bf16[2,512,256]{2,1,0:T(8,128)(2,1)S(1)}, bf16[2,512,256]{2,1,0:T(8,128)(2,1)S(1)}, u32[]{:S(2)}, u32[]{:S(2)}) collective-permute-start(bf16[2,512,256]{2,1,0:T(8,128)(2,1)S(1)} %get-tuple-element.125), channel_id=1, source_target_pairs={{0,6},{1,7},{2,4},{3,5},{4,2},{5,3},{6,0},{7,1},{8,14},{9,15},{10,... | collective-permute-start | bytes 1572872 | tf_op jit(solution)/shard_map/ppermute | solution.py:62
  81.0 17.9 %collective-permute-start.30 = (bf16[640,512]{1,0:T(8,128)(2,1)S(1)}, bf16[640,512]{1,0:T(8,128)(2,1)S(1)}, u32[]{:S(2)}, u32[]{:S(2)}) collective-permute-start(bf16[640,512]{1,0:T(8,128)(2,1)S(1)} %get-tuple-element.136), channel_id=1, source_target_pairs={{0,16},{8,24},{16,0},{24,8},{1,17},{9,25},{17,1},{25,9},{2,18},{10... | collective-permute-start | bytes 1966088 | tf_op jit(solution)/shard_map/ppermute | solution.py:50
  83.8 11.6 %collective-permute-start.26 = (bf16[2,256,512]{2,1,0:T(8,128)(2,1)S(1)}, bf16[2,256,512]{2,1,0:T(8,128)(2,1)S(1)}, u32[]{:S(2)}, u32[]{:S(2)}) collective-permute-start(bf16[2,256,512]{2,1,0:T(8,128)(2,1)S(1)} %get-tuple-element.129), channel_id=1, source_target_pairs={{0,32},{32,0},{64,96},{96,64},{1,33},{33,1},{65,97},{97,65},{2,34}... | collective-permute-start | bytes 1572872 | tf_op jit(solution)/shard_map/ppermute | solution.py:58
  84.1 12.8 %collective-permute-start.27 = (bf16[2,256,512]{2,1,0:T(8,128)(2,1)S(1)}, bf16[2,256,512]{2,1,0:T(8,128)(2,1)S(1)}, u32[]{:S(2)}, u32[]{:S(2)}) collective-permute-start(bf16[2,256,512]{2,1,0:T(8,128)(2,1)S(1)} %get-tuple-element.130), channel_id=1, source_target_pairs={{0,96},{32,64},{64,32},{96,0},{1,97},{33,65},{65,33},{97,1},{2,98}... | collective-permute-start | bytes 1572872 | tf_op jit(solution)/shard_map/ppermute | solution.py:58
  89.3 9.5 %collective-permute-start.28 = (bf16[512,256]{1,0:T(8,128)(2,1)S(1)}, bf16[512,256]{1,0:T(8,128)(2,1)S(1)}, u32[]{:S(2)}, u32[]{:S(2)}) collective-permute-start(bf16[512,256]{1,0:T(8,128)(2,1)S(1)} %get-tuple-element.134), channel_id=1, source_target_pairs={{0,6},{1,7},{2,4},{3,5},{4,2},{5,3},{6,0},{7,1},{8,14},{9,15},{10,... | collective-permute-start | bytes 786440 | tf_op jit(solution)/shard_map/ppermute | solution.py:62
  91.5 7.3 %collective-permute-start.29 = (bf16[512,256]{1,0:T(8,128)(2,1)S(1)}, bf16[512,256]{1,0:T(8,128)(2,1)S(1)}, u32[]{:S(2)}, u32[]{:S(2)}) collective-permute-start(bf16[512,256]{1,0:T(8,128)(2,1)S(1)} %get-tuple-element.135), channel_id=1, source_target_pairs={{0,2},{1,3},{2,0},{3,1},{4,6},{5,7},{6,4},{7,5},{8,10},{9,11},{10,... | collective-permute-start | bytes 786440 | tf_op jit(solution)/shard_map/ppermute | solution.py:62
  97.1 7.7 %collective-permute-start.31 = (bf16[256,512]{1,0:T(8,128)(2,1)S(1)}, bf16[256,512]{1,0:T(8,128)(2,1)S(1)}, u32[]{:S(2)}, u32[]{:S(2)}) collective-permute-start(bf16[256,512]{1,0:T(8,128)(2,1)S(1)} %get-tuple-element.140), channel_id=1, source_target_pairs={{0,96},{32,64},{64,32},{96,0},{1,97},{33,65},{65,33},{97,1},{2,98}... | collective-permute-start | bytes 786440 | tf_op jit(solution)/shard_map/ppermute | solution.py:58
  98.6 6.4 %collective-permute-start.32 = (bf16[256,512]{1,0:T(8,128)(2,1)S(1)}, bf16[256,512]{1,0:T(8,128)(2,1)S(1)}, u32[]{:S(2)}, u32[]{:S(2)}) collective-permute-start(bf16[256,512]{1,0:T(8,128)(2,1)S(1)} %get-tuple-element.141), channel_id=1, source_target_pairs={{0,32},{32,0},{64,96},{96,64},{1,33},{33,1},{65,97},{97,65},{2,34}... | collective-permute-start | bytes 786440 | tf_op jit(solution)/shard_map/ppermute | solution.py:58
  98.9 7.2 %collective-permute-start.33 = (bf16[512,256]{1,0:T(8,128)(2,1)S(1)}, bf16[512,256]{1,0:T(8,128)(2,1)S(1)}, u32[]{:S(2)}, u32[]{:S(2)}) collective-permute-start(bf16[512,256]{1,0:T(8,128)(2,1)S(1)} %get-tuple-element.146), channel_id=1, source_target_pairs={{0,1},{1,0},{2,3},{3,2},{4,5},{5,4},{6,7},{7,6},{8,9},{9,8},{10,11... | collective-permute-start | bytes 786440 | tf_op jit(solution)/shard_map/ppermute | solution.py:54

commit v5 on v4

--- a/solution.py
+++ b/solution.py
@@ -94,12 +94,16 @@
 def join_z_body(idx, z0, z1, z2, z3, zb):
     for m, z in enumerate((z0, z1, z2, z3)):
         zb[256 * m : 256 * m + 256] = z[...]
-    zb[1024:] = jnp.zeros((32, 256), BF)
+    zb[1024:] = jnp.zeros((16, 256), BF)
+
+
+def weight_at(idx, m, b, which):
+    base = (idx[Z] ^ m) * 1024 + (idx[YL] ^ b) * 512 + which * 256
+    return pl.ds(pl.multiple_of(base, 256), 256)
 
 
 def weight_rows(w, idx, m, b, which):
-    base = (idx[Z] ^ m) * 1024 + (idx[YL] ^ b) * 512 + which * 256
-    return w[idx[H], pl.ds(pl.multiple_of(base, 256), 256)]
+    return w[idx[H], weight_at(idx, m, b, which)]
 
 
 def product(idx, w, terms):
@@ -132,24 +136,28 @@
         acc[:, at] = acc_in[:, at] + product(idx, w, terms)
 
 
-def project_last_body(idx, wk, wv, acc, by20, by21, az20, az21, qg_own, qg_far, es_in, send, keep, es, total):
-    c = idx[C]
-    by2 = [by20[:256], by20[256:512], by21[:256], by21[256:512]]
-    for n, w in enumerate((wk, wv)):
-        at = slice(n * 512, n * 512 + 512)
-        total[:, at] = acc[:, at] + product(idx, w, [(az20[0], 2, 0, c), (az21[0], 2, 1, c)])
-        total[256:, at] += product(idx, w, [(by2[m], m, 0, 1 - c) for m in range(4)])
-    for out, which in ((keep, c), (send, 1 - c)):
-        out[:512, :256] = total[:, cols(which)].astype(BF)
-        out[:512, 256:] = total[:, cols(2 + which)].astype(BF)
+def project_last_body(idx, wk, wv, acc, by20, by21, az20, az21, qg_own, qg_far, send, keep):
+    h, c = idx[H], idx[C]
+    across = jnp.concatenate([az20[0], az21[0]], axis=1)
+    late = jnp.concatenate([by20[:256], by20[256:512], by21[:256], by21[256:512]], axis=1)
+    for out, head in ((send, 1 - c), (keep, c)):
+        for n, w in enumerate((wk, wv)):
+            rows = [weight_at(idx, 2, b, c) for b in range(2)]
+            right = jnp.concatenate([w[h, at, cols(head)] for at in rows], axis=0)
+            part = acc[:, cols(2 * n + head)] + jnp.dot(across, right, preferred_element_type=F32)
+            rows = [weight_at(idx, m, 0, 1 - c) for m in range(4)]
+            right = jnp.concatenate([w[h, at, cols(head)] for at in rows], axis=0)
+            more = jnp.dot(late, right, preferred_element_type=F32)
+            out[:256, 256 * n : 256 * n + 256] = part[:256].astype(BF)
+            out[256:512, 256 * n : 256 * n + 256] = (part[256:] + more).astype(BF)
     for i, qg in enumerate((qg_own, qg_far)):
         for n in range(2):
             send[512 + 128 * i : 640 + 128 * i, 256 * n : 256 * n + 256] = qg[n, :, cols(1 - c)]
+
+
+def turn_keep_body(idx, ya, az1, az20, az21, az3, by20, by21, es_in, out, es):
     es[2048:2560] = by20[:512]
     es[2560:3072] = by21[:512]
-
-
-def turn_keep_body(idx, ya, az1, az20, az21, az3, out):
     for r, block in enumerate(
         (ya[0], ya[1], az1[0], az1[1], az20[0], az21[0], az3[0], az3[1])
     ):
@@ -163,17 +171,17 @@
             out[2 * m + b, :, 256:] = block(es, 8 + 4 * b + m).T
 
 
-def attend_body(idx, kv_own, kv_oth, qg_own, qg_far, g, g_far, gq_own, gq_far, acc):
+def attend_body(idx, kv_own, kv_oth, qg_own, qg_far, g, g_far, gq_own, gq_far, ds_all, low_all):
     mine = cols(idx[C])
     scale = DH ** (-0.5)
-    acc[...] = jnp.zeros_like(acc)
     blocks = [
         (qg_own[0, :, mine], qg_own[1, :, mine], gq_own),
         (kv_oth[512:640, :256], kv_oth[512:640, 256:], g.at[2048:2176]),
         (qg_far[0, :, mine], qg_far[1, :, mine], gq_far),
         (kv_oth[640:, :256], kv_oth[640:, 256:], g.at[2176:]),
     ]
-    for q, gc, gq in blocks:
+    for n, (q, gc, _) in enumerate(blocks):
+        at = slice(128 * n, 128 * n + 128)
         s = [
             lax.dot_general(kv[:512, :256], q, NT, preferred_element_type=F32) * scale
             for kv in (kv_own, kv_oth)
@@ -192,19 +200,26 @@
         delta = jnp.sum(p[0] * dp[0], axis=0, keepdims=True) + jnp.sum(
             p[1] * dp[1], axis=0, keepdims=True
         )
-        ds = [(a * (b - delta) * scale).astype(BF) for a, b in zip(p, dp)]
-        low = [a.astype(BF) for a in p]
-        total_q = jnp.zeros((128, 256), F32)
-        for part, kv in enumerate((kv_own, kv_oth)):
-            rows = slice(part * 512, part * 512 + 512)
-            acc[0, rows] += jnp.dot(ds[part], q, preferred_element_type=F32).astype(BF).astype(F32)
-            acc[1, rows] += jnp.dot(low[part], gc, preferred_element_type=F32).astype(BF).astype(F32)
-            total_q += lax.dot_general(ds[part], kv[:512, :256], TN, preferred_element_type=F32)
-        gq[...] = total_q.astype(BF)
-    for n in range(2):
-        g[n * 1024 : n * 1024 + 1024] = acc[n].astype(BF)
-        g_far[0, n * 256 : n * 256 + 256] = acc[n, 256:512].astype(BF)
-        g_far[1, n * 256 : n * 256 + 256] = acc[n, 768:].astype(BF)
+        for part in range(2):
+            rows = slice(512 * part, 512 * part + 512)
+            ds_all[rows, at] = (p[part] * (dp[part] - delta) * scale).astype(BF)
+            low_all[rows, at] = p[part].astype(BF)
+    keys_t = jnp.concatenate([kv_own[:, :256].T, kv_oth[:512, :256].T], axis=1)
+    gq_t = jnp.dot(keys_t, ds_all[...], preferred_element_type=F32)
+    for n, (_, _, out) in enumerate(blocks):
+        out[...] = gq_t[:, 128 * n : 128 * n + 128].T.astype(BF)
+    for chunk in range(4):
+        rows = slice(256 * chunk, 256 * chunk + 256)
+        for kind, source in enumerate((ds_all, low_all)):
+            total = None
+            for n, pair in enumerate(blocks):
+                left = source[rows, 128 * n : 128 * n + 128]
+                part = jnp.dot(left, pair[kind], preferred_element_type=F32).astype(BF).astype(F32)
+                total = part if total is None else total + part
+            low = total.astype(BF)
+            g[1024 * kind + 256 * chunk : 1024 * kind + 256 * chunk + 256] = low
+            if chunk % 2 == 1:
+                g_far[chunk // 2, 256 * kind : 256 * kind + 256] = low
 
 
 def weight_job(idx, keep_t, oth_t, g, gp, n, dp_to, parity, out):
@@ -347,7 +362,7 @@
     other = lax.dynamic_index_in_dim(halves, 1 - c, 0, keepdims=False)
     from_y = [mine] + [swap_y(mine, m) for m in (1, 2, 3)]
     from_z = [other] + [swap_z(other, m) for m in (1, 2, 3)]
-    idx, zb = call(join_z_body, "join_z", [idx, *from_z], [arr((1056, 256))])
+    idx, zb = call(join_z_body, "join_z", [idx, *from_z], [arr((1040, 256))])
     idx, ya, qg0, qg_send = call(
         join_y_body, "join_y", [idx, *from_y, queries, grad_context],
         [arr((2, 512, 256)), qg_block, qg_block], [dma((2, 2))], hbm=(4, 5), flops=30_000_000_000,
@@ -366,14 +381,14 @@
     idx, acc = call(
         project_next_body, "project_next", [idx, *ws, acc, az1, az3], [arr((512, 1024), F32)]
     )
-    idx, kv_send, kv_own, es = call(
-        project_last_body, "project_last", [idx, *ws, acc, by20, by21, az20, az21, qg0, qg2, es],
-        [arr((768, 512)), arr((512, 512)), arr((4096, 256))], [pltpu.VMEM((512, 1024), F32)],
-        alias={10: 3},
+    idx, kv_send, kv_own = call(
+        project_last_body, "project_last", [idx, *ws, acc, by20, by21, az20, az21, qg0, qg2],
+        [arr((768, 512)), arr((512, 512))],
     )
     kv_oth = swap_seq(kv_send, 1)
-    idx, keep_t = call(
-        turn_keep_body, "turn_keep", [idx, ya, az1, az20, az21, az3], [arr((8, 256, 512))]
+    idx, keep_t, es = call(
+        turn_keep_body, "turn_keep", [idx, ya, az1, az20, az21, az3, by20, by21, es],
+        [arr((8, 256, 512)), arr((4096, 256))], alias={8: 2},
     )
     idx, es = call(relay_body, "relay_rows", [idx, es, kv_oth], [arr((4096, 256))], alias={1: 1})
     es_oth = swap_seq(es, 1)
@@ -381,7 +396,7 @@
     idx, g, g_far, gq_own, gq_far = call(
         attend_body, "attend", [idx, kv_own, kv_oth, qg0, qg2],
         [arr((2304, 256)), arr((2, 512, 256)), arr((128, 256)), arr((128, 256))],
-        [pltpu.VMEM((2, 1024, 256), F32)],
+        [pltpu.VMEM((1024, 512), BF)] * 2,
     )
     gp = swap_seq(g, 1)
     far = swap_seq(g_far, 2)

time: 107 us -> 107 us (level)
  transfers between devices with their start and end apart: 34 -> 34, of which waited for: 19 -> 20; matrix products, arithmetic and copies ran while one was open for 0% -> 0% of each run, Pallas kernels for 20% -> 20%
where the time goes in v5:
time: 107 us
  starting transfers between devices  45.4 us (42%)
  waiting for transfers between devices  35.6 us (33%)
  Pallas kernels  23.7 us (22%)
  local copies, waits for them, and re-layouts  1.1 us (1%)
    pallas_call x22, Pallas kernels, call(): pl.pallas_call(wrapped, in_specs=specs, out_specs=[ANY] + [VMEM] * len(ou...  23.7 us
    ppermute x11, starting transfers between devices, swap_z(): return lax.ppermute(x, 'tensor', [(t, t ^ 2 * m) for t in range(8)])  15.9 us
    ppermute x8, waiting for transfers between devices, swap_x(): return lax.ppermute(x, 'dp', [(d, d ^ m) for d in range(4)])  14.1 us
    ppermute x7, starting transfers between devices, swap_y(): return lax.ppermute(x, ('seq', 'tensor'), pairs)  11.5 us
    ppermute x8, starting transfers between devices, swap_x(): return lax.ppermute(x, 'dp', [(d, d ^ m) for d in range(4)])  9.12 us
    ppermute x7, waiting for transfers between devices, swap_seq(): return lax.ppermute(x, 'seq', [(s, s ^ m) for s in range(4)])  8.04 us
    ppermute x7, starting transfers between devices, swap_seq(): return lax.ppermute(x, 'seq', [(s, s ^ m) for s in range(4)])  7.52 us
    ppermute x7, waiting for transfers between devices, swap_y(): return lax.ppermute(x, ('seq', 'tensor'), pairs)  7.17 us
  transfers between devices with their start and end apart: 34, of which 20 were waited for; matrix products, arithmetic and copies ran while one was open for 0% of the time, Pallas kernels for 20%

profile of v5, /device:TPU:0, one launch (start us, length us, event | category | flops | bytes accessed | tf_op | source)
XLA Modules:
  0.0 106.8 jit_solution(9434096072551028905)
XLA Ops:
  0.6 1.0 fusion.4
  1.8 4.2 %collective-permute-start.2 = (bf16[256,256]{1,0:T(8,128)(2,1)S(1)}, bf16[256,256]{1,0:T(8,128)(2,1)S(1)}, u32[]{:S(2)}, u32[]{:S(2)}) collective-permute-start(bf16[256,256]{1,0:T(8,128)(2,1)S(1)} %get-tuple-element.151.refs_1_), channel_id=1, source_target_pairs={{0,6},{1,7},{2,4},{3,5},{4,2},{5,3},{6,0},{7,1},{8,14},{9,15},{10,... | collective-permute-start | bytes 393224 | tf_op jit(solution)/shard_map/ppermute | solution.py:62
  6.0 0.9 collective-permute-start
  6.9 3.0 %collective-permute-start.5 = (bf16[256,256]{1,0:T(8,128)(2,1)S(1)}, bf16[256,256]{1,0:T(8,128)(2,1)S(1)}, u32[]{:S(2)}, u32[]{:S(2)}) collective-permute-start(bf16[256,256]{1,0:T(8,128)(2,1)S(1)} %get-tuple-element.150.refs_1_), channel_id=1, source_target_pairs={{0,17},{1,16},{2,19},{3,18},{4,21},{5,20},{6,23},{7,22},{8,25},{9,... | collective-permute-start | bytes 393224 | tf_op jit(solution)/shard_map/ppermute | solution.py:71
  10.5 1.0 collective-permute-done.2.refs_4_
  11.5 1.6 %collective-permute-start.3 = (bf16[256,256]{1,0:T(8,128)(2,1)S(1)}, bf16[256,256]{1,0:T(8,128)(2,1)S(1)}, u32[]{:S(2)}, u32[]{:S(2)}) collective-permute-start(bf16[256,256]{1,0:T(8,128)(2,1)S(1)} %get-tuple-element.150.refs_1_), channel_id=1, source_target_pairs={{0,1},{1,0},{2,3},{3,2},{4,5},{5,4},{6,7},{7,6},{8,9},{9,8},{10,11... | collective-permute-start | bytes 393224 | tf_op jit(solution)/shard_map/ppermute | solution.py:71
  13.9 3.1 %collective-permute-start.7 = (bf16[1040,256]{1,0:T(8,128)(2,1)S(1)}, bf16[1040,256]{1,0:T(8,128)(2,1)S(1)}, u32[]{:S(2)}, u32[]{:S(2)}) collective-permute-start(bf16[1040,256]{1,0:T(8,128)(2,1)S(1)} %get-tuple-element.80.refs_4_), channel_id=1, source_target_pairs={{0,17},{1,16},{2,19},{3,18},{4,21},{5,20},{6,23},{7,22},{8,25},{9,... | collective-permute-start | bytes 1597448 | tf_op jit(solution)/shard_map/ppermute | solution.py:71
  17.2 1.3 %join_y.1 = (s32[8,128]{1,0:T(8,128)S(1)}, bf16[2,512,256]{2,1,0:T(8,128)(2,1)S(1)}, bf16[2,128,512]{2,1,0:T(8,128)(2,1)S(1)}, bf16[2,128,512]{2,1,0:T(8,128)(2,1)S(1)}) custom-call(s32[8,128]{1,0:T(8,128)S(1)} %get-tuple-element.77.refs_0_, bf16[256,256]{1,0:T(8,128)(2,1)S(1)} %get-tuple-element.150.refs_1_, ...), custom_call_target="tpu_custom_call", output_to_operand_aliasing={{0}: (0, {})} | custom-call | flops 30000001024 | bytes 1 | tf_op jit(solution)/shard_map/join_y/pallas_call | solution.py:36
  18.5 3.2 %collective-permute-start.9 = (bf16[2,512,256]{2,1,0:T(8,128)(2,1)S(1)}, bf16[2,512,256]{2,1,0:T(8,128)(2,1)S(1)}, u32[]{:S(2)}, u32[]{:S(2)}) collective-permute-start(bf16[2,512,256]{2,1,0:T(8,128)(2,1)S(1)} %get-tuple-element.79.refs_3_.refs_1_), channel_id=1, source_target_pairs={{0,6},{1,7},{2,4},{3,5},{4,2},{5,3},{6,0},{7,1},{8,14},{9,15},{10,... | collective-permute-start | bytes 1572872 | tf_op jit(solution)/shard_map/ppermute | solution.py:62
  22.0 5.9 %collective-permute-done.7.refs_6_ = bf16[1040,256]{1,0:T(8,128)(2,1)S(1)} collective-permute-done((bf16[1040,256]{1,0:T(8,128)(2,1)S(1)}, bf16[1040,256]{1,0:T(8,128)(2,1)S(1)}, u32[]{:S(2)}, u32[]{:S(2)}) %collective-permute-start.7) | collective-permute-done | bytes 532512 | tf_op jit(solution)/shard_map/ppermute | solution.py:71
  28.1 1.1 %collective-permute-done.6.refs_5_ = bf16[1040,256]{1,0:T(8,128)(2,1)S(1)} collective-permute-done((bf16[1040,256]{1,0:T(8,128)(2,1)S(1)}, bf16[1040,256]{1,0:T(8,128)(2,1)S(1)}, u32[]{:S(2)}, u32[]{:S(2)}) %collective-permute-start.6) | collective-permute-done | bytes 532512 | tf_op jit(solution)/shard_map/ppermute | solution.py:71
  29.2 2.9 %collective-permute-start.10 = (bf16[528,256]{1,0:T(8,128)(2,1)S(1)}, bf16[528,256]{1,0:T(8,128)(2,1)S(1)}, u32[]{:S(2)}, u32[]{:S(2)}) collective-permute-start(bf16[528,256]{1,0:T(8,128)(2,1)S(1)} %slice.28), channel_id=1, source_target_pairs={{0,17},{1,16},{2,19},{3,18},{4,21},{5,20},{6,23},{7,22},{8,25},{9,... | collective-permute-start | bytes 811016 | tf_op jit(solution)/shard_map/ppermute | solution.py:71
  32.1 0.9 collective-permute-start.14
  33.0 0.8 collective-permute-start.13
  33.8 0.8 collective-permute-done.8.refs_4_.refs_2_
  34.7 1.3 %collective-permute-start.12 = (bf16[1,512,256]{2,1,0:T(8,128)(2,1)S(1)}, bf16[1,512,256]{2,1,0:T(8,128)(2,1)S(1)}, u32[]{:S(2)}, u32[]{:S(2)}) collective-permute-start(bf16[1,512,256]{2,1,0:T(8,128)(2,1)S(1)} %slice.30), channel_id=1, source_target_pairs={{0,6},{1,7},{2,4},{3,5},{4,2},{5,3},{6,0},{7,1},{8,14},{9,15},{10,... | collective-permute-start | bytes 786440 | tf_op jit(solution)/shard_map/ppermute | solution.py:62
  36.0 2.3 %project_first.1 = (s32[8,128]{1,0:T(8,128)S(1)}, f32[512,1024]{1,0:T(8,128)S(1)}, bf16[4096,256]{1,0:T(8,128)(2,1)S(1)}) custom-call(s32[8,128]{1,0:T(8,128)S(1)} %get-tuple-element.78.refs_0_, bf16[2,4096,512]{2,1,0:T(8,128)(2,1)S(1)} %bitcast.5, bf16[2,4096,512]{2,1,0:T(8,128)(2,1)S(1)} %bitcast.7, ...), custom_call_target="tpu_custom_call", output_to_operand_aliasing={{0}: (0, {})} | custom-call | flops 1 | bytes 1 | tf_op jit(solution)/shard_map/project_first/pallas_call | solution.py:36
  38.4 1.3 %project_next.1 = (s32[8,128]{1,0:T(8,128)S(1)}, f32[512,1024]{1,0:T(8,128)S(1)}) custom-call(s32[8,128]{1,0:T(8,128)S(1)} %get-tuple-element.81.refs_0_, bf16[2,4096,512]{2,1,0:T(8,128)(2,1)S(1)} %bitcast.5, bf16[2,4096,512]{2,1,0:T(8,128)(2,1)S(1)} %bitcast.7, f32[512,1024]{1,0:T(8,128)S(1)} %get-tuple-element.82.refs_3_, ...), custom_call_target="tpu_custom_call", output_to_operand_aliasing={{0}: (0, {})} | custom-call | flops 1 | bytes 1 | tf_op jit(solution)/shard_map/project_next/pallas_call | solution.py:36
  39.7 2.5 %collective-permute-done.14.refs_9_.refs_4_ = bf16[2,128,512]{2,1,0:T(8,128)(2,1)S(1)} collective-permute-done((bf16[2,128,512]{2,1,0:T(8,128)(2,1)S(1)}, bf16[2,128,512]{2,1,0:T(8,128)(2,1)S(1)}, u32[]{:S(2)}, u32[]{:S(2)}) %collective-permute-start.14) | collective-permute-done | bytes 262176 | tf_op jit(solution)/shard_map/ppermute | solution.py:50
  42.5 1.3 %project_last.1 = (s32[8,128]{1,0:T(8,128)S(1)}, bf16[768,512]{1,0:T(8,128)(2,1)S(1)}, bf16[512,512]{1,0:T(8,128)(2,1)S(1)}) custom-call(s32[8,128]{1,0:T(8,128)S(1)} %get-tuple-element.83.refs_0_, bf16[2,4096,512]{2,1,0:T(8,128)(2,1)S(1)} %bitcast.5, bf16[2,4096,512]{2,1,0:T(8,128)(2,1)S(1)} %bitcast.7, ...), custom_call_target="tpu_custom_call", output_to_operand_aliasing={{0}: (0, {})} | custom-call | flops 1 | bytes 1 | tf_op jit(solution)/shard_map/project_last/pallas_call | solution.py:36
  44.5 1.7 %collective-permute-done.15.refs_2_ = bf16[768,512]{1,0:T(8,128)(2,1)S(1)} collective-permute-done((bf16[768,512]{1,0:T(8,128)(2,1)S(1)}, bf16[768,512]{1,0:T(8,128)(2,1)S(1)}, u32[]{:S(2)}, u32[]{:S(2)}) %collective-permute-start.15) | collective-permute-done | bytes 786464 | tf_op jit(solution)/shard_map/ppermute | solution.py:50
  46.3 3.8 %attend.1 = (s32[8,128]{1,0:T(8,128)S(1)}, bf16[2304,256]{1,0:T(8,128)(2,1)S(1)}, bf16[2,512,256]{2,1,0:T(8,128)(2,1)S(1)}, bf16[128,256]{1,0:T(8,128)(2,1)S(1)}, bf16[128,256]{1,0:T(8,128)(2,1)S(1)}) custom-call(s32[8,128]{1,0:T(8,128)S(1)} %get-tuple-element.92.refs_0_, ...), custom_call_target="tpu_custom_call", output_to_operand_aliasing={{0}: (0, {})} | custom-call | flops 1 | bytes 1 | tf_op jit(solution)/shard_map/attend/pallas_call | solution.py:36
  50.7 2.8 %collective-permute-start.18 = (bf16[2,512,256]{2,1,0:T(8,128)(2,1)S(1)}, bf16[2,512,256]{2,1,0:T(8,128)(2,1)S(1)}, u32[]{:S(2)}, u32[]{:S(2)}) collective-permute-start(bf16[2,512,256]{2,1,0:T(8,128)(2,1)S(1)} %get-tuple-element.103), channel_id=1, source_target_pairs={{0,16},{8,24},{16,0},{24,8},{1,17},{9,25},{17,1},{25,9},{2,18},{10... | collective-permute-start | bytes 1572872 | tf_op jit(solution)/shard_map/ppermute | solution.py:50
  54.1 1.3 %weights_first.1 = (s32[8,128]{1,0:T(8,128)S(1)}, bf16[2,256,512]{2,1,0:T(8,128)(2,1)S(1)}, bf16[2,256,512]{2,1,0:T(8,128)(2,1)S(1)}) custom-call(s32[8,128]{1,0:T(8,128)S(1)} %get-tuple-element.96.refs_0_, bf16[8,256,512]{2,1,0:T(8,128)(2,1)S(1)} %get-tuple-element.97.refs_1_, ...), custom_call_target="tpu_custom_call", output_to_operand_aliasing={{0}: (0, {})} | custom-call | flops 1 | bytes 1 | tf_op jit(solution)/shard_map/weights_first/pallas_call | solution.py:36
  55.3 1.6 %collective-permute-start.20 = (bf16[2,256,512]{2,1,0:T(8,128)(2,1)S(1)}, bf16[2,256,512]{2,1,0:T(8,128)(2,1)S(1)}, u32[]{:S(2)}, u32[]{:S(2)}) collective-permute-start(bf16[2,256,512]{2,1,0:T(8,128)(2,1)S(1)} %get-tuple-element.110), channel_id=1, source_target_pairs={{0,32},{32,0},{64,96},{96,64},{1,33},{33,1},{65,97},{97,65},{2,34}... | collective-permute-start | bytes 1572872 | tf_op jit(solution)/shard_map/ppermute | solution.py:58
  56.9 2.1 %collective-permute-start.21 = (bf16[2,256,512]{2,1,0:T(8,128)(2,1)S(1)}, bf16[2,256,512]{2,1,0:T(8,128)(2,1)S(1)}, u32[]{:S(2)}, u32[]{:S(2)}) collective-permute-start(bf16[2,256,512]{2,1,0:T(8,128)(2,1)S(1)} %get-tuple-element.111), channel_id=1, source_target_pairs={{0,96},{32,64},{64,32},{96,0},{1,97},{33,65},{65,33},{97,1},{2,98}... | collective-permute-start | bytes 1572872 | tf_op jit(solution)/shard_map/ppermute | solution.py:58
  59.0 3.4 %weights_rest.1 = (s32[8,128]{1,0:T(8,128)S(1)}, bf16[2,256,512]{2,1,0:T(8,128)(2,1)S(1)}, bf16[2,256,512]{2,1,0:T(8,128)(2,1)S(1)}, f32[2,256,512]{2,1,0:T(8,12...) custom-call(s32[8,128]{1,0:T(8,128)S(1)} %get-tuple-element.100.refs, ...), custom_call_target="tpu_custom_call", output_to_operand_aliasing={{0}: (0, {})} | custom-call | flops 1 | bytes 1 | tf_op jit(solution)/shard_map/weights_rest/pallas_call | solution.py:36
  62.4 1.4 %encoder_own.1 = (s32[8,128]{1,0:T(8,128)S(1)}, f32[2,2,512,256]{3,2,1,0:T(8,128)S(1)}) custom-call(s32[8,128]{1,0:T(8,128)S(1)} %get-tuple-element.101.refs_0_, bf16[2,4096,512]{2,1,0:T(8,128)(2,1)S(1)} %bitcast.5, bf16[2,4096,512]{2,1,0:T(8,128)(2,1)S(1)} %bitcast.7, ...), custom_call_target="tpu_custom_call", output_to_operand_aliasing={{0}: (0, {})} | custom-call | flops 1 | bytes 1 | tf_op jit(solution)/shard_map/encoder_own/pallas_call | solution.py:36
  63.8 2.4 %collective-permute-done.18.refs_1_ = bf16[2,512,256]{2,1,0:T(8,128)(2,1)S(1)} collective-permute-done((bf16[2,512,256]{2,1,0:T(8,128)(2,1)S(1)}, bf16[2,512,256]{2,1,0:T(8,128)(2,1)S(1)}, u32[]{:S(2)}, u32[]{:S(2)}) %collective-permute-start.18) | collective-permute-done | bytes 524320 | tf_op jit(solution)/shard_map/ppermute | solution.py:50
  66.3 1.5 %collective-permute-done.19.refs_5_.refs_6_ = bf16[1,512,256]{2,1,0:T(8,128)(2,1)S(1)} collective-permute-done((bf16[1,512,256]{2,1,0:T(8,128)(2,1)S(1)}, bf16[1,512,256]{2,1,0:T(8,128)(2,1)S(1)}, u32[]{:S(2)}, u32[]{:S(2)}) %collective-permute-start.19) | collective-permute-done | bytes 262176 | tf_op jit(solution)/shard_map/ppermute | solution.py:50
  67.8 1.4 %encoder_sent.1 = (s32[8,128]{1,0:T(8,128)S(1)}, bf16[2,512,256]{2,1,0:T(8,128)(2,1)S(1)}, bf16[2,512,256]{2,1,0:T(8,128)(2,1)S(1)}) custom-call(s32[8,128]{1,0:T(8,128)S(1)} %get-tuple-element.104.refs_0_, bf16[2,4096,512]{2,1,0:T(8,128)(2,1)S(1)} %bitcast.5, bf16[2,4096,512]{2,1,0:T(8,128)(2,1)S(1)} %bitcast.7, ...), custom_call_target="tpu_custom_call", output_to_operand_aliasing={{0}: (0, {})} | custom-call | flops 1 | bytes 1 | tf_op jit(solution)/shard_map/encoder_sent/pallas_call | solution.py:36
  69.2 2.4 %collective-permute-done.21.refs_4_ = bf16[2,256,512]{2,1,0:T(8,128)(2,1)S(1)} collective-permute-done((bf16[2,256,512]{2,1,0:T(8,128)(2,1)S(1)}, bf16[2,256,512]{2,1,0:T(8,128)(2,1)S(1)}, u32[]{:S(2)}, u32[]{:S(2)}) %collective-permute-start.21) | collective-permute-done | bytes 524320 | tf_op jit(solution)/shard_map/ppermute | solution.py:58
  71.7 2.2 %collective-permute-start.22 = (bf16[256,512]{1,0:T(8,128)(2,1)S(1)}, bf16[256,512]{1,0:T(8,128)(2,1)S(1)}, u32[]{:S(2)}, u32[]{:S(2)}) collective-permute-start(bf16[256,512]{1,0:T(8,128)(2,1)S(1)} %get-tuple-element.116), channel_id=1, source_target_pairs={{0,96},{32,64},{64,32},{96,0},{1,97},{33,65},{65,33},{97,1},{2,98}... | collective-permute-start | bytes 786440 | tf_op jit(solution)/shard_map/ppermute | solution.py:58
  73.9 1.0 collective-permute-start.24
  74.9 1.9 %collective-permute-start.25 = (bf16[2,512,256]{2,1,0:T(8,128)(2,1)S(1)}, bf16[2,512,256]{2,1,0:T(8,128)(2,1)S(1)}, u32[]{:S(2)}, u32[]{:S(2)}) collective-permute-start(bf16[2,512,256]{2,1,0:T(8,128)(2,1)S(1)} %get-tuple-element.125), channel_id=1, source_target_pairs={{0,6},{1,7},{2,4},{3,5},{4,2},{5,3},{6,0},{7,1},{8,14},{9,15},{10,... | collective-permute-start | bytes 1572872 | tf_op jit(solution)/shard_map/ppermute | solution.py:62
  76.8 2.4 %encoder_kept.1 = (s32[8,128]{1,0:T(8,128)S(1)}, f32[2,512,256]{2,1,0:T(8,128)S(1)}, f32[2,512,256]{2,1,0:T(8,128)S(1)}) custom-call(s32[8,128]{1,0:T(8,128)S(1)} %get-tuple-element.112.refs_0_, bf16[2,4096,512]{2,1,0:T(8,128)(2,1)S(1)} %bitcast.5, bf16[2,4096,512]{2,1,0:T(8,128)(2,1)S(1)} %bitcast.7, ...), custom_call_target="tpu_custom_call", output_to_operand_aliasing={{0}: (0, {})} | custom-call | flops 1 | bytes 1 | tf_op jit(solution)/shard_map/encoder_kept/pallas_call | solution.py:36
  80.6 2.9 %collective-permute-start.30 = (bf16[640,512]{1,0:T(8,128)(2,1)S(1)}, bf16[640,512]{1,0:T(8,128)(2,1)S(1)}, u32[]{:S(2)}, u32[]{:S(2)}) collective-permute-start(bf16[640,512]{1,0:T(8,128)(2,1)S(1)} %get-tuple-element.136), channel_id=1, source_target_pairs={{0,16},{8,24},{16,0},{24,8},{1,17},{9,25},{17,1},{25,9},{2,18},{10... | collective-permute-start | bytes 1966088 | tf_op jit(solution)/shard_map/ppermute | solution.py:50
  83.9 1.2 %collective-permute-start.27 = (bf16[2,256,512]{2,1,0:T(8,128)(2,1)S(1)}, bf16[2,256,512]{2,1,0:T(8,128)(2,1)S(1)}, u32[]{:S(2)}, u32[]{:S(2)}) collective-permute-start(bf16[2,256,512]{2,1,0:T(8,128)(2,1)S(1)} %get-tuple-element.130), channel_id=1, source_target_pairs={{0,96},{32,64},{64,32},{96,0},{1,97},{33,65},{65,33},{97,1},{2,98}... | collective-permute-start | bytes 1572872 | tf_op jit(solution)/shard_map/ppermute | solution.py:58
  85.1 1.1 %collective-permute-done.24.refs_3_ = bf16[2,512,256]{2,1,0:T(8,128)(2,1)S(1)} collective-permute-done((bf16[2,512,256]{2,1,0:T(8,128)(2,1)S(1)}, bf16[2,512,256]{2,1,0:T(8,128)(2,1)S(1)}, u32[]{:S(2)}, u32[]{:S(2)}) %collective-permute-start.24) | collective-permute-done | bytes 524320 | tf_op jit(solution)/shard_map/ppermute | solution.py:62
  86.2 2.4 %collective-permute-done.25.refs_4_ = bf16[2,512,256]{2,1,0:T(8,128)(2,1)S(1)} collective-permute-done((bf16[2,512,256]{2,1,0:T(8,128)(2,1)S(1)}, bf16[2,512,256]{2,1,0:T(8,128)(2,1)S(1)}, u32[]{:S(2)}, u32[]{:S(2)}) %collective-permute-start.25) | collective-permute-done | bytes 524320 | tf_op jit(solution)/shard_map/ppermute | solution.py:62
  88.8 2.2 %collective-permute-start.28 = (bf16[512,256]{1,0:T(8,128)(2,1)S(1)}, bf16[512,256]{1,0:T(8,128)(2,1)S(1)}, u32[]{:S(2)}, u32[]{:S(2)}) collective-permute-start(bf16[512,256]{1,0:T(8,128)(2,1)S(1)} %get-tuple-element.134), channel_id=1, source_target_pairs={{0,6},{1,7},{2,4},{3,5},{4,2},{5,3},{6,0},{7,1},{8,14},{9,15},{10,... | collective-permute-start | bytes 786440 | tf_op jit(solution)/shard_map/ppermute | solution.py:62
  90.9 4.2 %collective-permute-done.26.refs_3_ = bf16[2,256,512]{2,1,0:T(8,128)(2,1)S(1)} collective-permute-done((bf16[2,256,512]{2,1,0:T(8,128)(2,1)S(1)}, bf16[2,256,512]{2,1,0:T(8,128)(2,1)S(1)}, u32[]{:S(2)}, u32[]{:S(2)}) %collective-permute-start.26) | collective-permute-done | bytes 524320 | tf_op jit(solution)/shard_map/ppermute | solution.py:58
  95.2 1.5 %collective-permute-done.27.refs_4_ = bf16[2,256,512]{2,1,0:T(8,128)(2,1)S(1)} collective-permute-done((bf16[2,256,512]{2,1,0:T(8,128)(2,1)S(1)}, bf16[2,256,512]{2,1,0:T(8,128)(2,1)S(1)}, u32[]{:S(2)}, u32[]{:S(2)}) %collective-permute-start.27) | collective-permute-done | bytes 524320 | tf_op jit(solution)/shard_map/ppermute | solution.py:58
  96.8 1.6 %collective-permute-start.31 = (bf16[256,512]{1,0:T(8,128)(2,1)S(1)}, bf16[256,512]{1,0:T(8,128)(2,1)S(1)}, u32[]{:S(2)}, u32[]{:S(2)}) collective-permute-start(bf16[256,512]{1,0:T(8,128)(2,1)S(1)} %get-tuple-element.140), channel_id=1, source_target_pairs={{0,96},{32,64},{64,32},{96,0},{1,97},{33,65},{65,33},{97,1},{2,98}... | collective-permute-start | bytes 786440 | tf_op jit(solution)/shard_map/ppermute | solution.py:58
  98.7 1.4 %collective-permute-start.33 = (bf16[512,256]{1,0:T(8,128)(2,1)S(1)}, bf16[512,256]{1,0:T(8,128)(2,1)S(1)}, u32[]{:S(2)}, u32[]{:S(2)}) collective-permute-start(bf16[512,256]{1,0:T(8,128)(2,1)S(1)} %get-tuple-element.146), channel_id=1, source_target_pairs={{0,1},{1,0},{2,3},{3,2},{4,5},{5,4},{6,7},{7,6},{8,9},{9,8},{10,11... | collective-permute-start | bytes 786440 | tf_op jit(solution)/shard_map/ppermute | solution.py:54
  100.1 4.4 %collective-permute-done.31.refs_3_ = bf16[256,512]{1,0:T(8,128)(2,1)S(1)} collective-permute-done((bf16[256,512]{1,0:T(8,128)(2,1)S(1)}, bf16[256,512]{1,0:T(8,128)(2,1)S(1)}, u32[]{:S(2)}, u32[]{:S(2)}) %collective-permute-start.31) | collective-permute-done | bytes 262176 | tf_op jit(solution)/shard_map/ppermute | solution.py:58
  104.8 1.2 %finish_weights.1 = (s32[8,128]{1,0:T(8,128)S(1)}, bf16[2,256,512]{2,1,0:T(8,128)(2,1)}, bf16[2,256,512]{2,1,0:T(8,128)(2,1)}, bf16[2,1,128,512]{3,2,1,0:T(8,128)(2,1)}) custom-call(s32[8,128]{1,0:T(8,128)S(1)} %get-tuple-element.137.refs_0_, f32[256,512]{1,0:T(8,128)S(1)} %get-tuple-element.138.refs_1_, ...), custom_call_target="tpu_custom_call", output_to_operand_aliasing={{0}: (0, {})} | custom-call | flops 1 | bytes 1 | tf_op jit(solution)/shard_map/finish_weights/pallas_call | solution.py:36
  105.9 0.8 finish_encoder.1
  (60 shorter events, 7.7 us)
Async XLA Ops:
  1.8 9.8 %collective-permute-start.2 = (bf16[256,256]{1,0:T(8,128)(2,1)S(1)}, bf16[256,256]{1,0:T(8,128)(2,1)S(1)}, u32[]{:S(2)}, u32[]{:S(2)}) collective-permute-start(bf16[256,256]{1,0:T(8,128)(2,1)S(1)} %get-tuple-element.151.refs_1_), channel_id=1, source_target_pairs={{0,6},{1,7},{2,4},{3,5},{4,2},{5,3},{6,0},{7,1},{8,14},{9,15},{10,... | collective-permute-start | bytes 393224 | tf_op jit(solution)/shard_map/ppermute | solution.py:62
  6.0 7.9 %collective-permute-start.1 = (bf16[256,256]{1,0:T(8,128)(2,1)S(1)}, bf16[256,256]{1,0:T(8,128)(2,1)S(1)}, u32[]{:S(2)}, u32[]{:S(2)}) collective-permute-start(bf16[256,256]{1,0:T(8,128)(2,1)S(1)} %get-tuple-element.151.refs_1_), channel_id=1, source_target_pairs={{0,4},{1,5},{2,6},{3,7},{4,0},{5,1},{6,2},{7,3},{8,12},{9,13},{10,... | collective-permute-start | bytes 393224 | tf_op jit(solution)/shard_map/ppermute | solution.py:62
  6.0 7.9 %collective-permute-start = (bf16[256,256]{1,0:T(8,128)(2,1)S(1)}, bf16[256,256]{1,0:T(8,128)(2,1)S(1)}, u32[]{:S(2)}, u32[]{:S(2)}) collective-permute-start(bf16[256,256]{1,0:T(8,128)(2,1)S(1)} %get-tuple-element.151.refs_1_), channel_id=1, source_target_pairs={{0,2},{1,3},{2,0},{3,1},{4,6},{5,7},{6,4},{7,5},{8,10},{9,11},{10,... | collective-permute-start | bytes 393224 | tf_op jit(solution)/shard_map/ppermute | solution.py:62
  6.9 10.2 %collective-permute-start.5 = (bf16[256,256]{1,0:T(8,128)(2,1)S(1)}, bf16[256,256]{1,0:T(8,128)(2,1)S(1)}, u32[]{:S(2)}, u32[]{:S(2)}) collective-permute-start(bf16[256,256]{1,0:T(8,128)(2,1)S(1)} %get-tuple-element.150.refs_1_), channel_id=1, source_target_pairs={{0,17},{1,16},{2,19},{3,18},{4,21},{5,20},{6,23},{7,22},{8,25},{9,... | collective-permute-start | bytes 393224 | tf_op jit(solution)/shard_map/ppermute | solution.py:71
  9.9 7.2 %collective-permute-start.4 = (bf16[256,256]{1,0:T(8,128)(2,1)S(1)}, bf16[256,256]{1,0:T(8,128)(2,1)S(1)}, u32[]{:S(2)}, u32[]{:S(2)}) collective-permute-start(bf16[256,256]{1,0:T(8,128)(2,1)S(1)} %get-tuple-element.150.refs_1_), channel_id=1, source_target_pairs={{0,16},{1,17},{2,18},{3,19},{4,20},{5,21},{6,22},{7,23},{8,24},{9,... | collective-permute-start | bytes 393224 | tf_op jit(solution)/shard_map/ppermute | solution.py:71
  11.5 5.6 %collective-permute-start.3 = (bf16[256,256]{1,0:T(8,128)(2,1)S(1)}, bf16[256,256]{1,0:T(8,128)(2,1)S(1)}, u32[]{:S(2)}, u32[]{:S(2)}) collective-permute-start(bf16[256,256]{1,0:T(8,128)(2,1)S(1)} %get-tuple-element.150.refs_1_), channel_id=1, source_target_pairs={{0,1},{1,0},{2,3},{3,2},{4,5},{5,4},{6,7},{7,6},{8,9},{9,8},{10,11... | collective-permute-start | bytes 393224 | tf_op jit(solution)/shard_map/ppermute | solution.py:71
  13.9 14.0 %collective-permute-start.7 = (bf16[1040,256]{1,0:T(8,128)(2,1)S(1)}, bf16[1040,256]{1,0:T(8,128)(2,1)S(1)}, u32[]{:S(2)}, u32[]{:S(2)}) collective-permute-start(bf16[1040,256]{1,0:T(8,128)(2,1)S(1)} %get-tuple-element.80.refs_4_), channel_id=1, source_target_pairs={{0,17},{1,16},{2,19},{3,18},{4,21},{5,20},{6,23},{7,22},{8,25},{9,... | collective-permute-start | bytes 1597448 | tf_op jit(solution)/shard_map/ppermute | solution.py:71
  17.0 12.2 %collective-permute-start.6 = (bf16[1040,256]{1,0:T(8,128)(2,1)S(1)}, bf16[1040,256]{1,0:T(8,128)(2,1)S(1)}, u32[]{:S(2)}, u32[]{:S(2)}) collective-permute-start(bf16[1040,256]{1,0:T(8,128)(2,1)S(1)} %get-tuple-element.80.refs_4_), channel_id=1, source_target_pairs={{0,1},{1,0},{2,3},{3,2},{4,5},{5,4},{6,7},{7,6},{8,9},{9,8},{10,11... | collective-permute-start | bytes 1597448 | tf_op jit(solution)/shard_map/ppermute | solution.py:71
  17.1 18.9 %slice-start = ((s8[8388608]{0:T(1024)(128)(4,1)}), s8[4194304]{0:T(1024)(128)(4,1)S(1)}, s32[]{:S(2)}) async-start(s8[8388608]{0:T(1024)(128)(4,1)} %bitcast.4), calls=%async_computation | async-start | bytes 8388608
  17.1 18.9 %slice-start.2 = ((s8[8388608]{0:T(1024)(128)(4,1)}), s8[4194304]{0:T(1024)(128)(4,1)S(1)}, s32[]{:S(2)}) async-start(s8[8388608]{0:T(1024)(128)(4,1)} %bitcast.6), calls=%async_computation.2 | async-start | bytes 8388608
  17.1 18.9 %slice-start.1 = ((s8[8388608]{0:T(1024)(128)(4,1)}), s8[4194304]{0:T(1024)(128)(4,1)S(1)}, s32[]{:S(2)}) async-start(s8[8388608]{0:T(1024)(128)(4,1)} %bitcast.4), calls=%async_computation.1 | async-start | bytes 8388608
  17.1 18.9 %slice-start.3 = ((s8[8388608]{0:T(1024)(128)(4,1)}), s8[4194304]{0:T(1024)(128)(4,1)S(1)}, s32[]{:S(2)}) async-start(s8[8388608]{0:T(1024)(128)(4,1)} %bitcast.6), calls=%async_computation.3 | async-start | bytes 8388608
  18.5 14.5 %collective-permute-start.9 = (bf16[2,512,256]{2,1,0:T(8,128)(2,1)S(1)}, bf16[2,512,256]{2,1,0:T(8,128)(2,1)S(1)}, u32[]{:S(2)}, u32[]{:S(2)}) collective-permute-start(bf16[2,512,256]{2,1,0:T(8,128)(2,1)S(1)} %get-tuple-element.79.refs_3_.refs_1_), channel_id=1, source_target_pairs={{0,6},{1,7},{2,4},{3,5},{4,2},{5,3},{6,0},{7,1},{8,14},{9,15},{10,... | collective-permute-start | bytes 1572872 | tf_op jit(solution)/shard_map/ppermute | solution.py:62
  21.6 13.0 %collective-permute-start.8 = (bf16[2,512,256]{2,1,0:T(8,128)(2,1)S(1)}, bf16[2,512,256]{2,1,0:T(8,128)(2,1)S(1)}, u32[]{:S(2)}, u32[]{:S(2)}) collective-permute-start(bf16[2,512,256]{2,1,0:T(8,128)(2,1)S(1)} %get-tuple-element.79.refs_3_.refs_1_), channel_id=1, source_target_pairs={{0,2},{1,3},{2,0},{3,1},{4,6},{5,7},{6,4},{7,5},{8,10},{9,11},{10,... | collective-permute-start | bytes 1572872 | tf_op jit(solution)/shard_map/ppermute | solution.py:62
  27.9 14.4 %collective-permute-start.11 = (bf16[528,256]{1,0:T(8,128)(2,1)S(1)}, bf16[528,256]{1,0:T(8,128)(2,1)S(1)}, u32[]{:S(2)}, u32[]{:S(2)}) collective-permute-start(bf16[528,256]{1,0:T(8,128)(2,1)S(1)} %slice.29), channel_id=1, source_target_pairs={{0,1},{1,0},{2,3},{3,2},{4,5},{5,4},{6,7},{7,6},{8,9},{9,8},{10,11... | collective-permute-start | bytes 811016 | tf_op jit(solution)/shard_map/ppermute | solution.py:71
  29.2 13.3 %collective-permute-start.10 = (bf16[528,256]{1,0:T(8,128)(2,1)S(1)}, bf16[528,256]{1,0:T(8,128)(2,1)S(1)}, u32[]{:S(2)}, u32[]{:S(2)}) collective-permute-start(bf16[528,256]{1,0:T(8,128)(2,1)S(1)} %slice.28), channel_id=1, source_target_pairs={{0,17},{1,16},{2,19},{3,18},{4,21},{5,20},{6,23},{7,22},{8,25},{9,... | collective-permute-start | bytes 811016 | tf_op jit(solution)/shard_map/ppermute | solution.py:71
  32.1 10.0 %collective-permute-start.14 = (bf16[2,128,512]{2,1,0:T(8,128)(2,1)S(1)}, bf16[2,128,512]{2,1,0:T(8,128)(2,1)S(1)}, u32[]{:S(2)}, u32[]{:S(2)}) collective-permute-start(bf16[2,128,512]{2,1,0:T(8,128)(2,1)S(1)} %get-tuple-element.86), channel_id=1, source_target_pairs={{0,16},{8,24},{16,0},{24,8},{1,17},{9,25},{17,1},{25,9},{2,18},{10... | collective-permute-start | bytes 786440 | tf_op jit(solution)/shard_map/ppermute | solution.py:50
  33.0 9.1 %collective-permute-start.13 = (bf16[1,512,256]{2,1,0:T(8,128)(2,1)S(1)}, bf16[1,512,256]{2,1,0:T(8,128)(2,1)S(1)}, u32[]{:S(2)}, u32[]{:S(2)}) collective-permute-start(bf16[1,512,256]{2,1,0:T(8,128)(2,1)S(1)} %slice.31), channel_id=1, source_target_pairs={{0,2},{1,3},{2,0},{3,1},{4,6},{5,7},{6,4},{7,5},{8,10},{9,11},{10,... | collective-permute-start | bytes 786440 | tf_op jit(solution)/shard_map/ppermute | solution.py:62
  34.7 7.7 %collective-permute-start.12 = (bf16[1,512,256]{2,1,0:T(8,128)(2,1)S(1)}, bf16[1,512,256]{2,1,0:T(8,128)(2,1)S(1)}, u32[]{:S(2)}, u32[]{:S(2)}) collective-permute-start(bf16[1,512,256]{2,1,0:T(8,128)(2,1)S(1)} %slice.30), channel_id=1, source_target_pairs={{0,6},{1,7},{2,4},{3,5},{4,2},{5,3},{6,0},{7,1},{8,14},{9,15},{10,... | collective-permute-start | bytes 786440 | tf_op jit(solution)/shard_map/ppermute | solution.py:62
  43.8 2.4 %collective-permute-start.15 = (bf16[768,512]{1,0:T(8,128)(2,1)S(1)}, bf16[768,512]{1,0:T(8,128)(2,1)S(1)}, u32[]{:S(2)}, u32[]{:S(2)}) collective-permute-start(bf16[768,512]{1,0:T(8,128)(2,1)S(1)} %get-tuple-element.91), channel_id=1, source_target_pairs={{0,8},{8,0},{16,24},{24,16},{1,9},{9,1},{17,25},{25,17},{2,10},{10... | collective-permute-start | bytes 2359304 | tf_op jit(solution)/shard_map/ppermute | solution.py:50
  46.2 7.3 %collective-permute-start.16 = (bf16[4096,256]{1,0:T(8,128)(2,1)S(1)}, bf16[4096,256]{1,0:T(8,128)(2,1)S(1)}, u32[]{:S(2)}, u32[]{:S(2)}) collective-permute-start(bf16[4096,256]{1,0:T(8,128)(2,1)S(1)} %get-tuple-element.95), channel_id=1, source_target_pairs={{0,8},{8,0},{16,24},{24,16},{1,9},{9,1},{17,25},{25,17},{2,10},{10... | collective-permute-start | bytes 6291464 | tf_op jit(solution)/shard_map/ppermute | solution.py:50
  50.1 4.0 %collective-permute-start.17 = (bf16[2304,256]{1,0:T(8,128)(2,1)S(1)}, bf16[2304,256]{1,0:T(8,128)(2,1)S(1)}, u32[]{:S(2)}, u32[]{:S(2)}) collective-permute-start(bf16[2304,256]{1,0:T(8,128)(2,1)S(1)} %get-tuple-element.99.refs_3_), channel_id=1, source_target_pairs={{0,8},{8,0},{16,24},{24,16},{1,9},{9,1},{17,25},{25,17},{2,10},{10... | collective-permute-start | bytes 3538952 | tf_op jit(solution)/shard_map/ppermute | solution.py:50
  50.7 15.5 %collective-permute-start.18 = (bf16[2,512,256]{2,1,0:T(8,128)(2,1)S(1)}, bf16[2,512,256]{2,1,0:T(8,128)(2,1)S(1)}, u32[]{:S(2)}, u32[]{:S(2)}) collective-permute-start(bf16[2,512,256]{2,1,0:T(8,128)(2,1)S(1)} %get-tuple-element.103), channel_id=1, source_target_pairs={{0,16},{8,24},{16,0},{24,8},{1,17},{9,25},{17,1},{25,9},{2,18},{10... | collective-permute-start | bytes 1572872 | tf_op jit(solution)/shard_map/ppermute | solution.py:50
  55.3 13.8 %collective-permute-start.20 = (bf16[2,256,512]{2,1,0:T(8,128)(2,1)S(1)}, bf16[2,256,512]{2,1,0:T(8,128)(2,1)S(1)}, u32[]{:S(2)}, u32[]{:S(2)}) collective-permute-start(bf16[2,256,512]{2,1,0:T(8,128)(2,1)S(1)} %get-tuple-element.110), channel_id=1, source_target_pairs={{0,32},{32,0},{64,96},{96,64},{1,33},{33,1},{65,97},{97,65},{2,34}... | collective-permute-start | bytes 1572872 | tf_op jit(solution)/shard_map/ppermute | solution.py:58
  56.9 14.6 %collective-permute-start.21 = (bf16[2,256,512]{2,1,0:T(8,128)(2,1)S(1)}, bf16[2,256,512]{2,1,0:T(8,128)(2,1)S(1)}, u32[]{:S(2)}, u32[]{:S(2)}) collective-permute-start(bf16[2,256,512]{2,1,0:T(8,128)(2,1)S(1)} %get-tuple-element.111), channel_id=1, source_target_pairs={{0,96},{32,64},{64,32},{96,0},{1,97},{33,65},{65,33},{97,1},{2,98}... | collective-permute-start | bytes 1572872 | tf_op jit(solution)/shard_map/ppermute | solution.py:58
  66.2 1.6 %collective-permute-start.19 = (bf16[1,512,256]{2,1,0:T(8,128)(2,1)S(1)}, bf16[1,512,256]{2,1,0:T(8,128)(2,1)S(1)}, u32[]{:S(2)}, u32[]{:S(2)}) collective-permute-start(bf16[1,512,256]{2,1,0:T(8,128)(2,1)S(1)} %slice.27), channel_id=1, source_target_pairs={{0,8},{8,0},{16,24},{24,16},{1,9},{9,1},{17,25},{25,17},{2,10},{10... | collective-permute-start | bytes 786440 | tf_op jit(solution)/shard_map/ppermute | solution.py:50
  71.7 8.2 %collective-permute-start.22 = (bf16[256,512]{1,0:T(8,128)(2,1)S(1)}, bf16[256,512]{1,0:T(8,128)(2,1)S(1)}, u32[]{:S(2)}, u32[]{:S(2)}) collective-permute-start(bf16[256,512]{1,0:T(8,128)(2,1)S(1)} %get-tuple-element.116), channel_id=1, source_target_pairs={{0,96},{32,64},{64,32},{96,0},{1,97},{33,65},{65,33},{97,1},{2,98}... | collective-permute-start | bytes 786440 | tf_op jit(solution)/shard_map/ppermute | solution.py:58
  73.9 6.6 %collective-permute-start.23 = (bf16[256,512]{1,0:T(8,128)(2,1)S(1)}, bf16[256,512]{1,0:T(8,128)(2,1)S(1)}, u32[]{:S(2)}, u32[]{:S(2)}) collective-permute-start(bf16[256,512]{1,0:T(8,128)(2,1)S(1)} %get-tuple-element.117), channel_id=1, source_target_pairs={{0,32},{32,0},{64,96},{96,64},{1,33},{33,1},{65,97},{97,65},{2,34}... | collective-permute-start | bytes 786440 | tf_op jit(solution)/shard_map/ppermute | solution.py:58
  73.9 12.2 %collective-permute-start.24 = (bf16[2,512,256]{2,1,0:T(8,128)(2,1)S(1)}, bf16[2,512,256]{2,1,0:T(8,128)(2,1)S(1)}, u32[]{:S(2)}, u32[]{:S(2)}) collective-permute-start(bf16[2,512,256]{2,1,0:T(8,128)(2,1)S(1)} %get-tuple-element.124), channel_id=1, source_target_pairs={{0,2},{1,3},{2,0},{3,1},{4,6},{5,7},{6,4},{7,5},{8,10},{9,11},{10,... | collective-permute-start | bytes 1572872 | tf_op jit(solution)/shard_map/ppermute | solution.py:62
  74.9 13.7 %collective-permute-start.25 = (bf16[2,512,256]{2,1,0:T(8,128)(2,1)S(1)}, bf16[2,512,256]{2,1,0:T(8,128)(2,1)S(1)}, u32[]{:S(2)}, u32[]{:S(2)}) collective-permute-start(bf16[2,512,256]{2,1,0:T(8,128)(2,1)S(1)} %get-tuple-element.125), channel_id=1, source_target_pairs={{0,6},{1,7},{2,4},{3,5},{4,2},{5,3},{6,0},{7,1},{8,14},{9,15},{10,... | collective-permute-start | bytes 1572872 | tf_op jit(solution)/shard_map/ppermute | solution.py:62
  80.6 18.0 %collective-permute-start.30 = (bf16[640,512]{1,0:T(8,128)(2,1)S(1)}, bf16[640,512]{1,0:T(8,128)(2,1)S(1)}, u32[]{:S(2)}, u32[]{:S(2)}) collective-permute-start(bf16[640,512]{1,0:T(8,128)(2,1)S(1)} %get-tuple-element.136), channel_id=1, source_target_pairs={{0,16},{8,24},{16,0},{24,8},{1,17},{9,25},{17,1},{25,9},{2,18},{10... | collective-permute-start | bytes 1966088 | tf_op jit(solution)/shard_map/ppermute | solution.py:50
  83.6 11.6 %collective-permute-start.26 = (bf16[2,256,512]{2,1,0:T(8,128)(2,1)S(1)}, bf16[2,256,512]{2,1,0:T(8,128)(2,1)S(1)}, u32[]{:S(2)}, u32[]{:S(2)}) collective-permute-start(bf16[2,256,512]{2,1,0:T(8,128)(2,1)S(1)} %get-tuple-element.129), channel_id=1, source_target_pairs={{0,32},{32,0},{64,96},{96,64},{1,33},{33,1},{65,97},{97,65},{2,34}... | collective-permute-start | bytes 1572872 | tf_op jit(solution)/shard_map/ppermute | solution.py:58
  83.9 12.8 %collective-permute-start.27 = (bf16[2,256,512]{2,1,0:T(8,128)(2,1)S(1)}, bf16[2,256,512]{2,1,0:T(8,128)(2,1)S(1)}, u32[]{:S(2)}, u32[]{:S(2)}) collective-permute-start(bf16[2,256,512]{2,1,0:T(8,128)(2,1)S(1)} %get-tuple-element.130), channel_id=1, source_target_pairs={{0,96},{32,64},{64,32},{96,0},{1,97},{33,65},{65,33},{97,1},{2,98}... | collective-permute-start | bytes 1572872 | tf_op jit(solution)/shard_map/ppermute | solution.py:58
  88.8 9.8 %collective-permute-start.28 = (bf16[512,256]{1,0:T(8,128)(2,1)S(1)}, bf16[512,256]{1,0:T(8,128)(2,1)S(1)}, u32[]{:S(2)}, u32[]{:S(2)}) collective-permute-start(bf16[512,256]{1,0:T(8,128)(2,1)S(1)} %get-tuple-element.134), channel_id=1, source_target_pairs={{0,6},{1,7},{2,4},{3,5},{4,2},{5,3},{6,0},{7,1},{8,14},{9,15},{10,... | collective-permute-start | bytes 786440 | tf_op jit(solution)/shard_map/ppermute | solution.py:62
  90.9 7.7 %collective-permute-start.29 = (bf16[512,256]{1,0:T(8,128)(2,1)S(1)}, bf16[512,256]{1,0:T(8,128)(2,1)S(1)}, u32[]{:S(2)}, u32[]{:S(2)}) collective-permute-start(bf16[512,256]{1,0:T(8,128)(2,1)S(1)} %get-tuple-element.135), channel_id=1, source_target_pairs={{0,2},{1,3},{2,0},{3,1},{4,6},{5,7},{6,4},{7,5},{8,10},{9,11},{10,... | collective-permute-start | bytes 786440 | tf_op jit(solution)/shard_map/ppermute | solution.py:62
  96.8 7.7 %collective-permute-start.31 = (bf16[256,512]{1,0:T(8,128)(2,1)S(1)}, bf16[256,512]{1,0:T(8,128)(2,1)S(1)}, u32[]{:S(2)}, u32[]{:S(2)}) collective-permute-start(bf16[256,512]{1,0:T(8,128)(2,1)S(1)} %get-tuple-element.140), channel_id=1, source_target_pairs={{0,96},{32,64},{64,32},{96,0},{1,97},{33,65},{65,33},{97,1},{2,98}... | collective-permute-start | bytes 786440 | tf_op jit(solution)/shard_map/ppermute | solution.py:58
  98.4 6.4 %collective-permute-start.32 = (bf16[256,512]{1,0:T(8,128)(2,1)S(1)}, bf16[256,512]{1,0:T(8,128)(2,1)S(1)}, u32[]{:S(2)}, u32[]{:S(2)}) collective-permute-start(bf16[256,512]{1,0:T(8,128)(2,1)S(1)} %get-tuple-element.141), channel_id=1, source_target_pairs={{0,32},{32,0},{64,96},{96,64},{1,33},{33,1},{65,97},{97,65},{2,34}... | collective-permute-start | bytes 786440 | tf_op jit(solution)/shard_map/ppermute | solution.py:58
  98.7 7.2 %collective-permute-start.33 = (bf16[512,256]{1,0:T(8,128)(2,1)S(1)}, bf16[512,256]{1,0:T(8,128)(2,1)S(1)}, u32[]{:S(2)}, u32[]{:S(2)}) collective-permute-start(bf16[512,256]{1,0:T(8,128)(2,1)S(1)} %get-tuple-element.146), channel_id=1, source_target_pairs={{0,1},{1,0},{2,3},{3,2},{4,5},{5,4},{6,7},{7,6},{8,9},{9,8},{10,11... | collective-permute-start | bytes 786440 | tf_op jit(solution)/shard_map/ppermute | solution.py:54

commit v6 on v5

--- a/solution.py
+++ b/solution.py
@@ -75,20 +75,15 @@
     return pl.ds(pl.multiple_of(which * 256, 256), 256)
 
 
-def join_y_body(idx, y0, y1, y2, y3, q, gc, ya, qg_own, qg_send, sems):
-    h = idx[H]
-    copies = []
-    for i, (layer, out) in enumerate(((h, qg_own), (1 - h, qg_send))):
-        for n, x in enumerate((q, gc)):
-            copies.append(pltpu.make_async_copy(x.at[layer, 0], out.at[n], sems.at[i, n]))
-    for copy in copies:
-        copy.start()
+def join_y_body(idx, y0, y1, y2, y3, q, gc, ya, qg_own, qg_send):
     ya[0, :256] = y0[...]
     ya[0, 256:] = y2[...]
     ya[1, :256] = y1[...]
     ya[1, 256:] = y3[...]
-    for copy in copies:
-        copy.wait()
+    for layer, out in ((idx[H], qg_own), (1 - idx[H], qg_send)):
+        out[:128] = q[layer, 0]
+        out[128:256] = gc[layer, 0]
+        out[256:] = jnp.zeros((16, 512), BF)
 
 
 def join_z_body(idx, z0, z1, z2, z3, zb):
@@ -152,7 +147,7 @@
             out[256:512, 256 * n : 256 * n + 256] = (part[256:] + more).astype(BF)
     for i, qg in enumerate((qg_own, qg_far)):
         for n in range(2):
-            send[512 + 128 * i : 640 + 128 * i, 256 * n : 256 * n + 256] = qg[n, :, cols(1 - c)]
+            send[512 + 128 * i : 640 + 128 * i, 256 * n : 256 * n + 256] = qg[128 * n : 128 * n + 128, cols(1 - c)]
 
 
 def turn_keep_body(idx, ya, az1, az20, az21, az3, by20, by21, es_in, out, es):
@@ -175,9 +170,9 @@
     mine = cols(idx[C])
     scale = DH ** (-0.5)
     blocks = [
-        (qg_own[0, :, mine], qg_own[1, :, mine], gq_own),
+        (qg_own[:128, mine], qg_own[128:256, mine], gq_own),
         (kv_oth[512:640, :256], kv_oth[512:640, 256:], g.at[2048:2176]),
-        (qg_far[0, :, mine], qg_far[1, :, mine], gq_far),
+        (qg_far[:128, mine], qg_far[128:256, mine], gq_far),
         (kv_oth[640:, :256], kv_oth[640:, 256:], g.at[2176:]),
     ]
     for n, (q, gc, _) in enumerate(blocks):
@@ -354,18 +349,17 @@
 def on_device(encoder_out, w_key, w_value, queries, grad_context):
     idx = jnp.zeros((8, 128), jnp.int32)
     c = lax.axis_index("seq") & 1
-    dma = pltpu.SemaphoreType.DMA
-    qg_block = arr((2, 128, 512))
+    qg_block = arr((272, 512))
 
     halves = jnp.stack([encoder_out[0, :, :256], encoder_out[0, :, 256:]])
     mine = lax.dynamic_index_in_dim(halves, c, 0, keepdims=False)
     other = lax.dynamic_index_in_dim(halves, 1 - c, 0, keepdims=False)
     from_y = [mine] + [swap_y(mine, m) for m in (1, 2, 3)]
     from_z = [other] + [swap_z(other, m) for m in (1, 2, 3)]
-    idx, zb = call(join_z_body, "join_z", [idx, *from_z], [arr((1040, 256))])
+    idx, zb = call(join_z_body, "join_z", [idx, *from_z], [arr((1040, 256))], flops=10_000_000_000)
     idx, ya, qg0, qg_send = call(
         join_y_body, "join_y", [idx, *from_y, queries, grad_context],
-        [arr((2, 512, 256)), qg_block, qg_block], [dma((2, 2))], hbm=(4, 5), flops=30_000_000_000,
+        [arr((2, 512, 256)), qg_block, qg_block], flops=30_000_000_000,
     )
     by1, by3 = swap_y(zb, 1), swap_y(zb, 3)
     az1, az3 = swap_z(ya, 1), swap_z(ya, 3)

time: 107 us -> 107 us (level)
  starting transfers between devices: 45.4 us -> 47.7 us
  Pallas kernels: 23.7 us -> 22.5 us
    ppermute x7, starting transfers between devices: 7.52 us -> 11.7 us  [swap_seq(): return lax.ppermute(x, 'seq', [(s, s ^ m) for s in range(4)])]
    ppermute x7, waiting for transfers between devices: 8.04 us -> 5.12 us  [swap_seq(): return lax.ppermute(x, 'seq', [(s, s ^ m) for s in range(4)])]
    ppermute x8, waiting for transfers between devices: 14.1 us -> 16.8 us  [swap_x(): return lax.ppermute(x, 'dp', [(d, d ^ m) for d in range(4)])]
    ppermute x7, starting transfers between devices: 11.5 us -> 9.05 us  [swap_y(): return lax.ppermute(x, ('seq', 'tensor'), pairs)]
    ppermute x11, waiting for transfers between devices: 6.27 us -> 4.84 us  [swap_z(): return lax.ppermute(x, 'tensor', [(t, t ^ 2 * m) for t in range(8)])]
    ppermute x11, starting transfers between devices: 15.9 us -> 17.2 us  [swap_z(): return lax.ppermute(x, 'tensor', [(t, t ^ 2 * m) for t in range(8)])]
    pallas_call x22, Pallas kernels: 23.7 us -> 22.5 us  [call(): pl.pallas_call(wrapped, in_specs=specs, out_specs=[ANY] + [VMEM] * len(ou...]
  transfers between devices with their start and end apart: 34 -> 34, of which waited for: 20 -> 19; matrix products, arithmetic and copies ran while one was open for 0% -> 0% of each run, Pallas kernels for 20% -> 19%
where the time goes in v6:
time: 107 us
  starting transfers between devices  47.7 us (45%)
  waiting for transfers between devices  34.7 us (32%)
  Pallas kernels  22.5 us (21%)
  local copies, waits for them, and re-layouts  1.11 us (1%)
    pallas_call x22, Pallas kernels, call(): pl.pallas_call(wrapped, in_specs=specs, out_specs=[ANY] + [VMEM] * len(ou...  22.5 us
    ppermute x11, starting transfers between devices, swap_z(): return lax.ppermute(x, 'tensor', [(t, t ^ 2 * m) for t in range(8)])  17.2 us
    ppermute x8, waiting for transfers between devices, swap_x(): return lax.ppermute(x, 'dp', [(d, d ^ m) for d in range(4)])  16.8 us
    ppermute x7, starting transfers between devices, swap_seq(): return lax.ppermute(x, 'seq', [(s, s ^ m) for s in range(4)])  11.7 us
    ppermute x8, starting transfers between devices, swap_x(): return lax.ppermute(x, 'dp', [(d, d ^ m) for d in range(4)])  9.1 us
    ppermute x7, starting transfers between devices, swap_y(): return lax.ppermute(x, ('seq', 'tensor'), pairs)  9.05 us
    ppermute x7, waiting for transfers between devices, swap_y(): return lax.ppermute(x, ('seq', 'tensor'), pairs)  7.93 us
    ppermute x7, waiting for transfers between devices, swap_seq(): return lax.ppermute(x, 'seq', [(s, s ^ m) for s in range(4)])  5.12 us
  transfers between devices with their start and end apart: 34, of which 19 were waited for; matrix products, arithmetic and copies ran while one was open for 0% of the time, Pallas kernels for 19%

profile of v6, /device:TPU:0, one launch (start us, length us, event | category | flops | bytes accessed | tf_op | source)
XLA Modules:
  0.0 107.1 jit_solution(15771488434487866864)
XLA Ops:
  0.6 1.0 fusion.4
  1.8 4.2 %collective-permute-start.2 = (bf16[256,256]{1,0:T(8,128)(2,1)S(1)}, bf16[256,256]{1,0:T(8,128)(2,1)S(1)}, u32[]{:S(2)}, u32[]{:S(2)}) collective-permute-start(bf16[256,256]{1,0:T(8,128)(2,1)S(1)} %get-tuple-element.151.refs_1_), channel_id=1, source_target_pairs={{0,6},{1,7},{2,4},{3,5},{4,2},{5,3},{6,0},{7,1},{8,14},{9,15},{10,... | collective-permute-start | bytes 393224 | tf_op jit(solution)/shard_map/ppermute | solution.py:62
  6.0 0.9 collective-permute-start
  6.9 3.0 %collective-permute-start.5 = (bf16[256,256]{1,0:T(8,128)(2,1)S(1)}, bf16[256,256]{1,0:T(8,128)(2,1)S(1)}, u32[]{:S(2)}, u32[]{:S(2)}) collective-permute-start(bf16[256,256]{1,0:T(8,128)(2,1)S(1)} %get-tuple-element.150.refs_1_), channel_id=1, source_target_pairs={{0,17},{1,16},{2,19},{3,18},{4,21},{5,20},{6,23},{7,22},{8,25},{9,... | collective-permute-start | bytes 393224 | tf_op jit(solution)/shard_map/ppermute | solution.py:71
  9.9 0.6 collective-permute-start.4
  10.5 1.0 collective-permute-done.2.refs_4_
  11.5 1.6 %collective-permute-start.3 = (bf16[256,256]{1,0:T(8,128)(2,1)S(1)}, bf16[256,256]{1,0:T(8,128)(2,1)S(1)}, u32[]{:S(2)}, u32[]{:S(2)}) collective-permute-start(bf16[256,256]{1,0:T(8,128)(2,1)S(1)} %get-tuple-element.150.refs_1_), channel_id=1, source_target_pairs={{0,1},{1,0},{2,3},{3,2},{4,5},{5,4},{6,7},{7,6},{8,9},{9,8},{10,11... | collective-permute-start | bytes 393224 | tf_op jit(solution)/shard_map/ppermute | solution.py:71
  13.1 0.7 collective-permute-done.1.refs_3_
  13.9 3.1 %collective-permute-start.7 = (bf16[1040,256]{1,0:T(8,128)(2,1)S(1)}, bf16[1040,256]{1,0:T(8,128)(2,1)S(1)}, u32[]{:S(2)}, u32[]{:S(2)}) collective-permute-start(bf16[1040,256]{1,0:T(8,128)(2,1)S(1)} %get-tuple-element.80.refs_4_), channel_id=1, source_target_pairs={{0,17},{1,16},{2,19},{3,18},{4,21},{5,20},{6,23},{7,22},{8,25},{9,... | collective-permute-start | bytes 1597448 | tf_op jit(solution)/shard_map/ppermute | solution.py:71
  17.3 3.1 %collective-permute-start.9 = (bf16[2,512,256]{2,1,0:T(8,128)(2,1)S(1)}, bf16[2,512,256]{2,1,0:T(8,128)(2,1)S(1)}, u32[]{:S(2)}, u32[]{:S(2)}) collective-permute-start(bf16[2,512,256]{2,1,0:T(8,128)(2,1)S(1)} %get-tuple-element.79.refs_3_.refs_1_), channel_id=1, source_target_pairs={{0,6},{1,7},{2,4},{3,5},{4,2},{5,3},{6,0},{7,1},{8,14},{9,15},{10,... | collective-permute-start | bytes 1572872 | tf_op jit(solution)/shard_map/ppermute | solution.py:62
  20.8 4.2 %collective-permute-start.14 = (bf16[272,512]{1,0:T(8,128)(2,1)S(1)}, bf16[272,512]{1,0:T(8,128)(2,1)S(1)}, u32[]{:S(2)}, u32[]{:S(2)}) collective-permute-start(bf16[272,512]{1,0:T(8,128)(2,1)S(1)} %get-tuple-element.86), channel_id=1, source_target_pairs={{0,16},{8,24},{16,0},{24,8},{1,17},{9,25},{17,1},{25,9},{2,18},{10... | collective-permute-start | bytes 835592 | tf_op jit(solution)/shard_map/ppermute | solution.py:50
  25.0 3.5 %collective-permute-done.7.refs_6_ = bf16[1040,256]{1,0:T(8,128)(2,1)S(1)} collective-permute-done((bf16[1040,256]{1,0:T(8,128)(2,1)S(1)}, bf16[1040,256]{1,0:T(8,128)(2,1)S(1)}, u32[]{:S(2)}, u32[]{:S(2)}) %collective-permute-start.7) | collective-permute-done | bytes 532512 | tf_op jit(solution)/shard_map/ppermute | solution.py:71
  28.6 3.4 %collective-permute-done.6.refs_5_ = bf16[1040,256]{1,0:T(8,128)(2,1)S(1)} collective-permute-done((bf16[1040,256]{1,0:T(8,128)(2,1)S(1)}, bf16[1040,256]{1,0:T(8,128)(2,1)S(1)}, u32[]{:S(2)}, u32[]{:S(2)}) %collective-permute-start.6) | collective-permute-done | bytes 532512 | tf_op jit(solution)/shard_map/ppermute | solution.py:71
  32.6 0.7 collective-permute-start.13
  33.3 3.1 %collective-permute-start.12 = (bf16[1,512,256]{2,1,0:T(8,128)(2,1)S(1)}, bf16[1,512,256]{2,1,0:T(8,128)(2,1)S(1)}, u32[]{:S(2)}, u32[]{:S(2)}) collective-permute-start(bf16[1,512,256]{2,1,0:T(8,128)(2,1)S(1)} %slice.30), channel_id=1, source_target_pairs={{0,6},{1,7},{2,4},{3,5},{4,2},{5,3},{6,0},{7,1},{8,14},{9,15},{10,... | collective-permute-start | bytes 786440 | tf_op jit(solution)/shard_map/ppermute | solution.py:62
  36.4 2.3 %project_first.1 = (s32[8,128]{1,0:T(8,128)S(1)}, f32[512,1024]{1,0:T(8,128)S(1)}, bf16[4096,256]{1,0:T(8,128)(2,1)S(1)}) custom-call(s32[8,128]{1,0:T(8,128)S(1)} %get-tuple-element.78.refs_0_, bf16[2,4096,512]{2,1,0:T(8,128)(2,1)S(1)} %bitcast.5, bf16[2,4096,512]{2,1,0:T(8,128)(2,1)S(1)} %bitcast.7, ...), custom_call_target="tpu_custom_call", output_to_operand_aliasing={{0}: (0, {})} | custom-call | flops 1 | bytes 1 | tf_op jit(solution)/shard_map/project_first/pallas_call | solution.py:36
  38.8 1.3 %project_next.1 = (s32[8,128]{1,0:T(8,128)S(1)}, f32[512,1024]{1,0:T(8,128)S(1)}) custom-call(s32[8,128]{1,0:T(8,128)S(1)} %get-tuple-element.81.refs_0_, bf16[2,4096,512]{2,1,0:T(8,128)(2,1)S(1)} %bitcast.5, bf16[2,4096,512]{2,1,0:T(8,128)(2,1)S(1)} %bitcast.7, f32[512,1024]{1,0:T(8,128)S(1)} %get-tuple-element.82.refs_3_, ...), custom_call_target="tpu_custom_call", output_to_operand_aliasing={{0}: (0, {})} | custom-call | flops 1 | bytes 1 | tf_op jit(solution)/shard_map/project_next/pallas_call | solution.py:36
  40.1 0.9 collective-permute-done.12.refs_6_.refs_3_
  40.9 1.0 collective-permute-done.10.refs_4_.refs_6_
  42.0 1.3 %project_last.1 = (s32[8,128]{1,0:T(8,128)S(1)}, bf16[768,512]{1,0:T(8,128)(2,1)S(1)}, bf16[512,512]{1,0:T(8,128)(2,1)S(1)}) custom-call(s32[8,128]{1,0:T(8,128)S(1)} %get-tuple-element.83.refs_0_, bf16[2,4096,512]{2,1,0:T(8,128)(2,1)S(1)} %bitcast.5, bf16[2,4096,512]{2,1,0:T(8,128)(2,1)S(1)} %bitcast.7, ...), custom_call_target="tpu_custom_call", output_to_operand_aliasing={{0}: (0, {})} | custom-call | flops 1 | bytes 1 | tf_op jit(solution)/shard_map/project_last/pallas_call | solution.py:36
  44.0 1.7 %collective-permute-done.15.refs_2_ = bf16[768,512]{1,0:T(8,128)(2,1)S(1)} collective-permute-done((bf16[768,512]{1,0:T(8,128)(2,1)S(1)}, bf16[768,512]{1,0:T(8,128)(2,1)S(1)}, u32[]{:S(2)}, u32[]{:S(2)}) %collective-permute-start.15) | collective-permute-done | bytes 786464 | tf_op jit(solution)/shard_map/ppermute | solution.py:50
  45.8 3.8 %attend.1 = (s32[8,128]{1,0:T(8,128)S(1)}, bf16[2304,256]{1,0:T(8,128)(2,1)S(1)}, bf16[2,512,256]{2,1,0:T(8,128)(2,1)S(1)}, bf16[128,256]{1,0:T(8,128)(2,1)S(1)}, bf16[128,256]{1,0:T(8,128)(2,1)S(1)}) custom-call(s32[8,128]{1,0:T(8,128)S(1)} %get-tuple-element.92.refs_0_, ...), custom_call_target="tpu_custom_call", output_to_operand_aliasing={{0}: (0, {})} | custom-call | flops 1 | bytes 1 | tf_op jit(solution)/shard_map/attend/pallas_call | solution.py:36
  50.1 3.6 %collective-permute-start.18 = (bf16[2,512,256]{2,1,0:T(8,128)(2,1)S(1)}, bf16[2,512,256]{2,1,0:T(8,128)(2,1)S(1)}, u32[]{:S(2)}, u32[]{:S(2)}) collective-permute-start(bf16[2,512,256]{2,1,0:T(8,128)(2,1)S(1)} %get-tuple-element.103), channel_id=1, source_target_pairs={{0,16},{8,24},{16,0},{24,8},{1,17},{9,25},{17,1},{25,9},{2,18},{10... | collective-permute-start | bytes 1572872 | tf_op jit(solution)/shard_map/ppermute | solution.py:50
  54.3 1.3 %weights_first.1 = (s32[8,128]{1,0:T(8,128)S(1)}, bf16[2,256,512]{2,1,0:T(8,128)(2,1)S(1)}, bf16[2,256,512]{2,1,0:T(8,128)(2,1)S(1)}) custom-call(s32[8,128]{1,0:T(8,128)S(1)} %get-tuple-element.96.refs_0_, bf16[8,256,512]{2,1,0:T(8,128)(2,1)S(1)} %get-tuple-element.97.refs_1_, ...), custom_call_target="tpu_custom_call", output_to_operand_aliasing={{0}: (0, {})} | custom-call | flops 1 | bytes 1 | tf_op jit(solution)/shard_map/weights_first/pallas_call | solution.py:36
  55.6 1.6 %collective-permute-start.20 = (bf16[2,256,512]{2,1,0:T(8,128)(2,1)S(1)}, bf16[2,256,512]{2,1,0:T(8,128)(2,1)S(1)}, u32[]{:S(2)}, u32[]{:S(2)}) collective-permute-start(bf16[2,256,512]{2,1,0:T(8,128)(2,1)S(1)} %get-tuple-element.110), channel_id=1, source_target_pairs={{0,32},{32,0},{64,96},{96,64},{1,33},{33,1},{65,97},{97,65},{2,34}... | collective-permute-start | bytes 1572872 | tf_op jit(solution)/shard_map/ppermute | solution.py:58
  57.2 2.1 %collective-permute-start.21 = (bf16[2,256,512]{2,1,0:T(8,128)(2,1)S(1)}, bf16[2,256,512]{2,1,0:T(8,128)(2,1)S(1)}, u32[]{:S(2)}, u32[]{:S(2)}) collective-permute-start(bf16[2,256,512]{2,1,0:T(8,128)(2,1)S(1)} %get-tuple-element.111), channel_id=1, source_target_pairs={{0,96},{32,64},{64,32},{96,0},{1,97},{33,65},{65,33},{97,1},{2,98}... | collective-permute-start | bytes 1572872 | tf_op jit(solution)/shard_map/ppermute | solution.py:58
  59.3 3.4 %weights_rest.1 = (s32[8,128]{1,0:T(8,128)S(1)}, bf16[2,256,512]{2,1,0:T(8,128)(2,1)S(1)}, bf16[2,256,512]{2,1,0:T(8,128)(2,1)S(1)}, f32[2,256,512]{2,1,0:T(8,12...) custom-call(s32[8,128]{1,0:T(8,128)S(1)} %get-tuple-element.100.refs, ...), custom_call_target="tpu_custom_call", output_to_operand_aliasing={{0}: (0, {})} | custom-call | flops 1 | bytes 1 | tf_op jit(solution)/shard_map/weights_rest/pallas_call | solution.py:36
  62.7 1.4 %encoder_own.1 = (s32[8,128]{1,0:T(8,128)S(1)}, f32[2,2,512,256]{3,2,1,0:T(8,128)S(1)}) custom-call(s32[8,128]{1,0:T(8,128)S(1)} %get-tuple-element.101.refs_0_, bf16[2,4096,512]{2,1,0:T(8,128)(2,1)S(1)} %bitcast.5, bf16[2,4096,512]{2,1,0:T(8,128)(2,1)S(1)} %bitcast.7, ...), custom_call_target="tpu_custom_call", output_to_operand_aliasing={{0}: (0, {})} | custom-call | flops 1 | bytes 1 | tf_op jit(solution)/shard_map/encoder_own/pallas_call | solution.py:36
  64.1 1.9 %collective-permute-done.18.refs_1_ = bf16[2,512,256]{2,1,0:T(8,128)(2,1)S(1)} collective-permute-done((bf16[2,512,256]{2,1,0:T(8,128)(2,1)S(1)}, bf16[2,512,256]{2,1,0:T(8,128)(2,1)S(1)}, u32[]{:S(2)}, u32[]{:S(2)}) %collective-permute-start.18) | collective-permute-done | bytes 524320 | tf_op jit(solution)/shard_map/ppermute | solution.py:50
  66.1 1.5 %collective-permute-done.19.refs_5_.refs_6_ = bf16[1,512,256]{2,1,0:T(8,128)(2,1)S(1)} collective-permute-done((bf16[1,512,256]{2,1,0:T(8,128)(2,1)S(1)}, bf16[1,512,256]{2,1,0:T(8,128)(2,1)S(1)}, u32[]{:S(2)}, u32[]{:S(2)}) %collective-permute-start.19) | collective-permute-done | bytes 262176 | tf_op jit(solution)/shard_map/ppermute | solution.py:50
  67.6 1.4 %encoder_sent.1 = (s32[8,128]{1,0:T(8,128)S(1)}, bf16[2,512,256]{2,1,0:T(8,128)(2,1)S(1)}, bf16[2,512,256]{2,1,0:T(8,128)(2,1)S(1)}) custom-call(s32[8,128]{1,0:T(8,128)S(1)} %get-tuple-element.104.refs_0_, bf16[2,4096,512]{2,1,0:T(8,128)(2,1)S(1)} %bitcast.5, bf16[2,4096,512]{2,1,0:T(8,128)(2,1)S(1)} %bitcast.7, ...), custom_call_target="tpu_custom_call", output_to_operand_aliasing={{0}: (0, {})} | custom-call | flops 1 | bytes 1 | tf_op jit(solution)/shard_map/encoder_sent/pallas_call | solution.py:36
  69.4 2.4 %collective-permute-done.21.refs_4_ = bf16[2,256,512]{2,1,0:T(8,128)(2,1)S(1)} collective-permute-done((bf16[2,256,512]{2,1,0:T(8,128)(2,1)S(1)}, bf16[2,256,512]{2,1,0:T(8,128)(2,1)S(1)}, u32[]{:S(2)}, u32[]{:S(2)}) %collective-permute-start.21) | collective-permute-done | bytes 524320 | tf_op jit(solution)/shard_map/ppermute | solution.py:58
  72.0 2.2 %collective-permute-start.22 = (bf16[256,512]{1,0:T(8,128)(2,1)S(1)}, bf16[256,512]{1,0:T(8,128)(2,1)S(1)}, u32[]{:S(2)}, u32[]{:S(2)}) collective-permute-start(bf16[256,512]{1,0:T(8,128)(2,1)S(1)} %get-tuple-element.116), channel_id=1, source_target_pairs={{0,96},{32,64},{64,32},{96,0},{1,97},{33,65},{65,33},{97,1},{2,98}... | collective-permute-start | bytes 786440 | tf_op jit(solution)/shard_map/ppermute | solution.py:58
  74.2 2.0 %collective-permute-start.25 = (bf16[2,512,256]{2,1,0:T(8,128)(2,1)S(1)}, bf16[2,512,256]{2,1,0:T(8,128)(2,1)S(1)}, u32[]{:S(2)}, u32[]{:S(2)}) collective-permute-start(bf16[2,512,256]{2,1,0:T(8,128)(2,1)S(1)} %get-tuple-element.125), channel_id=1, source_target_pairs={{0,6},{1,7},{2,4},{3,5},{4,2},{5,3},{6,0},{7,1},{8,14},{9,15},{10,... | collective-permute-start | bytes 1572872 | tf_op jit(solution)/shard_map/ppermute | solution.py:62
  76.2 2.4 %encoder_kept.1 = (s32[8,128]{1,0:T(8,128)S(1)}, f32[2,512,256]{2,1,0:T(8,128)S(1)}, f32[2,512,256]{2,1,0:T(8,128)S(1)}) custom-call(s32[8,128]{1,0:T(8,128)S(1)} %get-tuple-element.112.refs_0_, bf16[2,4096,512]{2,1,0:T(8,128)(2,1)S(1)} %bitcast.5, bf16[2,4096,512]{2,1,0:T(8,128)(2,1)S(1)} %bitcast.7, ...), custom_call_target="tpu_custom_call", output_to_operand_aliasing={{0}: (0, {})} | custom-call | flops 1 | bytes 1 | tf_op jit(solution)/shard_map/encoder_kept/pallas_call | solution.py:36
  78.6 1.6 %collective-permute-done.22.refs_3_ = bf16[256,512]{1,0:T(8,128)(2,1)S(1)} collective-permute-done((bf16[256,512]{1,0:T(8,128)(2,1)S(1)}, bf16[256,512]{1,0:T(8,128)(2,1)S(1)}, u32[]{:S(2)}, u32[]{:S(2)}) %collective-permute-start.22) | collective-permute-done | bytes 262176 | tf_op jit(solution)/shard_map/ppermute | solution.py:58
  80.9 3.0 %collective-permute-start.30 = (bf16[640,512]{1,0:T(8,128)(2,1)S(1)}, bf16[640,512]{1,0:T(8,128)(2,1)S(1)}, u32[]{:S(2)}, u32[]{:S(2)}) collective-permute-start(bf16[640,512]{1,0:T(8,128)(2,1)S(1)} %get-tuple-element.136), channel_id=1, source_target_pairs={{0,16},{8,24},{16,0},{24,8},{1,17},{9,25},{17,1},{25,9},{2,18},{10... | collective-permute-start | bytes 1966088 | tf_op jit(solution)/shard_map/ppermute | solution.py:50
  84.1 1.2 %collective-permute-start.27 = (bf16[2,256,512]{2,1,0:T(8,128)(2,1)S(1)}, bf16[2,256,512]{2,1,0:T(8,128)(2,1)S(1)}, u32[]{:S(2)}, u32[]{:S(2)}) collective-permute-start(bf16[2,256,512]{2,1,0:T(8,128)(2,1)S(1)} %get-tuple-element.130), channel_id=1, source_target_pairs={{0,96},{32,64},{64,32},{96,0},{1,97},{33,65},{65,33},{97,1},{2,98}... | collective-permute-start | bytes 1572872 | tf_op jit(solution)/shard_map/ppermute | solution.py:58
  85.4 1.0 collective-permute-done.24.refs_3_
  86.4 1.2 %collective-permute-done.25.refs_4_ = bf16[2,512,256]{2,1,0:T(8,128)(2,1)S(1)} collective-permute-done((bf16[2,512,256]{2,1,0:T(8,128)(2,1)S(1)}, bf16[2,512,256]{2,1,0:T(8,128)(2,1)S(1)}, u32[]{:S(2)}, u32[]{:S(2)}) %collective-permute-start.25) | collective-permute-done | bytes 524320 | tf_op jit(solution)/shard_map/ppermute | solution.py:62
  87.8 2.6 %collective-permute-start.28 = (bf16[512,256]{1,0:T(8,128)(2,1)S(1)}, bf16[512,256]{1,0:T(8,128)(2,1)S(1)}, u32[]{:S(2)}, u32[]{:S(2)}) collective-permute-start(bf16[512,256]{1,0:T(8,128)(2,1)S(1)} %get-tuple-element.134), channel_id=1, source_target_pairs={{0,6},{1,7},{2,4},{3,5},{4,2},{5,3},{6,0},{7,1},{8,14},{9,15},{10,... | collective-permute-start | bytes 786440 | tf_op jit(solution)/shard_map/ppermute | solution.py:62
  90.4 5.0 %collective-permute-done.26.refs_3_ = bf16[2,256,512]{2,1,0:T(8,128)(2,1)S(1)} collective-permute-done((bf16[2,256,512]{2,1,0:T(8,128)(2,1)S(1)}, bf16[2,256,512]{2,1,0:T(8,128)(2,1)S(1)}, u32[]{:S(2)}, u32[]{:S(2)}) %collective-permute-start.26) | collective-permute-done | bytes 524320 | tf_op jit(solution)/shard_map/ppermute | solution.py:58
  95.4 1.5 %collective-permute-done.27.refs_4_ = bf16[2,256,512]{2,1,0:T(8,128)(2,1)S(1)} collective-permute-done((bf16[2,256,512]{2,1,0:T(8,128)(2,1)S(1)}, bf16[2,256,512]{2,1,0:T(8,128)(2,1)S(1)}, u32[]{:S(2)}, u32[]{:S(2)}) %collective-permute-start.27) | collective-permute-done | bytes 524320 | tf_op jit(solution)/shard_map/ppermute | solution.py:58
  97.1 1.6 %collective-permute-start.31 = (bf16[256,512]{1,0:T(8,128)(2,1)S(1)}, bf16[256,512]{1,0:T(8,128)(2,1)S(1)}, u32[]{:S(2)}, u32[]{:S(2)}) collective-permute-start(bf16[256,512]{1,0:T(8,128)(2,1)S(1)} %get-tuple-element.140), channel_id=1, source_target_pairs={{0,96},{32,64},{64,32},{96,0},{1,97},{33,65},{65,33},{97,1},{2,98}... | collective-permute-start | bytes 786440 | tf_op jit(solution)/shard_map/ppermute | solution.py:58
  99.0 0.8 collective-permute-start.33
  99.7 5.0 %collective-permute-done.31.refs_3_ = bf16[256,512]{1,0:T(8,128)(2,1)S(1)} collective-permute-done((bf16[256,512]{1,0:T(8,128)(2,1)S(1)}, bf16[256,512]{1,0:T(8,128)(2,1)S(1)}, u32[]{:S(2)}, u32[]{:S(2)}) %collective-permute-start.31) | collective-permute-done | bytes 262176 | tf_op jit(solution)/shard_map/ppermute | solution.py:58
  105.1 1.2 %finish_weights.1 = (s32[8,128]{1,0:T(8,128)S(1)}, bf16[2,256,512]{2,1,0:T(8,128)(2,1)}, bf16[2,256,512]{2,1,0:T(8,128)(2,1)}, bf16[2,1,128,512]{3,2,1,0:T(8,128)(2,1)}) custom-call(s32[8,128]{1,0:T(8,128)S(1)} %get-tuple-element.137.refs_0_, f32[256,512]{1,0:T(8,128)S(1)} %get-tuple-element.138.refs_1_, ...), custom_call_target="tpu_custom_call", output_to_operand_aliasing={{0}: (0, {})} | custom-call | flops 1 | bytes 1 | tf_op jit(solution)/shard_map/finish_weights/pallas_call | solution.py:36
  106.2 0.8 finish_encoder.1
  (64 shorter events, 6.1 us)
Async XLA Ops:
  1.8 9.8 %collective-permute-start.2 = (bf16[256,256]{1,0:T(8,128)(2,1)S(1)}, bf16[256,256]{1,0:T(8,128)(2,1)S(1)}, u32[]{:S(2)}, u32[]{:S(2)}) collective-permute-start(bf16[256,256]{1,0:T(8,128)(2,1)S(1)} %get-tuple-element.151.refs_1_), channel_id=1, source_target_pairs={{0,6},{1,7},{2,4},{3,5},{4,2},{5,3},{6,0},{7,1},{8,14},{9,15},{10,... | collective-permute-start | bytes 393224 | tf_op jit(solution)/shard_map/ppermute | solution.py:62
  6.0 7.9 %collective-permute-start.1 = (bf16[256,256]{1,0:T(8,128)(2,1)S(1)}, bf16[256,256]{1,0:T(8,128)(2,1)S(1)}, u32[]{:S(2)}, u32[]{:S(2)}) collective-permute-start(bf16[256,256]{1,0:T(8,128)(2,1)S(1)} %get-tuple-element.151.refs_1_), channel_id=1, source_target_pairs={{0,4},{1,5},{2,6},{3,7},{4,0},{5,1},{6,2},{7,3},{8,12},{9,13},{10,... | collective-permute-start | bytes 393224 | tf_op jit(solution)/shard_map/ppermute | solution.py:62
  6.0 7.9 %collective-permute-start = (bf16[256,256]{1,0:T(8,128)(2,1)S(1)}, bf16[256,256]{1,0:T(8,128)(2,1)S(1)}, u32[]{:S(2)}, u32[]{:S(2)}) collective-permute-start(bf16[256,256]{1,0:T(8,128)(2,1)S(1)} %get-tuple-element.151.refs_1_), channel_id=1, source_target_pairs={{0,2},{1,3},{2,0},{3,1},{4,6},{5,7},{6,4},{7,5},{8,10},{9,11},{10,... | collective-permute-start | bytes 393224 | tf_op jit(solution)/shard_map/ppermute | solution.py:62
  6.9 10.2 %collective-permute-start.5 = (bf16[256,256]{1,0:T(8,128)(2,1)S(1)}, bf16[256,256]{1,0:T(8,128)(2,1)S(1)}, u32[]{:S(2)}, u32[]{:S(2)}) collective-permute-start(bf16[256,256]{1,0:T(8,128)(2,1)S(1)} %get-tuple-element.150.refs_1_), channel_id=1, source_target_pairs={{0,17},{1,16},{2,19},{3,18},{4,21},{5,20},{6,23},{7,22},{8,25},{9,... | collective-permute-start | bytes 393224 | tf_op jit(solution)/shard_map/ppermute | solution.py:71
  9.9 7.2 %collective-permute-start.4 = (bf16[256,256]{1,0:T(8,128)(2,1)S(1)}, bf16[256,256]{1,0:T(8,128)(2,1)S(1)}, u32[]{:S(2)}, u32[]{:S(2)}) collective-permute-start(bf16[256,256]{1,0:T(8,128)(2,1)S(1)} %get-tuple-element.150.refs_1_), channel_id=1, source_target_pairs={{0,16},{1,17},{2,18},{3,19},{4,20},{5,21},{6,22},{7,23},{8,24},{9,... | collective-permute-start | bytes 393224 | tf_op jit(solution)/shard_map/ppermute | solution.py:71
  11.5 5.6 %collective-permute-start.3 = (bf16[256,256]{1,0:T(8,128)(2,1)S(1)}, bf16[256,256]{1,0:T(8,128)(2,1)S(1)}, u32[]{:S(2)}, u32[]{:S(2)}) collective-permute-start(bf16[256,256]{1,0:T(8,128)(2,1)S(1)} %get-tuple-element.150.refs_1_), channel_id=1, source_target_pairs={{0,1},{1,0},{2,3},{3,2},{4,5},{5,4},{6,7},{7,6},{8,9},{9,8},{10,11... | collective-permute-start | bytes 393224 | tf_op jit(solution)/shard_map/ppermute | solution.py:71
  13.8 3.3 %copy-start = (bf16[2,1,128,512]{3,2,1,0:T(8,128)(2,1)S(1)}, bf16[2,1,128,512]{3,2,1,0:T(8,128)(2,1)}, u32[]{:S(2)}) copy-start(bf16[2,1,128,512]{3,2,1,0:T(8,128)(2,1)} %refs_5_.1) | copy-start | bytes 786436
  13.8 3.3 %copy-start.1 = (bf16[2,1,128,512]{3,2,1,0:T(8,128)(2,1)S(1)}, bf16[2,1,128,512]{3,2,1,0:T(8,128)(2,1)}, u32[]{:S(2)}) copy-start(bf16[2,1,128,512]{3,2,1,0:T(8,128)(2,1)} %refs_6_.1) | copy-start | bytes 786436
  13.9 14.6 %collective-permute-start.7 = (bf16[1040,256]{1,0:T(8,128)(2,1)S(1)}, bf16[1040,256]{1,0:T(8,128)(2,1)S(1)}, u32[]{:S(2)}, u32[]{:S(2)}) collective-permute-start(bf16[1040,256]{1,0:T(8,128)(2,1)S(1)} %get-tuple-element.80.refs_4_), channel_id=1, source_target_pairs={{0,17},{1,16},{2,19},{3,18},{4,21},{5,20},{6,23},{7,22},{8,25},{9,... | collective-permute-start | bytes 1597448 | tf_op jit(solution)/shard_map/ppermute | solution.py:71
  17.0 15.0 %collective-permute-start.6 = (bf16[1040,256]{1,0:T(8,128)(2,1)S(1)}, bf16[1040,256]{1,0:T(8,128)(2,1)S(1)}, u32[]{:S(2)}, u32[]{:S(2)}) collective-permute-start(bf16[1040,256]{1,0:T(8,128)(2,1)S(1)} %get-tuple-element.80.refs_4_), channel_id=1, source_target_pairs={{0,1},{1,0},{2,3},{3,2},{4,5},{5,4},{6,7},{7,6},{8,9},{9,8},{10,11... | collective-permute-start | bytes 1597448 | tf_op jit(solution)/shard_map/ppermute | solution.py:71
  17.1 19.3 %slice-start = ((s8[8388608]{0:T(1024)(128)(4,1)}), s8[4194304]{0:T(1024)(128)(4,1)S(1)}, s32[]{:S(2)}) async-start(s8[8388608]{0:T(1024)(128)(4,1)} %bitcast.4), calls=%async_computation | async-start | bytes 8388608
  17.1 19.3 %slice-start.2 = ((s8[8388608]{0:T(1024)(128)(4,1)}), s8[4194304]{0:T(1024)(128)(4,1)S(1)}, s32[]{:S(2)}) async-start(s8[8388608]{0:T(1024)(128)(4,1)} %bitcast.6), calls=%async_computation.2 | async-start | bytes 8388608
  17.2 19.2 %slice-start.1 = ((s8[8388608]{0:T(1024)(128)(4,1)}), s8[4194304]{0:T(1024)(128)(4,1)S(1)}, s32[]{:S(2)}) async-start(s8[8388608]{0:T(1024)(128)(4,1)} %bitcast.4), calls=%async_computation.1 | async-start | bytes 8388608
  17.2 19.2 %slice-start.3 = ((s8[8388608]{0:T(1024)(128)(4,1)}), s8[4194304]{0:T(1024)(128)(4,1)S(1)}, s32[]{:S(2)}) async-start(s8[8388608]{0:T(1024)(128)(4,1)} %bitcast.6), calls=%async_computation.3 | async-start | bytes 8388608
  17.3 15.3 %collective-permute-start.9 = (bf16[2,512,256]{2,1,0:T(8,128)(2,1)S(1)}, bf16[2,512,256]{2,1,0:T(8,128)(2,1)S(1)}, u32[]{:S(2)}, u32[]{:S(2)}) collective-permute-start(bf16[2,512,256]{2,1,0:T(8,128)(2,1)S(1)} %get-tuple-element.79.refs_3_.refs_1_), channel_id=1, source_target_pairs={{0,6},{1,7},{2,4},{3,5},{4,2},{5,3},{6,0},{7,1},{8,14},{9,15},{10,... | collective-permute-start | bytes 1572872 | tf_op jit(solution)/shard_map/ppermute | solution.py:62
  20.4 12.8 %collective-permute-start.8 = (bf16[2,512,256]{2,1,0:T(8,128)(2,1)S(1)}, bf16[2,512,256]{2,1,0:T(8,128)(2,1)S(1)}, u32[]{:S(2)}, u32[]{:S(2)}) collective-permute-start(bf16[2,512,256]{2,1,0:T(8,128)(2,1)S(1)} %get-tuple-element.79.refs_3_.refs_1_), channel_id=1, source_target_pairs={{0,2},{1,3},{2,0},{3,1},{4,6},{5,7},{6,4},{7,5},{8,10},{9,11},{10,... | collective-permute-start | bytes 1572872 | tf_op jit(solution)/shard_map/ppermute | solution.py:62
  20.8 19.2 %collective-permute-start.14 = (bf16[272,512]{1,0:T(8,128)(2,1)S(1)}, bf16[272,512]{1,0:T(8,128)(2,1)S(1)}, u32[]{:S(2)}, u32[]{:S(2)}) collective-permute-start(bf16[272,512]{1,0:T(8,128)(2,1)S(1)} %get-tuple-element.86), channel_id=1, source_target_pairs={{0,16},{8,24},{16,0},{24,8},{1,17},{9,25},{17,1},{25,9},{2,18},{10... | collective-permute-start | bytes 835592 | tf_op jit(solution)/shard_map/ppermute | solution.py:50
  28.5 12.4 %collective-permute-start.11 = (bf16[528,256]{1,0:T(8,128)(2,1)S(1)}, bf16[528,256]{1,0:T(8,128)(2,1)S(1)}, u32[]{:S(2)}, u32[]{:S(2)}) collective-permute-start(bf16[528,256]{1,0:T(8,128)(2,1)S(1)} %slice.29), channel_id=1, source_target_pairs={{0,1},{1,0},{2,3},{3,2},{4,5},{5,4},{6,7},{7,6},{8,9},{9,8},{10,11... | collective-permute-start | bytes 811016 | tf_op jit(solution)/shard_map/ppermute | solution.py:71
  32.0 9.9 %collective-permute-start.10 = (bf16[528,256]{1,0:T(8,128)(2,1)S(1)}, bf16[528,256]{1,0:T(8,128)(2,1)S(1)}, u32[]{:S(2)}, u32[]{:S(2)}) collective-permute-start(bf16[528,256]{1,0:T(8,128)(2,1)S(1)} %slice.28), channel_id=1, source_target_pairs={{0,17},{1,16},{2,19},{3,18},{4,21},{5,20},{6,23},{7,22},{8,25},{9,... | collective-permute-start | bytes 811016 | tf_op jit(solution)/shard_map/ppermute | solution.py:71
  32.6 7.5 %collective-permute-start.13 = (bf16[1,512,256]{2,1,0:T(8,128)(2,1)S(1)}, bf16[1,512,256]{2,1,0:T(8,128)(2,1)S(1)}, u32[]{:S(2)}, u32[]{:S(2)}) collective-permute-start(bf16[1,512,256]{2,1,0:T(8,128)(2,1)S(1)} %slice.31), channel_id=1, source_target_pairs={{0,2},{1,3},{2,0},{3,1},{4,6},{5,7},{6,4},{7,5},{8,10},{9,11},{10,... | collective-permute-start | bytes 786440 | tf_op jit(solution)/shard_map/ppermute | solution.py:62
  33.3 7.7 %collective-permute-start.12 = (bf16[1,512,256]{2,1,0:T(8,128)(2,1)S(1)}, bf16[1,512,256]{2,1,0:T(8,128)(2,1)S(1)}, u32[]{:S(2)}, u32[]{:S(2)}) collective-permute-start(bf16[1,512,256]{2,1,0:T(8,128)(2,1)S(1)} %slice.30), channel_id=1, source_target_pairs={{0,6},{1,7},{2,4},{3,5},{4,2},{5,3},{6,0},{7,1},{8,14},{9,15},{10,... | collective-permute-start | bytes 786440 | tf_op jit(solution)/shard_map/ppermute | solution.py:62
  43.3 2.4 %collective-permute-start.15 = (bf16[768,512]{1,0:T(8,128)(2,1)S(1)}, bf16[768,512]{1,0:T(8,128)(2,1)S(1)}, u32[]{:S(2)}, u32[]{:S(2)}) collective-permute-start(bf16[768,512]{1,0:T(8,128)(2,1)S(1)} %get-tuple-element.91), channel_id=1, source_target_pairs={{0,8},{8,0},{16,24},{24,16},{1,9},{9,1},{17,25},{25,17},{2,10},{10... | collective-permute-start | bytes 2359304 | tf_op jit(solution)/shard_map/ppermute | solution.py:50
  45.6 8.1 %collective-permute-start.16 = (bf16[4096,256]{1,0:T(8,128)(2,1)S(1)}, bf16[4096,256]{1,0:T(8,128)(2,1)S(1)}, u32[]{:S(2)}, u32[]{:S(2)}) collective-permute-start(bf16[4096,256]{1,0:T(8,128)(2,1)S(1)} %get-tuple-element.95), channel_id=1, source_target_pairs={{0,8},{8,0},{16,24},{24,16},{1,9},{9,1},{17,25},{25,17},{2,10},{10... | collective-permute-start | bytes 6291464 | tf_op jit(solution)/shard_map/ppermute | solution.py:50
  49.5 4.8 %collective-permute-start.17 = (bf16[2304,256]{1,0:T(8,128)(2,1)S(1)}, bf16[2304,256]{1,0:T(8,128)(2,1)S(1)}, u32[]{:S(2)}, u32[]{:S(2)}) collective-permute-start(bf16[2304,256]{1,0:T(8,128)(2,1)S(1)} %get-tuple-element.99.refs_3_), channel_id=1, source_target_pairs={{0,8},{8,0},{16,24},{24,16},{1,9},{9,1},{17,25},{25,17},{2,10},{10... | collective-permute-start | bytes 3538952 | tf_op jit(solution)/shard_map/ppermute | solution.py:50
  50.1 15.9 %collective-permute-start.18 = (bf16[2,512,256]{2,1,0:T(8,128)(2,1)S(1)}, bf16[2,512,256]{2,1,0:T(8,128)(2,1)S(1)}, u32[]{:S(2)}, u32[]{:S(2)}) collective-permute-start(bf16[2,512,256]{2,1,0:T(8,128)(2,1)S(1)} %get-tuple-element.103), channel_id=1, source_target_pairs={{0,16},{8,24},{16,0},{24,8},{1,17},{9,25},{17,1},{25,9},{2,18},{10... | collective-permute-start | bytes 1572872 | tf_op jit(solution)/shard_map/ppermute | solution.py:50
  55.6 13.8 %collective-permute-start.20 = (bf16[2,256,512]{2,1,0:T(8,128)(2,1)S(1)}, bf16[2,256,512]{2,1,0:T(8,128)(2,1)S(1)}, u32[]{:S(2)}, u32[]{:S(2)}) collective-permute-start(bf16[2,256,512]{2,1,0:T(8,128)(2,1)S(1)} %get-tuple-element.110), channel_id=1, source_target_pairs={{0,32},{32,0},{64,96},{96,64},{1,33},{33,1},{65,97},{97,65},{2,34}... | collective-permute-start | bytes 1572872 | tf_op jit(solution)/shard_map/ppermute | solution.py:58
  57.2 14.6 %collective-permute-start.21 = (bf16[2,256,512]{2,1,0:T(8,128)(2,1)S(1)}, bf16[2,256,512]{2,1,0:T(8,128)(2,1)S(1)}, u32[]{:S(2)}, u32[]{:S(2)}) collective-permute-start(bf16[2,256,512]{2,1,0:T(8,128)(2,1)S(1)} %get-tuple-element.111), channel_id=1, source_target_pairs={{0,96},{32,64},{64,32},{96,0},{1,97},{33,65},{65,33},{97,1},{2,98}... | collective-permute-start | bytes 1572872 | tf_op jit(solution)/shard_map/ppermute | solution.py:58
  66.0 1.6 %collective-permute-start.19 = (bf16[1,512,256]{2,1,0:T(8,128)(2,1)S(1)}, bf16[1,512,256]{2,1,0:T(8,128)(2,1)S(1)}, u32[]{:S(2)}, u32[]{:S(2)}) collective-permute-start(bf16[1,512,256]{2,1,0:T(8,128)(2,1)S(1)} %slice.27), channel_id=1, source_target_pairs={{0,8},{8,0},{16,24},{24,16},{1,9},{9,1},{17,25},{25,17},{2,10},{10... | collective-permute-start | bytes 786440 | tf_op jit(solution)/shard_map/ppermute | solution.py:50
  72.0 8.2 %collective-permute-start.22 = (bf16[256,512]{1,0:T(8,128)(2,1)S(1)}, bf16[256,512]{1,0:T(8,128)(2,1)S(1)}, u32[]{:S(2)}, u32[]{:S(2)}) collective-permute-start(bf16[256,512]{1,0:T(8,128)(2,1)S(1)} %get-tuple-element.116), channel_id=1, source_target_pairs={{0,96},{32,64},{64,32},{96,0},{1,97},{33,65},{65,33},{97,1},{2,98}... | collective-permute-start | bytes 786440 | tf_op jit(solution)/shard_map/ppermute | solution.py:58
  74.2 6.6 %collective-permute-start.23 = (bf16[256,512]{1,0:T(8,128)(2,1)S(1)}, bf16[256,512]{1,0:T(8,128)(2,1)S(1)}, u32[]{:S(2)}, u32[]{:S(2)}) collective-permute-start(bf16[256,512]{1,0:T(8,128)(2,1)S(1)} %get-tuple-element.117), channel_id=1, source_target_pairs={{0,32},{32,0},{64,96},{96,64},{1,33},{33,1},{65,97},{97,65},{2,34}... | collective-permute-start | bytes 786440 | tf_op jit(solution)/shard_map/ppermute | solution.py:58
  74.2 12.2 %collective-permute-start.24 = (bf16[2,512,256]{2,1,0:T(8,128)(2,1)S(1)}, bf16[2,512,256]{2,1,0:T(8,128)(2,1)S(1)}, u32[]{:S(2)}, u32[]{:S(2)}) collective-permute-start(bf16[2,512,256]{2,1,0:T(8,128)(2,1)S(1)} %get-tuple-element.124), channel_id=1, source_target_pairs={{0,2},{1,3},{2,0},{3,1},{4,6},{5,7},{6,4},{7,5},{8,10},{9,11},{10,... | collective-permute-start | bytes 1572872 | tf_op jit(solution)/shard_map/ppermute | solution.py:62
  74.2 13.4 %collective-permute-start.25 = (bf16[2,512,256]{2,1,0:T(8,128)(2,1)S(1)}, bf16[2,512,256]{2,1,0:T(8,128)(2,1)S(1)}, u32[]{:S(2)}, u32[]{:S(2)}) collective-permute-start(bf16[2,512,256]{2,1,0:T(8,128)(2,1)S(1)} %get-tuple-element.125), channel_id=1, source_target_pairs={{0,6},{1,7},{2,4},{3,5},{4,2},{5,3},{6,0},{7,1},{8,14},{9,15},{10,... | collective-permute-start | bytes 1572872 | tf_op jit(solution)/shard_map/ppermute | solution.py:62
  80.9 18.0 %collective-permute-start.30 = (bf16[640,512]{1,0:T(8,128)(2,1)S(1)}, bf16[640,512]{1,0:T(8,128)(2,1)S(1)}, u32[]{:S(2)}, u32[]{:S(2)}) collective-permute-start(bf16[640,512]{1,0:T(8,128)(2,1)S(1)} %get-tuple-element.136), channel_id=1, source_target_pairs={{0,16},{8,24},{16,0},{24,8},{1,17},{9,25},{17,1},{25,9},{2,18},{10... | collective-permute-start | bytes 1966088 | tf_op jit(solution)/shard_map/ppermute | solution.py:50
  83.9 11.6 %collective-permute-start.26 = (bf16[2,256,512]{2,1,0:T(8,128)(2,1)S(1)}, bf16[2,256,512]{2,1,0:T(8,128)(2,1)S(1)}, u32[]{:S(2)}, u32[]{:S(2)}) collective-permute-start(bf16[2,256,512]{2,1,0:T(8,128)(2,1)S(1)} %get-tuple-element.129), channel_id=1, source_target_pairs={{0,32},{32,0},{64,96},{96,64},{1,33},{33,1},{65,97},{97,65},{2,34}... | collective-permute-start | bytes 1572872 | tf_op jit(solution)/shard_map/ppermute | solution.py:58
  84.1 12.8 %collective-permute-start.27 = (bf16[2,256,512]{2,1,0:T(8,128)(2,1)S(1)}, bf16[2,256,512]{2,1,0:T(8,128)(2,1)S(1)}, u32[]{:S(2)}, u32[]{:S(2)}) collective-permute-start(bf16[2,256,512]{2,1,0:T(8,128)(2,1)S(1)} %get-tuple-element.130), channel_id=1, source_target_pairs={{0,96},{32,64},{64,32},{96,0},{1,97},{33,65},{65,33},{97,1},{2,98}... | collective-permute-start | bytes 1572872 | tf_op jit(solution)/shard_map/ppermute | solution.py:58
  87.8 11.1 %collective-permute-start.28 = (bf16[512,256]{1,0:T(8,128)(2,1)S(1)}, bf16[512,256]{1,0:T(8,128)(2,1)S(1)}, u32[]{:S(2)}, u32[]{:S(2)}) collective-permute-start(bf16[512,256]{1,0:T(8,128)(2,1)S(1)} %get-tuple-element.134), channel_id=1, source_target_pairs={{0,6},{1,7},{2,4},{3,5},{4,2},{5,3},{6,0},{7,1},{8,14},{9,15},{10,... | collective-permute-start | bytes 786440 | tf_op jit(solution)/shard_map/ppermute | solution.py:62
  90.4 8.4 %collective-permute-start.29 = (bf16[512,256]{1,0:T(8,128)(2,1)S(1)}, bf16[512,256]{1,0:T(8,128)(2,1)S(1)}, u32[]{:S(2)}, u32[]{:S(2)}) collective-permute-start(bf16[512,256]{1,0:T(8,128)(2,1)S(1)} %get-tuple-element.135), channel_id=1, source_target_pairs={{0,2},{1,3},{2,0},{3,1},{4,6},{5,7},{6,4},{7,5},{8,10},{9,11},{10,... | collective-permute-start | bytes 786440 | tf_op jit(solution)/shard_map/ppermute | solution.py:62
  97.1 7.7 %collective-permute-start.31 = (bf16[256,512]{1,0:T(8,128)(2,1)S(1)}, bf16[256,512]{1,0:T(8,128)(2,1)S(1)}, u32[]{:S(2)}, u32[]{:S(2)}) collective-permute-start(bf16[256,512]{1,0:T(8,128)(2,1)S(1)} %get-tuple-element.140), channel_id=1, source_target_pairs={{0,96},{32,64},{64,32},{96,0},{1,97},{33,65},{65,33},{97,1},{2,98}... | collective-permute-start | bytes 786440 | tf_op jit(solution)/shard_map/ppermute | solution.py:58
  98.7 6.4 %collective-permute-start.32 = (bf16[256,512]{1,0:T(8,128)(2,1)S(1)}, bf16[256,512]{1,0:T(8,128)(2,1)S(1)}, u32[]{:S(2)}, u32[]{:S(2)}) collective-permute-start(bf16[256,512]{1,0:T(8,128)(2,1)S(1)} %get-tuple-element.141), channel_id=1, source_target_pairs={{0,32},{32,0},{64,96},{96,64},{1,33},{33,1},{65,97},{97,65},{2,34}... | collective-permute-start | bytes 786440 | tf_op jit(solution)/shard_map/ppermute | solution.py:58
  99.0 7.2 %collective-permute-start.33 = (bf16[512,256]{1,0:T(8,128)(2,1)S(1)}, bf16[512,256]{1,0:T(8,128)(2,1)S(1)}, u32[]{:S(2)}, u32[]{:S(2)}) collective-permute-start(bf16[512,256]{1,0:T(8,128)(2,1)S(1)} %get-tuple-element.146), channel_id=1, source_target_pairs={{0,1},{1,0},{2,3},{3,2},{4,5},{5,4},{6,7},{7,6},{8,9},{9,8},{10,11... | collective-permute-start | bytes 786440 | tf_op jit(solution)/shard_map/ppermute | solution.py:54
